TPU v7x, 256 devices: a whole 4x4x8 slice. The times are simulated.
256 devices in a mesh: vid: 16 (over x, z_lo), aud: 8 (over y, z_hi), pair: 2 (over core).
Axes of the slice: x: 4, y: 4, z: 8 (z_hi: 2, z_lo: 4; z = z_hi * 4 + z_lo), core: 2. Of those that a mesh axis runs over, the one named last changes fastest.
Arguments:
- video_q: bfloat16 [2, 2048, 3072], P('pair', 'vid', 'aud'), may hold values from -200 to 200
- video_k: bfloat16 [2, 2048, 3072], P('pair', 'vid', 'aud'), may hold values from -7 to 7
- video_v: bfloat16 [2, 2048, 3072], P('pair', 'vid', 'aud'), may hold values from -6 to 6
- audio_q: bfloat16 [2, 1024, 3072], P('pair', 'aud'), may hold values from -200 to 200
- audio_k: bfloat16 [2, 1024, 3072], P('pair', 'aud'), may hold values from -7 to 7
- audio_v: bfloat16 [2, 1024, 3072], P('pair', 'aud'), may hold values from -6 to 6
- video_gate: float32 [3072], P('aud'), may hold values from 0.3 to 1.7
- audio_gate: float32 [3072], P('aud'), may hold values from 0.3 to 1.7
- audio_len: int32 [2], P('pair'), may hold values from 256 to 1024, as said below
- d_video_out: bfloat16 [2, 2048, 3072], P('pair', 'vid', 'aud'), may hold values from -6 to 6
- d_audio_out: bfloat16 [2, 1024, 3072], P('pair', 'vid', 'aud'), may hold values from -6 to 6
Outputs:
- video_out: bfloat16 [2, 2048, 3072], P('pair', 'vid', 'aud')
- audio_out: bfloat16 [2, 1024, 3072], P('pair', 'vid', 'aud')
- grad_video_q: bfloat16 [2, 2048, 3072], P('pair', 'vid', 'aud')
- grad_video_k: bfloat16 [2, 2048, 3072], P('pair', 'vid', 'aud')
- grad_video_v: bfloat16 [2, 2048, 3072], P('pair', 'vid', 'aud')
- grad_audio_q: bfloat16 [2, 1024, 3072], P('pair', 'vid', 'aud')
- grad_audio_k: bfloat16 [2, 1024, 3072], P('pair', 'vid', 'aud')
- grad_audio_v: bfloat16 [2, 1024, 3072], P('pair', 'vid', 'aud')
- grad_video_gate: float32 [3072], P('aud')
- grad_audio_gate: float32 [3072], P('aud')
Inputs may be any that keep to these rules, and one draw needn't show every extreme that they name: `audio_len`: at least one member's audio has all 1024 tokens unpadded.
All inputs are finite; a program needn't handle non-finite values.
Results may differ from a plain program's by a relative error of at most 0.04.
Values may be sent and summed in bfloat16 or wider, within the bound.
No kernel may reach another device: no remote copies, remote signals or barrier semaphores. Data moves between devices by JAX's collectives and lax.ppermute only.
A program may use at most 128 MiB of HBM per device.

v0:
```python
import jax
import jax.numpy as jnp
from jax import lax
from jax.sharding import PartitionSpec as P

HEAD_DIM = 128


def heads_view(matrix):
    return matrix.reshape(matrix.shape[0], matrix.shape[1] // HEAD_DIM, HEAD_DIM)


def logits(queries, keys, allowed):
    raw = jnp.einsum(
        "qhd,khd->hqk", heads_view(queries), heads_view(keys), preferred_element_type=jnp.float32
    ) * HEAD_DIM ** (-0.5)
    return jnp.where(allowed[None, None, :], raw, -1e30)


def attend(queries, keys, values, allowed):
    scored = logits(queries, keys, allowed)
    peak = jnp.max(scored, axis=-1)
    expon = jnp.exp(scored - peak[..., None])
    total = jnp.sum(expon, axis=-1)
    weights = (expon / total[..., None]).astype(jnp.bfloat16)
    output = jnp.einsum(
        "hqk,khd->qhd", weights, heads_view(values), preferred_element_type=jnp.float32
    )
    return (output.reshape(queries.shape[0], -1), peak + jnp.log(total))


def row_delta(upstream, output):
    product = upstream.astype(jnp.float32) * output
    return jnp.sum(heads_view(product), axis=-1).T


def attend_back(queries, keys, values, allowed, upstream, delta, log_total):
    scored = logits(queries, keys, allowed)
    probs = jnp.exp(scored - log_total[..., None])
    up_heads = heads_view(upstream)
    grad_values = jnp.einsum(
        "hqk,qhd->khd", probs.astype(jnp.bfloat16), up_heads, preferred_element_type=jnp.float32
    )
    grad_probs = jnp.einsum(
        "qhd,khd->hqk", up_heads, heads_view(values), preferred_element_type=jnp.float32
    )
    grad_scores = (probs * (grad_probs - delta[..., None])).astype(jnp.bfloat16)
    scale = HEAD_DIM ** (-0.5)
    grad_queries = (
        jnp.einsum(
            "hqk,khd->qhd", grad_scores, heads_view(keys), preferred_element_type=jnp.float32
        )
        * scale
    )
    grad_keys = (
        jnp.einsum(
            "hqk,qhd->khd", grad_scores, heads_view(queries), preferred_element_type=jnp.float32
        )
        * scale
    )
    query_rows = queries.shape[0]
    key_rows = keys.shape[0]
    return (
        grad_queries.reshape(query_rows, -1),
        grad_keys.reshape(key_rows, -1),
        grad_values.reshape(key_rows, -1),
    )


def shards(
    video_q,
    video_k,
    video_v,
    audio_q,
    audio_k,
    audio_v,
    video_gate,
    audio_gate,
    audio_len,
    d_video_out,
    d_audio_out,
):
    keys_all, values_all = (
        lax.all_gather(video_k, "vid", axis=1, tiled=True),
        lax.all_gather(video_v, "vid", axis=1, tiled=True),
    )
    keys_all = keys_all[0]
    values_all = values_all[0]
    aud_query_all, aud_keys, aud_values = (
        lax.all_to_all(audio_q, "aud", split_axis=2, concat_axis=1, tiled=True),
        lax.all_to_all(audio_k, "aud", split_axis=2, concat_axis=1, tiled=True),
        lax.all_to_all(audio_v, "aud", split_axis=2, concat_axis=1, tiled=True),
    )
    aud_query_all = aud_query_all[0]
    aud_keys = aud_keys[0]
    aud_values = aud_values[0]
    share = aud_keys.shape[0] // lax.axis_size("vid")
    offset = lax.axis_index("vid") * share
    aud_query = lax.dynamic_slice_in_dim(aud_query_all, offset, share, 0)
    positions = jnp.arange(aud_keys.shape[0], dtype=jnp.int32)
    aud_allowed = positions < audio_len[0]
    vid_allowed = jnp.ones((keys_all.shape[0],), dtype=bool)
    vid_query = video_q[0]
    up_video = d_video_out[0]
    up_audio = d_audio_out[0]
    out_vs, lse_vs = attend(vid_query, keys_all, values_all, vid_allowed)
    out_vc, lse_vc = attend(vid_query, aud_keys, aud_values, aud_allowed)
    out_as, lse_as = attend(aud_query, aud_keys, aud_values, aud_allowed)
    out_ac, lse_ac = attend(aud_query, keys_all, values_all, vid_allowed)
    video_out = (out_vs + video_gate * out_vc).astype(jnp.bfloat16)
    audio_out = (out_as + audio_gate * out_ac).astype(jnp.bfloat16)
    up_vc = (video_gate * up_video.astype(jnp.float32)).astype(jnp.bfloat16)
    up_ac = (audio_gate * up_audio.astype(jnp.float32)).astype(jnp.bfloat16)
    delta_vs = row_delta(up_video, out_vs)
    delta_vc = row_delta(up_vc, out_vc)
    delta_as = row_delta(up_audio, out_as)
    delta_ac = row_delta(up_ac, out_ac)
    gq_vs, gk_vs, gv_vs = attend_back(
        vid_query, keys_all, values_all, vid_allowed, up_video, delta_vs, lse_vs
    )
    gq_vc, gk_vc, gv_vc = attend_back(
        vid_query, aud_keys, aud_values, aud_allowed, up_vc, delta_vc, lse_vc
    )
    gq_as, gk_as, gv_as = attend_back(
        aud_query, aud_keys, aud_values, aud_allowed, up_audio, delta_as, lse_as
    )
    gq_ac, gk_ac, gv_ac = attend_back(
        aud_query, keys_all, values_all, vid_allowed, up_ac, delta_ac, lse_ac
    )
    grad_video_q = (gq_vs + gq_vc).astype(jnp.bfloat16)
    grad_audio_q = (gq_as + gq_ac).astype(jnp.bfloat16)
    width_local = vid_query.shape[1]
    video_term = jnp.concatenate([gk_vs + gk_ac, gv_vs + gv_ac], axis=1)
    audio_term = jnp.concatenate([gk_vc + gk_as, gv_vc + gv_as], axis=1)
    video_part, audio_part = (
        lax.psum_scatter(video_term, "vid", scatter_dimension=0, tiled=True),
        lax.psum_scatter(audio_term, "vid", scatter_dimension=0, tiled=True),
    )
    grad_video_k = video_part[:, :width_local].astype(jnp.bfloat16)
    grad_video_v = video_part[:, width_local:].astype(jnp.bfloat16)
    grad_audio_k = audio_part[:, :width_local].astype(jnp.bfloat16)
    grad_audio_v = audio_part[:, width_local:].astype(jnp.bfloat16)
    video_gate_part = jnp.sum(up_video.astype(jnp.float32) * out_vc, axis=0)
    audio_gate_part = jnp.sum(up_audio.astype(jnp.float32) * out_ac, axis=0)
    grad_video_gate, grad_audio_gate = lax.psum((video_gate_part, audio_gate_part), ("vid", "pair"))
    return (
        video_out[None],
        audio_out[None],
        grad_video_q[None],
        grad_video_k[None],
        grad_video_v[None],
        grad_audio_q[None],
        grad_audio_k[None],
        grad_audio_v[None],
        grad_video_gate,
        grad_audio_gate,
    )


def solution(mesh):
    return jax.shard_map(
        shards,
        mesh=mesh,
        in_specs=(
            P("pair", "vid", "aud"),
            P("pair", "vid", "aud"),
            P("pair", "vid", "aud"),
            P("pair", "aud", None),
            P("pair", "aud", None),
            P("pair", "aud", None),
            P("aud"),
            P("aud"),
            P("pair"),
            P("pair", "vid", "aud"),
            P("pair", "vid", "aud"),
        ),
        out_specs=(
            P("pair", "vid", "aud"),
            P("pair", "vid", "aud"),
            P("pair", "vid", "aud"),
            P("pair", "vid", "aud"),
            P("pair", "vid", "aud"),
            P("pair", "vid", "aud"),
            P("pair", "vid", "aud"),
            P("pair", "vid", "aud"),
            P("aud"),
            P("aud"),
        ),
        check_vma=False,
    )
```

profile of v0, /device:TPU:1, one launch (start us, length us, event | category | flops | bytes accessed | tf_op | source)
XLA Modules:
  0.0 507.7 jit_solution(819241140333967432)
XLA Ops:
  7.2 3.7 copy.173
  11.4 17.0 %reduce.3 = bf16[3072,128]{1,0:T(8,128)(2,1)S(1)} reduce(bf16[3072,1,128]{2,1,0:T(2,128)(2,1)S(1)} %bitcast.149, bf16[]{:T(256)} %broadcast.129), dimensions={1}, to_apply=%bitcast.92.reduce_sub_computation | reduce | bytes 1572866
  29.5 11.8 %all-to-all-start = ((bf16[8,2,24576]{2,1,0:T(2,128)(2,1)}), bf16[8,2,24576]{2,1,0:T(2,128)(2,1)S(1)}, u32[]{:S(2)}, u32[]{:S(2)}) async-start(bf16[8,2,24576]{2,1,0:T(2,128)(2,1)} %reshape.272), calls=%async_computation | async-start | bytes 1572864 | tf_op jit(solution)/shard_map/all_to_all | solution.py:91
  44.0 17.0 %reduce.4 = bf16[3072,128]{1,0:T(8,128)(2,1)S(1)} reduce(bf16[3072,1,128]{2,1,0:T(2,128)(2,1)S(1)} %bitcast.154, bf16[]{:T(256)} %broadcast.129), dimensions={1}, to_apply=%bitcast.94.reduce_sub_computation | reduce | bytes 1572866
  62.0 9.1 %all-to-all-start.2 = ((bf16[8,2,24576]{2,1,0:T(2,128)(2,1)}), bf16[8,2,24576]{2,1,0:T(2,128)(2,1)}, u32[]{:S(2)}, u32[]{:S(2)}) async-start(bf16[8,2,24576]{2,1,0:T(2,128)(2,1)} %reshape.274), calls=%async_computation.2 | async-start | bytes 1572864 | tf_op jit(solution)/shard_map/all_to_all | solution.py:90
  73.1 17.0 %reduce.2 = bf16[3072,128]{1,0:T(8,128)(2,1)S(1)} reduce(bf16[3072,1,128]{2,1,0:T(2,128)(2,1)S(1)} %bitcast.150, bf16[]{:T(256)} %broadcast.129), dimensions={1}, to_apply=%bitcast.90.reduce_sub_computation | reduce | bytes 1572866
  91.2 5.1 all-to-all-done.2
  96.2 4.2 all-to-all-start.1
  104.1 4.3 reshape.275
  109.7 9.9 %all-to-all-done.1 = bf16[8,2,24576]{2,1,0:T(2,128)(2,1)} async-done(((bf16[8,2,24576]{2,1,0:T(2,128)(2,1)}), bf16[8,2,24576]{2,1,0:T(2,128)(2,1)}, u32[]{:S(2)}, u32[]{:S(2)}) %all-to-all-start.1) | async-done | bytes 786464 | tf_op jit(solution)/shard_map/all_to_all | solution.py:92
  119.6 4.1 reshape.271
  129.6 3.0 copy.209
  133.0 13.5 %all-gather.3.cloned.1.call-done = bf16[1,2048,384]{1,2,0:T(8,128)(2,1)} async-done(((bf16[1,128,384]{1,2,0:T(8,128)(2,1)}), bf16[1,2048,384]{1,2,0:T(8,128)(2,1)}) %all-gather.3.cloned.1.call-update) | async-done | bytes 1572880 | tf_op jit(solution)/shard_map/all_gather | solution.py:84
  151.2 78.0 %all-gather.5.cloned.1.call-done = bf16[1,2048,384]{2,1,0:T(8,128)(2,1)} async-done(((bf16[1,128,384]{2,1,0:T(8,128)(2,1)}), bf16[1,2048,384]{2,1,0:T(8,128)(2,1)}) %all-gather.5.cloned.1.call-update) | async-done | bytes 1572880 | tf_op jit(solution)/shard_map/all_gather | solution.py:85
  229.2 2.6 copy.172
  231.9 3.9 fusion.39
  245.4 3.0 copy.208
  248.4 3.8 pad_maximum_fusion.1
  253.9 2.5 fusion.3
  261.5 3.5 copy.199
  269.5 3.7 copy.200
  273.3 5.0 pad_maximum_fusion
  287.2 78.9 %all-reduce = (f32[384]{0:T(512)}, f32[384]{0:T(512)}) all-reduce(f32[384]{0:T(512)S(1)} %bitcast.185, f32[384]{0:T(512)S(1)} %bitcast.184), channel_id=1, replica_groups=mesh['vid'=16,'aud'=8,'pair'=2] {'vid','pair'}, use_global_device_ids=true, to_apply=%region_15.16 | all-reduce | flops 768 | bytes 6144 | tf_op jit(solution)/shard_map/psum | solution.py:145
  368.9 130.5 %reduce-scatter.3.cloned.1.call-done = f32[128,768]{1,0:T(8,128)} async-done(((f32[2048,768]{1,0:T(8,128)}), f32[128,768]{1,0:T(8,128)}) %reduce-scatter.3.cloned.1.call-update) | async-done | bytes 393232 | tf_op jit(solution)/shard_map/reduce_scatter | solution.py:136
  (185 shorter events, 57.3 us)
Async XLA Ops:
  28.3 12.9 %copy-start.35 = (bf16[1,128,384]{2,1,0:T(8,128)(2,1)S(1)}, bf16[1,128,384]{2,1,0:T(8,128)(2,1)}, u32[]{:S(2)}) copy-start(bf16[1,128,384]{2,1,0:T(8,128)(2,1)} %param.12) | copy-start | bytes 294916
  29.5 12.6 %copy-start.27 = (bf16[1,128,3072]{2,1,0:T(8,128)(2,1)S(1)}, bf16[1,128,3072]{2,1,0:T(8,128)(2,1)}, u32[]{:S(2)}) copy-start(bf16[1,128,3072]{2,1,0:T(8,128)(2,1)} %param.14) | copy-start | bytes 2359300
  29.5 32.6 %all-to-all-start = ((bf16[8,2,24576]{2,1,0:T(2,128)(2,1)}), bf16[8,2,24576]{2,1,0:T(2,128)(2,1)S(1)}, u32[]{:S(2)}, u32[]{:S(2)}) async-start(bf16[8,2,24576]{2,1,0:T(2,128)(2,1)} %reshape.272), calls=%async_computation | async-start | bytes 1572864 | tf_op jit(solution)/shard_map/all_to_all | solution.py:91
  41.2 105.3 %all-gather.3.cloned.1.call-start = ((), (), s32[]{:S(2)}) async-start(), calls=%async_computation.5 | async-start | bytes 1671168 | tf_op jit(solution)/shard_map/all_gather | solution.py:84
  62.0 9.1 %copy-start.28 = (bf16[1,128,3072]{2,1,0:T(8,128)(2,1)S(1)}, bf16[1,128,3072]{2,1,0:T(8,128)(2,1)}, u32[]{:S(2)}) copy-start(bf16[1,128,3072]{2,1,0:T(8,128)(2,1)} %param.16) | copy-start | bytes 2359300
  62.0 34.2 %all-to-all-start.2 = ((bf16[8,2,24576]{2,1,0:T(2,128)(2,1)}), bf16[8,2,24576]{2,1,0:T(2,128)(2,1)}, u32[]{:S(2)}, u32[]{:S(2)}) async-start(bf16[8,2,24576]{2,1,0:T(2,128)(2,1)} %reshape.274), calls=%async_computation.2 | async-start | bytes 1572864 | tf_op jit(solution)/shard_map/all_to_all | solution.py:90
  90.0 11.9 %copy-start.38 = (bf16[1,64,384]{2,1,0:T(8,128)(2,1)S(1)}, bf16[1,64,384]{2,1,0:T(8,128)(2,1)}, u32[]{:S(2)}) copy-start(bf16[1,64,384]{2,1,0:T(8,128)(2,1)} %param.21) | copy-start | bytes 147460
  90.1 11.9 %copy-start.36 = (bf16[1,128,384]{2,1,0:T(8,128)(2,1)S(1)}, bf16[1,128,384]{2,1,0:T(8,128)(2,1)}, u32[]{:S(2)}) copy-start(bf16[1,128,384]{2,1,0:T(8,128)(2,1)} %param.11) | copy-start | bytes 294916
  90.1 12.0 %copy-start.37 = (bf16[1,128,384]{2,1,0:T(8,128)(2,1)S(1)}, bf16[1,128,384]{2,1,0:T(8,128)(2,1)}, u32[]{:S(2)}) copy-start(bf16[1,128,384]{2,1,0:T(8,128)(2,1)} %param.20) | copy-start | bytes 294916
  96.2 23.4 %all-to-all-start.1 = ((bf16[8,2,24576]{2,1,0:T(2,128)(2,1)}), bf16[8,2,24576]{2,1,0:T(2,128)(2,1)}, u32[]{:S(2)}, u32[]{:S(2)}) async-start(bf16[8,2,24576]{2,1,0:T(2,128)(2,1)} %reshape.270), calls=%async_computation.1 | async-start | bytes 1572864 | tf_op jit(solution)/shard_map/all_to_all | solution.py:92
  100.5 128.7 %all-gather.5.cloned.1.call-start = ((), (), s32[]{:S(2)}) async-start(), calls=%async_computation.6 | async-start | bytes 1671168 | tf_op jit(solution)/shard_map/all_gather | solution.py:85
  101.2 266.1 %reduce-scatter.5.cloned.1.call-start = ((), (), s32[]{:S(2)}) async-start(), calls=%async_computation.8 | async-start | bytes 3342336 | tf_op jit(solution)/shard_map/reduce_scatter | solution.py:137
  102.0 129.9 %copy-start.26 = (bf16[64,3,128]{2,1,0:T(4,128)(2,1)}, bf16[64,3,128]{2,1,0:T(4,128)(2,1)S(1)}, u32[]{:S(2)}) copy-start(bf16[64,3,128]{2,1,0:T(4,128)(2,1)S(1)} %squeeze.12) | copy-start | bytes 147460
  102.1 47.8 %copy-start.19 = (bf16[1,128,384]{1,2,0:T(8,128)(2,1)}, bf16[1,128,384]{1,2,0:T(8,128)(2,1)S(1)}, u32[]{:S(2)}) copy-start(bf16[1,128,384]{1,2,0:T(8,128)(2,1)S(1)} %copy.168) | copy-start | bytes 294916
  102.2 25.4 %copy-start.22 = (bf16[1,128,384]{1,2,0:T(8,128)(2,1)}, bf16[1,128,384]{1,2,0:T(8,128)(2,1)S(1)}, u32[]{:S(2)}) copy-start(bf16[1,128,384]{1,2,0:T(8,128)(2,1)S(1)} %copy.191) | copy-start | bytes 294916
  104.1 22.1 %copy-start.5 = (bf16[1024,3,128]{0,2,1:T(8,128)(2,1)}, bf16[1024,3,128]{0,2,1:T(8,128)(2,1)S(1)}, u32[]{:S(2)}) copy-start(bf16[1024,3,128]{0,2,1:T(8,128)(2,1)S(1)} %reshape_squeeze.15) | copy-start | bytes 2359300
  124.7 7.9 %copy-start.15 = (bf16[1024,3,128]{0,2,1:T(8,128)(2,1)}, bf16[1024,3,128]{0,2,1:T(8,128)(2,1)S(1)}, u32[]{:S(2)}) copy-start(bf16[1024,3,128]{0,2,1:T(8,128)(2,1)S(1)} %reshape_squeeze.16) | copy-start | bytes 2359300
  125.9 6.7 %copy-start.11 = (f32[3,64,1024]{2,1,0:T(8,128)}, f32[3,64,1024]{2,1,0:T(8,128)S(1)}, u32[]{:S(2)}) copy-start(f32[3,64,1024]{2,1,0:T(8,128)S(1)} %get-tuple-element.77) | copy-start | bytes 2359300
  133.0 98.8 %copy-start.33 = (f32[64,3,128]{2,0,1:T(8,128)}, f32[64,3,128]{2,0,1:T(8,128)S(1)}, u32[]{:S(2)}) copy-start(f32[64,3,128]{2,0,1:T(8,128)S(1)} %convolution_bitcast_fusion) | copy-start | bytes 294916
  150.4 81.4 %copy-start.48 = (f32[3,64]{1,0:T(4,128)}, f32[3,64]{1,0:T(4,128)S(1)}, u32[]{:S(2)}) copy-start(f32[3,64]{1,0:T(4,128)S(1)} %fusion.8) | copy-start | bytes 2308
  151.1 80.7 %copy-start.39 = (f32[384]{0:T(512)S(1)}, f32[384]{0:T(512)}, u32[]{:S(2)}) copy-start(f32[384]{0:T(512)} %param.18) | copy-start | bytes 4612
  252.2 247.2 %reduce-scatter.3.cloned.1.call-start = ((), (), s32[]{:S(2)}) async-start(), calls=%async_computation.7 | async-start | bytes 6684672 | tf_op jit(solution)/shard_map/reduce_scatter | solution.py:136
  285.6 80.5 %copy-start.29 = (f32[1,64,384]{2,1,0:T(8,128)S(1)}, f32[1,64,384]{2,1,0:T(8,128)}, u32[]{:S(2)}) copy-start(f32[1,64,384]{2,1,0:T(8,128)} %reshape.268) | copy-start | bytes 294916
  285.6 81.1 %copy-start.41 = (f32[384]{0:T(512)S(1)}, f32[384]{0:T(512)}, u32[]{:S(2)}) copy-start(f32[384]{0:T(512)} %param.17) | copy-start | bytes 4612
  (38 other events, 75.5 us)
Sparse Core Ops, SparseCore 0:
  44.4 102.1 all-gather.2
  148.3 80.8 all-gather.4
  252.4 93.5 reduce-scatter.4
  348.4 151.0 reduce-scatter.2
where the time goes:
time: 509 us; the launch traced here: 508 us
  waiting for transfers between devices  238 us (47%)
  blocking collectives  78.9 us (16%)
  other arithmetic  65.9 us (13%)
  local copies, waits for them, and re-layouts  50.8 us (10%)
  matrix products  33.5 us (7%)
  starting transfers between devices  25.5 us (5%)
  between operations  15.2 us (3%)
    reduce_scatter x1, waiting for transfers between devices, shards(): lax.psum_scatter(video_term, 'vid', scatter_dimension=0, tiled=True)  130 us
    psum x1, blocking collectives, shards(): lax.psum((video_gate_part, audio_gate_part), ('vid', 'pair'))  78.9 us
    all_gather x1, waiting for transfers between devices, shards(): lax.all_gather(video_v, 'vid', axis=1, tiled=True)  78 us
    unnamed x3, other arithmetic  50.9 us
    unnamed x127, local copies, waits for them, and re-layouts  26.2 us
    all_gather x1, waiting for transfers between devices, shards(): lax.all_gather(video_k, 'vid', axis=1, tiled=True)  13.5 us
    all_to_all x1, starting transfers between devices, shards(): lax.all_to_all(audio_k, 'aud', split_axis=2, concat_axis=1, tiled=True)  11.8 us
  transfers between devices with their start and end apart: 7, of which 5 were waited for; matrix products, arithmetic and copies ran while one was open for 20% of the time, Pallas kernels for 0%

commit v1 on v0

v1 whole, which is shorter than its diff:
```python
import jax
import jax.numpy as jnp
from jax import lax
from jax.experimental import pallas as pl
from jax.experimental.pallas import tpu as pltpu
from jax.sharding import PartitionSpec as P

HEAD_DIM = 128
SCALE = HEAD_DIM ** (-0.5)
SIDE = 4
F32 = jnp.float32
BF16 = jnp.bfloat16

ALONG_X = [[x * SIDE + z for x in range(SIDE)] for z in range(SIDE)]
ALONG_Z = [[x * SIDE + z for z in range(SIDE)] for x in range(SIDE)]


def rows_of(ref, part, video_rows):
    block = ref[:, part]
    count, rows, width = block.shape
    video = block[:, :video_rows].reshape(count * video_rows, width)
    audio = block[:, video_rows:].reshape(count * (rows - video_rows), width)
    return video, audio


def gated(rows, gate_row):
    return (gate_row * rows.astype(F32)).astype(BF16)


def nt(a, b):
    return lax.dot_general(a, b, (((1,), (1,)), ((), ())), preferred_element_type=F32)


def nn(a, b):
    return lax.dot_general(a, b, (((1,), (0,)), ((), ())), preferred_element_type=F32)


def upstreams(q_ref, gates_ref, video_rows):
    up_video, up_audio = rows_of(q_ref, 1, video_rows)
    on_video_keys = jnp.concatenate([up_video, gated(up_audio, gates_ref[1:2, :])], axis=0)
    on_audio_keys = jnp.concatenate([gated(up_video, gates_ref[0:1, :]), up_audio], axis=0)
    return on_video_keys, on_audio_keys


def forward_kernel(video_rows, limit_ref, q_ref, k_ref, gates_ref, e_ref, o_ref, stats_ref):
    queries = jnp.concatenate(rows_of(q_ref, 0, video_rows), axis=0)
    keys = rows_of(k_ref, 0, video_rows)
    values = rows_of(k_ref, 1, video_rows)
    ups = upstreams(q_ref, gates_ref, video_rows)
    split = keys[0].shape[0]
    stats = []
    for part in (0, 1):
        raw = nt(keys[part], queries)
        if part == 1:
            position = lax.broadcasted_iota(jnp.int32, raw.shape, 0)
            raw = jnp.where(position < limit_ref[0], raw, -1e30)
        peak = jnp.max(raw, axis=0, keepdims=True)
        expon = jnp.exp((raw - peak) * SCALE)
        total = jnp.sum(expon, axis=0, keepdims=True)
        expon = expon.astype(BF16)
        if part == 0:
            e_ref[0, :split] = expon
        else:
            e_ref[0, split:] = expon
        output = nn(values[part].T, expon)
        o_ref[0, part] = output
        weighted = jnp.sum(ups[part].astype(F32).T * output, axis=0, keepdims=True)
        stats.append((peak, total, weighted))
    stats_ref[0] = jnp.concatenate(
        [stats[0][0], stats[1][0], stats[0][1], stats[1][1], stats[0][2], stats[1][2], stats[0][0], stats[1][0]],
        axis=0,
    )


def backward_kernel(
    video_rows, q_ref, k_ref, gates_ref, columns_ref, e_ref, o_ref, own_ref, all_ref, qside_ref, kside_ref, gate_ref
):
    queries = jnp.concatenate(rows_of(q_ref, 0, video_rows), axis=0)
    keys = rows_of(k_ref, 0, video_rows)
    values = rows_of(k_ref, 1, video_rows)
    ups = upstreams(q_ref, gates_ref, video_rows)
    split = keys[0].shape[0]
    count = q_ref.shape[0]
    video_q = count * video_rows
    peers = all_ref.shape[0]
    grad_queries = None
    outputs = []
    for part in (0, 1):
        peak = all_ref[0, 0, part : part + 1]
        for peer in range(1, peers):
            peak = jnp.maximum(peak, all_ref[peer, 0, part : part + 1])
        total = jnp.zeros_like(peak)
        weighted = jnp.zeros_like(peak)
        for peer in range(peers):
            weight = jnp.exp((all_ref[peer, 0, part : part + 1] - peak) * SCALE)
            total += weight * all_ref[peer, 0, part + 2 : part + 3]
            weighted += weight * all_ref[peer, 0, part + 4 : part + 5]
        delta = weighted / total
        factor = jnp.exp((own_ref[0, part : part + 1] - peak) * SCALE) / total
        expon = e_ref[0, :split] if part == 0 else e_ref[0, split:]
        probs = expon.astype(F32) * factor
        grad_values = nn(probs.astype(BF16), ups[part])
        grad_probs = nt(values[part], ups[part])
        grad_scores = (probs * (grad_probs - delta)).astype(BF16)
        grad_keys = nn(grad_scores, queries) * SCALE
        term = nn(keys[part].T, grad_scores)
        grad_queries = term if grad_queries is None else grad_queries + term
        outputs.append(o_ref[0, part] * factor)
        lo, hi = (0, video_rows) if part == 0 else (video_rows, kside_ref.shape[2])
        kside_ref[:, 0, lo:hi] = grad_keys.astype(BF16).reshape(count, hi - lo, HEAD_DIM)
        kside_ref[:, 1, lo:hi] = grad_values.astype(BF16).reshape(count, hi - lo, HEAD_DIM)
    video_gate = columns_ref[:, 0:1]
    audio_gate = columns_ref[:, 1:2]
    cross_video = outputs[1][:, :video_q]
    cross_audio = outputs[0][:, video_q:]
    merged = jnp.concatenate(
        [outputs[0][:, :video_q] + video_gate * cross_video, outputs[1][:, video_q:] + audio_gate * cross_audio], axis=1
    )
    up_video, up_audio = rows_of(q_ref, 1, video_rows)
    video_sum = jnp.sum(up_video.astype(F32).T * cross_video, axis=1, keepdims=True)
    audio_sum = jnp.sum(up_audio.astype(F32).T * cross_audio, axis=1, keepdims=True)
    sums = jnp.concatenate(
        [jnp.broadcast_to(video_sum, (HEAD_DIM, 8)), jnp.broadcast_to(audio_sum, (HEAD_DIM, HEAD_DIM - 8))], axis=1
    )
    gate_ref[...] = sums.T[0:16]
    merged = merged.T.astype(BF16)
    grad_queries = (grad_queries.T * SCALE).astype(BF16)
    for index, array in ((0, merged), (1, grad_queries)):
        qside_ref[:, index, :video_rows] = array[:video_q].reshape(count, video_rows, HEAD_DIM)
        qside_ref[:, index, video_rows:] = array[video_q:].reshape(count, -1, HEAD_DIM)


def attention_forward(limit, qside, kside, gates, video_rows):
    count, _, rows, width = qside.shape
    heads = width // HEAD_DIM
    total = count * rows
    block = pl.BlockSpec((count, 2, rows, HEAD_DIM), lambda h: (0, 0, 0, h))
    return pl.pallas_call(
        lambda *refs: forward_kernel(video_rows, *refs),
        grid=(heads,),
        in_specs=[
            pl.BlockSpec(memory_space=pltpu.SMEM),
            block,
            block,
            pl.BlockSpec((2, HEAD_DIM), lambda h: (0, h)),
        ],
        out_specs=[
            pl.BlockSpec((1, total, total), lambda h: (h, 0, 0)),
            pl.BlockSpec((1, 2, HEAD_DIM, total), lambda h: (h, 0, 0, 0)),
            pl.BlockSpec((1, 8, total), lambda h: (h, 0, 0)),
        ],
        out_shape=[
            jax.ShapeDtypeStruct((heads, total, total), BF16),
            jax.ShapeDtypeStruct((heads, 2, HEAD_DIM, total), F32),
            jax.ShapeDtypeStruct((heads, 8, total), F32),
        ],
        compiler_params=pltpu.CompilerParams(vmem_limit_bytes=48 * 2**20),
        name="attention_forward",
    )(limit, qside, kside, gates)


def attention_backward(qside, kside, gates, expon, outputs, stats, stats_all, video_rows):
    count, _, rows, width = qside.shape
    heads = width // HEAD_DIM
    total = count * rows
    block = pl.BlockSpec((count, 2, rows, HEAD_DIM), lambda h: (0, 0, 0, h))
    return pl.pallas_call(
        lambda *refs: backward_kernel(video_rows, *refs),
        grid=(heads,),
        in_specs=[
            block,
            block,
            pl.BlockSpec((2, HEAD_DIM), lambda h: (0, h)),
            pl.BlockSpec((HEAD_DIM, 2), lambda h: (h, 0)),
            pl.BlockSpec((1, total, total), lambda h: (h, 0, 0)),
            pl.BlockSpec((1, 2, HEAD_DIM, total), lambda h: (h, 0, 0, 0)),
            pl.BlockSpec((1, 8, total), lambda h: (h, 0, 0)),
            pl.BlockSpec((stats_all.shape[0], 1, 8, total), lambda h: (0, h, 0, 0)),
        ],
        out_specs=[block, block, pl.BlockSpec((16, HEAD_DIM), lambda h: (0, h))],
        out_shape=[
            jax.ShapeDtypeStruct(qside.shape, BF16),
            jax.ShapeDtypeStruct(kside.shape, BF16),
            jax.ShapeDtypeStruct((16, width), F32),
        ],
        compiler_params=pltpu.CompilerParams(vmem_limit_bytes=56 * 2**20),
        name="attention_backward",
    )(qside, kside, gates, gates.T, expon, outputs, stats, stats_all)


def own_audio(audio, vid, aud, columns, rows):
    count = lax.axis_size("aud")
    sends = [
        lax.dynamic_slice(array[0], ((vid % 2) * rows, (vid // 2) * columns), (rows, columns)) for array in audio
    ]
    pairs = [
        (v * count + a, (2 * a + v % 2) * count + v // 2) for v in range(lax.axis_size("vid")) for a in range(count)
    ]
    return lax.ppermute(jnp.stack(sends), ("vid", "aud"), pairs)


def shards(
    video_q, video_k, video_v, audio_q, audio_k, audio_v, video_gate, audio_gate, audio_len, d_video_out, d_audio_out
):
    vid = lax.axis_index("vid")
    aud = lax.axis_index("aud")
    video_rows, columns = video_q.shape[1:]
    audio_rows = d_audio_out.shape[1]
    aud_q, aud_k, aud_v = own_audio((audio_q, audio_k, audio_v), vid, aud, columns, audio_rows)
    qside = jnp.stack(
        [jnp.concatenate([video_q[0], aud_q], axis=0), jnp.concatenate([d_video_out[0], d_audio_out[0]], axis=0)]
    )
    kside = jnp.stack(
        [jnp.concatenate([video_k[0], aud_k], axis=0), jnp.concatenate([video_v[0], aud_v], axis=0)]
    )
    qside = lax.all_gather(qside, "vid", axis=0, axis_index_groups=ALONG_X)
    kside = lax.all_gather(kside, "vid", axis=0, axis_index_groups=ALONG_Z)
    gates = jnp.stack([video_gate, audio_gate])
    limit = audio_len - (vid // SIDE) * (SIDE * audio_rows)
    expon, outputs, stats = attention_forward(limit, qside, kside, gates, video_rows)
    stats_all = lax.all_gather(stats, "vid", axis=0, axis_index_groups=ALONG_X)
    qside, kside, gate_part = attention_backward(
        qside, kside, gates, expon, outputs, stats, stats_all, video_rows
    )
    gate_all = lax.all_gather(gate_part[7:9], ("vid", "pair"), axis=0)
    gate_grad = jnp.sum(gate_all, axis=0)
    qside = lax.all_to_all(qside, "vid", 0, 0, axis_index_groups=ALONG_X, tiled=True)
    kside = lax.all_to_all(kside, "vid", 0, 0, axis_index_groups=ALONG_Z, tiled=True)
    qside = jnp.sum(qside.astype(F32), axis=0).astype(BF16)
    kside = jnp.sum(kside.astype(F32), axis=0).astype(BF16)
    return (
        qside[0:1, :video_rows],
        qside[0:1, video_rows:],
        qside[1:2, :video_rows],
        kside[0:1, :video_rows],
        kside[1:2, :video_rows],
        qside[1:2, video_rows:],
        kside[0:1, video_rows:],
        kside[1:2, video_rows:],
        gate_grad[0],
        gate_grad[1],
    )


def solution(mesh):
    split = P("pair", "vid", "aud")
    rows = P("pair", "aud", None)
    return jax.shard_map(
        shards,
        mesh=mesh,
        in_specs=(split, split, split, rows, rows, rows, P("aud"), P("aud"), P("pair"), split, split),
        out_specs=(split,) * 8 + (P("aud"), P("aud")),
        check_vma=False,
    )
```

time: 509 us -> 213 us (0.42)
  waiting for transfers between devices: 238 us -> 80.1 us
  other arithmetic: 65.9 us -> 3.1 us
  local copies, waits for them, and re-layouts: 50.8 us -> 10.8 us
  matrix products: 33.5 us -> 0 us
  starting transfers between devices: 25.5 us -> 5.27 us
  Pallas kernels: 0 us -> 12.6 us
  blocking collectives: 78.9 us -> 85.2 us
    reduce_scatter x2 -> x0, waiting for transfers between devices: 130 us -> none  [the longest x1 130 us: shards(): lax.psum_scatter(video_term, 'vid', scatter_dimension=0, tiled=True)]
    psum x1 -> x0, blocking collectives: 78.9 us -> none  [shards(): lax.psum((video_gate_part, audio_gate_part), ('vid', 'pair'))]
    all_gather x0 -> x2, blocking collectives: none -> 69.7 us  [the longest x1 59.1 us: shards(): gate_all = lax.all_gather(gate_part[7:9], ('vid', 'pair'), axis=0)]
    unnamed x3 -> x0, other arithmetic: 50.9 us -> none
    dot_general x24 -> x0, matrix products: 33.5 us -> none  [the longest x4 7.17 us: attend(): jnp.einsum('hqk,khd->qhd', weights, heads_view(values), preferred_element...]
    all_to_all x3 -> x1, starting transfers between devices: 25.1 us -> 4.52 us  [shards(): lax.all_to_all(kside, 'vid', 0, 0, axis_index_groups=ALONG_Z, tiled=True)]
    unnamed x127 -> x25, local copies, waits for them, and re-layouts: 26.2 us -> 5.78 us
    all_to_all x0 -> x1, blocking collectives: none -> 15.5 us  [shards(): lax.all_to_all(qside, 'vid', 0, 0, axis_index_groups=ALONG_X, tiled=True)]
  transfers between devices with their start and end apart: 7 -> 4, of which waited for: 5 -> 2; matrix products, arithmetic and copies ran while one was open for 20% -> 2% of each run, Pallas kernels for 0% -> 0%
where the time goes in v1:
time: 213 us; the launch traced here: 212 us
  blocking collectives  85.2 us (40%)
  waiting for transfers between devices  80.1 us (38%)
  between operations  14.9 us (7%)
  Pallas kernels  12.6 us (6%)
  local copies, waits for them, and re-layouts  10.8 us (5%)
  starting transfers between devices  5.27 us (2%)
  other arithmetic  3.1 us (1%)
    all_gather x1, blocking collectives, shards(): gate_all = lax.all_gather(gate_part[7:9], ('vid', 'pair'), axis=0)  59.1 us
    all_gather x1, waiting for transfers between devices, shards(): kside = lax.all_gather(kside, 'vid', axis=0, axis_index_groups=ALONG_Z)  53 us
    all_gather x1, waiting for transfers between devices, shards(): qside = lax.all_gather(qside, 'vid', axis=0, axis_index_groups=ALONG_X)  27.1 us
    all_to_all x1, blocking collectives, shards(): lax.all_to_all(qside, 'vid', 0, 0, axis_index_groups=ALONG_X, tiled=True)  15.5 us
    all_gather x1, blocking collectives, shards(): stats_all = lax.all_gather(stats, 'vid', axis=0, axis_index_groups=ALONG_X)  10.6 us
    pallas_call x1, Pallas kernels, attention_backward(): pl.pallas_call(lambda *refs: backward_kernel(video_rows, *refs), grid=(he...  7.3 us
    unnamed x25, local copies, waits for them, and re-layouts  5.78 us
    pallas_call x1, Pallas kernels, attention_forward(): pl.pallas_call(lambda *refs: forward_kernel(video_rows, *refs), grid=(hea...  5.27 us
  transfers between devices with their start and end apart: 4, of which 2 were waited for; matrix products, arithmetic and copies ran while one was open for 2% of the time, Pallas kernels for 0%

profile of v1, /device:TPU:1, one launch (start us, length us, event | category | flops | bytes accessed | tf_op | source)
XLA Modules:
  0.0 212.0 jit_solution(481118644797665743)
XLA Ops:
  7.3 1.0 copy-done
  8.3 0.9 constant_dynamic-slice_fusion
  9.3 0.7 collective-permute-start
  10.0 0.9 maximum_bitcast_fusion.2
  10.9 0.7 pad_maximum_fusion.1
  11.8 0.7 pad_maximum_fusion
  13.3 0.8 copy.27
  14.2 53.0 %all-gather.10.cloned.1.call-done = bf16[8,192,384]{2,1,0:T(8,128)(2,1)} async-done(((bf16[2,192,384]{2,1,0:T(8,128)(2,1)}), bf16[8,192,384]{2,1,0:T(8,128)(2,1)}) %all-gather.10.cloned.1.call-update) | async-done | bytes 1179664 | tf_op jit(solution)/shard_map/all_gather | solution.py:217
  67.1 27.1 %all-gather.8.cloned.1.call-done = bf16[8,192,384]{2,1,0:T(8,128)(2,1)} async-done(((bf16[2,192,384]{2,1,0:T(8,128)(2,1)}), bf16[8,192,384]{2,1,0:T(8,128)(2,1)}) %all-gather.8.cloned.1.call-update) | async-done | bytes 1179664 | tf_op jit(solution)/shard_map/all_gather | solution.py:216
  94.3 1.3 copy-done.1
  95.5 1.3 copy-done.2
  96.8 5.3 %attention_forward.1 = (bf16[3,768,768]{2,1,0:T(8,128)(2,1)}, f32[3,2,128,768]{3,2,1,0:T(8,128)S(1)}, f32[3,8,768]{2,1,0:T(8,128)S(1)}) custom-call(s32[1]{0:T(128)S(6)} %sub.18.refs_0_, bf16[4,2,192,384]{3,2,1,0:T(8,128)(2,1)S(1)} %bitcast.29, bf16[4,2,192,384]{3,2,1,0:T(8,128)(2,1)S(1)} %bitcast.27, f32[2,384]{1,0:T(2,128)S(1)} %pad_maximum_fusion.3.refs_3_.refs_2_), custom_call_target="tpu_custom_call" | custom-call | tf_op jit(solution)/shard_map/attention_forward/pallas_call | solution.py:138
  102.1 1.4 copy-done.3
  103.5 10.6 %all-gather.2 = f32[12,8,768]{2,1,0:T(8,128)} all-gather(f32[3,8,768]{2,1,0:T(8,128)S(1)} %get-tuple-element.18.refs_6_), channel_id=4, replica_groups={{0,64,128,192},{16,80,144,208},{32,96,160,224},{48,112,176,240},{1,65,1..., dimensions={0}, use_global_device_ids=true | all-gather | bytes 368640 | tf_op jit(solution)/shard_map/all_gather | solution.py:221
  114.1 7.3 %attention_backward.1 = (bf16[4,2,192,384]{3,2,1,0:T(8,128)(2,1)}, bf16[4,2,192,384]{3,2,1,0:T(8,128)(2,1)}, f32[16,384]{1,0:T(8,128)}) custom-call(bf16[4,2,192,384]{3,2,1,0:T(8,128)(2,1)} %bitcast.28, bf16[4,2,192,384]{3,2,1,0:T(8,128)(2,1)} %bitcast.26, f32[2,384]{1,0:T(2,128)} %copy-done.5, f32[384,2]{1,0:T(8,128)} %bitcast.31, ...), custom_call_target="tpu_custom_call" | custom-call | tf_op jit(solution)/shard_map/attention_backward/pallas_call | solution.py:167
  121.4 15.5 %all_to_all.10 = bf16[4,2,192,384]{3,2,1,0:T(8,128)(2,1)S(1)} all-to-all(bf16[4,2,192,384]{3,2,1,0:T(8,128)(2,1)} %get-tuple-element.19), channel_id=1, replica_groups={{0,64,128,192},{16,80,144,208},{32,96,160,224},{48,112,176,240},{1,65,1..., dimensions={0} | all-to-all | bytes 2359296 | tf_op jit(solution)/shard_map/all_to_all | solution.py:227
  136.9 4.5 %all-to-all-start.1 = ((bf16[4,2,192,384]{3,2,1,0:T(8,128)(2,1)}), bf16[4,2,192,384]{3,2,1,0:T(8,128)(2,1)S(1)}, u32[]{:S(2)}, u32[]{:S(2)}) async-start(bf16[4,2,192,384]{3,2,1,0:T(8,128)(2,1)} %get-tuple-element.20), calls=%async_computation.1 | async-start | bytes 2359296 | tf_op jit(solution)/shard_map/all_to_all | solution.py:228
  141.4 0.7 slice_bitcast_fusion.3
  142.2 59.1 %all-gather.4 = f32[32,2,384]{2,1,0:T(2,128)S(1)} all-gather(f32[1,2,384]{2,1,0:T(2,128)S(1)} %slice_bitcast_fusion.3), channel_id=5, replica_groups=mesh['vid'=16,'aud'=8,'pair'=2] {'vid','pair'}, dimensions={0}, use_global_device_ids=true | all-gather | bytes 101376 | tf_op jit(solution)/shard_map/all_gather | solution.py:225
  201.4 0.6 slice_reduce_fusion
  202.2 0.6 fusion.1
  202.9 0.7 fusion.3
  203.9 0.6 fusion
  204.5 0.7 fusion.2
  (38 shorter events, 0.9 us)
Async XLA Ops:
  7.2 1.1 copy-start
  7.2 3.7 %copy-start.6 = (bf16[1,128,384]{2,1,0:T(8,128)(2,1)S(1)}, bf16[1,128,384]{2,1,0:T(8,128)(2,1)}, u32[]{:S(2)}) copy-start(bf16[1,128,384]{2,1,0:T(8,128)(2,1)} %param.13) | copy-start | bytes 294916
  7.2 59.9 %all-gather.10.cloned.1.call-start = ((), (), s32[]{:S(2)}) async-start(), calls=%async_computation.3 | async-start | bytes 1474560 | tf_op jit(solution)/shard_map/all_gather | solution.py:217
  8.3 3.4 %copy-start.7 = (bf16[1,128,384]{2,1,0:T(8,128)(2,1)S(1)}, bf16[1,128,384]{2,1,0:T(8,128)(2,1)}, u32[]{:S(2)}) copy-start(bf16[1,128,384]{2,1,0:T(8,128)(2,1)} %param.20) | copy-start | bytes 294916
  8.3 3.4 %copy-start.9 = (bf16[1,64,384]{2,1,0:T(8,128)(2,1)S(1)}, bf16[1,64,384]{2,1,0:T(8,128)(2,1)}, u32[]{:S(2)}) copy-start(bf16[1,64,384]{2,1,0:T(8,128)(2,1)} %param.21) | copy-start | bytes 147460
  9.2 2.6 %copy-start.8 = (bf16[1,128,384]{2,1,0:T(8,128)(2,1)S(1)}, bf16[1,128,384]{2,1,0:T(8,128)(2,1)}, u32[]{:S(2)}) copy-start(bf16[1,128,384]{2,1,0:T(8,128)(2,1)} %param.11) | copy-start | bytes 294916
  9.3 0.7 collective-permute-start
  10.9 2.3 %copy-start.10 = (f32[384]{0:T(512)S(1)}, f32[384]{0:T(512)}, u32[]{:S(2)}) copy-start(f32[384]{0:T(512)} %param.17) | copy-start | bytes 4612
  10.9 2.4 %copy-start.11 = (f32[384]{0:T(512)S(1)}, f32[384]{0:T(512)}, u32[]{:S(2)}) copy-start(f32[384]{0:T(512)} %param.18) | copy-start | bytes 4612
  11.7 82.5 %all-gather.8.cloned.1.call-start = ((), (), s32[]{:S(2)}) async-start(), calls=%async_computation.2 | async-start | bytes 1474560 | tf_op jit(solution)/shard_map/all_gather | solution.py:216
  13.3 88.7 %copy-start.5 = (f32[2,384]{1,0:T(2,128)}, f32[2,384]{1,0:T(2,128)S(1)}, u32[]{:S(2)}) copy-start(f32[2,384]{1,0:T(2,128)S(1)} %pad_maximum_fusion.3.refs_3_.refs_2_) | copy-start | bytes 9220
  94.2 1.3 copy-start.1
  95.5 1.3 copy-start.2
  102.1 1.4 copy-start.3
  103.5 10.6 %copy-start.4 = (f32[3,8,768]{2,1,0:T(8,128)}, f32[3,8,768]{2,1,0:T(8,128)S(1)}, u32[]{:S(2)}) copy-start(f32[3,8,768]{2,1,0:T(8,128)S(1)} %get-tuple-element.18.refs_6_) | copy-start | bytes 221188
  136.9 66.7 %all-to-all-start.1 = ((bf16[4,2,192,384]{3,2,1,0:T(8,128)(2,1)}), bf16[4,2,192,384]{3,2,1,0:T(8,128)(2,1)S(1)}, u32[]{:S(2)}, u32[]{:S(2)}) async-start(bf16[4,2,192,384]{3,2,1,0:T(8,128)(2,1)} %get-tuple-element.20), calls=%async_computation.1 | async-start | bytes 2359296 | tf_op jit(solution)/shard_map/all_to_all | solution.py:228
Sparse Core Ops, SparseCore 0:
  11.8 55.2 all-gather.9
  68.9 25.2 all-gather.7

commit v2 on v1

v2 whole, which is shorter than its diff:
```python
import functools

import jax
import jax.numpy as jnp
from jax import lax
from jax.experimental import pallas as pl
from jax.experimental.pallas import tpu as pltpu
from jax.sharding import PartitionSpec as P

HEAD_DIM = 128
SCALE = HEAD_DIM ** (-0.5)
SIDE = 4
F32 = jnp.float32
BF16 = jnp.bfloat16
VIDEO, AUDIO = 0, 1


def along_x(array, shift):
    pairs = [(x * SIDE + z, (x + shift) % SIDE * SIDE + z) for x in range(SIDE) for z in range(SIDE)]
    return lax.ppermute(array, "vid", pairs)


def along_z(array, shift):
    pairs = [(x * SIDE + z, x * SIDE + (z + shift) % SIDE) for x in range(SIDE) for z in range(SIDE)]
    return lax.ppermute(array, "vid", pairs)


def gathered(array, along):
    return [array] + [along(array, shift) for shift in range(1, SIDE)]


def returned(parts, along):
    return [parts[0]] + [along(parts[place], SIDE - place) for place in range(1, SIDE)]


def nt(a, b):
    return lax.dot_general(a, b, (((1,), (1,)), ((), ())), preferred_element_type=F32)


def nn(a, b):
    return lax.dot_general(a, b, (((1,), (0,)), ((), ())), preferred_element_type=F32)


def joined(refs, index):
    return jnp.concatenate([ref[index] for ref in refs], axis=0)


def gated(rows, gate_row):
    return (gate_row * rows.astype(F32)).astype(BF16)


def upstreams(q_refs, gates_ref):
    up_video, up_audio = joined(q_refs[VIDEO], 1), joined(q_refs[AUDIO], 1)
    return (
        jnp.concatenate([up_video, gated(up_audio, gates_ref[1:2, :])], axis=0),
        jnp.concatenate([gated(up_video, gates_ref[0:1, :]), up_audio], axis=0),
    )


def sides(refs):
    return (refs[0:4], refs[4:8]), (refs[8:12], refs[12:16])


def forward_kernel(*refs):
    (q_refs, k_refs), (limit_ref, gates_ref, e_ref, o_ref, video_ref, audio_ref) = sides(refs[:16]), refs[16:]
    queries = jnp.concatenate([joined(q_refs[VIDEO], 0), joined(q_refs[AUDIO], 0)], axis=0)
    ups = upstreams(q_refs, gates_ref)
    split = sum(ref.shape[1] for ref in k_refs[VIDEO])
    video_q = sum(ref.shape[1] for ref in q_refs[VIDEO])
    stats = []
    for part in (VIDEO, AUDIO):
        raw = nt(joined(k_refs[part], 0), queries)
        if part == AUDIO:
            rows = k_refs[AUDIO][0].shape[1]
            position = lax.broadcasted_iota(jnp.int32, (rows, raw.shape[1]), 0)
            raw = jnp.concatenate(
                [
                    jnp.where(position < limit_ref[place], raw[place * rows : (place + 1) * rows], -1e30)
                    for place in range(SIDE)
                ],
                axis=0,
            )
        peak = jnp.max(raw, axis=0, keepdims=True)
        expon = jnp.exp((raw - peak) * SCALE)
        total = jnp.sum(expon, axis=0, keepdims=True)
        expon = expon.astype(BF16)
        if part == VIDEO:
            e_ref[0, :split] = expon
        else:
            e_ref[0, split:] = expon
        output = nn(joined(k_refs[part], 1).T, expon)
        o_ref[0, part] = output
        weighted = jnp.sum(ups[part].astype(F32).T * output, axis=0, keepdims=True)
        stats.append((peak, total, weighted))
    rows = [stats[part][kind] for kind in range(3) for part in (VIDEO, AUDIO)]
    stats = jnp.concatenate(rows + rows[:2], axis=0)
    video_ref[0] = stats[:, :video_q]
    audio_ref[0] = stats[:, video_q:]


def backward_kernel(*refs):
    q_refs, k_refs = sides(refs[:16])
    gates_ref, columns_ref, e_ref, o_ref = refs[16:20]
    video_stats, audio_stats = refs[20:24], refs[24:28]
    q_outs, k_outs, gate_ref = refs[28:32], refs[32:36], refs[36]
    queries = jnp.concatenate([joined(q_refs[VIDEO], 0), joined(q_refs[AUDIO], 0)], axis=0)
    ups = upstreams(q_refs, gates_ref)
    split = sum(ref.shape[1] for ref in k_refs[VIDEO])
    video_q = sum(ref.shape[1] for ref in q_refs[VIDEO])
    video_rows, audio_rows = q_refs[VIDEO][0].shape[1], q_refs[AUDIO][0].shape[1]
    stats = []
    for shift in range(SIDE):
        video, audio = video_stats[shift][0], audio_stats[shift][0]
        if shift:
            video = pltpu.roll(video, shift * video_rows, 1)
            audio = pltpu.roll(audio, shift * audio_rows, 1)
        stats.append(jnp.concatenate([video, audio], axis=1))
    grad_queries = None
    outputs = []
    for part in (VIDEO, AUDIO):
        peaks = [array[part : part + 1] for array in stats]
        peak = functools.reduce(jnp.maximum, peaks)
        weights = [jnp.exp((local - peak) * SCALE) for local in peaks]
        total = sum(weight * array[part + 2 : part + 3] for weight, array in zip(weights, stats))
        delta = sum(weight * array[part + 4 : part + 5] for weight, array in zip(weights, stats)) / total
        factor = weights[0] / total
        expon = e_ref[0, :split] if part == VIDEO else e_ref[0, split:]
        probs = expon.astype(F32) * factor
        grad_values = nn(probs.astype(BF16), ups[part]).astype(BF16)
        grad_probs = nt(joined(k_refs[part], 1), ups[part])
        grad_scores = (probs * (grad_probs - delta)).astype(BF16)
        grad_keys = (nn(grad_scores, queries) * SCALE).astype(BF16)
        term = nn(joined(k_refs[part], 0).T, grad_scores)
        grad_queries = term if grad_queries is None else grad_queries + term
        outputs.append(o_ref[0, part] * factor)
        rows, first = (video_rows, 0) if part == VIDEO else (audio_rows, video_rows)
        for place in range(SIDE):
            taken = slice(place * rows, (place + 1) * rows)
            k_outs[place][0, first : first + rows] = grad_keys[taken]
            k_outs[place][1, first : first + rows] = grad_values[taken]
    cross_video = outputs[AUDIO][:, :video_q]
    cross_audio = outputs[VIDEO][:, video_q:]
    merged = jnp.concatenate(
        [
            outputs[VIDEO][:, :video_q] + columns_ref[:, 0:1] * cross_video,
            outputs[AUDIO][:, video_q:] + columns_ref[:, 1:2] * cross_audio,
        ],
        axis=1,
    )
    video_sum = jnp.sum(joined(q_refs[VIDEO], 1).astype(F32).T * cross_video, axis=1, keepdims=True)
    audio_sum = jnp.sum(joined(q_refs[AUDIO], 1).astype(F32).T * cross_audio, axis=1, keepdims=True)
    sums = jnp.concatenate(
        [jnp.broadcast_to(video_sum, (HEAD_DIM, 4)), jnp.broadcast_to(audio_sum, (HEAD_DIM, HEAD_DIM - 4))], axis=1
    )
    gate_ref[...] = sums.T[0:8]
    for index, array in ((0, merged.T.astype(BF16)), (1, (grad_queries.T * SCALE).astype(BF16))):
        for place in range(SIDE):
            q_outs[place][index, :video_rows] = array[place * video_rows : (place + 1) * video_rows]
            first = video_q + place * audio_rows
            q_outs[place][index, video_rows:] = array[first : first + audio_rows]


def chunk_spec(rows):
    return pl.BlockSpec((2, rows, HEAD_DIM), lambda h: (0, 0, h))


def head_spec(*shape):
    return pl.BlockSpec((1, *shape), lambda h: (h,) + (0,) * len(shape))


def attention_forward(sides_in, limits, gates):
    video_rows, audio_rows = sides_in[0].shape[1], sides_in[4].shape[1]
    heads = gates.shape[1] // HEAD_DIM
    video, audio = SIDE * video_rows, SIDE * audio_rows
    total = video + audio
    shapes = [((total, total), BF16), ((2, HEAD_DIM, total), F32), ((8, video), F32), ((8, audio), F32)]
    return pl.pallas_call(
        forward_kernel,
        grid=(heads,),
        in_specs=[chunk_spec(array.shape[1]) for array in sides_in]
        + [pl.BlockSpec(memory_space=pltpu.SMEM), pl.BlockSpec((2, HEAD_DIM), lambda h: (0, h))],
        out_specs=[head_spec(*shape) for shape, _ in shapes],
        out_shape=[jax.ShapeDtypeStruct((heads, *shape), kind) for shape, kind in shapes],
        compiler_params=pltpu.CompilerParams(vmem_limit_bytes=48 * 2**20),
        name="attention_forward",
    )(*sides_in, limits, gates)


def attention_backward(sides_in, gates, expon, outputs, video_stats, audio_stats):
    video_rows, audio_rows = sides_in[0].shape[1], sides_in[4].shape[1]
    width = gates.shape[1]
    rows = video_rows + audio_rows
    given = [expon, outputs, *video_stats, *audio_stats]
    outs = pl.pallas_call(
        backward_kernel,
        grid=(width // HEAD_DIM,),
        in_specs=[chunk_spec(array.shape[1]) for array in sides_in]
        + [pl.BlockSpec((2, HEAD_DIM), lambda h: (0, h)), pl.BlockSpec((HEAD_DIM, 2), lambda h: (h, 0))]
        + [head_spec(*array.shape[1:]) for array in given],
        out_specs=[chunk_spec(rows)] * 8 + [pl.BlockSpec((8, HEAD_DIM), lambda h: (0, h))],
        out_shape=[jax.ShapeDtypeStruct((2, rows, width), BF16)] * 8 + [jax.ShapeDtypeStruct((8, width), F32)],
        compiler_params=pltpu.CompilerParams(vmem_limit_bytes=56 * 2**20),
        name="attention_backward",
    )(*sides_in, gates, gates.T, *given)
    return outs[0:4], outs[4:8], outs[8]


def own_audio(audio, vid, columns, rows):
    count = lax.axis_size("aud")
    sends = [
        lax.dynamic_slice(array[0], ((vid % 2) * rows, (vid // 2) * columns), (rows, columns)) for array in audio
    ]
    pairs = [
        (v * count + a, (2 * a + v % 2) * count + v // 2) for v in range(lax.axis_size("vid")) for a in range(count)
    ]
    return lax.ppermute(jnp.stack(sends), ("vid", "aud"), pairs)


def summed(parts):
    return sum(part.astype(F32) for part in parts)


def shards(
    video_q, video_k, video_v, audio_q, audio_k, audio_v, video_gate, audio_gate, audio_len, d_video_out, d_audio_out
):
    vid = lax.axis_index("vid")
    video_rows, columns = video_q.shape[1:]
    audio_rows = d_audio_out.shape[1]
    aud_q, aud_k, aud_v = own_audio((audio_q, audio_k, audio_v), vid, columns, audio_rows)
    video_queries = gathered(jnp.concatenate([video_q, d_video_out]), along_x)
    video_keys = gathered(jnp.concatenate([video_k, video_v]), along_z)
    audio_queries = gathered(jnp.stack([aud_q, d_audio_out[0]]), along_x)
    audio_keys = gathered(jnp.stack([aud_k, aud_v]), along_z)
    sides_in = (*video_queries, *audio_queries, *video_keys, *audio_keys)
    gates = jnp.stack([video_gate, audio_gate])
    column, row = vid // SIDE, vid % SIDE
    limits = jnp.stack(
        [audio_len[0] - (column * SIDE + (row - place) % SIDE) * audio_rows for place in range(SIDE)]
    )
    expon, outputs, video_stats, audio_stats = attention_forward(sides_in, limits, gates)
    video_stats = gathered(video_stats, along_x)
    audio_stats = gathered(audio_stats, along_x)
    q_parts, k_parts, gate = attention_backward(sides_in, gates, expon, outputs, video_stats, audio_stats)
    k_side = summed(returned(k_parts, along_z)).astype(BF16)
    q_side = summed(returned(q_parts, along_x)).astype(BF16)
    gate = sum(gathered(gate, along_x))
    gate = sum(gathered(gate, along_z))
    gate = gate + lax.ppermute(gate, "pair", [(0, 1), (1, 0)])
    return (
        q_side[0:1, :video_rows],
        q_side[0:1, video_rows:],
        q_side[1:2, :video_rows],
        k_side[0:1, :video_rows],
        k_side[1:2, :video_rows],
        q_side[1:2, video_rows:],
        k_side[0:1, video_rows:],
        k_side[1:2, video_rows:],
        gate[0],
        gate[7],
    )


def solution(mesh):
    split = P("pair", "vid", "aud")
    rows = P("pair", "aud", None)
    return jax.shard_map(
        shards,
        mesh=mesh,
        in_specs=(split, split, split, rows, rows, rows, P("aud"), P("aud"), P("pair"), split, split),
        out_specs=(split,) * 8 + (P("aud"), P("aud")),
        check_vma=False,
    )
```

time: 213 us -> 127 us (0.60)
  blocking collectives: 85.2 us -> 0 us
  starting transfers between devices: 5.27 us -> 63.7 us
  waiting for transfers between devices: 80.1 us -> 31.7 us
  between operations: 14.9 us -> 1.76 us
    all_gather x2 -> x0, waiting for transfers between devices: 80.1 us -> none  [the longest x1 53 us: shards(): kside = lax.all_gather(kside, 'vid', axis=0, axis_index_groups=ALONG_Z)]
    all_gather x2 -> x0, blocking collectives: 69.7 us -> none  [the longest x1 59.1 us: shards(): gate_all = lax.all_gather(gate_part[7:9], ('vid', 'pair'), axis=0)]
    ppermute x0 -> x31, starting transfers between devices: none -> 63 us  [the longest x12 30.1 us: along_z(): return lax.ppermute(array, 'vid', pairs)]
    ppermute x0 -> x31, waiting for transfers between devices: none -> 31.7 us  [the longest x12 25.4 us: along_z(): return lax.ppermute(array, 'vid', pairs)]
    all_to_all x1 -> x0, blocking collectives: 15.5 us -> none  [shards(): lax.all_to_all(qside, 'vid', 0, 0, axis_index_groups=ALONG_X, tiled=True)]
    all_to_all x1 -> x0, starting transfers between devices: 4.52 us -> none  [shards(): lax.all_to_all(kside, 'vid', 0, 0, axis_index_groups=ALONG_Z, tiled=True)]
    convert_element_type x0 -> x2, other arithmetic: none -> 2.22 us  [the longest x1 1.11 us: shards(): q_side = summed(returned(q_parts, along_x)).astype(BF16)]
    unnamed x25 -> x56, local copies, waits for them, and re-layouts: 5.78 us -> 3.85 us
  transfers between devices with their start and end apart: 4 -> 32, of which waited for: 2 -> 10; matrix products, arithmetic and copies ran while one was open for 2% -> 7% of each run, Pallas kernels for 0% -> 0%
where the time goes in v2:
time: 127 us
  starting transfers between devices  63.7 us (50%)
  waiting for transfers between devices  31.7 us (25%)
  Pallas kernels  13.5 us (11%)
  local copies, waits for them, and re-layouts  12 us (9%)
  other arithmetic  3.87 us (3%)
  between operations  1.76 us (1%)
    ppermute x12, starting transfers between devices, along_z(): return lax.ppermute(array, 'vid', pairs)  30.1 us
    ppermute x12, waiting for transfers between devices, along_z(): return lax.ppermute(array, 'vid', pairs)  25.4 us
    ppermute x18, starting transfers between devices, along_x(): return lax.ppermute(array, 'vid', pairs)  23.6 us
    ppermute x1, starting transfers between devices, shards(): gate = gate + lax.ppermute(gate, 'pair', [(0, 1), (1, 0)])  9.39 us
    pallas_call x1, Pallas kernels, attention_backward(): pl.pallas_call(backward_kernel, grid=(width // HEAD_DIM,), in_specs=[chun...  7.64 us
    ppermute x18, waiting for transfers between devices, along_x(): return lax.ppermute(array, 'vid', pairs)  5.96 us
    pallas_call x1, Pallas kernels, attention_forward(): pl.pallas_call(forward_kernel, grid=(heads,), in_specs=[chunk_spec(array....  5.89 us
    unnamed x56, local copies, waits for them, and re-layouts  3.85 us
  transfers between devices with their start and end apart: 32, of which 10 were waited for; matrix products, arithmetic and copies ran while one was open for 7% of the time, Pallas kernels for 0%

profile of v2, /device:TPU:1, one launch (start us, length us, event | category | flops | bytes accessed | tf_op | source)
XLA Modules:
  0.0 126.5 jit_solution(7230207636821049594)
XLA Ops:
  2.6 5.3 %collective-permute-start.9 = (bf16[2,128,384]{2,1,0:T(8,128)(2,1)S(1)}, bf16[2,128,384]{2,1,0:T(8,128)(2,1)S(1)}, u32[]{:S(2)}, u32[]{:S(2)}) collective-permute-start(bf16[2,128,384]{2,1,0:T(8,128)(2,1)S(1)} %constant_dynamic-update-slice_fusion.2.refs_8_), channel_id=1, source_target_pairs={{0,48},{16,0},{32,16},{48,32},{64,112},{80,64},{96,80},{112,96},{1... | collective-permute-start | bytes 589832 | tf_op jit(solution)/shard_map/ppermute | solution.py:25
  11.6 6.4 %collective-permute-start.2 = (bf16[2,128,384]{2,1,0:T(8,128)(2,1)S(1)}, bf16[2,128,384]{2,1,0:T(8,128)(2,1)S(1)}, u32[]{:S(2)}, u32[]{:S(2)}) collective-permute-start(bf16[2,128,384]{2,1,0:T(8,128)(2,1)S(1)} %constant_dynamic-update-slice_fusion.refs_0_), channel_id=1, source_target_pairs={{0,192},{16,208},{32,224},{48,240},{64,0},{80,16},{96,32},{112,48}... | collective-permute-start | bytes 589832 | tf_op jit(solution)/shard_map/ppermute | solution.py:20
  20.1 3.0 %collective-permute-start.1 = (bf16[2,128,384]{2,1,0:T(8,128)(2,1)S(1)}, bf16[2,128,384]{2,1,0:T(8,128)(2,1)S(1)}, u32[]{:S(2)}, u32[]{:S(2)}) collective-permute-start(bf16[2,128,384]{2,1,0:T(8,128)(2,1)S(1)} %constant_dynamic-update-slice_fusion.refs_0_), channel_id=1, source_target_pairs={{0,128},{16,144},{32,160},{48,176},{64,192},{80,208},{96,224},{112... | collective-permute-start | bytes 589832 | tf_op jit(solution)/shard_map/ppermute | solution.py:20
  24.8 2.1 %collective-permute-start.6 = (bf16[2,64,384]{2,1,0:T(8,128)(2,1)S(1)}, bf16[2,64,384]{2,1,0:T(8,128)(2,1)S(1)}, u32[]{:S(2)}, u32[]{:S(2)}) collective-permute-start(bf16[2,64,384]{2,1,0:T(8,128)(2,1)S(1)} %pad_maximum_fusion.1.refs_4_), channel_id=1, source_target_pairs={{0,192},{16,208},{32,224},{48,240},{64,0},{80,16},{96,32},{112,48}... | collective-permute-start | bytes 294920 | tf_op jit(solution)/shard_map/ppermute | solution.py:20
  27.6 12.7 %collective-permute-start.12 = (bf16[2,64,384]{2,1,0:T(8,128)(2,1)S(1)}, bf16[2,64,384]{2,1,0:T(8,128)(2,1)S(1)}, u32[]{:S(2)}, u32[]{:S(2)}) collective-permute-start(bf16[2,64,384]{2,1,0:T(8,128)(2,1)S(1)} %stack.47.refs_12_), channel_id=1, source_target_pairs={{0,48},{16,0},{32,16},{48,32},{64,112},{80,64},{96,80},{112,96},{1... | collective-permute-start | bytes 294920 | tf_op jit(solution)/shard_map/ppermute | solution.py:25
  40.3 4.9 %collective-permute-start.10 = (bf16[2,64,384]{2,1,0:T(8,128)(2,1)S(1)}, bf16[2,64,384]{2,1,0:T(8,128)(2,1)S(1)}, u32[]{:S(2)}, u32[]{:S(2)}) collective-permute-start(bf16[2,64,384]{2,1,0:T(8,128)(2,1)S(1)} %stack.47.refs_12_), channel_id=1, source_target_pairs={{0,16},{16,32},{32,48},{48,0},{64,80},{80,96},{96,112},{112,64},{1... | collective-permute-start | bytes 294920 | tf_op jit(solution)/shard_map/ppermute | solution.py:25
  45.4 2.7 %collective-permute-done.10.refs_13_ = bf16[2,64,384]{2,1,0:T(8,128)(2,1)S(1)} collective-permute-done((bf16[2,64,384]{2,1,0:T(8,128)(2,1)S(1)}, bf16[2,64,384]{2,1,0:T(8,128)(2,1)S(1)}, u32[]{:S(2)}, u32[]{:S(2)}) %collective-permute-start.10) | collective-permute-done | bytes 98336 | tf_op jit(solution)/shard_map/ppermute | solution.py:25
  48.1 5.9 %attention_forward.1 = (bf16[3,768,768]{2,1,0:T(8,128)(2,1)}, f32[3,2,128,768]{3,2,1,0:T(8,128)S(1)}, f32[3,8,512]{2,1,0:T(8,128)S(1)}, f32[3,8,256]{2,1,0:T(8,128)S(1)}) custom-call(bf16[2,128,384]{2,1,0:T(8,128)(2,1)S(1)} %constant_dynamic-update-slice_fusion.refs_0_, bf16[2,128,384]{2,1,0:T(8,128)(2,1)S(1)} %collective-permute-done.refs_1_, ...), custom_call_target="tpu_custom_call" | custom-call | tf_op jit(solution)/shard_map/attention_forward/pallas_call | solution.py:177
  54.0 1.5 %copy-done.1 = f32[3,2,128,768]{3,2,1,0:T(8,128)} copy-done((f32[3,2,128,768]{3,2,1,0:T(8,128)}, f32[3,2,128,768]{3,2,1,0:T(8,128)S(1)}, u32[]{:S(2)}) %copy-start.1) | copy-done | bytes 2359320
  56.4 2.3 %collective-permute-start.14 = (f32[3,8,512]{2,1,0:T(8,128)S(1)}, f32[3,8,512]{2,1,0:T(8,128)S(1)}, u32[]{:S(2)}, u32[]{:S(2)}) collective-permute-start(f32[3,8,512]{2,1,0:T(8,128)S(1)} %get-tuple-element.25.refs_20_), channel_id=1, source_target_pairs={{0,128},{16,144},{32,160},{48,176},{64,192},{80,208},{96,224},{112... | collective-permute-start | bytes 147464 | tf_op jit(solution)/shard_map/ppermute | solution.py:20
  59.0 1.8 %collective-permute-start.17 = (f32[3,8,256]{2,1,0:T(8,128)S(1)}, f32[3,8,256]{2,1,0:T(8,128)S(1)}, u32[]{:S(2)}, u32[]{:S(2)}) collective-permute-start(f32[3,8,256]{2,1,0:T(8,128)S(1)} %get-tuple-element.26.refs_24_), channel_id=1, source_target_pairs={{0,128},{16,144},{32,160},{48,176},{64,192},{80,208},{96,224},{112... | collective-permute-start | bytes 73736 | tf_op jit(solution)/shard_map/ppermute | solution.py:20
  60.8 1.1 collective-permute-start.16
  63.2 1.5 %collective-permute-done.16.refs_25_ = f32[3,8,256]{2,1,0:T(8,128)S(1)} collective-permute-done((f32[3,8,256]{2,1,0:T(8,128)S(1)}, f32[3,8,256]{2,1,0:T(8,128)S(1)}, u32[]{:S(2)}, u32[]{:S(2)}) %collective-permute-start.16) | collective-permute-done | bytes 24608 | tf_op jit(solution)/shard_map/ppermute | solution.py:20
  65.4 7.6 %attention_backward.1 = (bf16[2,192,384]{2,1,0:T(8,128)(2,1)}, bf16[2,192,384]{2,1,0:T(8,128)(2,1)}, bf16[2,192,384]{2,1,0:T(8,128)(2,1)}, bf16[2,192,384]{2,1,0...) custom-call(bf16[2,128,384]{2,1,0:T(8,128)(2,1)} %copy-done.3, ...), custom_call_target="tpu_custom_call" | custom-call | tf_op jit(solution)/shard_map/attention_backward/pallas_call | solution.py:194
  74.8 1.1 collective-permute-done.27
  75.9 2.3 %collective-permute-done.26 = f32[8,384]{1,0:T(8,128)S(1)} collective-permute-done((f32[8,384]{1,0:T(8,128)}, f32[8,384]{1,0:T(8,128)S(1)}, u32[]{:S(2)}, u32[]{:S(2)}) %collective-permute-start.26) | collective-permute-done | bytes 12320 | tf_op jit(solution)/shard_map/ppermute | solution.py:20
  79.5 3.4 %collective-permute-start.30 = (f32[8,384]{1,0:T(8,128)S(1)}, f32[8,384]{1,0:T(8,128)S(1)}, u32[]{:S(2)}, u32[]{:S(2)}) collective-permute-start(f32[8,384]{1,0:T(8,128)S(1)} %add_add_fusion.1), channel_id=1, source_target_pairs={{0,48},{16,0},{32,16},{48,32},{64,112},{80,64},{96,80},{112,96},{1... | collective-permute-start | bytes 36872 | tf_op jit(solution)/shard_map/ppermute | solution.py:25
  83.6 1.4 %collective-permute-start.28 = (f32[8,384]{1,0:T(8,128)S(1)}, f32[8,384]{1,0:T(8,128)S(1)}, u32[]{:S(2)}, u32[]{:S(2)}) collective-permute-start(f32[8,384]{1,0:T(8,128)S(1)} %add_add_fusion.1), channel_id=1, source_target_pairs={{0,16},{16,32},{32,48},{48,0},{64,80},{80,96},{96,112},{112,64},{1... | collective-permute-start | bytes 36872 | tf_op jit(solution)/shard_map/ppermute | solution.py:25
  85.0 1.4 %collective-permute-start.19 = (bf16[2,192,384]{2,1,0:T(8,128)(2,1)}, bf16[2,192,384]{2,1,0:T(8,128)(2,1)S(1)}, u32[]{:S(2)}, u32[]{:S(2)}) collective-permute-start(bf16[2,192,384]{2,1,0:T(8,128)(2,1)} %get-tuple-element.28), channel_id=1, source_target_pairs={{0,192},{16,208},{32,224},{48,240},{64,0},{80,16},{96,32},{112,48}... | collective-permute-start | bytes 884744 | tf_op jit(solution)/shard_map/ppermute | solution.py:20
  88.0 9.4 %collective-permute-start.31 = (f32[8,384]{1,0:T(8,128)S(1)}, f32[8,384]{1,0:T(8,128)S(1)}, u32[]{:S(2)}, u32[]{:S(2)}) collective-permute-start(f32[8,384]{1,0:T(8,128)S(1)} %add_add_fusion), channel_id=1, source_target_pairs={{0,1},{1,0},{2,3},{3,2},{4,5},{5,4},{6,7},{7,6},{8,9},{9,8},{10,11... | collective-permute-start | bytes 36872 | tf_op jit(solution)/shard_map/ppermute | solution.py:248
  99.6 1.1 add_convert_fusion.1
  102.0 4.8 %collective-permute-done.22 = bf16[2,192,384]{2,1,0:T(8,128)(2,1)S(1)} collective-permute-done((bf16[2,192,384]{2,1,0:T(8,128)(2,1)}, bf16[2,192,384]{2,1,0:T(8,128)(2,1)S(1)}, u32[]{:S(2)}, u32[]{:S(2)}) %collective-permute-start.22) | collective-permute-done | bytes 294944 | tf_op jit(solution)/shard_map/ppermute | solution.py:25
  106.9 17.2 %collective-permute-done.23 = bf16[2,192,384]{2,1,0:T(8,128)(2,1)S(1)} collective-permute-done((bf16[2,192,384]{2,1,0:T(8,128)(2,1)}, bf16[2,192,384]{2,1,0:T(8,128)(2,1)S(1)}, u32[]{:S(2)}, u32[]{:S(2)}) %collective-permute-start.23) | collective-permute-done | bytes 294944 | tf_op jit(solution)/shard_map/ppermute | solution.py:25
  124.1 1.1 add_convert_fusion
  (121 shorter events, 22.7 us)
Async XLA Ops:
  2.6 20.6 %collective-permute-start.9 = (bf16[2,128,384]{2,1,0:T(8,128)(2,1)S(1)}, bf16[2,128,384]{2,1,0:T(8,128)(2,1)S(1)}, u32[]{:S(2)}, u32[]{:S(2)}) collective-permute-start(bf16[2,128,384]{2,1,0:T(8,128)(2,1)S(1)} %constant_dynamic-update-slice_fusion.2.refs_8_), channel_id=1, source_target_pairs={{0,48},{16,0},{32,16},{48,32},{64,112},{80,64},{96,80},{112,96},{1... | collective-permute-start | bytes 589832 | tf_op jit(solution)/shard_map/ppermute | solution.py:25
  7.8 16.9 %collective-permute-start.8 = (bf16[2,128,384]{2,1,0:T(8,128)(2,1)S(1)}, bf16[2,128,384]{2,1,0:T(8,128)(2,1)S(1)}, u32[]{:S(2)}, u32[]{:S(2)}) collective-permute-start(bf16[2,128,384]{2,1,0:T(8,128)(2,1)S(1)} %constant_dynamic-update-slice_fusion.2.refs_8_), channel_id=1, source_target_pairs={{0,32},{16,48},{32,0},{48,16},{64,96},{80,112},{96,64},{112,80},{1... | collective-permute-start | bytes 589832 | tf_op jit(solution)/shard_map/ppermute | solution.py:25
  7.8 19.0 %collective-permute-start.7 = (bf16[2,128,384]{2,1,0:T(8,128)(2,1)S(1)}, bf16[2,128,384]{2,1,0:T(8,128)(2,1)S(1)}, u32[]{:S(2)}, u32[]{:S(2)}) collective-permute-start(bf16[2,128,384]{2,1,0:T(8,128)(2,1)S(1)} %constant_dynamic-update-slice_fusion.2.refs_8_), channel_id=1, source_target_pairs={{0,16},{16,32},{32,48},{48,0},{64,80},{80,96},{96,112},{112,64},{1... | collective-permute-start | bytes 589832 | tf_op jit(solution)/shard_map/ppermute | solution.py:25
  9.1 11.0 %collective-permute-start.3 = (bf16[3,64,384]{2,1,0:T(8,128)(2,1)S(1)}, bf16[3,64,384]{2,1,0:T(8,128)(2,1)S(1)}, u32[]{:S(2)}, u32[]{:S(2)}) collective-permute-start(bf16[3,64,384]{2,1,0:T(8,128)(2,1)S(1)} %pad_maximum_fusion), channel_id=1, source_target_pairs={{0,0},{2,32},{4,64},{6,96},{8,128},{10,160},{12,192},{14,224},{16,... | collective-permute-start | bytes 442376 | tf_op jit(solution)/shard_map/ppermute | solution.py:216
  11.6 15.4 %collective-permute-start.2 = (bf16[2,128,384]{2,1,0:T(8,128)(2,1)S(1)}, bf16[2,128,384]{2,1,0:T(8,128)(2,1)S(1)}, u32[]{:S(2)}, u32[]{:S(2)}) collective-permute-start(bf16[2,128,384]{2,1,0:T(8,128)(2,1)S(1)} %constant_dynamic-update-slice_fusion.refs_0_), channel_id=1, source_target_pairs={{0,192},{16,208},{32,224},{48,240},{64,0},{80,16},{96,32},{112,48}... | collective-permute-start | bytes 589832 | tf_op jit(solution)/shard_map/ppermute | solution.py:20
  20.1 7.5 %collective-permute-start.1 = (bf16[2,128,384]{2,1,0:T(8,128)(2,1)S(1)}, bf16[2,128,384]{2,1,0:T(8,128)(2,1)S(1)}, u32[]{:S(2)}, u32[]{:S(2)}) collective-permute-start(bf16[2,128,384]{2,1,0:T(8,128)(2,1)S(1)} %constant_dynamic-update-slice_fusion.refs_0_), channel_id=1, source_target_pairs={{0,128},{16,144},{32,160},{48,176},{64,192},{80,208},{96,224},{112... | collective-permute-start | bytes 589832 | tf_op jit(solution)/shard_map/ppermute | solution.py:20
  23.1 17.2 %collective-permute-start = (bf16[2,128,384]{2,1,0:T(8,128)(2,1)S(1)}, bf16[2,128,384]{2,1,0:T(8,128)(2,1)S(1)}, u32[]{:S(2)}, u32[]{:S(2)}) collective-permute-start(bf16[2,128,384]{2,1,0:T(8,128)(2,1)S(1)} %constant_dynamic-update-slice_fusion.refs_0_), channel_id=1, source_target_pairs={{0,64},{16,80},{32,96},{48,112},{64,128},{80,144},{96,160},{112,17... | collective-permute-start | bytes 589832 | tf_op jit(solution)/shard_map/ppermute | solution.py:20
  24.8 15.5 %collective-permute-start.6 = (bf16[2,64,384]{2,1,0:T(8,128)(2,1)S(1)}, bf16[2,64,384]{2,1,0:T(8,128)(2,1)S(1)}, u32[]{:S(2)}, u32[]{:S(2)}) collective-permute-start(bf16[2,64,384]{2,1,0:T(8,128)(2,1)S(1)} %pad_maximum_fusion.1.refs_4_), channel_id=1, source_target_pairs={{0,192},{16,208},{32,224},{48,240},{64,0},{80,16},{96,32},{112,48}... | collective-permute-start | bytes 294920 | tf_op jit(solution)/shard_map/ppermute | solution.py:20
  26.9 18.5 %collective-permute-start.5 = (bf16[2,64,384]{2,1,0:T(8,128)(2,1)S(1)}, bf16[2,64,384]{2,1,0:T(8,128)(2,1)S(1)}, u32[]{:S(2)}, u32[]{:S(2)}) collective-permute-start(bf16[2,64,384]{2,1,0:T(8,128)(2,1)S(1)} %pad_maximum_fusion.1.refs_4_), channel_id=1, source_target_pairs={{0,128},{16,144},{32,160},{48,176},{64,192},{80,208},{96,224},{112... | collective-permute-start | bytes 294920 | tf_op jit(solution)/shard_map/ppermute | solution.py:20
  27.0 18.3 %collective-permute-start.4 = (bf16[2,64,384]{2,1,0:T(8,128)(2,1)S(1)}, bf16[2,64,384]{2,1,0:T(8,128)(2,1)S(1)}, u32[]{:S(2)}, u32[]{:S(2)}) collective-permute-start(bf16[2,64,384]{2,1,0:T(8,128)(2,1)S(1)} %pad_maximum_fusion.1.refs_4_), channel_id=1, source_target_pairs={{0,64},{16,80},{32,96},{48,112},{64,128},{80,144},{96,160},{112,17... | collective-permute-start | bytes 294920 | tf_op jit(solution)/shard_map/ppermute | solution.py:20
  27.6 17.8 %collective-permute-start.12 = (bf16[2,64,384]{2,1,0:T(8,128)(2,1)S(1)}, bf16[2,64,384]{2,1,0:T(8,128)(2,1)S(1)}, u32[]{:S(2)}, u32[]{:S(2)}) collective-permute-start(bf16[2,64,384]{2,1,0:T(8,128)(2,1)S(1)} %stack.47.refs_12_), channel_id=1, source_target_pairs={{0,48},{16,0},{32,16},{48,32},{64,112},{80,64},{96,80},{112,96},{1... | collective-permute-start | bytes 294920 | tf_op jit(solution)/shard_map/ppermute | solution.py:25
  40.3 7.7 %collective-permute-start.10 = (bf16[2,64,384]{2,1,0:T(8,128)(2,1)S(1)}, bf16[2,64,384]{2,1,0:T(8,128)(2,1)S(1)}, u32[]{:S(2)}, u32[]{:S(2)}) collective-permute-start(bf16[2,64,384]{2,1,0:T(8,128)(2,1)S(1)} %stack.47.refs_12_), channel_id=1, source_target_pairs={{0,16},{16,32},{32,48},{48,0},{64,80},{80,96},{96,112},{112,64},{1... | collective-permute-start | bytes 294920 | tf_op jit(solution)/shard_map/ppermute | solution.py:25
  55.4 5.4 %collective-permute-start.18 = (f32[3,8,256]{2,1,0:T(8,128)S(1)}, f32[3,8,256]{2,1,0:T(8,128)S(1)}, u32[]{:S(2)}, u32[]{:S(2)}) collective-permute-start(f32[3,8,256]{2,1,0:T(8,128)S(1)} %get-tuple-element.26.refs_24_), channel_id=1, source_target_pairs={{0,192},{16,208},{32,224},{48,240},{64,0},{80,16},{96,32},{112,48}... | collective-permute-start | bytes 73736 | tf_op jit(solution)/shard_map/ppermute | solution.py:20
  55.8 8.9 %collective-permute-start.15 = (f32[3,8,512]{2,1,0:T(8,128)S(1)}, f32[3,8,512]{2,1,0:T(8,128)S(1)}, u32[]{:S(2)}, u32[]{:S(2)}) collective-permute-start(f32[3,8,512]{2,1,0:T(8,128)S(1)} %get-tuple-element.25.refs_20_), channel_id=1, source_target_pairs={{0,192},{16,208},{32,224},{48,240},{64,0},{80,16},{96,32},{112,48}... | collective-permute-start | bytes 147464 | tf_op jit(solution)/shard_map/ppermute | solution.py:20
  56.4 8.3 %collective-permute-start.14 = (f32[3,8,512]{2,1,0:T(8,128)S(1)}, f32[3,8,512]{2,1,0:T(8,128)S(1)}, u32[]{:S(2)}, u32[]{:S(2)}) collective-permute-start(f32[3,8,512]{2,1,0:T(8,128)S(1)} %get-tuple-element.25.refs_20_), channel_id=1, source_target_pairs={{0,128},{16,144},{32,160},{48,176},{64,192},{80,208},{96,224},{112... | collective-permute-start | bytes 147464 | tf_op jit(solution)/shard_map/ppermute | solution.py:20
  58.7 6.1 %collective-permute-start.13 = (f32[3,8,512]{2,1,0:T(8,128)S(1)}, f32[3,8,512]{2,1,0:T(8,128)S(1)}, u32[]{:S(2)}, u32[]{:S(2)}) collective-permute-start(f32[3,8,512]{2,1,0:T(8,128)S(1)} %get-tuple-element.25.refs_20_), channel_id=1, source_target_pairs={{0,64},{16,80},{32,96},{48,112},{64,128},{80,144},{96,160},{112,17... | collective-permute-start | bytes 147464 | tf_op jit(solution)/shard_map/ppermute | solution.py:20
  79.5 7.9 %collective-permute-start.30 = (f32[8,384]{1,0:T(8,128)S(1)}, f32[8,384]{1,0:T(8,128)S(1)}, u32[]{:S(2)}, u32[]{:S(2)}) collective-permute-start(f32[8,384]{1,0:T(8,128)S(1)} %add_add_fusion.1), channel_id=1, source_target_pairs={{0,48},{16,0},{32,16},{48,32},{64,112},{80,64},{96,80},{112,96},{1... | collective-permute-start | bytes 36872 | tf_op jit(solution)/shard_map/ppermute | solution.py:25
  85.0 13.8 %collective-permute-start.19 = (bf16[2,192,384]{2,1,0:T(8,128)(2,1)}, bf16[2,192,384]{2,1,0:T(8,128)(2,1)S(1)}, u32[]{:S(2)}, u32[]{:S(2)}) collective-permute-start(bf16[2,192,384]{2,1,0:T(8,128)(2,1)} %get-tuple-element.28), channel_id=1, source_target_pairs={{0,192},{16,208},{32,224},{48,240},{64,0},{80,16},{96,32},{112,48}... | collective-permute-start | bytes 884744 | tf_op jit(solution)/shard_map/ppermute | solution.py:20
  86.4 13.1 %collective-permute-start.20 = (bf16[2,192,384]{2,1,0:T(8,128)(2,1)}, bf16[2,192,384]{2,1,0:T(8,128)(2,1)S(1)}, u32[]{:S(2)}, u32[]{:S(2)}) collective-permute-start(bf16[2,192,384]{2,1,0:T(8,128)(2,1)} %get-tuple-element.29), channel_id=1, source_target_pairs={{0,128},{16,144},{32,160},{48,176},{64,192},{80,208},{96,224},{112... | collective-permute-start | bytes 884744 | tf_op jit(solution)/shard_map/ppermute | solution.py:20
  87.3 12.2 %collective-permute-start.21 = (bf16[2,192,384]{2,1,0:T(8,128)(2,1)}, bf16[2,192,384]{2,1,0:T(8,128)(2,1)S(1)}, u32[]{:S(2)}, u32[]{:S(2)}) collective-permute-start(bf16[2,192,384]{2,1,0:T(8,128)(2,1)} %get-tuple-element.30), channel_id=1, source_target_pairs={{0,64},{16,80},{32,96},{48,112},{64,128},{80,144},{96,160},{112,17... | collective-permute-start | bytes 884744 | tf_op jit(solution)/shard_map/ppermute | solution.py:20
  88.0 10.2 %collective-permute-start.31 = (f32[8,384]{1,0:T(8,128)S(1)}, f32[8,384]{1,0:T(8,128)S(1)}, u32[]{:S(2)}, u32[]{:S(2)}) collective-permute-start(f32[8,384]{1,0:T(8,128)S(1)} %add_add_fusion), channel_id=1, source_target_pairs={{0,1},{1,0},{2,3},{3,2},{4,5},{5,4},{6,7},{7,6},{8,9},{9,8},{10,11... | collective-permute-start | bytes 36872 | tf_op jit(solution)/shard_map/ppermute | solution.py:248
  97.4 9.5 %collective-permute-start.22 = (bf16[2,192,384]{2,1,0:T(8,128)(2,1)}, bf16[2,192,384]{2,1,0:T(8,128)(2,1)S(1)}, u32[]{:S(2)}, u32[]{:S(2)}) collective-permute-start(bf16[2,192,384]{2,1,0:T(8,128)(2,1)} %get-tuple-element.32), channel_id=1, source_target_pairs={{0,48},{16,0},{32,16},{48,32},{64,112},{80,64},{96,80},{112,96},{1... | collective-permute-start | bytes 884744 | tf_op jit(solution)/shard_map/ppermute | solution.py:25
  98.2 25.9 %collective-permute-start.23 = (bf16[2,192,384]{2,1,0:T(8,128)(2,1)}, bf16[2,192,384]{2,1,0:T(8,128)(2,1)S(1)}, u32[]{:S(2)}, u32[]{:S(2)}) collective-permute-start(bf16[2,192,384]{2,1,0:T(8,128)(2,1)} %get-tuple-element.33), channel_id=1, source_target_pairs={{0,32},{16,48},{32,0},{48,16},{64,96},{80,112},{96,64},{112,80},{1... | collective-permute-start | bytes 884744 | tf_op jit(solution)/shard_map/ppermute | solution.py:25
  98.8 25.3 %collective-permute-start.24 = (bf16[2,192,384]{2,1,0:T(8,128)(2,1)}, bf16[2,192,384]{2,1,0:T(8,128)(2,1)S(1)}, u32[]{:S(2)}, u32[]{:S(2)}) collective-permute-start(bf16[2,192,384]{2,1,0:T(8,128)(2,1)} %get-tuple-element.34), channel_id=1, source_target_pairs={{0,16},{16,32},{32,48},{48,0},{64,80},{80,96},{96,112},{112,64},{1... | collective-permute-start | bytes 884744 | tf_op jit(solution)/shard_map/ppermute | solution.py:25
  (35 other events, 640.3 us)

commit v3 on v2

v3 whole, which is shorter than its diff:
```python
import functools

import jax
import jax.numpy as jnp
from jax import lax
from jax.experimental import pallas as pl
from jax.experimental.pallas import tpu as pltpu
from jax.sharding import PartitionSpec as P

HEAD_DIM = 128
SCALE = HEAD_DIM ** (-0.5)
SIDE = 4
F32 = jnp.float32
BF16 = jnp.bfloat16
VIDEO, AUDIO = 0, 1
GATE_ROWS = 16


def along_x(array, shift):
    pairs = [(x * SIDE + z, (x + shift) % SIDE * SIDE + z) for x in range(SIDE) for z in range(SIDE)]
    return lax.ppermute(array, "vid", pairs)


def along_z(array, shift):
    pairs = [(x * SIDE + z, x * SIDE + (z + shift) % SIDE) for x in range(SIDE) for z in range(SIDE)]
    return lax.ppermute(array, "vid", pairs)


def beside_z(array, distance):
    pairs = [(x * SIDE + z, x * SIDE + (z ^ distance)) for x in range(SIDE) for z in range(SIDE)]
    return lax.ppermute(array, "vid", pairs)


def gathered(array, along):
    return [array] + [along(array, shift) for shift in range(1, SIDE)]


def returned(parts, along):
    return [parts[0]] + [along(parts[place], SIDE - place) for place in range(1, SIDE)]


def nt(a, b):
    return lax.dot_general(a, b, (((1,), (1,)), ((), ())), preferred_element_type=F32)


def nn(a, b):
    return lax.dot_general(a, b, (((1,), (0,)), ((), ())), preferred_element_type=F32)


def joined(refs, index):
    return jnp.concatenate([ref[index] for ref in refs], axis=0)


def gated(rows, gate_row):
    return (gate_row * rows.astype(F32)).astype(BF16)


def query_rows(refs, index, video_rows):
    video = [ref[index, :video_rows] for ref in refs]
    audio = [ref[index, video_rows:] for ref in refs]
    return jnp.concatenate(video, axis=0), jnp.concatenate(audio, axis=0)


def upstream(refs, gates_ref, video_rows, part):
    video, audio = query_rows(refs, 1, video_rows)
    if part == VIDEO:
        audio = gated(audio, gates_ref[1:2, :])
    else:
        video = gated(video, gates_ref[0:1, :])
    return jnp.concatenate([video, audio], axis=0)


def prepare_kernel(place_ref, aq_ref, ak_ref, av_ref, vq_ref, vk_ref, vv_ref, dv_ref, da_ref, *outs):
    audio, video_kv, queries = outs
    rows = vq_ref.shape[1]
    audio[0] = aq_ref[0]
    audio[1] = ak_ref[0]
    audio[2] = av_ref[0]
    video_kv[0] = vk_ref[0]
    video_kv[1] = vv_ref[0]
    queries[0, :rows] = vq_ref[0]
    queries[0, rows:] = jnp.zeros_like(da_ref[0])
    queries[1, :rows] = dv_ref[0]
    queries[1, rows:] = da_ref[0]


def prepare(place, audio_q, audio_k, audio_v, video_q, video_k, video_v, d_video, d_audio):
    _, video_rows, width = video_q.shape
    audio_rows = d_audio.shape[1]
    cut = pl.BlockSpec((1, audio_rows, width), lambda i, place: (0, place[0], place[1]))
    whole = lambda *shape: pl.BlockSpec(shape, lambda i, place: (0,) * len(shape))
    shapes = [
        (3, audio_rows, width),
        (2, video_rows, width),
        (2, video_rows + audio_rows, width),
    ]
    return pl.pallas_call(
        prepare_kernel,
        grid_spec=pltpu.PrefetchScalarGridSpec(
            num_scalar_prefetch=1,
            grid=(1,),
            in_specs=[cut] * 3 + [whole(*video_q.shape)] * 4 + [whole(*d_audio.shape)],
            out_specs=[whole(*shape) for shape in shapes],
        ),
        out_shape=[jax.ShapeDtypeStruct(shape, BF16) for shape in shapes],
        compiler_params=pltpu.CompilerParams(vmem_limit_bytes=56 * 2**20),
        name="prepare",
    )(place, audio_q, audio_k, audio_v, video_q, video_k, video_v, d_video, d_audio)


def forward_kernel(part, video_rows, *refs):
    q_refs, k_refs, limit_ref, gates_ref = refs[:4], refs[4:8], refs[8], refs[9]
    e_ref, o_ref, stats_ref = refs[-3:]
    queries = jnp.concatenate(query_rows(q_refs, 0, video_rows), axis=0)
    raw = nt(joined(k_refs, 0), queries)
    if part == AUDIO:
        rows = k_refs[0].shape[1]
        position = lax.broadcasted_iota(jnp.int32, (rows, raw.shape[1]), 0)
        pieces = [raw[place * rows : (place + 1) * rows] for place in range(SIDE)]
        pieces = [jnp.where(position < limit_ref[place], pieces[place], -1e30) for place in range(SIDE)]
        raw = jnp.concatenate(pieces, axis=0)
    peak = jnp.max(raw, axis=0, keepdims=True)
    expon = jnp.exp((raw - peak) * SCALE)
    total = jnp.sum(expon, axis=0, keepdims=True)
    expon = expon.astype(BF16)
    e_ref[0] = expon
    output = nn(joined(k_refs, 1).T, expon)
    o_ref[0] = output
    up = upstream(q_refs, gates_ref, video_rows, part)
    weighted = jnp.sum(up.astype(F32).T * output, axis=0, keepdims=True)
    if part == VIDEO:
        stats_ref[0] = jnp.concatenate([peak, total, weighted, jnp.broadcast_to(peak, (5, peak.shape[1]))], axis=0)
    else:
        stats_ref[0] = jnp.concatenate([refs[10][0, 0:3], peak, total, weighted, peak, peak], axis=0)


def rolled_stats(refs, video_rows, audio_rows):
    video = SIDE * video_rows
    stats = [refs[0][0]]
    for shift in range(1, SIDE):
        array = refs[shift][0]
        stats.append(
            jnp.concatenate(
                [
                    pltpu.roll(array[:, :video], shift * video_rows, 1),
                    pltpu.roll(array[:, video:], shift * audio_rows, 1),
                ],
                axis=1,
            )
        )
    return stats


def merged_stats(stats, part):
    peaks = [array[3 * part : 3 * part + 1] for array in stats]
    peak = functools.reduce(jnp.maximum, peaks)
    weights = [jnp.exp((local - peak) * SCALE) for local in peaks]
    total = sum(weight * array[3 * part + 1 : 3 * part + 2] for weight, array in zip(weights, stats))
    delta = sum(weight * array[3 * part + 2 : 3 * part + 3] for weight, array in zip(weights, stats)) / total
    return weights[0] / total, delta


def backward_keys(part, queries, up, stats, k_refs, e_ref, k_outs, first):
    factor, delta = merged_stats(stats, part)
    probs = e_ref[0].astype(F32) * factor
    grad_values = nn(probs.astype(BF16), up).astype(BF16)
    grad_probs = nt(joined(k_refs, 1), up)
    grad_scores = (probs * (grad_probs - delta)).astype(BF16)
    grad_keys = (nn(grad_scores, queries) * SCALE).astype(BF16)
    rows = k_refs[0].shape[1]
    for place in range(SIDE):
        k_outs[place][0, first : first + rows] = grad_keys[place * rows : (place + 1) * rows]
        k_outs[place][1, first : first + rows] = grad_values[place * rows : (place + 1) * rows]
    return nn(joined(k_refs, 0).T, grad_scores), factor


def backward_kernel(video_rows, *refs):
    q_refs, k_video, k_audio, stats_refs = refs[:4], refs[4:8], refs[8:12], refs[12:16]
    gates_ref, columns_ref, e_video, e_audio, o_video, o_audio = refs[16:22]
    k_outs, q_outs = refs[22:26], refs[26:30]
    rows = q_refs[0].shape[1]
    audio_rows = rows - video_rows
    video = SIDE * video_rows
    queries = jnp.concatenate(query_rows(q_refs, 0, video_rows), axis=0)
    stats = rolled_stats(stats_refs, video_rows, audio_rows)
    up = upstream(q_refs, gates_ref, video_rows, VIDEO)
    term_video, factor = backward_keys(VIDEO, queries, up, stats, k_video, e_video, k_outs, 0)
    on_video = o_video[0] * factor
    up = upstream(q_refs, gates_ref, video_rows, AUDIO)
    term_audio, factor = backward_keys(AUDIO, queries, up, stats, k_audio, e_audio, k_outs, video_rows)
    on_audio = o_audio[0] * factor
    grad_queries = term_video + term_audio
    cross_video, cross_audio = on_audio[:, :video], on_video[:, video:]
    merged = jnp.concatenate(
        [
            on_video[:, :video] + columns_ref[:, 0:1] * cross_video,
            on_audio[:, video:] + columns_ref[:, 1:2] * cross_audio,
        ],
        axis=1,
    )
    up_video, up_audio = query_rows(q_refs, 1, video_rows)
    video_sum = jnp.sum(up_video.astype(F32).T * cross_video, axis=1, keepdims=True)
    audio_sum = jnp.sum(up_audio.astype(F32).T * cross_audio, axis=1, keepdims=True)
    sums = jnp.concatenate(
        [jnp.broadcast_to(video_sum, (HEAD_DIM, 4)), jnp.broadcast_to(audio_sum, (HEAD_DIM, HEAD_DIM - 4))], axis=1
    ).T[0:GATE_ROWS]
    high = sums.astype(BF16)
    low = (sums - high.astype(F32)).astype(BF16)
    even = lax.broadcasted_iota(jnp.int32, sums.shape, 0) % 2 == 0
    sums = jnp.where(even, high.astype(F32), low.astype(F32)).astype(BF16)
    merged = merged.T.astype(BF16)
    grad_queries = (grad_queries.T * SCALE).astype(BF16)
    for place in range(SIDE):
        for index, array in ((0, merged), (1, grad_queries)):
            first = index * rows
            q_outs[place][first : first + video_rows] = array[place * video_rows : (place + 1) * video_rows]
            start = video + place * audio_rows
            q_outs[place][first + video_rows : first + rows] = array[start : start + audio_rows]
        q_outs[place][2 * rows :] = sums


def chunk_spec(array):
    shape = array.shape[:-1]
    return pl.BlockSpec((*shape, HEAD_DIM), lambda h: (0,) * len(shape) + (h,))


def head_spec(array):
    shape = array.shape[1:]
    return pl.BlockSpec((1, *shape), lambda h: (h,) + (0,) * len(shape))


def like(*shape, kind=BF16):
    return jax.ShapeDtypeStruct(shape, kind)


def cost(keys, queries, heads, products):
    return pl.CostEstimate(
        flops=2 * products * heads * keys * queries * HEAD_DIM,
        bytes_accessed=4 * heads * keys * queries,
        transcendentals=heads * keys * queries,
    )


def attention_forward(part, q_chunks, k_chunks, limits, gates, earlier, video_rows):
    heads = gates.shape[1] // HEAD_DIM
    keys, queries = SIDE * k_chunks[0].shape[1], SIDE * q_chunks[0].shape[1]
    outs = [
        like(heads, keys, queries),
        like(heads, HEAD_DIM, queries, kind=F32),
        like(heads, 8, queries, kind=F32),
    ]
    return pl.pallas_call(
        functools.partial(forward_kernel, part, video_rows),
        grid=(heads,),
        in_specs=[chunk_spec(array) for array in (*q_chunks, *k_chunks)]
        + [pl.BlockSpec(memory_space=pltpu.SMEM), chunk_spec(gates)]
        + [head_spec(array) for array in earlier],
        out_specs=[head_spec(array) for array in outs],
        out_shape=outs,
        cost_estimate=cost(keys, queries, heads, 2),
        compiler_params=pltpu.CompilerParams(vmem_limit_bytes=24 * 2**20),
        name=("forward_video", "forward_audio")[part],
    )(*q_chunks, *k_chunks, limits, gates, *earlier)


def attention_backward(q_chunks, video_keys, audio_keys, stats, gates, by_head, video_rows):
    width = gates.shape[1]
    heads = width // HEAD_DIM
    rows, q_rows = video_keys[0].shape[1] + audio_keys[0].shape[1], q_chunks[0].shape[1]
    outs = [like(2, rows, width)] * SIDE + [like(2 * q_rows + GATE_ROWS, width)] * SIDE
    chunks = [*q_chunks, *video_keys, *audio_keys]
    outs = pl.pallas_call(
        functools.partial(backward_kernel, video_rows),
        grid=(heads,),
        in_specs=[chunk_spec(array) for array in chunks]
        + [head_spec(array) for array in stats]
        + [chunk_spec(gates), pl.BlockSpec((HEAD_DIM, 2), lambda h: (h, 0))]
        + [head_spec(array) for array in by_head],
        out_specs=[chunk_spec(array) for array in outs],
        out_shape=outs,
        cost_estimate=cost(SIDE * rows, SIDE * q_rows, heads, 4),
        compiler_params=pltpu.CompilerParams(vmem_limit_bytes=32 * 2**20),
        name="backward",
    )(*chunks, *stats, gates, gates.T, *by_head)
    return outs[:SIDE], outs[SIDE:]


def total_of(refs, *index):
    return sum(ref[index].astype(F32) for ref in refs)


def finish_queries_kernel(*refs):
    parts, (video_out, audio_out, video_q, audio_q, gate_ref) = refs[:SIDE], refs[SIDE:]
    video_rows, audio_rows = video_out.shape[1], audio_out.shape[1]
    rows = video_rows + audio_rows
    for index, video, audio in ((0, video_out, audio_out), (1, video_q, audio_q)):
        first = index * rows
        video[0] = total_of(parts, slice(first, first + video_rows)).astype(BF16)
        audio[0] = total_of(parts, slice(first + video_rows, first + rows)).astype(BF16)
    gates = total_of(parts, slice(2 * rows, None))
    video_gate = gates[0:1] + gates[1:2]
    audio_gate = gates[4:5] + gates[5:6]
    gate_ref[...] = jnp.concatenate([jnp.broadcast_to(video_gate, (4, gates.shape[1])), jnp.broadcast_to(audio_gate, (4, gates.shape[1]))], axis=0)


def finish_queries(parts, video_rows, audio_rows):
    width = parts[0].shape[1]
    video, audio = like(1, video_rows, width), like(1, audio_rows, width)
    return pl.pallas_call(
        finish_queries_kernel,
        out_shape=[video, audio, video, audio, like(8, width, kind=F32)],
        name="finish_queries",
    )(*parts)


def finish_keys_kernel(*refs):
    parts, (video_k, video_v, audio_k, audio_v) = refs[:SIDE], refs[SIDE:]
    rows = video_k.shape[1]
    for index, video, audio in ((0, video_k, audio_k), (1, video_v, audio_v)):
        video[0] = total_of(parts, index, slice(0, rows)).astype(BF16)
        audio[0] = total_of(parts, index, slice(rows, None)).astype(BF16)


def finish_keys(parts, video_rows, audio_rows):
    width = parts[0].shape[2]
    video, audio = like(1, video_rows, width), like(1, audio_rows, width)
    return pl.pallas_call(finish_keys_kernel, out_shape=[video, video, audio, audio], name="finish_keys")(*parts)


def own_audio(array, vid_size, aud_size):
    pairs = [
        (v * aud_size + a, (2 * a + v % 2) * aud_size + v // 2) for v in range(vid_size) for a in range(aud_size)
    ]
    return lax.ppermute(array, ("vid", "aud"), pairs)


def fenced(holds, function, *arrays):
    outs = jax.eval_shape(function, *arrays)
    return lax.cond(
        holds, function, lambda *_: jax.tree.map(lambda out: jnp.zeros(out.shape, out.dtype), outs), *arrays
    )


def shards(
    video_q, video_k, video_v, audio_q, audio_k, audio_v, video_gate, audio_gate, audio_len, d_video_out, d_audio_out
):
    vid = lax.axis_index("vid")
    sizes = lax.axis_size("vid"), lax.axis_size("aud")
    video_rows, audio_rows = video_q.shape[1], d_audio_out.shape[1]
    holds = audio_len[0] > 0
    place = jnp.stack([vid % 2, vid // 2]).astype(jnp.int32)
    send_audio, video_kv, queries = prepare(
        place, audio_q, audio_k, audio_v, video_q, video_k, video_v, d_video_out, d_audio_out
    )

    def first_chunks(send_audio, video_kv):
        return own_audio(send_audio, *sizes), along_z(video_kv, 1), along_z(video_kv, SIDE - 1)

    audio, before, behind = fenced(holds, first_chunks, send_audio, video_kv)
    audio_kv = audio[1:]
    q_chunks = gathered(lax.dynamic_update_slice(queries, audio[0:1], (0, video_rows, 0)), along_x)
    video_keys = [video_kv, before, along_z(video_kv, 2), behind]
    audio_keys = gathered(audio_kv, along_z)
    gates = jnp.stack([video_gate, audio_gate])
    column, row = vid // SIDE, vid % SIDE
    limits = jnp.stack([audio_len[0] - (column * SIDE + (row - p) % SIDE) * audio_rows for p in range(SIDE)])
    e_video, o_video, stats = attention_forward(VIDEO, q_chunks, video_keys, limits, gates, (), video_rows)
    e_audio, o_audio, stats = attention_forward(AUDIO, q_chunks, audio_keys, limits, gates, (stats,), video_rows)
    stats = gathered(stats, along_x)
    key_parts, query_parts = attention_backward(
        q_chunks, video_keys, audio_keys, stats, gates, (e_video, e_audio, o_video, o_audio), video_rows
    )

    def query_results(*parts):
        *results, gate = finish_queries(parts, video_rows, audio_rows)
        for distance in (1, 2):
            gate = gate + beside_z(gate, distance)
        return (*results, gate + lax.ppermute(gate, "pair", [(0, 1), (1, 0)]))

    query_parts = fenced(holds, lambda *parts: tuple(returned(parts, along_x)), *query_parts)
    video_out, audio_out, grad_video_q, grad_audio_q, gate = fenced(holds, query_results, *query_parts)
    key_parts = returned(key_parts, along_z)
    grad_video_k, grad_video_v, grad_audio_k, grad_audio_v = finish_keys(key_parts, video_rows, audio_rows)
    return (
        video_out,
        audio_out,
        grad_video_q,
        grad_video_k,
        grad_video_v,
        grad_audio_q,
        grad_audio_k,
        grad_audio_v,
        gate[0],
        gate[7],
    )


def solution(mesh):
    split = P("pair", "vid", "aud")
    rows = P("pair", "aud", None)
    return jax.shard_map(
        shards,
        mesh=mesh,
        in_specs=(split, split, split, rows, rows, rows, P("aud"), P("aud"), P("pair"), split, split),
        out_specs=(split,) * 8 + (P("aud"), P("aud")),
        check_vma=False,
    )
```

time: 127 us -> 137 us (1.079)
  starting transfers between devices: 63.7 us -> 44.9 us
  local copies, waits for them, and re-layouts: 12 us -> 25.8 us
  waiting for transfers between devices: 31.7 us -> 39.9 us
  Pallas kernels: 13.5 us -> 20.5 us
    unnamed x56 -> x70, local copies, waits for them, and re-layouts: 3.85 us -> 22 us
    ppermute x12 -> x9, waiting for transfers between devices: 25.4 us -> 8.35 us  [along_z(): return lax.ppermute(array, 'vid', pairs)]
    ppermute x18 -> x9, waiting for transfers between devices: 5.96 us -> 19.8 us  [along_x(): return lax.ppermute(array, 'vid', pairs)]
    ppermute x2 -> x4, waiting for transfers between devices: 0.35 us -> 11.7 us  [the longest x2 10.9 us: beside_z(): return lax.ppermute(array, 'vid', pairs)]
    ppermute x18 -> x9, starting transfers between devices: 23.6 us -> 14.4 us  [along_x(): return lax.ppermute(array, 'vid', pairs)]
    pallas_call x2 -> x6, Pallas kernels: 13.5 us -> 20.5 us  [the longest x2 7.71 us: attention_forward(): pl.pallas_call(functools.partial(forward_kernel, part, video_rows), grid=...]
    ppermute x2 -> x4, starting transfers between devices: 10.1 us -> 4.43 us  [the longest x1 2.1 us: query_results(): return (*results, gate + lax.ppermute(gate, 'pair', [(0, 1), (1, 0)]))]
    ppermute x12 -> x9, starting transfers between devices: 30.1 us -> 26.1 us  [along_z(): return lax.ppermute(array, 'vid', pairs)]
  transfers between devices with their start and end apart: 32 -> 22, of which waited for: 10 -> 9; matrix products, arithmetic and copies ran while one was open for 7% -> 4% of each run, Pallas kernels for 0% -> 4%
where the time goes in v3:
time: 137 us; the launch traced here: 136 us
  starting transfers between devices  44.9 us (33%)
  waiting for transfers between devices  39.9 us (29%)
  local copies, waits for them, and re-layouts  25.8 us (19%)
  Pallas kernels  20.5 us (15%)
  other arithmetic  2.79 us (2%)
  between operations  1.66 us (1%)
    ppermute x9, starting transfers between devices, along_z(): return lax.ppermute(array, 'vid', pairs)  26.1 us
    unnamed x70, local copies, waits for them, and re-layouts  22 us
    ppermute x9, waiting for transfers between devices, along_x(): return lax.ppermute(array, 'vid', pairs)  19.8 us
    ppermute x9, starting transfers between devices, along_x(): return lax.ppermute(array, 'vid', pairs)  14.4 us
    ppermute x2, waiting for transfers between devices, beside_z(): return lax.ppermute(array, 'vid', pairs)  10.9 us
    ppermute x9, waiting for transfers between devices, along_z(): return lax.ppermute(array, 'vid', pairs)  8.35 us
    pallas_call x2, Pallas kernels, attention_forward(): pl.pallas_call(functools.partial(forward_kernel, part, video_rows), grid=...  7.71 us
    pallas_call x1, Pallas kernels, attention_backward(): pl.pallas_call(functools.partial(backward_kernel, video_rows), grid=(head...  6.27 us
  transfers between devices with their start and end apart: 22, of which 9 were waited for; matrix products, arithmetic and copies ran while one was open for 4% of the time, Pallas kernels for 4%

profile of v3, /device:TPU:1, one launch (start us, length us, event | category | flops | bytes accessed | tf_op | source)
XLA Modules:
  0.0 135.7 jit_solution(7572026026683969252)
XLA Ops:
  1.9 2.5 %prepare.1 = (bf16[3,64,384]{2,1,0:T(8,128)(2,1)S(1)}, bf16[2,128,384]{2,1,0:T(8,128)(2,1)S(1)}, bf16[2,192,384]{2,1,0:T(8,128)(2,1)}) custom-call(s32[2]{0:T(128)} %pad_add_fusion.place_ref, bf16[1,128,3072]{2,1,0:T(8,128)(2,1)} %aq_ref.1, bf16[1,128,3072]{2,1,0:T(8,128)(2,1)} %ak_ref.1, bf16[1,128,3072]{2,1,0:T(8,128)(2,1)} %av_ref.1, ...), custom_call_target="tpu_custom_call" | custom-call | tf_op jit(solution)/shard_map/prepare/pallas_call | solution.py:97
  4.4 17.3 %conditional.3 = (bf16[3,64,384]{2,1,0:T(8,128)(2,1)}, bf16[2,128,384]{2,1,0:T(8,128)(2,1)}, bf16[2,128,384]{2,1,0:T(8,128)(2,1)}, bf16[1,64,384]{2,1,0:T(8,128)(2,1)S(1)}, bf16[2,64,384]{2,1,0:T(8,128)(2,1)}) conditional(s32[]{:T(128)} %convert_element_type.2, () %tuple.37, (bf16[3,64,384]{2,1,0:T(8,128)(2,1)S(1)}, ...), branch_computations={%region_0.1_spmd, %region_1.2_spmd} | conditional | bytes 2457760 | solution.py:339
  4.4 5.3 %collective-permute-start.2 = (bf16[2,128,384]{2,1,0:T(8,128)(2,1)S(1)}, bf16[2,128,384]{2,1,0:T(8,128)(2,1)}, u32[]{:S(2)}, u32[]{:S(2)}) collective-permute-start(bf16[2,128,384]{2,1,0:T(8,128)(2,1)S(1)} %get-tuple-element.27), channel_id=1, source_target_pairs={{0,48},{16,0},{32,16},{48,32},{64,112},{80,64},{96,80},{112,96},{1... | collective-permute-start | bytes 589832 | tf_op jit(solution)/shard_map/cond/branch_1_fun/ppermute | solution.py:26
  13.3 8.3 %collective-permute-done.1 = bf16[2,128,384]{2,1,0:T(8,128)(2,1)} collective-permute-done((bf16[2,128,384]{2,1,0:T(8,128)(2,1)S(1)}, bf16[2,128,384]{2,1,0:T(8,128)(2,1)}, u32[]{:S(2)}, u32[]{:S(2)}) %collective-permute-start.1) | collective-permute-done | bytes 196640 | tf_op jit(solution)/shard_map/cond/branch_1_fun/ppermute | solution.py:26
  22.3 5.1 %collective-permute-start.11 = (bf16[2,192,384]{2,1,0:T(8,128)(2,1)}, bf16[2,192,384]{2,1,0:T(8,128)(2,1)S(1)}, u32[]{:S(2)}, u32[]{:S(2)}) collective-permute-start(bf16[2,192,384]{2,1,0:T(8,128)(2,1)} %constant_dynamic-update-slice_fusion.refs_0_), channel_id=1, source_target_pairs={{0,192},{16,208},{32,224},{48,240},{64,0},{80,16},{96,32},{112,48}... | collective-permute-start | bytes 884744 | tf_op jit(solution)/shard_map/ppermute | solution.py:21
  28.4 2.6 %collective-permute-start.10 = (bf16[2,192,384]{2,1,0:T(8,128)(2,1)}, bf16[2,192,384]{2,1,0:T(8,128)(2,1)S(1)}, u32[]{:S(2)}, u32[]{:S(2)}) collective-permute-start(bf16[2,192,384]{2,1,0:T(8,128)(2,1)} %constant_dynamic-update-slice_fusion.refs_0_), channel_id=1, source_target_pairs={{0,128},{16,144},{32,160},{48,176},{64,192},{80,208},{96,224},{112... | collective-permute-start | bytes 884744 | tf_op jit(solution)/shard_map/ppermute | solution.py:21
  31.8 7.6 %collective-permute-start.15 = (bf16[2,64,384]{2,1,0:T(8,128)(2,1)}, bf16[2,64,384]{2,1,0:T(8,128)(2,1)}, u32[]{:S(2)}, u32[]{:S(2)}) collective-permute-start(bf16[2,64,384]{2,1,0:T(8,128)(2,1)} %get-tuple-element.88.refs_4_.refs_8_), channel_id=1, source_target_pairs={{0,48},{16,0},{32,16},{48,32},{64,112},{80,64},{96,80},{112,96},{1... | collective-permute-start | bytes 294920 | tf_op jit(solution)/shard_map/ppermute | solution.py:26
  42.3 2.2 %collective-permute-start.13 = (bf16[2,64,384]{2,1,0:T(8,128)(2,1)}, bf16[2,64,384]{2,1,0:T(8,128)(2,1)S(1)}, u32[]{:S(2)}, u32[]{:S(2)}) collective-permute-start(bf16[2,64,384]{2,1,0:T(8,128)(2,1)} %get-tuple-element.88.refs_4_.refs_8_), channel_id=1, source_target_pairs={{0,16},{16,32},{32,48},{48,0},{64,80},{80,96},{96,112},{112,64},{1... | collective-permute-start | bytes 294920 | tf_op jit(solution)/shard_map/ppermute | solution.py:26
  50.8 4.0 %forward_video.1 = (bf16[3,512,768]{2,1,0:T(8,128)(2,1)S(1)}, f32[3,128,768]{2,1,0:T(8,128)S(1)}, f32[3,8,768]{2,1,0:T(8,128)S(1)}) custom-call(bf16[2,192,384]{2,1,0:T(8,128)(2,1)S(1)} %copy-done.13, bf16[2,192,384]{2,1,0:T(8,128)(2,1)S(1)} %copy-done.11, bf16[2,192,384]{2,1,0:T(8,128)(2,1)S(1)} %copy-done.8, bf16[2,192,384]{2,1,0:T(8,128)(2,1)S(1)} %copy-done.5, ...), custom_call_target="tpu_custom_call" | custom-call | flops 603979776 | bytes 4718592 | tf_op jit(solution)/shard_map/forward_video/pallas_call | solution.py:252
  54.9 3.7 %forward_audio.1 = (bf16[3,256,768]{2,1,0:T(8,128)(2,1)S(1)}, f32[3,128,768]{2,1,0:T(8,128)S(1)}, f32[3,8,768]{2,1,0:T(8,128)}) custom-call(bf16[2,192,384]{2,1,0:T(8,128)(2,1)S(1)} %copy-done.14, bf16[2,192,384]{2,1,0:T(8,128)(2,1)S(1)} %copy-done.11, bf16[2,192,384]{2,1,0:T(8,128)(2,1)S(1)} %copy-done.8, bf16[2,192,384]{2,1,0:T(8,128)(2,1)S(1)} %copy-done.5, ...), custom_call_target="tpu_custom_call" | custom-call | flops 301989888 | bytes 2359296 | tf_op jit(solution)/shard_map/forward_audio/pallas_call | solution.py:252
  60.7 2.2 %collective-permute-start.18 = (f32[3,8,768]{2,1,0:T(8,128)}, f32[3,8,768]{2,1,0:T(8,128)}, u32[]{:S(2)}, u32[]{:S(2)}) collective-permute-start(f32[3,8,768]{2,1,0:T(8,128)} %get-tuple-element.90.refs_12_), channel_id=1, source_target_pairs={{0,192},{16,208},{32,224},{48,240},{64,0},{80,16},{96,32},{112,48}... | collective-permute-start | bytes 221192 | tf_op jit(solution)/shard_map/ppermute | solution.py:21
  65.7 2.2 %collective-permute-done.17.refs_14_ = f32[3,8,768]{2,1,0:T(8,128)} collective-permute-done((f32[3,8,768]{2,1,0:T(8,128)}, f32[3,8,768]{2,1,0:T(8,128)}, u32[]{:S(2)}, u32[]{:S(2)}) %collective-permute-start.17) | collective-permute-done | bytes 73760 | tf_op jit(solution)/shard_map/ppermute | solution.py:21
  78.7 6.3 %backward.1 = (bf16[2,192,384]{2,1,0:T(8,128)(2,1)S(1)}, bf16[2,192,384]{2,1,0:T(8,128)(2,1)}, bf16[2,192,384]{2,1,0:T(8,128)(2,1)}, bf16[2,192,384]{2,1,0:T(8,1...) custom-call(bf16[2,192,384]{2,1,0:T(8,128)(2,1)S(1)} %copy-done.15, ...), custom_call_target="tpu_custom_call" | custom-call | flops 1811939328 | bytes 7077888 | tf_op jit(solution)/shard_map/backward/pallas_call | solution.py:272
  86.5 6.3 %collective-permute-start.19 = (bf16[2,192,384]{2,1,0:T(8,128)(2,1)}, bf16[2,192,384]{2,1,0:T(8,128)(2,1)S(1)}, u32[]{:S(2)}, u32[]{:S(2)}) collective-permute-start(bf16[2,192,384]{2,1,0:T(8,128)(2,1)} %get-tuple-element.103), channel_id=1, source_target_pairs={{0,48},{16,0},{32,16},{48,32},{64,112},{80,64},{96,80},{112,96},{1... | collective-permute-start | bytes 884744 | tf_op jit(solution)/shard_map/ppermute | solution.py:26
  92.8 2.4 %collective-permute-start.20 = (bf16[2,192,384]{2,1,0:T(8,128)(2,1)}, bf16[2,192,384]{2,1,0:T(8,128)(2,1)S(1)}, u32[]{:S(2)}, u32[]{:S(2)}) collective-permute-start(bf16[2,192,384]{2,1,0:T(8,128)(2,1)} %get-tuple-element.104), channel_id=1, source_target_pairs={{0,32},{16,48},{32,0},{48,16},{64,96},{80,112},{96,64},{112,80},{1... | collective-permute-start | bytes 884744 | tf_op jit(solution)/shard_map/ppermute | solution.py:26
  95.1 18.4 %conditional.4 = (bf16[400,384]{1,0:T(8,128)(2,1)}, bf16[400,384]{1,0:T(8,128)(2,1)}, bf16[400,384]{1,0:T(8,128)(2,1)}, bf16[400,384]{1,0:T(8,128)(2,1)}) conditional(s32[]{:T(128)} %convert_element_type.2, () %tuple.36, (bf16[400,384]{1,0:T(8,128)(2,1)S(1)}, bf16[400,384]{1,0:T(8,128)(2,1)S(1)}, bf16[400,384]{1,0:T(8,128)(2,1)S(1)}, ...), branch_computations={%region_2.3_spmd, %region_3.4_spmd} | conditional | bytes 3686552 | solution.py:339
  96.8 4.4 %collective-permute-done.3 = bf16[400,384]{1,0:T(8,128)(2,1)} collective-permute-done((bf16[400,384]{1,0:T(8,128)(2,1)S(1)}, bf16[400,384]{1,0:T(8,128)(2,1)}, u32[]{:S(2)}, u32[]{:S(2)}) %collective-permute-start.3) | collective-permute-done | bytes 307232 | tf_op jit(solution)/shard_map/cond/branch_1_fun/ppermute | solution.py:21
  101.1 3.1 %collective-permute-done.4 = bf16[400,384]{1,0:T(8,128)(2,1)} collective-permute-done((bf16[400,384]{1,0:T(8,128)(2,1)S(1)}, bf16[400,384]{1,0:T(8,128)(2,1)}, u32[]{:S(2)}, u32[]{:S(2)}) %collective-permute-start.4) | collective-permute-done | bytes 307232 | tf_op jit(solution)/shard_map/cond/branch_1_fun/ppermute | solution.py:21
  104.2 9.4 %collective-permute-done.5 = bf16[400,384]{1,0:T(8,128)(2,1)} collective-permute-done((bf16[400,384]{1,0:T(8,128)(2,1)S(1)}, bf16[400,384]{1,0:T(8,128)(2,1)}, u32[]{:S(2)}, u32[]{:S(2)}) %collective-permute-start.5) | collective-permute-done | bytes 307232 | tf_op jit(solution)/shard_map/cond/branch_1_fun/ppermute | solution.py:21
  113.6 19.0 %conditional.5 = (bf16[1,128,384]{2,1,0:T(8,128)(2,1)}, bf16[1,64,384]{2,1,0:T(8,128)(2,1)}, bf16[1,128,384]{2,1,0:T(8,128)(2,1)}, bf16[1,64,384]{2,1,0:T(8,128)...) conditional(s32[]{:T(128)} %convert_element_type.2, () %tuple.35, ...), branch_computations={%region_4.5_spmd, %region_5.6_spmd} | conditional | flops 9984 | bytes 311908 | solution.py:339
  113.6 2.0 %finish_queries.1 = (bf16[1,128,384]{2,1,0:T(8,128)(2,1)}, bf16[1,64,384]{2,1,0:T(8,128)(2,1)}, bf16[1,128,384]{2,1,0:T(8,128)(2,1)}, bf16[1,64,384]{2,1,0:T(8,128)(2,1)}, f32[8,384]{1,0:T(8,128)}) custom-call(bf16[400,384]{1,0:T(8,128)(2,1)} %get-tuple-element.32.refs_0_, bf16[400,384]{1,0:T(8,128)(2,1)} %get-tuple-element.33.refs_1_, ...), custom_call_target="tpu_custom_call" | custom-call | tf_op jit(solution)/shard_map/cond/branch_1_fun/finish_queries/pallas_call | solution.py:309
  116.6 7.5 %collective-permute-done.6 = f32[8,384]{1,0:T(8,128)S(1)} collective-permute-done((f32[8,384]{1,0:T(8,128)}, f32[8,384]{1,0:T(8,128)S(1)}, u32[]{:S(2)}, u32[]{:S(2)}) %collective-permute-start.6) | collective-permute-done | bytes 12320 | tf_op jit(solution)/shard_map/cond/branch_1_fun/ppermute | solution.py:31
  124.8 3.4 %collective-permute-done.7 = f32[8,384]{1,0:T(8,128)S(1)} collective-permute-done((f32[8,384]{1,0:T(8,128)S(1)}, f32[8,384]{1,0:T(8,128)S(1)}, u32[]{:S(2)}, u32[]{:S(2)}) %collective-permute-start.7) | collective-permute-done | bytes 12320 | tf_op jit(solution)/shard_map/cond/branch_1_fun/ppermute | solution.py:31
  128.3 2.1 %collective-permute-start.8 = (f32[8,384]{1,0:T(8,128)S(1)}, f32[8,384]{1,0:T(8,128)S(1)}, u32[]{:S(2)}, u32[]{:S(2)}) collective-permute-start(f32[8,384]{1,0:T(8,128)S(1)} %add.33), channel_id=1, source_target_pairs={{0,1},{1,0},{2,3},{3,2},{4,5},{5,4},{6,7},{7,6},{8,9},{9,8},{10,11... | collective-permute-start | bytes 36872 | tf_op jit(solution)/shard_map/cond/branch_1_fun/ppermute | solution.py:378
  (112 shorter events, 41.5 us)
Async XLA Ops:
  4.4 41.6 %copy-start.30 = (bf16[2,128,384]{2,1,0:T(8,128)(2,1)}, bf16[2,128,384]{2,1,0:T(8,128)(2,1)S(1)}, u32[]{:S(2)}) copy-start(bf16[2,128,384]{2,1,0:T(8,128)(2,1)S(1)} %get-tuple-element.84.refs_4_) | copy-start | bytes 589828
  4.4 35.0 %copy-start.32 = (f32[384]{0:T(512)S(1)}, f32[384]{0:T(512)}, u32[]{:S(2)}) copy-start(f32[384]{0:T(512)} %param.24) | copy-start | bytes 4612
  4.4 8.9 %collective-permute-start.2 = (bf16[2,128,384]{2,1,0:T(8,128)(2,1)S(1)}, bf16[2,128,384]{2,1,0:T(8,128)(2,1)}, u32[]{:S(2)}, u32[]{:S(2)}) collective-permute-start(bf16[2,128,384]{2,1,0:T(8,128)(2,1)S(1)} %get-tuple-element.27), channel_id=1, source_target_pairs={{0,48},{16,0},{32,16},{48,32},{64,112},{80,64},{96,80},{112,96},{1... | collective-permute-start | bytes 589832 | tf_op jit(solution)/shard_map/cond/branch_1_fun/ppermute | solution.py:26
  9.7 12.0 %collective-permute-start.1 = (bf16[2,128,384]{2,1,0:T(8,128)(2,1)S(1)}, bf16[2,128,384]{2,1,0:T(8,128)(2,1)}, u32[]{:S(2)}, u32[]{:S(2)}) collective-permute-start(bf16[2,128,384]{2,1,0:T(8,128)(2,1)S(1)} %get-tuple-element.27), channel_id=1, source_target_pairs={{0,16},{16,32},{32,48},{48,0},{64,80},{80,96},{96,112},{112,64},{1... | collective-permute-start | bytes 589832 | tf_op jit(solution)/shard_map/cond/branch_1_fun/ppermute | solution.py:26
  9.7 1.3 collective-permute-start
  22.3 19.3 %collective-permute-start.11 = (bf16[2,192,384]{2,1,0:T(8,128)(2,1)}, bf16[2,192,384]{2,1,0:T(8,128)(2,1)S(1)}, u32[]{:S(2)}, u32[]{:S(2)}) collective-permute-start(bf16[2,192,384]{2,1,0:T(8,128)(2,1)} %constant_dynamic-update-slice_fusion.refs_0_), channel_id=1, source_target_pairs={{0,192},{16,208},{32,224},{48,240},{64,0},{80,16},{96,32},{112,48}... | collective-permute-start | bytes 884744 | tf_op jit(solution)/shard_map/ppermute | solution.py:21
  27.4 12.0 %collective-permute-start.12 = (bf16[2,128,384]{2,1,0:T(8,128)(2,1)S(1)}, bf16[2,128,384]{2,1,0:T(8,128)(2,1)S(1)}, u32[]{:S(2)}, u32[]{:S(2)}) collective-permute-start(bf16[2,128,384]{2,1,0:T(8,128)(2,1)S(1)} %get-tuple-element.84.refs_4_), channel_id=1, source_target_pairs={{0,32},{16,48},{32,0},{48,16},{64,96},{80,112},{96,64},{112,80},{1... | collective-permute-start | bytes 589832 | tf_op jit(solution)/shard_map/ppermute | solution.py:26
  28.4 16.2 %collective-permute-start.10 = (bf16[2,192,384]{2,1,0:T(8,128)(2,1)}, bf16[2,192,384]{2,1,0:T(8,128)(2,1)S(1)}, u32[]{:S(2)}, u32[]{:S(2)}) collective-permute-start(bf16[2,192,384]{2,1,0:T(8,128)(2,1)} %constant_dynamic-update-slice_fusion.refs_0_), channel_id=1, source_target_pairs={{0,128},{16,144},{32,160},{48,176},{64,192},{80,208},{96,224},{112... | collective-permute-start | bytes 884744 | tf_op jit(solution)/shard_map/ppermute | solution.py:21
  31.0 14.4 %collective-permute-start.9 = (bf16[2,192,384]{2,1,0:T(8,128)(2,1)}, bf16[2,192,384]{2,1,0:T(8,128)(2,1)S(1)}, u32[]{:S(2)}, u32[]{:S(2)}) collective-permute-start(bf16[2,192,384]{2,1,0:T(8,128)(2,1)} %constant_dynamic-update-slice_fusion.refs_0_), channel_id=1, source_target_pairs={{0,64},{16,80},{32,96},{48,112},{64,128},{80,144},{96,160},{112,17... | collective-permute-start | bytes 884744 | tf_op jit(solution)/shard_map/ppermute | solution.py:21
  31.8 23.0 %collective-permute-start.15 = (bf16[2,64,384]{2,1,0:T(8,128)(2,1)}, bf16[2,64,384]{2,1,0:T(8,128)(2,1)}, u32[]{:S(2)}, u32[]{:S(2)}) collective-permute-start(bf16[2,64,384]{2,1,0:T(8,128)(2,1)} %get-tuple-element.88.refs_4_.refs_8_), channel_id=1, source_target_pairs={{0,48},{16,0},{32,16},{48,32},{64,112},{80,64},{96,80},{112,96},{1... | collective-permute-start | bytes 294920 | tf_op jit(solution)/shard_map/ppermute | solution.py:26
  40.1 14.7 %collective-permute-start.14 = (bf16[2,64,384]{2,1,0:T(8,128)(2,1)}, bf16[2,64,384]{2,1,0:T(8,128)(2,1)S(1)}, u32[]{:S(2)}, u32[]{:S(2)}) collective-permute-start(bf16[2,64,384]{2,1,0:T(8,128)(2,1)} %get-tuple-element.88.refs_4_.refs_8_), channel_id=1, source_target_pairs={{0,32},{16,48},{32,0},{48,16},{64,96},{80,112},{96,64},{112,80},{1... | collective-permute-start | bytes 294920 | tf_op jit(solution)/shard_map/ppermute | solution.py:26
  42.3 12.6 %collective-permute-start.13 = (bf16[2,64,384]{2,1,0:T(8,128)(2,1)}, bf16[2,64,384]{2,1,0:T(8,128)(2,1)S(1)}, u32[]{:S(2)}, u32[]{:S(2)}) collective-permute-start(bf16[2,64,384]{2,1,0:T(8,128)(2,1)} %get-tuple-element.88.refs_4_.refs_8_), channel_id=1, source_target_pairs={{0,16},{16,32},{32,48},{48,0},{64,80},{80,96},{96,112},{112,64},{1... | collective-permute-start | bytes 294920 | tf_op jit(solution)/shard_map/ppermute | solution.py:26
  60.7 5.0 %collective-permute-start.18 = (f32[3,8,768]{2,1,0:T(8,128)}, f32[3,8,768]{2,1,0:T(8,128)}, u32[]{:S(2)}, u32[]{:S(2)}) collective-permute-start(f32[3,8,768]{2,1,0:T(8,128)} %get-tuple-element.90.refs_12_), channel_id=1, source_target_pairs={{0,192},{16,208},{32,224},{48,240},{64,0},{80,16},{96,32},{112,48}... | collective-permute-start | bytes 221192 | tf_op jit(solution)/shard_map/ppermute | solution.py:21
  62.9 5.0 %collective-permute-start.17 = (f32[3,8,768]{2,1,0:T(8,128)}, f32[3,8,768]{2,1,0:T(8,128)}, u32[]{:S(2)}, u32[]{:S(2)}) collective-permute-start(f32[3,8,768]{2,1,0:T(8,128)} %get-tuple-element.90.refs_12_), channel_id=1, source_target_pairs={{0,128},{16,144},{32,160},{48,176},{64,192},{80,208},{96,224},{112... | collective-permute-start | bytes 221192 | tf_op jit(solution)/shard_map/ppermute | solution.py:21
  64.0 4.7 %collective-permute-start.16 = (f32[3,8,768]{2,1,0:T(8,128)}, f32[3,8,768]{2,1,0:T(8,128)}, u32[]{:S(2)}, u32[]{:S(2)}) collective-permute-start(f32[3,8,768]{2,1,0:T(8,128)} %get-tuple-element.90.refs_12_), channel_id=1, source_target_pairs={{0,64},{16,80},{32,96},{48,112},{64,128},{80,144},{96,160},{112,17... | collective-permute-start | bytes 221192 | tf_op jit(solution)/shard_map/ppermute | solution.py:21
  86.5 46.2 %collective-permute-start.19 = (bf16[2,192,384]{2,1,0:T(8,128)(2,1)}, bf16[2,192,384]{2,1,0:T(8,128)(2,1)S(1)}, u32[]{:S(2)}, u32[]{:S(2)}) collective-permute-start(bf16[2,192,384]{2,1,0:T(8,128)(2,1)} %get-tuple-element.103), channel_id=1, source_target_pairs={{0,48},{16,0},{32,16},{48,32},{64,112},{80,64},{96,80},{112,96},{1... | collective-permute-start | bytes 884744 | tf_op jit(solution)/shard_map/ppermute | solution.py:26
  92.8 39.9 %collective-permute-start.20 = (bf16[2,192,384]{2,1,0:T(8,128)(2,1)}, bf16[2,192,384]{2,1,0:T(8,128)(2,1)S(1)}, u32[]{:S(2)}, u32[]{:S(2)}) collective-permute-start(bf16[2,192,384]{2,1,0:T(8,128)(2,1)} %get-tuple-element.104), channel_id=1, source_target_pairs={{0,32},{16,48},{32,0},{48,16},{64,96},{80,112},{96,64},{112,80},{1... | collective-permute-start | bytes 884744 | tf_op jit(solution)/shard_map/ppermute | solution.py:26
  95.1 6.0 %collective-permute-start.3 = (bf16[400,384]{1,0:T(8,128)(2,1)S(1)}, bf16[400,384]{1,0:T(8,128)(2,1)}, u32[]{:S(2)}, u32[]{:S(2)}) collective-permute-start(bf16[400,384]{1,0:T(8,128)(2,1)S(1)} %get-tuple-element.29), channel_id=1, source_target_pairs={{0,192},{16,208},{32,224},{48,240},{64,0},{80,16},{96,32},{112,48}... | collective-permute-start | bytes 921608 | tf_op jit(solution)/shard_map/cond/branch_1_fun/ppermute | solution.py:21
  96.2 8.0 %collective-permute-start.4 = (bf16[400,384]{1,0:T(8,128)(2,1)S(1)}, bf16[400,384]{1,0:T(8,128)(2,1)}, u32[]{:S(2)}, u32[]{:S(2)}) collective-permute-start(bf16[400,384]{1,0:T(8,128)(2,1)S(1)} %get-tuple-element.30), channel_id=1, source_target_pairs={{0,128},{16,144},{32,160},{48,176},{64,192},{80,208},{96,224},{112... | collective-permute-start | bytes 921608 | tf_op jit(solution)/shard_map/cond/branch_1_fun/ppermute | solution.py:21
  96.5 17.1 %collective-permute-start.5 = (bf16[400,384]{1,0:T(8,128)(2,1)S(1)}, bf16[400,384]{1,0:T(8,128)(2,1)}, u32[]{:S(2)}, u32[]{:S(2)}) collective-permute-start(bf16[400,384]{1,0:T(8,128)(2,1)S(1)} %get-tuple-element.31), channel_id=1, source_target_pairs={{0,64},{16,80},{32,96},{48,112},{64,128},{80,144},{96,160},{112,17... | collective-permute-start | bytes 921608 | tf_op jit(solution)/shard_map/cond/branch_1_fun/ppermute | solution.py:21
  113.6 19.1 %collective-permute-start.21 = (bf16[2,192,384]{2,1,0:T(8,128)(2,1)S(1)}, bf16[2,192,384]{2,1,0:T(8,128)(2,1)S(1)}, u32[]{:S(2)}, u32[]{:S(2)}) collective-permute-start(bf16[2,192,384]{2,1,0:T(8,128)(2,1)S(1)} %copy-done.26), channel_id=1, source_target_pairs={{0,16},{16,32},{32,48},{48,0},{64,80},{80,96},{96,112},{112,64},{1... | collective-permute-start | bytes 884744 | tf_op jit(solution)/shard_map/ppermute | solution.py:26
  115.6 8.5 %collective-permute-start.6 = (f32[8,384]{1,0:T(8,128)}, f32[8,384]{1,0:T(8,128)S(1)}, u32[]{:S(2)}, u32[]{:S(2)}) collective-permute-start(f32[8,384]{1,0:T(8,128)} %get-tuple-element.40), channel_id=1, source_target_pairs={{0,16},{16,0},{32,48},{48,32},{64,80},{80,64},{96,112},{112,96},{1... | collective-permute-start | bytes 36872 | tf_op jit(solution)/shard_map/cond/branch_1_fun/ppermute | solution.py:31
  124.8 3.4 %collective-permute-start.7 = (f32[8,384]{1,0:T(8,128)S(1)}, f32[8,384]{1,0:T(8,128)S(1)}, u32[]{:S(2)}, u32[]{:S(2)}) collective-permute-start(f32[8,384]{1,0:T(8,128)S(1)} %add.32), channel_id=1, source_target_pairs={{0,32},{16,48},{32,0},{48,16},{64,96},{80,112},{96,64},{112,80},{1... | collective-permute-start | bytes 36872 | tf_op jit(solution)/shard_map/cond/branch_1_fun/ppermute | solution.py:31
  128.3 2.9 %collective-permute-start.8 = (f32[8,384]{1,0:T(8,128)S(1)}, f32[8,384]{1,0:T(8,128)S(1)}, u32[]{:S(2)}, u32[]{:S(2)}) collective-permute-start(f32[8,384]{1,0:T(8,128)S(1)} %add.33), channel_id=1, source_target_pairs={{0,1},{1,0},{2,3},{3,2},{4,5},{5,4},{6,7},{7,6},{8,9},{9,8},{10,11... | collective-permute-start | bytes 36872 | tf_op jit(solution)/shard_map/cond/branch_1_fun/ppermute | solution.py:378
  (33 other events, 105.2 us)

commit v4 on v3

v4 whole, which is shorter than its diff:
```python
import functools

import jax
import jax.numpy as jnp
from jax import lax
from jax.experimental import pallas as pl
from jax.experimental.pallas import tpu as pltpu
from jax.sharding import PartitionSpec as P

HEAD_DIM = 128
SCALE = HEAD_DIM ** (-0.5)
SIDE = 4
F32 = jnp.float32
BF16 = jnp.bfloat16
VIDEO, AUDIO = 0, 1
GATE_ROWS = 16
VMEM = 60 * 2**20

ALONG_X = [[x * SIDE + z for x in range(SIDE)] for z in range(SIDE)]


def along_x(array, shift):
    pairs = [(x * SIDE + z, (x + shift) % SIDE * SIDE + z) for x in range(SIDE) for z in range(SIDE)]
    return lax.ppermute(array, "vid", pairs)


def along_z(array, shift):
    pairs = [(x * SIDE + z, x * SIDE + (z + shift) % SIDE) for x in range(SIDE) for z in range(SIDE)]
    return lax.ppermute(array, "vid", pairs)


def beside_z(array, distance):
    pairs = [(x * SIDE + z, x * SIDE + (z ^ distance)) for x in range(SIDE) for z in range(SIDE)]
    return lax.ppermute(array, "vid", pairs)


def all_along_x(array):
    return lax.all_gather(array, "vid", axis=0, axis_index_groups=ALONG_X)


def gathered(array, along):
    return [array] + [along(array, shift) for shift in range(1, SIDE)]


def returned(parts, along):
    return [parts[0]] + [along(parts[place], SIDE - place) for place in range(1, SIDE)]


def nt(a, b):
    return lax.dot_general(a, b, (((1,), (1,)), ((), ())), preferred_element_type=F32)


def nn(a, b):
    return lax.dot_general(a, b, (((1,), (0,)), ((), ())), preferred_element_type=F32)


def joined(refs, index):
    return jnp.concatenate([ref[index] for ref in refs], axis=0)


def gated(rows, gate_row):
    return (gate_row * rows.astype(F32)).astype(BF16)


def query_rows(refs, index):
    blocks = [ref[:, index] for ref in refs]
    return tuple(block.reshape(-1, block.shape[-1]) for block in blocks)


def upstream(refs, gates_ref, part):
    video, audio = query_rows(refs, 1)
    if part == VIDEO:
        audio = gated(audio, gates_ref[1:2, :])
    else:
        video = gated(video, gates_ref[0:1, :])
    return jnp.concatenate([video, audio], axis=0)


def prepare_kernel(place_ref, aq_ref, ak_ref, av_ref, vq_ref, vk_ref, vv_ref, dv_ref, *outs):
    audio_q, audio_kv, video_kv, queries = outs
    audio_q[...] = aq_ref[0]
    audio_kv[0] = ak_ref[0]
    audio_kv[1] = av_ref[0]
    video_kv[0] = vk_ref[0]
    video_kv[1] = vv_ref[0]
    queries[0] = vq_ref[0]
    queries[1] = dv_ref[0]


def prepare(place, audio_rows, audio_q, audio_k, audio_v, video_q, video_k, video_v, d_video):
    _, video_rows, width = video_q.shape
    cut = pl.BlockSpec((1, audio_rows, width), lambda i, place: (0, place[0], place[1]))
    whole = lambda *shape: pl.BlockSpec(shape, lambda i, place: (0,) * len(shape))
    shapes = [(audio_rows, width), (2, audio_rows, width), (2, video_rows, width), (2, video_rows, width)]
    return pl.pallas_call(
        prepare_kernel,
        grid_spec=pltpu.PrefetchScalarGridSpec(
            num_scalar_prefetch=1,
            grid=(1,),
            in_specs=[cut] * 3 + [whole(*video_q.shape)] * 4,
            out_specs=[whole(*shape) for shape in shapes],
        ),
        out_shape=[jax.ShapeDtypeStruct(shape, BF16) for shape in shapes],
        compiler_params=pltpu.CompilerParams(vmem_limit_bytes=VMEM),
        name="prepare",
    )(place, audio_q, audio_k, audio_v, video_q, video_k, video_v, d_video)


def forward_kernel(part, *refs):
    q_refs, k_refs, limit_ref, gates_ref = refs[:2], refs[2:6], refs[6], refs[7]
    e_ref, o_ref, stats_ref = refs[-3:]
    queries = jnp.concatenate(query_rows(q_refs, 0), axis=0)
    raw = nt(joined(k_refs, 0), queries)
    if part == AUDIO:
        rows = k_refs[0].shape[1]
        position = lax.broadcasted_iota(jnp.int32, (rows, raw.shape[1]), 0)
        pieces = [raw[place * rows : (place + 1) * rows] for place in range(SIDE)]
        pieces = [jnp.where(position < limit_ref[place], pieces[place], -1e30) for place in range(SIDE)]
        raw = jnp.concatenate(pieces, axis=0)
    peak = jnp.max(raw, axis=0, keepdims=True)
    expon = jnp.exp((raw - peak) * SCALE)
    total = jnp.sum(expon, axis=0, keepdims=True)
    expon = (expon * (1.0 / total)).astype(BF16)
    e_ref[0] = expon
    output = nn(joined(k_refs, 1).T, expon)
    o_ref[0] = output
    up = upstream(q_refs, gates_ref, part)
    delta = jnp.sum(up.astype(F32).T * output, axis=0, keepdims=True)
    log_total = peak * SCALE + jnp.log(total)
    if part == VIDEO:
        stats_ref[0] = jnp.concatenate([log_total, delta, log_total, delta], axis=0)
    else:
        stats_ref[0] = jnp.concatenate([refs[8][0, 0:2], log_total, delta], axis=0)


def merged_stats(refs, part):
    logs = [ref[0, 2 * part : 2 * part + 1] for ref in refs]
    peak = functools.reduce(jnp.maximum, logs)
    weights = [jnp.exp(local - peak) for local in logs]
    scale = 1.0 / sum(weights)
    delta = sum(weight * ref[0, 2 * part + 1 : 2 * part + 2] for weight, ref in zip(weights, refs)) * scale
    return weights[0] * scale, delta


def backward_keys(part, queries, up, stats_refs, k_refs, e_ref, k_outs, first):
    factor, delta = merged_stats(stats_refs, part)
    probs = e_ref[0].astype(F32) * factor
    grad_values = nn(probs.astype(BF16), up).astype(BF16)
    grad_probs = nt(joined(k_refs, 1), up)
    grad_scores = (probs * (grad_probs - delta)).astype(BF16)
    grad_keys = (nn(grad_scores, queries) * SCALE).astype(BF16)
    rows = k_refs[0].shape[1]
    for place in range(SIDE):
        k_outs[place][0, first : first + rows] = grad_keys[place * rows : (place + 1) * rows]
        k_outs[place][1, first : first + rows] = grad_values[place * rows : (place + 1) * rows]
    return nn(joined(k_refs, 0).T, grad_scores), factor


def backward_kernel(*refs):
    q_refs, k_video, k_audio, stats_refs = refs[:2], refs[2:6], refs[6:10], refs[10:14]
    gates_ref, columns_ref, e_video, e_audio, o_video, o_audio = refs[14:20]
    k_outs, q_out = refs[20:24], refs[24]
    video_rows, audio_rows = (ref.shape[2] for ref in q_refs)
    rows = video_rows + audio_rows
    video = SIDE * video_rows
    queries = jnp.concatenate(query_rows(q_refs, 0), axis=0)
    up = upstream(q_refs, gates_ref, VIDEO)
    term_video, factor = backward_keys(VIDEO, queries, up, stats_refs, k_video, e_video, k_outs, 0)
    on_video = o_video[0] * factor
    up = upstream(q_refs, gates_ref, AUDIO)
    term_audio, factor = backward_keys(AUDIO, queries, up, stats_refs, k_audio, e_audio, k_outs, video_rows)
    on_audio = o_audio[0] * factor
    grad_queries = term_video + term_audio
    cross_video, cross_audio = on_audio[:, :video], on_video[:, video:]
    merged = jnp.concatenate(
        [
            on_video[:, :video] + columns_ref[:, 0:1] * cross_video,
            on_audio[:, video:] + columns_ref[:, 1:2] * cross_audio,
        ],
        axis=1,
    )
    up_video, up_audio = query_rows(q_refs, 1)
    video_sum = jnp.sum(up_video.astype(F32).T * cross_video, axis=1, keepdims=True)
    audio_sum = jnp.sum(up_audio.astype(F32).T * cross_audio, axis=1, keepdims=True)
    sums = jnp.concatenate(
        [jnp.broadcast_to(video_sum, (HEAD_DIM, 4)), jnp.broadcast_to(audio_sum, (HEAD_DIM, HEAD_DIM - 4))], axis=1
    ).T[0:GATE_ROWS]
    high = sums.astype(BF16)
    low = (sums - high.astype(F32)).astype(BF16)
    even = lax.broadcasted_iota(jnp.int32, sums.shape, 0) % 2 == 0
    sums = jnp.where(even, high.astype(F32), low.astype(F32)).astype(BF16)
    merged = merged.T.astype(BF16)
    grad_queries = (grad_queries.T * SCALE).astype(BF16)
    for index, array in ((0, merged), (1, grad_queries)):
        first = index * rows
        q_out[:, first : first + video_rows] = array[:video].reshape(SIDE, video_rows, HEAD_DIM)
        q_out[:, first + video_rows : first + rows] = array[video:].reshape(SIDE, audio_rows, HEAD_DIM)
    q_out[:, 2 * rows :] = jnp.broadcast_to(sums, (SIDE, *sums.shape))


def chunk_spec(array):
    shape = array.shape[:-1]
    return pl.BlockSpec((*shape, HEAD_DIM), lambda h: (0,) * len(shape) + (h,))


def head_spec(array):
    shape = array.shape[1:]
    return pl.BlockSpec((1, *shape), lambda h: (h,) + (0,) * len(shape))


def like(*shape, kind=BF16):
    return jax.ShapeDtypeStruct(shape, kind)


def cost(keys, queries, heads, products):
    return pl.CostEstimate(
        flops=2 * products * heads * keys * queries * HEAD_DIM,
        bytes_accessed=4 * heads * keys * queries,
        transcendentals=heads * keys * queries,
    )


def attention_forward(part, q_chunks, k_chunks, limits, gates, earlier):
    heads = gates.shape[1] // HEAD_DIM
    keys, queries = SIDE * k_chunks[0].shape[1], sum(SIDE * array.shape[2] for array in q_chunks)
    outs = [
        like(heads, keys, queries),
        like(heads, HEAD_DIM, queries, kind=F32),
        like(heads, 4, queries, kind=F32),
    ]
    return pl.pallas_call(
        functools.partial(forward_kernel, part),
        grid=(heads,),
        in_specs=[chunk_spec(array) for array in (*q_chunks, *k_chunks)]
        + [pl.BlockSpec(memory_space=pltpu.SMEM), chunk_spec(gates)]
        + [head_spec(array) for array in earlier],
        out_specs=[head_spec(array) for array in outs],
        out_shape=outs,
        cost_estimate=cost(keys, queries, heads, 2),
        compiler_params=pltpu.CompilerParams(vmem_limit_bytes=VMEM),
        name=("forward_video", "forward_audio")[part],
    )(*q_chunks, *k_chunks, limits, gates, *earlier)


def attention_backward(q_chunks, video_keys, audio_keys, stats, gates, by_head):
    width = gates.shape[1]
    heads = width // HEAD_DIM
    rows, q_rows = video_keys[0].shape[1] + audio_keys[0].shape[1], sum(array.shape[2] for array in q_chunks)
    outs = [like(2, rows, width)] * SIDE + [like(SIDE, 2 * q_rows + GATE_ROWS, width)]
    chunks = [*q_chunks, *video_keys, *audio_keys]
    *key_parts, query_parts = pl.pallas_call(
        backward_kernel,
        grid=(heads,),
        in_specs=[chunk_spec(array) for array in chunks]
        + [head_spec(array) for array in stats]
        + [chunk_spec(gates), pl.BlockSpec((HEAD_DIM, 2), lambda h: (h, 0))]
        + [head_spec(array) for array in by_head],
        out_specs=[chunk_spec(array) for array in outs],
        out_shape=outs,
        cost_estimate=cost(SIDE * rows, SIDE * q_rows, heads, 4),
        compiler_params=pltpu.CompilerParams(vmem_limit_bytes=VMEM),
        name="backward",
    )(*chunks, *stats, gates, gates.T, *by_head)
    return key_parts, query_parts


def total_of(refs, *index):
    return sum(ref[index].astype(F32) for ref in refs)


def finish_queries_kernel(parts_ref, video_out, audio_out, video_q, audio_q, gate_ref):
    video_rows, audio_rows = video_out.shape[1], audio_out.shape[1]
    rows = video_rows + audio_rows
    parts = [parts_ref.at[place] for place in range(SIDE)]
    for index, video, audio in ((0, video_out, audio_out), (1, video_q, audio_q)):
        first = index * rows
        video[0] = total_of(parts, slice(first, first + video_rows)).astype(BF16)
        audio[0] = total_of(parts, slice(first + video_rows, first + rows)).astype(BF16)
    gates = total_of(parts, slice(2 * rows, None))
    width = gates.shape[1]
    video_gate = jnp.broadcast_to(gates[0:1] + gates[1:2], (4, width))
    audio_gate = jnp.broadcast_to(gates[4:5] + gates[5:6], (4, width))
    gate_ref[...] = jnp.concatenate([video_gate, audio_gate], axis=0)


def finish_queries(parts, video_rows, audio_rows):
    width = parts.shape[2]
    video, audio = like(1, video_rows, width), like(1, audio_rows, width)
    return pl.pallas_call(
        finish_queries_kernel,
        out_shape=[video, audio, video, audio, like(8, width, kind=F32)],
        compiler_params=pltpu.CompilerParams(vmem_limit_bytes=8 * 2**20),
        name="finish_queries",
    )(parts)


def finish_keys_kernel(*refs):
    parts, (video_k, video_v, audio_k, audio_v) = refs[:SIDE], refs[SIDE:]
    rows = video_k.shape[1]
    for index, video, audio in ((0, video_k, audio_k), (1, video_v, audio_v)):
        video[0] = total_of(parts, index, slice(0, rows)).astype(BF16)
        audio[0] = total_of(parts, index, slice(rows, None)).astype(BF16)


def finish_keys(parts, video_rows, audio_rows):
    width = parts[0].shape[2]
    video, audio = like(1, video_rows, width), like(1, audio_rows, width)
    return pl.pallas_call(
        finish_keys_kernel,
        out_shape=[video, video, audio, audio],
        compiler_params=pltpu.CompilerParams(vmem_limit_bytes=8 * 2**20),
        name="finish_keys",
    )(*parts)


def own_audio(array, vid_size, aud_size):
    pairs = [
        (v * aud_size + a, (2 * a + v % 2) * aud_size + v // 2) for v in range(vid_size) for a in range(aud_size)
    ]
    return lax.ppermute(array, ("vid", "aud"), pairs)


def fenced(holds, function, *arrays):
    outs = jax.eval_shape(function, *arrays)
    return lax.cond(
        holds, function, lambda *_: jax.tree.map(lambda out: jnp.zeros(out.shape, out.dtype), outs), *arrays
    )


def shards(
    video_q, video_k, video_v, audio_q, audio_k, audio_v, video_gate, audio_gate, audio_len, d_video_out, d_audio_out
):
    vid = lax.axis_index("vid")
    sizes = lax.axis_size("vid"), lax.axis_size("aud")
    video_rows, audio_rows = video_q.shape[1], d_audio_out.shape[1]
    holds = audio_len[0] > 0
    place = jnp.stack([vid % 2, vid // 2]).astype(jnp.int32)
    send_q, send_kv, video_kv, video_queries = prepare(
        place, audio_rows, audio_q, audio_k, audio_v, video_q, video_k, video_v, d_video_out
    )

    def first_chunks(send_q, send_kv, video_kv, video_queries):
        audio = own_audio(send_q, *sizes), own_audio(send_kv, *sizes)
        keys = gathered(video_kv, along_z)
        return audio, tuple(keys[1:]), all_along_x(video_queries)

    (aud_q, aud_kv), video_keys, video_queries = fenced(
        holds, first_chunks, send_q, send_kv, video_kv, video_queries
    )
    video_keys = [video_kv, *video_keys]
    audio_keys = gathered(aud_kv, along_z)
    q_chunks = video_queries, all_along_x(jnp.stack([aud_q, d_audio_out[0]]))
    gates = jnp.stack([video_gate, audio_gate])
    column, row = vid // SIDE, vid % SIDE
    limits = jnp.stack([audio_len[0] - (column * SIDE + (row - p) % SIDE) * audio_rows for p in range(SIDE)])
    e_video, o_video, stats = attention_forward(VIDEO, q_chunks, video_keys, limits, gates, ())
    e_audio, o_audio, stats = attention_forward(AUDIO, q_chunks, audio_keys, limits, gates, (stats,))
    stats = gathered(stats, along_x)
    key_parts, query_parts = attention_backward(
        q_chunks, video_keys, audio_keys, stats, gates, (e_video, e_audio, o_video, o_audio)
    )

    def query_results(parts):
        parts = lax.all_to_all(parts, "vid", 0, 0, axis_index_groups=ALONG_X, tiled=True)
        *results, gate = finish_queries(parts, video_rows, audio_rows)
        for distance in (1, 2):
            gate = gate + beside_z(gate, distance)
        return (*results, gate + lax.ppermute(gate, "pair", [(0, 1), (1, 0)]))

    video_out, audio_out, grad_video_q, grad_audio_q, gate = fenced(holds, query_results, query_parts)
    key_parts = returned(key_parts, along_z)
    grad_video_k, grad_video_v, grad_audio_k, grad_audio_v = finish_keys(key_parts, video_rows, audio_rows)
    return (
        video_out,
        audio_out,
        grad_video_q,
        grad_video_k,
        grad_video_v,
        grad_audio_q,
        grad_audio_k,
        grad_audio_v,
        gate[0],
        gate[7],
    )


def solution(mesh):
    split = P("pair", "vid", "aud")
    rows = P("pair", "aud", None)
    return jax.shard_map(
        shards,
        mesh=mesh,
        in_specs=(split, split, split, rows, rows, rows, P("aud"), P("aud"), P("pair"), split, split),
        out_specs=(split,) * 8 + (P("aud"), P("aud")),
        check_vma=False,
    )
```

time: 137 us -> 118 us (0.86)
  blocking collectives: 0 us -> 44.5 us
  waiting for transfers between devices: 39.9 us -> 8.9 us
  local copies, waits for them, and re-layouts: 25.8 us -> 2.15 us
  starting transfers between devices: 44.9 us -> 36.6 us
    all_gather x0 -> x2, blocking collectives: none -> 31.3 us  [all_along_x(): return lax.all_gather(array, 'vid', axis=0, axis_index_groups=ALONG_X)]
    unnamed x70 -> x26, local copies, waits for them, and re-layouts: 22 us -> 1.32 us
    ppermute x9 -> x3, waiting for transfers between devices: 19.8 us -> 2.87 us  [along_x(): return lax.ppermute(array, 'vid', pairs)]
    all_to_all x0 -> x1, blocking collectives: none -> 13.2 us  [query_results(): lax.all_to_all(parts, 'vid', 0, 0, axis_index_groups=ALONG_X, tiled=True)]
    ppermute x9 -> x3, starting transfers between devices: 14.4 us -> 2.09 us  [along_x(): return lax.ppermute(array, 'vid', pairs)]
    ppermute x9, starting transfers between devices: 26.1 us -> 16.7 us  [along_z(): return lax.ppermute(array, 'vid', pairs)]
    ppermute x1, starting transfers between devices: 2.1 us -> 11.5 us  [query_results(): return (*results, gate + lax.ppermute(gate, 'pair', [(0, 1), (1, 0)]))]
    ppermute x9, waiting for transfers between devices: 8.35 us -> 0.02 us  [along_z(): return lax.ppermute(array, 'vid', pairs)]
  transfers between devices with their start and end apart: 22 -> 17, of which waited for: 9 -> 6; matrix products, arithmetic and copies ran while one was open for 4% -> 4% of each run, Pallas kernels for 4% -> 5%
where the time goes in v4:
time: 118 us
  blocking collectives  44.5 us (38%)
  starting transfers between devices  36.6 us (31%)
  Pallas kernels  19.8 us (17%)
  waiting for transfers between devices  8.9 us (8%)
  other arithmetic  3.98 us (3%)
  local copies, waits for them, and re-layouts  2.15 us (2%)
  between operations  1.6 us (1%)
    all_gather x2, blocking collectives, all_along_x(): return lax.all_gather(array, 'vid', axis=0, axis_index_groups=ALONG_X)  31.3 us
    ppermute x9, starting transfers between devices, along_z(): return lax.ppermute(array, 'vid', pairs)  16.7 us
    all_to_all x1, blocking collectives, query_results(): lax.all_to_all(parts, 'vid', 0, 0, axis_index_groups=ALONG_X, tiled=True)  13.2 us
    ppermute x1, starting transfers between devices, query_results(): return (*results, gate + lax.ppermute(gate, 'pair', [(0, 1), (1, 0)]))  11.5 us
    pallas_call x2, Pallas kernels, attention_forward(): pl.pallas_call(functools.partial(forward_kernel, part), grid=(heads,), in...  9.29 us
    pallas_call x1, Pallas kernels, attention_backward(): pl.pallas_call(backward_kernel, grid=(heads,), in_specs=[chunk_spec(array...  7.08 us
    ppermute x2, waiting for transfers between devices, beside_z(): return lax.ppermute(array, 'vid', pairs)  5.17 us
    ppermute x2, starting transfers between devices, beside_z(): return lax.ppermute(array, 'vid', pairs)  3.83 us
  transfers between devices with their start and end apart: 17, of which 6 were waited for; matrix products, arithmetic and copies ran while one was open for 4% of the time, Pallas kernels for 5%

profile of v4, /device:TPU:1, one launch (start us, length us, event | category | flops | bytes accessed | tf_op | source)
XLA Modules:
  0.0 117.5 jit_solution(1151226068850508886)
XLA Ops:
  1.9 1.8 %prepare.1 = (bf16[64,384]{1,0:T(8,128)(2,1)S(1)}, bf16[2,64,384]{2,1,0:T(8,128)(2,1)S(1)}, bf16[2,128,384]{2,1,0:T(8,128)(2,1)S(1)}, bf16[2,128,384]{2,1,0:T(8,128)(2,1)S(1)}) custom-call(s32[2]{0:T(128)} %pad_add_fusion.place_ref, bf16[1,128,3072]{2,1,0:T(8,128)(2,1)} %aq_ref.1, bf16[1,128,3072]{2,1,0:T(8,128)(2,1)} %ak_ref.1, ...), custom_call_target="tpu_custom_call" | custom-call | tf_op jit(solution)/shard_map/prepare/pallas_call | solution.py:95
  3.8 28.4 %conditional.2 = (bf16[2,64,384]{2,1,0:T(8,128)(2,1)}, bf16[2,128,384]{2,1,0:T(8,128)(2,1)}, bf16[2,128,384]{2,1,0:T(8,128)(2,1)}, bf16[2,128,384]{2,1,0:T(8,128...) conditional(s32[]{:T(128)} %convert_element_type.4, () %tuple.29, ...), branch_computations={%region_0.1_spmd, %region_1.2_spmd} | conditional | bytes 3932408 | solution.py:325
  3.8 5.3 %collective-permute-start.3 = (bf16[2,128,384]{2,1,0:T(8,128)(2,1)S(1)}, bf16[2,128,384]{2,1,0:T(8,128)(2,1)}, u32[]{:S(2)}, u32[]{:S(2)}) collective-permute-start(bf16[2,128,384]{2,1,0:T(8,128)(2,1)S(1)} %get-tuple-element.15), channel_id=1, source_target_pairs={{0,48},{16,0},{32,16},{48,32},{64,112},{80,64},{96,80},{112,96},{1... | collective-permute-start | bytes 589832 | tf_op jit(solution)/shard_map/cond/branch_1_fun/ppermute | solution.py:29
  9.4 1.3 %collective-permute-start.4 = (bf16[64,384]{1,0:T(8,128)(2,1)S(1)}, bf16[64,384]{1,0:T(8,128)(2,1)}, u32[]{:S(2)}, u32[]{:S(2)}) collective-permute-start(bf16[64,384]{1,0:T(8,128)(2,1)S(1)} %get-tuple-element.17), channel_id=1, source_target_pairs={{0,0},{2,32},{4,64},{6,96},{8,128},{10,160},{12,192},{14,224},{16,... | collective-permute-start | bytes 147464 | tf_op jit(solution)/shard_map/cond/branch_1_fun/ppermute | solution.py:320
  10.7 1.3 %collective-permute-start = (bf16[2,64,384]{2,1,0:T(8,128)(2,1)S(1)}, bf16[2,64,384]{2,1,0:T(8,128)(2,1)}, u32[]{:S(2)}, u32[]{:S(2)}) collective-permute-start(bf16[2,64,384]{2,1,0:T(8,128)(2,1)S(1)} %get-tuple-element.14), channel_id=1, source_target_pairs={{0,0},{2,32},{4,64},{6,96},{8,128},{10,160},{12,192},{14,224},{16,... | collective-permute-start | bytes 294920 | tf_op jit(solution)/shard_map/cond/branch_1_fun/ppermute | solution.py:320
  12.0 20.2 %all-gather = bf16[8,128,384]{2,1,0:T(8,128)(2,1)S(1)} all-gather(bf16[2,128,384]{2,1,0:T(8,128)(2,1)S(1)} %get-tuple-element.16), channel_id=2, replica_groups={{0,64,128,192},{16,80,144,208},{32,96,160,224},{48,112,176,240},{1,65,1..., dimensions={0}, use_global_device_ids=true | all-gather | bytes 983040 | tf_op jit(solution)/shard_map/cond/branch_1_fun/all_gather | solution.py:38
  32.2 8.0 %collective-permute-start.10 = (bf16[2,64,384]{2,1,0:T(8,128)(2,1)}, bf16[2,64,384]{2,1,0:T(8,128)(2,1)S(1)}, u32[]{:S(2)}, u32[]{:S(2)}) collective-permute-start(bf16[2,64,384]{2,1,0:T(8,128)(2,1)} %get-tuple-element.73.refs_2_.refs_6_), channel_id=1, source_target_pairs={{0,48},{16,0},{32,16},{48,32},{64,112},{80,64},{96,80},{112,96},{1... | collective-permute-start | bytes 294920 | tf_op jit(solution)/shard_map/ppermute | solution.py:29
  40.5 0.8 pad_maximum_fusion
  41.4 11.1 %all-gather.1 = bf16[8,64,384]{2,1,0:T(8,128)(2,1)} all-gather(bf16[2,64,384]{2,1,0:T(8,128)(2,1)S(1)} %pad_maximum_fusion), channel_id=3, replica_groups={{0,64,128,192},{16,80,144,208},{32,96,160,224},{48,112,176,240},{1,65,1..., dimensions={0}, use_global_device_ids=true | all-gather | bytes 491520 | tf_op jit(solution)/shard_map/all_gather | solution.py:38
  53.6 5.1 %forward_video.1 = (bf16[3,512,768]{2,1,0:T(8,128)(2,1)}, f32[3,128,768]{2,1,0:T(8,128)}, f32[3,4,768]{2,1,0:T(4,128)}) custom-call(bf16[4,2,128,384]{3,2,1,0:T(8,128)(2,1)S(1)} %get-tuple-element.68.refs_0_, bf16[4,2,64,384]{3,2,1,0:T(8,128)(2,1)} %bitcast.17, bf16[2,128,384]{2,1,0:T(8,128)(2,1)S(1)} %get-tuple-element.65.refs_2_, ...), custom_call_target="tpu_custom_call" | custom-call | flops 603979776 | bytes 4718592 | tf_op jit(solution)/shard_map/forward_video/pallas_call | solution.py:231
  59.4 4.2 %forward_audio.1 = (bf16[3,256,768]{2,1,0:T(8,128)(2,1)}, f32[3,128,768]{2,1,0:T(8,128)}, f32[3,4,768]{2,1,0:T(4,128)}) custom-call(bf16[4,2,128,384]{3,2,1,0:T(8,128)(2,1)S(1)} %get-tuple-element.68.refs_0_, bf16[4,2,64,384]{3,2,1,0:T(8,128)(2,1)} %bitcast.18, bf16[2,64,384]{2,1,0:T(8,128)(2,1)} %get-tuple-element.73.refs_2_.refs_6_, ...), custom_call_target="tpu_custom_call" | custom-call | flops 301989888 | bytes 2359296 | tf_op jit(solution)/shard_map/forward_audio/pallas_call | solution.py:231
  63.6 0.9 collective-permute-start.13
  65.7 0.8 copy.29
  66.7 2.3 %collective-permute-done.12.refs_12_ = f32[3,4,768]{2,1,0:T(4,128)S(1)} collective-permute-done((f32[3,4,768]{2,1,0:T(4,128)}, f32[3,4,768]{2,1,0:T(4,128)S(1)}, u32[]{:S(2)}, u32[]{:S(2)}) %collective-permute-start.12) | collective-permute-done | bytes 36896 | tf_op jit(solution)/shard_map/ppermute | solution.py:24
  70.0 7.1 %backward.1 = (bf16[2,192,384]{2,1,0:T(8,128)(2,1)}, bf16[2,192,384]{2,1,0:T(8,128)(2,1)}, bf16[2,192,384]{2,1,0:T(8,128)(2,1)}, bf16[2,192,384]{2,1,0:T(8,128)(2,1)}, bf16[4,400,384]{2,1,0:T(8,128)(2,1)S(1)}) custom-call(bf16[4,2,128,384]{3,2,1,0:T(8,128)(2,1)S(1)} %get-tuple-element.68.refs_0_, bf16[4,2,64,384]{3,2,1,0:T(8,128)(2,1)} %bitcast.19, ...), custom_call_target="tpu_custom_call" | custom-call | flops 1811939328 | bytes 7077888 | tf_op jit(solution)/shard_map/backward/pallas_call | solution.py:251
  77.1 2.3 %collective-permute-start.14 = (bf16[2,192,384]{2,1,0:T(8,128)(2,1)}, bf16[2,192,384]{2,1,0:T(8,128)(2,1)S(1)}, u32[]{:S(2)}, u32[]{:S(2)}) collective-permute-start(bf16[2,192,384]{2,1,0:T(8,128)(2,1)} %get-tuple-element.85), channel_id=1, source_target_pairs={{0,48},{16,0},{32,16},{48,32},{64,112},{80,64},{96,80},{112,96},{1... | collective-permute-start | bytes 884744 | tf_op jit(solution)/shard_map/ppermute | solution.py:29
  79.8 36.7 %conditional.3 = (bf16[1,128,384]{2,1,0:T(8,128)(2,1)}, bf16[1,64,384]{2,1,0:T(8,128)(2,1)}, bf16[1,128,384]{2,1,0:T(8,128)(2,1)}, bf16[1,64,384]{2,1,0:T(8,128)...) conditional(s32[]{:T(128)} %convert_element_type.4, () %tuple.28, ...), branch_computations={%region_2.3_spmd, %region_3.4_spmd} | conditional | flops 9984 | bytes 2723520 | solution.py:325
  79.8 13.2 %all_to_all.4.parts_ref = bf16[4,400,384]{2,1,0:T(8,128)(2,1)S(1)} all-to-all(bf16[4,400,384]{2,1,0:T(8,128)(2,1)S(1)} %param.3), channel_id=1, replica_groups={{0,64,128,192},{16,80,144,208},{32,96,160,224},{48,112,176,240},{1,65,1..., dimensions={0} | all-to-all | bytes 2457600 | tf_op jit(solution)/shard_map/cond/branch_1_fun/all_to_all | solution.py:364
  93.8 2.3 %collective-permute-start.5 = (f32[8,384]{1,0:T(8,128)S(1)}, f32[8,384]{1,0:T(8,128)S(1)}, u32[]{:S(2)}, u32[]{:S(2)}) collective-permute-start(f32[8,384]{1,0:T(8,128)S(1)} %get-tuple-element.22), channel_id=1, source_target_pairs={{0,16},{16,0},{32,48},{48,32},{64,80},{80,64},{96,112},{112,96},{1... | collective-permute-start | bytes 36872 | tf_op jit(solution)/shard_map/cond/branch_1_fun/ppermute | solution.py:34
  96.1 1.4 %collective-permute-done.5 = f32[8,384]{1,0:T(8,128)S(1)} collective-permute-done((f32[8,384]{1,0:T(8,128)S(1)}, f32[8,384]{1,0:T(8,128)S(1)}, u32[]{:S(2)}, u32[]{:S(2)}) %collective-permute-start.5) | collective-permute-done | bytes 12320 | tf_op jit(solution)/shard_map/cond/branch_1_fun/ppermute | solution.py:34
  97.5 1.6 %collective-permute-start.6 = (f32[8,384]{1,0:T(8,128)S(1)}, f32[8,384]{1,0:T(8,128)S(1)}, u32[]{:S(2)}, u32[]{:S(2)}) collective-permute-start(f32[8,384]{1,0:T(8,128)S(1)} %add.32), channel_id=1, source_target_pairs={{0,32},{16,48},{32,0},{48,16},{64,96},{80,112},{96,64},{112,80},{1... | collective-permute-start | bytes 36872 | tf_op jit(solution)/shard_map/cond/branch_1_fun/ppermute | solution.py:34
  99.1 3.8 %collective-permute-done.6 = f32[8,384]{1,0:T(8,128)S(1)} collective-permute-done((f32[8,384]{1,0:T(8,128)S(1)}, f32[8,384]{1,0:T(8,128)S(1)}, u32[]{:S(2)}, u32[]{:S(2)}) %collective-permute-start.6) | collective-permute-done | bytes 12320 | tf_op jit(solution)/shard_map/cond/branch_1_fun/ppermute | solution.py:34
  102.8 11.5 %collective-permute-start.7 = (f32[8,384]{1,0:T(8,128)S(1)}, f32[8,384]{1,0:T(8,128)S(1)}, u32[]{:S(2)}, u32[]{:S(2)}) collective-permute-start(f32[8,384]{1,0:T(8,128)S(1)} %add.33), channel_id=1, source_target_pairs={{0,1},{1,0},{2,3},{3,2},{4,5},{5,4},{6,7},{7,6},{8,9},{9,8},{10,11... | collective-permute-start | bytes 36872 | tf_op jit(solution)/shard_map/cond/branch_1_fun/ppermute | solution.py:368
  114.3 0.8 collective-permute-done.7
  (58 shorter events, 9.0 us)
Async XLA Ops:
  3.7 36.8 %copy-start.9 = (f32[384]{0:T(512)S(1)}, f32[384]{0:T(512)}, u32[]{:S(2)}) copy-start(f32[384]{0:T(512)} %param.21) | copy-start | bytes 4612
  3.7 36.8 %copy-start.10 = (f32[384]{0:T(512)S(1)}, f32[384]{0:T(512)}, u32[]{:S(2)}) copy-start(f32[384]{0:T(512)} %param.22) | copy-start | bytes 4612
  3.7 36.8 %copy-start.5 = (bf16[1,64,384]{2,1,0:T(8,128)(2,1)S(1)}, bf16[1,64,384]{2,1,0:T(8,128)(2,1)}, u32[]{:S(2)}) copy-start(bf16[1,64,384]{2,1,0:T(8,128)(2,1)} %param.25) | copy-start | bytes 147460
  3.8 28.4 %collective-permute-start.3 = (bf16[2,128,384]{2,1,0:T(8,128)(2,1)S(1)}, bf16[2,128,384]{2,1,0:T(8,128)(2,1)}, u32[]{:S(2)}, u32[]{:S(2)}) collective-permute-start(bf16[2,128,384]{2,1,0:T(8,128)(2,1)S(1)} %get-tuple-element.15), channel_id=1, source_target_pairs={{0,48},{16,0},{32,16},{48,32},{64,112},{80,64},{96,80},{112,96},{1... | collective-permute-start | bytes 589832 | tf_op jit(solution)/shard_map/cond/branch_1_fun/ppermute | solution.py:29
  9.0 23.1 %collective-permute-start.2 = (bf16[2,128,384]{2,1,0:T(8,128)(2,1)S(1)}, bf16[2,128,384]{2,1,0:T(8,128)(2,1)}, u32[]{:S(2)}, u32[]{:S(2)}) collective-permute-start(bf16[2,128,384]{2,1,0:T(8,128)(2,1)S(1)} %get-tuple-element.15), channel_id=1, source_target_pairs={{0,32},{16,48},{32,0},{48,16},{64,96},{80,112},{96,64},{112,80},{1... | collective-permute-start | bytes 589832 | tf_op jit(solution)/shard_map/cond/branch_1_fun/ppermute | solution.py:29
  9.0 23.1 %collective-permute-start.1 = (bf16[2,128,384]{2,1,0:T(8,128)(2,1)S(1)}, bf16[2,128,384]{2,1,0:T(8,128)(2,1)}, u32[]{:S(2)}, u32[]{:S(2)}) collective-permute-start(bf16[2,128,384]{2,1,0:T(8,128)(2,1)S(1)} %get-tuple-element.15), channel_id=1, source_target_pairs={{0,16},{16,32},{32,48},{48,0},{64,80},{80,96},{96,112},{112,64},{1... | collective-permute-start | bytes 589832 | tf_op jit(solution)/shard_map/cond/branch_1_fun/ppermute | solution.py:29
  9.4 22.7 %collective-permute-start.4 = (bf16[64,384]{1,0:T(8,128)(2,1)S(1)}, bf16[64,384]{1,0:T(8,128)(2,1)}, u32[]{:S(2)}, u32[]{:S(2)}) collective-permute-start(bf16[64,384]{1,0:T(8,128)(2,1)S(1)} %get-tuple-element.17), channel_id=1, source_target_pairs={{0,0},{2,32},{4,64},{6,96},{8,128},{10,160},{12,192},{14,224},{16,... | collective-permute-start | bytes 147464 | tf_op jit(solution)/shard_map/cond/branch_1_fun/ppermute | solution.py:320
  10.7 21.5 %collective-permute-start = (bf16[2,64,384]{2,1,0:T(8,128)(2,1)S(1)}, bf16[2,64,384]{2,1,0:T(8,128)(2,1)}, u32[]{:S(2)}, u32[]{:S(2)}) collective-permute-start(bf16[2,64,384]{2,1,0:T(8,128)(2,1)S(1)} %get-tuple-element.14), channel_id=1, source_target_pairs={{0,0},{2,32},{4,64},{6,96},{8,128},{10,160},{12,192},{14,224},{16,... | collective-permute-start | bytes 294920 | tf_op jit(solution)/shard_map/cond/branch_1_fun/ppermute | solution.py:320
  32.2 26.6 %collective-permute-start.10 = (bf16[2,64,384]{2,1,0:T(8,128)(2,1)}, bf16[2,64,384]{2,1,0:T(8,128)(2,1)S(1)}, u32[]{:S(2)}, u32[]{:S(2)}) collective-permute-start(bf16[2,64,384]{2,1,0:T(8,128)(2,1)} %get-tuple-element.73.refs_2_.refs_6_), channel_id=1, source_target_pairs={{0,48},{16,0},{32,16},{48,32},{64,112},{80,64},{96,80},{112,96},{1... | collective-permute-start | bytes 294920 | tf_op jit(solution)/shard_map/ppermute | solution.py:29
  40.1 18.6 %collective-permute-start.9 = (bf16[2,64,384]{2,1,0:T(8,128)(2,1)}, bf16[2,64,384]{2,1,0:T(8,128)(2,1)S(1)}, u32[]{:S(2)}, u32[]{:S(2)}) collective-permute-start(bf16[2,64,384]{2,1,0:T(8,128)(2,1)} %get-tuple-element.73.refs_2_.refs_6_), channel_id=1, source_target_pairs={{0,32},{16,48},{32,0},{48,16},{64,96},{80,112},{96,64},{112,80},{1... | collective-permute-start | bytes 294920 | tf_op jit(solution)/shard_map/ppermute | solution.py:29
  40.1 18.6 %collective-permute-start.8 = (bf16[2,64,384]{2,1,0:T(8,128)(2,1)}, bf16[2,64,384]{2,1,0:T(8,128)(2,1)S(1)}, u32[]{:S(2)}, u32[]{:S(2)}) collective-permute-start(bf16[2,64,384]{2,1,0:T(8,128)(2,1)} %get-tuple-element.73.refs_2_.refs_6_), channel_id=1, source_target_pairs={{0,16},{16,32},{32,48},{48,0},{64,80},{80,96},{96,112},{112,64},{1... | collective-permute-start | bytes 294920 | tf_op jit(solution)/shard_map/ppermute | solution.py:29
  58.7 7.0 %copy-start.4 = (f32[2,384]{1,0:T(2,128)S(1)}, f32[2,384]{1,0:T(2,128)}, u32[]{:S(2)}) copy-start(f32[2,384]{1,0:T(2,128)} %pad_maximum_fusion.1.refs_7_.refs_14_) | copy-start | bytes 9220
  63.6 3.1 %collective-permute-start.13 = (f32[3,4,768]{2,1,0:T(4,128)}, f32[3,4,768]{2,1,0:T(4,128)S(1)}, u32[]{:S(2)}, u32[]{:S(2)}) collective-permute-start(f32[3,4,768]{2,1,0:T(4,128)} %get-tuple-element.75.refs_10_), channel_id=1, source_target_pairs={{0,192},{16,208},{32,224},{48,240},{64,0},{80,16},{96,32},{112,48}... | collective-permute-start | bytes 110600 | tf_op jit(solution)/shard_map/ppermute | solution.py:24
  64.5 4.5 %collective-permute-start.12 = (f32[3,4,768]{2,1,0:T(4,128)}, f32[3,4,768]{2,1,0:T(4,128)S(1)}, u32[]{:S(2)}, u32[]{:S(2)}) collective-permute-start(f32[3,4,768]{2,1,0:T(4,128)} %get-tuple-element.75.refs_10_), channel_id=1, source_target_pairs={{0,128},{16,144},{32,160},{48,176},{64,192},{80,208},{96,224},{112... | collective-permute-start | bytes 110600 | tf_op jit(solution)/shard_map/ppermute | solution.py:24
  65.1 4.3 %collective-permute-start.11 = (f32[3,4,768]{2,1,0:T(4,128)}, f32[3,4,768]{2,1,0:T(4,128)S(1)}, u32[]{:S(2)}, u32[]{:S(2)}) collective-permute-start(f32[3,4,768]{2,1,0:T(4,128)} %get-tuple-element.75.refs_10_), channel_id=1, source_target_pairs={{0,64},{16,80},{32,96},{48,112},{64,128},{80,144},{96,160},{112,17... | collective-permute-start | bytes 110600 | tf_op jit(solution)/shard_map/ppermute | solution.py:24
  66.7 2.7 %copy-start.6 = (f32[3,4,768]{2,1,0:T(4,128)}, f32[3,4,768]{2,1,0:T(4,128)S(1)}, u32[]{:S(2)}) copy-start(f32[3,4,768]{2,1,0:T(4,128)S(1)} %collective-permute-done.13.refs_13_) | copy-start | bytes 110596
  77.1 39.4 %collective-permute-start.14 = (bf16[2,192,384]{2,1,0:T(8,128)(2,1)}, bf16[2,192,384]{2,1,0:T(8,128)(2,1)S(1)}, u32[]{:S(2)}, u32[]{:S(2)}) collective-permute-start(bf16[2,192,384]{2,1,0:T(8,128)(2,1)} %get-tuple-element.85), channel_id=1, source_target_pairs={{0,48},{16,0},{32,16},{48,32},{64,112},{80,64},{96,80},{112,96},{1... | collective-permute-start | bytes 884744 | tf_op jit(solution)/shard_map/ppermute | solution.py:29
  79.4 37.1 %collective-permute-start.15 = (bf16[2,192,384]{2,1,0:T(8,128)(2,1)}, bf16[2,192,384]{2,1,0:T(8,128)(2,1)S(1)}, u32[]{:S(2)}, u32[]{:S(2)}) collective-permute-start(bf16[2,192,384]{2,1,0:T(8,128)(2,1)} %get-tuple-element.86), channel_id=1, source_target_pairs={{0,32},{16,48},{32,0},{48,16},{64,96},{80,112},{96,64},{112,80},{1... | collective-permute-start | bytes 884744 | tf_op jit(solution)/shard_map/ppermute | solution.py:29
  79.7 36.8 %collective-permute-start.16 = (bf16[2,192,384]{2,1,0:T(8,128)(2,1)}, bf16[2,192,384]{2,1,0:T(8,128)(2,1)S(1)}, u32[]{:S(2)}, u32[]{:S(2)}) collective-permute-start(bf16[2,192,384]{2,1,0:T(8,128)(2,1)} %get-tuple-element.87), channel_id=1, source_target_pairs={{0,16},{16,32},{32,48},{48,0},{64,80},{80,96},{96,112},{112,64},{1... | collective-permute-start | bytes 884744 | tf_op jit(solution)/shard_map/ppermute | solution.py:29
  79.8 36.8 %copy-start = (bf16[2,192,384]{2,1,0:T(8,128)(2,1)S(1)}, bf16[2,192,384]{2,1,0:T(8,128)(2,1)}, u32[]{:S(2)}) copy-start(bf16[2,192,384]{2,1,0:T(8,128)(2,1)} %get-tuple-element.84.refs_0_) | copy-start | bytes 884740
  93.8 3.7 %collective-permute-start.5 = (f32[8,384]{1,0:T(8,128)S(1)}, f32[8,384]{1,0:T(8,128)S(1)}, u32[]{:S(2)}, u32[]{:S(2)}) collective-permute-start(f32[8,384]{1,0:T(8,128)S(1)} %get-tuple-element.22), channel_id=1, source_target_pairs={{0,16},{16,0},{32,48},{48,32},{64,80},{80,64},{96,112},{112,96},{1... | collective-permute-start | bytes 36872 | tf_op jit(solution)/shard_map/cond/branch_1_fun/ppermute | solution.py:34
  97.5 5.3 %collective-permute-start.6 = (f32[8,384]{1,0:T(8,128)S(1)}, f32[8,384]{1,0:T(8,128)S(1)}, u32[]{:S(2)}, u32[]{:S(2)}) collective-permute-start(f32[8,384]{1,0:T(8,128)S(1)} %add.32), channel_id=1, source_target_pairs={{0,32},{16,48},{32,0},{48,16},{64,96},{80,112},{96,64},{112,80},{1... | collective-permute-start | bytes 36872 | tf_op jit(solution)/shard_map/cond/branch_1_fun/ppermute | solution.py:34
  102.8 12.3 %collective-permute-start.7 = (f32[8,384]{1,0:T(8,128)S(1)}, f32[8,384]{1,0:T(8,128)S(1)}, u32[]{:S(2)}, u32[]{:S(2)}) collective-permute-start(f32[8,384]{1,0:T(8,128)S(1)} %add.33), channel_id=1, source_target_pairs={{0,1},{1,0},{2,3},{3,2},{4,5},{5,4},{6,7},{7,6},{8,9},{9,8},{10,11... | collective-permute-start | bytes 36872 | tf_op jit(solution)/shard_map/cond/branch_1_fun/ppermute | solution.py:368
  116.5 0.9 copy-start.11
  (6 other events, 4.0 us)

commit v5 on v4

--- a/solution.py
+++ b/solution.py
@@ -62,13 +62,20 @@
     return (gate_row * rows.astype(F32)).astype(BF16)
 
 
-def query_rows(refs, index):
-    blocks = [ref[:, index] for ref in refs]
-    return tuple(block.reshape(-1, block.shape[-1]) for block in blocks)
-
-
-def upstream(refs, gates_ref, part):
-    video, audio = query_rows(refs, 1)
+def flat(block):
+    return block.reshape(-1, block.shape[-1])
+
+
+def queries_of(gathered_ref, audio_ref, video_rows):
+    return jnp.concatenate([flat(gathered_ref[:, :video_rows]), flat(audio_ref[...])], axis=0)
+
+
+def upstreams_of(gathered_ref, video_rows):
+    return flat(gathered_ref[:, video_rows : 2 * video_rows]), flat(gathered_ref[:, 2 * video_rows :])
+
+
+def upstream(gathered_ref, gates_ref, video_rows, part):
+    video, audio = upstreams_of(gathered_ref, video_rows)
     if part == VIDEO:
         audio = gated(audio, gates_ref[1:2, :])
     else:
@@ -76,61 +83,70 @@
     return jnp.concatenate([video, audio], axis=0)
 
 
-def prepare_kernel(place_ref, aq_ref, ak_ref, av_ref, vq_ref, vk_ref, vv_ref, dv_ref, *outs):
+def prepare_kernel(place_ref, aq_ref, ak_ref, av_ref, vq_ref, vk_ref, vv_ref, dv_ref, da_ref, *outs):
     audio_q, audio_kv, video_kv, queries = outs
+    rows = vq_ref.shape[1]
     audio_q[...] = aq_ref[0]
     audio_kv[0] = ak_ref[0]
     audio_kv[1] = av_ref[0]
     video_kv[0] = vk_ref[0]
     video_kv[1] = vv_ref[0]
-    queries[0] = vq_ref[0]
-    queries[1] = dv_ref[0]
-
-
-def prepare(place, audio_rows, audio_q, audio_k, audio_v, video_q, video_k, video_v, d_video):
+    queries[:rows] = vq_ref[0]
+    queries[rows : 2 * rows] = dv_ref[0]
+    queries[2 * rows :] = da_ref[0]
+
+
+def prepare(place, audio_q, audio_k, audio_v, video_q, video_k, video_v, d_video, d_audio):
     _, video_rows, width = video_q.shape
+    audio_rows = d_audio.shape[1]
     cut = pl.BlockSpec((1, audio_rows, width), lambda i, place: (0, place[0], place[1]))
     whole = lambda *shape: pl.BlockSpec(shape, lambda i, place: (0,) * len(shape))
-    shapes = [(audio_rows, width), (2, audio_rows, width), (2, video_rows, width), (2, video_rows, width)]
+    shapes = [
+        (audio_rows, width),
+        (2, audio_rows, width),
+        (2, video_rows, width),
+        (2 * video_rows + audio_rows, width),
+    ]
     return pl.pallas_call(
         prepare_kernel,
         grid_spec=pltpu.PrefetchScalarGridSpec(
             num_scalar_prefetch=1,
             grid=(1,),
-            in_specs=[cut] * 3 + [whole(*video_q.shape)] * 4,
+            in_specs=[cut] * 3 + [whole(*video_q.shape)] * 4 + [whole(*d_audio.shape)],
             out_specs=[whole(*shape) for shape in shapes],
         ),
         out_shape=[jax.ShapeDtypeStruct(shape, BF16) for shape in shapes],
         compiler_params=pltpu.CompilerParams(vmem_limit_bytes=VMEM),
         name="prepare",
-    )(place, audio_q, audio_k, audio_v, video_q, video_k, video_v, d_video)
-
-
-def forward_kernel(part, *refs):
-    q_refs, k_refs, limit_ref, gates_ref = refs[:2], refs[2:6], refs[6], refs[7]
-    e_ref, o_ref, stats_ref = refs[-3:]
-    queries = jnp.concatenate(query_rows(q_refs, 0), axis=0)
-    raw = nt(joined(k_refs, 0), queries)
-    if part == AUDIO:
-        rows = k_refs[0].shape[1]
-        position = lax.broadcasted_iota(jnp.int32, (rows, raw.shape[1]), 0)
-        pieces = [raw[place * rows : (place + 1) * rows] for place in range(SIDE)]
-        pieces = [jnp.where(position < limit_ref[place], pieces[place], -1e30) for place in range(SIDE)]
-        raw = jnp.concatenate(pieces, axis=0)
-    peak = jnp.max(raw, axis=0, keepdims=True)
-    expon = jnp.exp((raw - peak) * SCALE)
-    total = jnp.sum(expon, axis=0, keepdims=True)
-    expon = (expon * (1.0 / total)).astype(BF16)
-    e_ref[0] = expon
-    output = nn(joined(k_refs, 1).T, expon)
-    o_ref[0] = output
-    up = upstream(q_refs, gates_ref, part)
-    delta = jnp.sum(up.astype(F32).T * output, axis=0, keepdims=True)
-    log_total = peak * SCALE + jnp.log(total)
-    if part == VIDEO:
-        stats_ref[0] = jnp.concatenate([log_total, delta, log_total, delta], axis=0)
-    else:
-        stats_ref[0] = jnp.concatenate([refs[8][0, 0:2], log_total, delta], axis=0)
+    )(place, audio_q, audio_k, audio_v, video_q, video_k, video_v, d_video, d_audio)
+
+
+def forward_kernel(video_rows, *refs):
+    gathered_ref, audio_q, k_refs, numbers_ref, gates_ref = refs[0], refs[1:5], (refs[5:9], refs[9:13]), refs[13], refs[14]
+    e_refs, o_ref, stats_ref, ordered_ref = refs[15:17], refs[17], refs[18], refs[19]
+    for place in range(SIDE):
+        ordered_ref[lax.rem(numbers_ref[SIDE] + SIDE - place, SIDE)] = audio_q[place][...]
+    queries = queries_of(gathered_ref, ordered_ref, video_rows)
+    stats = []
+    for part in (VIDEO, AUDIO):
+        raw = nt(joined(k_refs[part], 0), queries)
+        if part == AUDIO:
+            rows = k_refs[part][0].shape[1]
+            position = lax.broadcasted_iota(jnp.int32, (rows, raw.shape[1]), 0)
+            pieces = [raw[place * rows : (place + 1) * rows] for place in range(SIDE)]
+            pieces = [jnp.where(position < numbers_ref[place], pieces[place], -1e30) for place in range(SIDE)]
+            raw = jnp.concatenate(pieces, axis=0)
+        peak = jnp.max(raw, axis=0, keepdims=True)
+        expon = jnp.exp((raw - peak) * SCALE)
+        total = jnp.sum(expon, axis=0, keepdims=True)
+        expon = (expon * (1.0 / total)).astype(BF16)
+        e_refs[part][0] = expon
+        output = nn(joined(k_refs[part], 1).T, expon)
+        o_ref[0, part] = output
+        up = upstream(gathered_ref, gates_ref, video_rows, part)
+        stats.append(peak * SCALE + jnp.log(total))
+        stats.append(jnp.sum(up.astype(F32).T * output, axis=0, keepdims=True))
+    stats_ref[0] = jnp.concatenate(stats, axis=0)
 
 
 def merged_stats(refs, part):
@@ -156,20 +172,20 @@
     return nn(joined(k_refs, 0).T, grad_scores), factor
 
 
-def backward_kernel(*refs):
-    q_refs, k_video, k_audio, stats_refs = refs[:2], refs[2:6], refs[6:10], refs[10:14]
-    gates_ref, columns_ref, e_video, e_audio, o_video, o_audio = refs[14:20]
-    k_outs, q_out = refs[20:24], refs[24]
-    video_rows, audio_rows = (ref.shape[2] for ref in q_refs)
+def backward_kernel(video_rows, *refs):
+    gathered_ref, audio_q, k_video, k_audio, stats_refs = refs[0], refs[1], refs[2:6], refs[6:10], refs[10:14]
+    gates_ref, columns_ref, e_video, e_audio, o_ref = refs[14:19]
+    k_outs, q_out = refs[19:23], refs[23]
+    audio_rows = audio_q.shape[1]
     rows = video_rows + audio_rows
     video = SIDE * video_rows
-    queries = jnp.concatenate(query_rows(q_refs, 0), axis=0)
-    up = upstream(q_refs, gates_ref, VIDEO)
+    queries = queries_of(gathered_ref, audio_q, video_rows)
+    up = upstream(gathered_ref, gates_ref, video_rows, VIDEO)
     term_video, factor = backward_keys(VIDEO, queries, up, stats_refs, k_video, e_video, k_outs, 0)
-    on_video = o_video[0] * factor
-    up = upstream(q_refs, gates_ref, AUDIO)
+    on_video = o_ref[0, VIDEO] * factor
+    up = upstream(gathered_ref, gates_ref, video_rows, AUDIO)
     term_audio, factor = backward_keys(AUDIO, queries, up, stats_refs, k_audio, e_audio, k_outs, video_rows)
-    on_audio = o_audio[0] * factor
+    on_audio = o_ref[0, AUDIO] * factor
     grad_queries = term_video + term_audio
     cross_video, cross_audio = on_audio[:, :video], on_video[:, video:]
     merged = jnp.concatenate(
@@ -179,7 +195,7 @@
         ],
         axis=1,
     )
-    up_video, up_audio = query_rows(q_refs, 1)
+    up_video, up_audio = upstreams_of(gathered_ref, video_rows)
     video_sum = jnp.sum(up_video.astype(F32).T * cross_video, axis=1, keepdims=True)
     audio_sum = jnp.sum(up_audio.astype(F32).T * cross_audio, axis=1, keepdims=True)
     sums = jnp.concatenate(
@@ -220,36 +236,39 @@
     )
 
 
-def attention_forward(part, q_chunks, k_chunks, limits, gates, earlier):
+def attention_forward(queries, audio_q, video_keys, audio_keys, numbers, gates, video_rows):
     heads = gates.shape[1] // HEAD_DIM
-    keys, queries = SIDE * k_chunks[0].shape[1], sum(SIDE * array.shape[2] for array in q_chunks)
+    audio_rows, width = audio_q[0].shape
+    video, audio = SIDE * video_rows, SIDE * audio_rows
+    total = video + audio
     outs = [
-        like(heads, keys, queries),
-        like(heads, HEAD_DIM, queries, kind=F32),
-        like(heads, 4, queries, kind=F32),
+        like(heads, video, total),
+        like(heads, audio, total),
+        like(heads, 2, HEAD_DIM, total, kind=F32),
+        like(heads, 4, total, kind=F32),
     ]
+    ordered = like(SIDE, audio_rows, width)
+    chunks = [queries, *audio_q, *video_keys, *audio_keys]
     return pl.pallas_call(
-        functools.partial(forward_kernel, part),
+        functools.partial(forward_kernel, video_rows),
         grid=(heads,),
-        in_specs=[chunk_spec(array) for array in (*q_chunks, *k_chunks)]
-        + [pl.BlockSpec(memory_space=pltpu.SMEM), chunk_spec(gates)]
-        + [head_spec(array) for array in earlier],
-        out_specs=[head_spec(array) for array in outs],
-        out_shape=outs,
-        cost_estimate=cost(keys, queries, heads, 2),
+        in_specs=[chunk_spec(array) for array in chunks] + [pl.BlockSpec(memory_space=pltpu.SMEM), chunk_spec(gates)],
+        out_specs=[head_spec(array) for array in outs] + [chunk_spec(ordered)],
+        out_shape=[*outs, ordered],
+        cost_estimate=cost(total, total, heads, 2),
         compiler_params=pltpu.CompilerParams(vmem_limit_bytes=VMEM),
-        name=("forward_video", "forward_audio")[part],
-    )(*q_chunks, *k_chunks, limits, gates, *earlier)
-
-
-def attention_backward(q_chunks, video_keys, audio_keys, stats, gates, by_head):
+        name="forward",
+    )(*chunks, numbers, gates)
+
+
+def attention_backward(queries, audio_q, video_keys, audio_keys, stats, gates, by_head, video_rows):
     width = gates.shape[1]
     heads = width // HEAD_DIM
-    rows, q_rows = video_keys[0].shape[1] + audio_keys[0].shape[1], sum(array.shape[2] for array in q_chunks)
-    outs = [like(2, rows, width)] * SIDE + [like(SIDE, 2 * q_rows + GATE_ROWS, width)]
-    chunks = [*q_chunks, *video_keys, *audio_keys]
+    rows = video_rows + audio_q.shape[1]
+    outs = [like(2, rows, width)] * SIDE + [like(SIDE, 2 * rows + GATE_ROWS, width)]
+    chunks = [queries, audio_q, *video_keys, *audio_keys]
     *key_parts, query_parts = pl.pallas_call(
-        backward_kernel,
+        functools.partial(backward_kernel, video_rows),
         grid=(heads,),
         in_specs=[chunk_spec(array) for array in chunks]
         + [head_spec(array) for array in stats]
@@ -257,7 +276,7 @@
         + [head_spec(array) for array in by_head],
         out_specs=[chunk_spec(array) for array in outs],
         out_shape=outs,
-        cost_estimate=cost(SIDE * rows, SIDE * q_rows, heads, 4),
+        cost_estimate=cost(SIDE * rows, SIDE * rows, heads, 4),
         compiler_params=pltpu.CompilerParams(vmem_limit_bytes=VMEM),
         name="backward",
     )(*chunks, *stats, gates, gates.T, *by_head)
@@ -335,29 +354,28 @@
     video_rows, audio_rows = video_q.shape[1], d_audio_out.shape[1]
     holds = audio_len[0] > 0
     place = jnp.stack([vid % 2, vid // 2]).astype(jnp.int32)
-    send_q, send_kv, video_kv, video_queries = prepare(
-        place, audio_rows, audio_q, audio_k, audio_v, video_q, video_k, video_v, d_video_out
-    )
-
-    def first_chunks(send_q, send_kv, video_kv, video_queries):
-        audio = own_audio(send_q, *sizes), own_audio(send_kv, *sizes)
-        keys = gathered(video_kv, along_z)
-        return audio, tuple(keys[1:]), all_along_x(video_queries)
-
-    (aud_q, aud_kv), video_keys, video_queries = fenced(
-        holds, first_chunks, send_q, send_kv, video_kv, video_queries
-    )
+    send_q, send_kv, video_kv, queries = prepare(
+        place, audio_q, audio_k, audio_v, video_q, video_k, video_v, d_video_out, d_audio_out
+    )
+
+    def video_chunks(video_kv, queries):
+        return tuple(gathered(video_kv, along_z)[1:]), all_along_x(queries)
+
+    aud_q, aud_kv = own_audio(send_q, *sizes), own_audio(send_kv, *sizes)
+    video_keys, queries = fenced(holds, video_chunks, video_kv, queries)
+    aud_q, aud_kv, queries = lax.optimization_barrier((aud_q, aud_kv, queries))
     video_keys = [video_kv, *video_keys]
+    audio_queries = gathered(aud_q, along_x)
     audio_keys = gathered(aud_kv, along_z)
-    q_chunks = video_queries, all_along_x(jnp.stack([aud_q, d_audio_out[0]]))
     gates = jnp.stack([video_gate, audio_gate])
     column, row = vid // SIDE, vid % SIDE
-    limits = jnp.stack([audio_len[0] - (column * SIDE + (row - p) % SIDE) * audio_rows for p in range(SIDE)])
-    e_video, o_video, stats = attention_forward(VIDEO, q_chunks, video_keys, limits, gates, ())
-    e_audio, o_audio, stats = attention_forward(AUDIO, q_chunks, audio_keys, limits, gates, (stats,))
-    stats = gathered(stats, along_x)
+    limits = [audio_len[0] - (column * SIDE + (row - p) % SIDE) * audio_rows for p in range(SIDE)]
+    numbers = jnp.stack([*limits, column])
+    *by_head, stats, audio_queries = attention_forward(
+        queries, audio_queries, video_keys, audio_keys, numbers, gates, video_rows
+    )
     key_parts, query_parts = attention_backward(
-        q_chunks, video_keys, audio_keys, stats, gates, (e_video, e_audio, o_video, o_audio)
+        queries, audio_queries, video_keys, audio_keys, gathered(stats, along_x), gates, by_head, video_rows
     )
 
     def query_results(parts):

time: 118 us -> 111 us (0.941)
  blocking collectives: 44.5 us -> 32.7 us
  waiting for transfers between devices: 8.9 us -> 15.9 us
  Pallas kernels: 19.8 us -> 17.7 us
  other arithmetic: 3.98 us -> 2.59 us
    all_gather x2 -> x1, blocking collectives: 31.3 us -> 17.9 us  [all_along_x(): return lax.all_gather(array, 'vid', axis=0, axis_index_groups=ALONG_X)]
    ppermute x3 -> x6, starting transfers between devices: 2.09 us -> 8.4 us  [along_x(): return lax.ppermute(array, 'vid', pairs)]
    ppermute x1, starting transfers between devices: 11.5 us -> 6.41 us  [query_results(): return (*results, gate + lax.ppermute(gate, 'pair', [(0, 1), (1, 0)]))]
    ppermute x2, starting transfers between devices: 3.83 us -> 0.01 us  [beside_z(): return lax.ppermute(array, 'vid', pairs)]
    ppermute x2, waiting for transfers between devices: 5.17 us -> 8.68 us  [beside_z(): return lax.ppermute(array, 'vid', pairs)]
    ppermute x9, starting transfers between devices: 16.7 us -> 19.9 us  [along_z(): return lax.ppermute(array, 'vid', pairs)]
    ppermute x9, waiting for transfers between devices: 0.02 us -> 3.01 us  [along_z(): return lax.ppermute(array, 'vid', pairs)]
    pallas_call x3 -> x2, Pallas kernels: 16.4 us -> 13.7 us  [the longest x1 7.07 us: attention_backward(): pl.pallas_call(functools.partial(backward_kernel, video_rows), grid=(head...]
  transfers between devices with their start and end apart: 17 -> 20, of which waited for: 6 -> 7; matrix products, arithmetic and copies ran while one was open for 4% -> 3% of each run, Pallas kernels for 5% -> 1%
where the time goes in v5:
time: 111 us
  starting transfers between devices  37.7 us (34%)
  blocking collectives  32.7 us (29%)
  Pallas kernels  17.7 us (16%)
  waiting for transfers between devices  15.9 us (14%)
  local copies, waits for them, and re-layouts  2.73 us (2%)
  other arithmetic  2.59 us (2%)
  between operations  1.63 us (1%)
    ppermute x9, starting transfers between devices, along_z(): return lax.ppermute(array, 'vid', pairs)  19.9 us
    all_gather x1, blocking collectives, all_along_x(): return lax.all_gather(array, 'vid', axis=0, axis_index_groups=ALONG_X)  17.9 us
    all_to_all x1, blocking collectives, query_results(): lax.all_to_all(parts, 'vid', 0, 0, axis_index_groups=ALONG_X, tiled=True)  14.8 us
    ppermute x2, waiting for transfers between devices, beside_z(): return lax.ppermute(array, 'vid', pairs)  8.68 us
    ppermute x6, starting transfers between devices, along_x(): return lax.ppermute(array, 'vid', pairs)  8.4 us
    pallas_call x1, Pallas kernels, attention_backward(): pl.pallas_call(functools.partial(backward_kernel, video_rows), grid=(head...  7.07 us
    pallas_call x1, Pallas kernels, attention_forward(): pl.pallas_call(functools.partial(forward_kernel, video_rows), grid=(heads...  6.63 us
    ppermute x1, starting transfers between devices, query_results(): return (*results, gate + lax.ppermute(gate, 'pair', [(0, 1), (1, 0)]))  6.41 us
  transfers between devices with their start and end apart: 20, of which 7 were waited for; matrix products, arithmetic and copies ran while one was open for 3% of the time, Pallas kernels for 1%

profile of v5, /device:TPU:1, one launch (start us, length us, event | category | flops | bytes accessed | tf_op | source)
XLA Modules:
  0.0 111.0 jit_solution(7956444005557276534)
XLA Ops:
  1.2 2.4 %prepare.1 = (bf16[64,384]{1,0:T(8,128)(2,1)}, bf16[2,64,384]{2,1,0:T(8,128)(2,1)}, bf16[2,128,384]{2,1,0:T(8,128)(2,1)S(1)}, bf16[320,384]{1,0:T(8,128)(2,1)S(1)}) custom-call(s32[2]{0:T(128)} %pad_add_fusion.place_ref, bf16[1,128,3072]{2,1,0:T(8,128)(2,1)} %aq_ref.1, bf16[1,128,3072]{2,1,0:T(8,128)(2,1)} %ak_ref.1, bf16[1,128,3072]{2,1,0:T(8,128)(2,1)} %av_ref.1, ...), custom_call_target="tpu_custom_call" | custom-call | tf_op jit(solution)/shard_map/prepare/pallas_call | solution.py:110
  3.7 1.5 %collective-permute-start.7 = (bf16[2,64,384]{2,1,0:T(8,128)(2,1)}, bf16[2,64,384]{2,1,0:T(8,128)(2,1)S(1)}, u32[]{:S(2)}, u32[]{:S(2)}) collective-permute-start(bf16[2,64,384]{2,1,0:T(8,128)(2,1)} %get-tuple-element.58), channel_id=1, source_target_pairs={{0,0},{2,32},{4,64},{6,96},{8,128},{10,160},{12,192},{14,224},{16,... | collective-permute-start | bytes 294920 | tf_op jit(solution)/shard_map/ppermute | solution.py:339
  5.2 1.4 %collective-permute-start.6 = (bf16[64,384]{1,0:T(8,128)(2,1)}, bf16[64,384]{1,0:T(8,128)(2,1)S(1)}, u32[]{:S(2)}, u32[]{:S(2)}) collective-permute-start(bf16[64,384]{1,0:T(8,128)(2,1)} %get-tuple-element.57), channel_id=1, source_target_pairs={{0,0},{2,32},{4,64},{6,96},{8,128},{10,160},{12,192},{14,224},{16,... | collective-permute-start | bytes 147464 | tf_op jit(solution)/shard_map/ppermute | solution.py:339
  7.4 28.4 %conditional.2 = (bf16[2,128,384]{2,1,0:T(8,128)(2,1)}, bf16[2,128,384]{2,1,0:T(8,128)(2,1)}, bf16[2,128,384]{2,1,0:T(8,128)(2,1)}, bf16[4,320,384]{2,1,0:T(8,128)(2,1)S(1)}) conditional(s32[]{:T(128)} %convert_element_type.4, () %tuple.28, (bf16[2,128,384]{2,1,0:T(8,128)(2,1)S(1)}, bf16[320,384]{1,0:T(8,128)(2,1)S(1)}) %tuple.29), branch_computations={%region_0.1_spmd, %region_1.2_spmd} | conditional | bytes 3588248 | solution.py:344
  7.4 9.7 %collective-permute-start.2 = (bf16[2,128,384]{2,1,0:T(8,128)(2,1)S(1)}, bf16[2,128,384]{2,1,0:T(8,128)(2,1)}, u32[]{:S(2)}, u32[]{:S(2)}) collective-permute-start(bf16[2,128,384]{2,1,0:T(8,128)(2,1)S(1)} %get-tuple-element.9), channel_id=1, source_target_pairs={{0,48},{16,0},{32,16},{48,32},{64,112},{80,64},{96,80},{112,96},{1... | collective-permute-start | bytes 589832 | tf_op jit(solution)/shard_map/cond/branch_1_fun/ppermute | solution.py:29
  17.8 17.9 %all-gather = bf16[1280,384]{1,0:T(8,128)(2,1)S(1)} all-gather(bf16[320,384]{1,0:T(8,128)(2,1)S(1)} %get-tuple-element.10), channel_id=2, replica_groups={{0,64,128,192},{16,80,144,208},{32,96,160,224},{48,112,176,240},{1,65,1..., dimensions={0}, use_global_device_ids=true | all-gather | bytes 1228800 | tf_op jit(solution)/shard_map/cond/branch_1_fun/all_gather | solution.py:38
  35.8 3.7 %collective-permute-start.10 = (bf16[64,384]{1,0:T(8,128)(2,1)S(1)}, bf16[64,384]{1,0:T(8,128)(2,1)S(1)}, u32[]{:S(2)}, u32[]{:S(2)}) collective-permute-start(bf16[64,384]{1,0:T(8,128)(2,1)S(1)} %collective-permute-done.6.refs_1_), channel_id=1, source_target_pairs={{0,192},{16,208},{32,224},{48,240},{64,0},{80,16},{96,32},{112,48}... | collective-permute-start | bytes 147464 | tf_op jit(solution)/shard_map/ppermute | solution.py:24
  39.5 1.0 collective-permute-start.9
  41.3 3.2 %collective-permute-start.12 = (bf16[2,64,384]{2,1,0:T(8,128)(2,1)S(1)}, bf16[2,64,384]{2,1,0:T(8,128)(2,1)S(1)}, u32[]{:S(2)}, u32[]{:S(2)}) collective-permute-start(bf16[2,64,384]{2,1,0:T(8,128)(2,1)S(1)} %collective-permute-done.7.refs_9_.refs_6_), channel_id=1, source_target_pairs={{0,32},{16,48},{32,0},{48,16},{64,96},{80,112},{96,64},{112,80},{1... | collective-permute-start | bytes 294920 | tf_op jit(solution)/shard_map/ppermute | solution.py:29
  44.5 1.5 %collective-permute-start.11 = (bf16[2,64,384]{2,1,0:T(8,128)(2,1)S(1)}, bf16[2,64,384]{2,1,0:T(8,128)(2,1)S(1)}, u32[]{:S(2)}, u32[]{:S(2)}) collective-permute-start(bf16[2,64,384]{2,1,0:T(8,128)(2,1)S(1)} %collective-permute-done.7.refs_9_.refs_6_), channel_id=1, source_target_pairs={{0,16},{16,32},{32,48},{48,0},{64,80},{80,96},{96,112},{112,64},{1... | collective-permute-start | bytes 294920 | tf_op jit(solution)/shard_map/ppermute | solution.py:29
  47.6 2.6 %collective-permute-done.11.refs_10_.refs_7_ = bf16[2,64,384]{2,1,0:T(8,128)(2,1)S(1)} collective-permute-done((bf16[2,64,384]{2,1,0:T(8,128)(2,1)S(1)}, bf16[2,64,384]{2,1,0:T(8,128)(2,1)S(1)}, u32[]{:S(2)}, u32[]{:S(2)}) %collective-permute-start.11) | collective-permute-done | bytes 98336 | tf_op jit(solution)/shard_map/ppermute | solution.py:29
  50.9 6.6 %forward.1 = (bf16[3,512,768]{2,1,0:T(8,128)(2,1)}, bf16[3,256,768]{2,1,0:T(8,128)(2,1)}, f32[3,2,128,768]{3,2,1,0:T(8,128)}, f32[3,4,768]{2,1,0:T(4,128)}, bf16[4,64,384]{2,1,0:T(8,128)(2,1)}) custom-call(bf16[4,320,384]{2,1,0:T(8,128)(2,1)S(1)} %get-tuple-element.62.refs_0_, bf16[64,384]{1,0:T(8,128)(2,1)} %copy-done.13, bf16[64,384]{1,0:T(8,128)(2,1)} %copy-done.16, ...), custom_call_target="tpu_custom_call" | custom-call | flops 905969664 | bytes 7077888 | tf_op jit(solution)/shard_map/forward/pallas_call | solution.py:252
  57.5 2.2 %collective-permute-start.16 = (f32[3,4,768]{2,1,0:T(4,128)}, f32[3,4,768]{2,1,0:T(4,128)S(1)}, u32[]{:S(2)}, u32[]{:S(2)}) collective-permute-start(f32[3,4,768]{2,1,0:T(4,128)} %get-tuple-element.69.refs_10_), channel_id=1, source_target_pairs={{0,192},{16,208},{32,224},{48,240},{64,0},{80,16},{96,32},{112,48}... | collective-permute-start | bytes 110600 | tf_op jit(solution)/shard_map/ppermute | solution.py:24
  60.4 0.8 copy.27
  61.2 3.0 %collective-permute-done.15.refs_12_ = f32[3,4,768]{2,1,0:T(4,128)S(1)} collective-permute-done((f32[3,4,768]{2,1,0:T(4,128)}, f32[3,4,768]{2,1,0:T(4,128)S(1)}, u32[]{:S(2)}, u32[]{:S(2)}) %collective-permute-start.15) | collective-permute-done | bytes 36896 | tf_op jit(solution)/shard_map/ppermute | solution.py:24
  65.3 7.1 %backward.1 = (bf16[2,192,384]{2,1,0:T(8,128)(2,1)}, bf16[2,192,384]{2,1,0:T(8,128)(2,1)}, bf16[2,192,384]{2,1,0:T(8,128)(2,1)}, bf16[2,192,384]{2,1,0:T(8,128)(2,1)}, bf16[4,400,384]{2,1,0:T(8,128)(2,1)S(1)}) custom-call(bf16[4,320,384]{2,1,0:T(8,128)(2,1)S(1)} %get-tuple-element.62.refs_0_, bf16[4,64,384]{2,1,0:T(8,128)(2,1)} %get-tuple-element.68.refs_1_, ...), custom_call_target="tpu_custom_call" | custom-call | flops 1811939328 | bytes 7077888 | tf_op jit(solution)/shard_map/backward/pallas_call | solution.py:270
  72.3 1.6 %collective-permute-start.17 = (bf16[2,192,384]{2,1,0:T(8,128)(2,1)}, bf16[2,192,384]{2,1,0:T(8,128)(2,1)S(1)}, u32[]{:S(2)}, u32[]{:S(2)}) collective-permute-start(bf16[2,192,384]{2,1,0:T(8,128)(2,1)} %get-tuple-element.78), channel_id=1, source_target_pairs={{0,48},{16,0},{32,16},{48,32},{64,112},{80,64},{96,80},{112,96},{1... | collective-permute-start | bytes 884744 | tf_op jit(solution)/shard_map/ppermute | solution.py:29
  73.9 1.9 %collective-permute-start.18 = (bf16[2,192,384]{2,1,0:T(8,128)(2,1)}, bf16[2,192,384]{2,1,0:T(8,128)(2,1)S(1)}, u32[]{:S(2)}, u32[]{:S(2)}) collective-permute-start(bf16[2,192,384]{2,1,0:T(8,128)(2,1)} %get-tuple-element.79), channel_id=1, source_target_pairs={{0,32},{16,48},{32,0},{48,16},{64,96},{80,112},{96,64},{112,80},{1... | collective-permute-start | bytes 884744 | tf_op jit(solution)/shard_map/ppermute | solution.py:29
  75.8 1.4 %collective-permute-start.19 = (bf16[2,192,384]{2,1,0:T(8,128)(2,1)}, bf16[2,192,384]{2,1,0:T(8,128)(2,1)S(1)}, u32[]{:S(2)}, u32[]{:S(2)}) collective-permute-start(bf16[2,192,384]{2,1,0:T(8,128)(2,1)} %get-tuple-element.80), channel_id=1, source_target_pairs={{0,16},{16,32},{32,48},{48,0},{64,80},{80,96},{96,112},{112,64},{1... | collective-permute-start | bytes 884744 | tf_op jit(solution)/shard_map/ppermute | solution.py:29
  77.2 32.9 %conditional.3 = (bf16[1,128,384]{2,1,0:T(8,128)(2,1)}, bf16[1,64,384]{2,1,0:T(8,128)(2,1)}, bf16[1,128,384]{2,1,0:T(8,128)(2,1)}, bf16[1,64,384]{2,1,0:T(8,128)...) conditional(s32[]{:T(128)} %convert_element_type.4, () %tuple.27, ...), branch_computations={%region_2.3_spmd, %region_3.4_spmd} | conditional | flops 9984 | bytes 2723520 | solution.py:344
  77.2 14.8 %all_to_all.4.parts_ref = bf16[4,400,384]{2,1,0:T(8,128)(2,1)S(1)} all-to-all(bf16[4,400,384]{2,1,0:T(8,128)(2,1)S(1)} %param.3), channel_id=1, replica_groups={{0,64,128,192},{16,80,144,208},{32,96,160,224},{48,112,176,240},{1,65,1..., dimensions={0} | all-to-all | bytes 2457600 | tf_op jit(solution)/shard_map/cond/branch_1_fun/all_to_all | solution.py:382
  92.7 4.8 %collective-permute-done.3 = f32[8,384]{1,0:T(8,128)S(1)} collective-permute-done((f32[8,384]{1,0:T(8,128)S(1)}, f32[8,384]{1,0:T(8,128)S(1)}, u32[]{:S(2)}, u32[]{:S(2)}) %collective-permute-start.3) | collective-permute-done | bytes 12320 | tf_op jit(solution)/shard_map/cond/branch_1_fun/ppermute | solution.py:34
  97.5 3.9 %collective-permute-done.4 = f32[8,384]{1,0:T(8,128)S(1)} collective-permute-done((f32[8,384]{1,0:T(8,128)S(1)}, f32[8,384]{1,0:T(8,128)S(1)}, u32[]{:S(2)}, u32[]{:S(2)}) %collective-permute-start.4) | collective-permute-done | bytes 12320 | tf_op jit(solution)/shard_map/cond/branch_1_fun/ppermute | solution.py:34
  101.4 6.4 %collective-permute-start.5 = (f32[8,384]{1,0:T(8,128)S(1)}, f32[8,384]{1,0:T(8,128)S(1)}, u32[]{:S(2)}, u32[]{:S(2)}) collective-permute-start(f32[8,384]{1,0:T(8,128)S(1)} %add.33), channel_id=1, source_target_pairs={{0,1},{1,0},{2,3},{3,2},{4,5},{5,4},{6,7},{7,6},{8,9},{9,8},{10,11... | collective-permute-start | bytes 36872 | tf_op jit(solution)/shard_map/cond/branch_1_fun/ppermute | solution.py:386
  (69 shorter events, 10.0 us)
Async XLA Ops:
  3.7 32.1 %collective-permute-start.7 = (bf16[2,64,384]{2,1,0:T(8,128)(2,1)}, bf16[2,64,384]{2,1,0:T(8,128)(2,1)S(1)}, u32[]{:S(2)}, u32[]{:S(2)}) collective-permute-start(bf16[2,64,384]{2,1,0:T(8,128)(2,1)} %get-tuple-element.58), channel_id=1, source_target_pairs={{0,0},{2,32},{4,64},{6,96},{8,128},{10,160},{12,192},{14,224},{16,... | collective-permute-start | bytes 294920 | tf_op jit(solution)/shard_map/ppermute | solution.py:339
  5.2 30.5 %collective-permute-start.6 = (bf16[64,384]{1,0:T(8,128)(2,1)}, bf16[64,384]{1,0:T(8,128)(2,1)S(1)}, u32[]{:S(2)}, u32[]{:S(2)}) collective-permute-start(bf16[64,384]{1,0:T(8,128)(2,1)} %get-tuple-element.57), channel_id=1, source_target_pairs={{0,0},{2,32},{4,64},{6,96},{8,128},{10,160},{12,192},{14,224},{16,... | collective-permute-start | bytes 147464 | tf_op jit(solution)/shard_map/ppermute | solution.py:339
  7.3 32.1 %copy-start.9 = (f32[384]{0:T(512)S(1)}, f32[384]{0:T(512)}, u32[]{:S(2)}) copy-start(f32[384]{0:T(512)} %param.21) | copy-start | bytes 4612
  7.3 32.1 %copy-start.10 = (f32[384]{0:T(512)S(1)}, f32[384]{0:T(512)}, u32[]{:S(2)}) copy-start(f32[384]{0:T(512)} %param.22) | copy-start | bytes 4612
  7.4 28.4 %collective-permute-start.2 = (bf16[2,128,384]{2,1,0:T(8,128)(2,1)S(1)}, bf16[2,128,384]{2,1,0:T(8,128)(2,1)}, u32[]{:S(2)}, u32[]{:S(2)}) collective-permute-start(bf16[2,128,384]{2,1,0:T(8,128)(2,1)S(1)} %get-tuple-element.9), channel_id=1, source_target_pairs={{0,48},{16,0},{32,16},{48,32},{64,112},{80,64},{96,80},{112,96},{1... | collective-permute-start | bytes 589832 | tf_op jit(solution)/shard_map/cond/branch_1_fun/ppermute | solution.py:29
  17.0 18.7 %collective-permute-start.1 = (bf16[2,128,384]{2,1,0:T(8,128)(2,1)S(1)}, bf16[2,128,384]{2,1,0:T(8,128)(2,1)}, u32[]{:S(2)}, u32[]{:S(2)}) collective-permute-start(bf16[2,128,384]{2,1,0:T(8,128)(2,1)S(1)} %get-tuple-element.9), channel_id=1, source_target_pairs={{0,32},{16,48},{32,0},{48,16},{64,96},{80,112},{96,64},{112,80},{1... | collective-permute-start | bytes 589832 | tf_op jit(solution)/shard_map/cond/branch_1_fun/ppermute | solution.py:29
  17.0 18.7 %collective-permute-start = (bf16[2,128,384]{2,1,0:T(8,128)(2,1)S(1)}, bf16[2,128,384]{2,1,0:T(8,128)(2,1)}, u32[]{:S(2)}, u32[]{:S(2)}) collective-permute-start(bf16[2,128,384]{2,1,0:T(8,128)(2,1)S(1)} %get-tuple-element.9), channel_id=1, source_target_pairs={{0,16},{16,32},{32,48},{48,0},{64,80},{80,96},{96,112},{112,64},{1... | collective-permute-start | bytes 589832 | tf_op jit(solution)/shard_map/cond/branch_1_fun/ppermute | solution.py:29
  35.7 14.5 %copy-start.13 = (bf16[64,384]{1,0:T(8,128)(2,1)}, bf16[64,384]{1,0:T(8,128)(2,1)S(1)}, u32[]{:S(2)}) copy-start(bf16[64,384]{1,0:T(8,128)(2,1)S(1)} %collective-permute-done.6.refs_1_) | copy-start | bytes 147460
  35.8 8.7 %collective-permute-start.10 = (bf16[64,384]{1,0:T(8,128)(2,1)S(1)}, bf16[64,384]{1,0:T(8,128)(2,1)S(1)}, u32[]{:S(2)}, u32[]{:S(2)}) collective-permute-start(bf16[64,384]{1,0:T(8,128)(2,1)S(1)} %collective-permute-done.6.refs_1_), channel_id=1, source_target_pairs={{0,192},{16,208},{32,224},{48,240},{64,0},{80,16},{96,32},{112,48}... | collective-permute-start | bytes 147464 | tf_op jit(solution)/shard_map/ppermute | solution.py:24
  39.5 7.7 %collective-permute-start.9 = (bf16[64,384]{1,0:T(8,128)(2,1)S(1)}, bf16[64,384]{1,0:T(8,128)(2,1)S(1)}, u32[]{:S(2)}, u32[]{:S(2)}) collective-permute-start(bf16[64,384]{1,0:T(8,128)(2,1)S(1)} %collective-permute-done.6.refs_1_), channel_id=1, source_target_pairs={{0,128},{16,144},{32,160},{48,176},{64,192},{80,208},{96,224},{112... | collective-permute-start | bytes 147464 | tf_op jit(solution)/shard_map/ppermute | solution.py:24
  40.5 6.7 %collective-permute-start.8 = (bf16[64,384]{1,0:T(8,128)(2,1)S(1)}, bf16[64,384]{1,0:T(8,128)(2,1)S(1)}, u32[]{:S(2)}, u32[]{:S(2)}) collective-permute-start(bf16[64,384]{1,0:T(8,128)(2,1)S(1)} %collective-permute-done.6.refs_1_), channel_id=1, source_target_pairs={{0,64},{16,80},{32,96},{48,112},{64,128},{80,144},{96,160},{112,17... | collective-permute-start | bytes 147464 | tf_op jit(solution)/shard_map/ppermute | solution.py:24
  41.3 5.9 %collective-permute-start.13 = (bf16[2,64,384]{2,1,0:T(8,128)(2,1)S(1)}, bf16[2,64,384]{2,1,0:T(8,128)(2,1)S(1)}, u32[]{:S(2)}, u32[]{:S(2)}) collective-permute-start(bf16[2,64,384]{2,1,0:T(8,128)(2,1)S(1)} %collective-permute-done.7.refs_9_.refs_6_), channel_id=1, source_target_pairs={{0,48},{16,0},{32,16},{48,32},{64,112},{80,64},{96,80},{112,96},{1... | collective-permute-start | bytes 294920 | tf_op jit(solution)/shard_map/ppermute | solution.py:29
  41.3 6.3 %collective-permute-start.12 = (bf16[2,64,384]{2,1,0:T(8,128)(2,1)S(1)}, bf16[2,64,384]{2,1,0:T(8,128)(2,1)S(1)}, u32[]{:S(2)}, u32[]{:S(2)}) collective-permute-start(bf16[2,64,384]{2,1,0:T(8,128)(2,1)S(1)} %collective-permute-done.7.refs_9_.refs_6_), channel_id=1, source_target_pairs={{0,32},{16,48},{32,0},{48,16},{64,96},{80,112},{96,64},{112,80},{1... | collective-permute-start | bytes 294920 | tf_op jit(solution)/shard_map/ppermute | solution.py:29
  44.5 5.7 %collective-permute-start.11 = (bf16[2,64,384]{2,1,0:T(8,128)(2,1)S(1)}, bf16[2,64,384]{2,1,0:T(8,128)(2,1)S(1)}, u32[]{:S(2)}, u32[]{:S(2)}) collective-permute-start(bf16[2,64,384]{2,1,0:T(8,128)(2,1)S(1)} %collective-permute-done.7.refs_9_.refs_6_), channel_id=1, source_target_pairs={{0,16},{16,32},{32,48},{48,0},{64,80},{80,96},{96,112},{112,64},{1... | collective-permute-start | bytes 294920 | tf_op jit(solution)/shard_map/ppermute | solution.py:29
  57.5 3.8 %collective-permute-start.16 = (f32[3,4,768]{2,1,0:T(4,128)}, f32[3,4,768]{2,1,0:T(4,128)S(1)}, u32[]{:S(2)}, u32[]{:S(2)}) collective-permute-start(f32[3,4,768]{2,1,0:T(4,128)} %get-tuple-element.69.refs_10_), channel_id=1, source_target_pairs={{0,192},{16,208},{32,224},{48,240},{64,0},{80,16},{96,32},{112,48}... | collective-permute-start | bytes 110600 | tf_op jit(solution)/shard_map/ppermute | solution.py:24
  59.7 4.5 %collective-permute-start.15 = (f32[3,4,768]{2,1,0:T(4,128)}, f32[3,4,768]{2,1,0:T(4,128)S(1)}, u32[]{:S(2)}, u32[]{:S(2)}) collective-permute-start(f32[3,4,768]{2,1,0:T(4,128)} %get-tuple-element.69.refs_10_), channel_id=1, source_target_pairs={{0,128},{16,144},{32,160},{48,176},{64,192},{80,208},{96,224},{112... | collective-permute-start | bytes 110600 | tf_op jit(solution)/shard_map/ppermute | solution.py:24
  60.3 4.3 %collective-permute-start.14 = (f32[3,4,768]{2,1,0:T(4,128)}, f32[3,4,768]{2,1,0:T(4,128)S(1)}, u32[]{:S(2)}, u32[]{:S(2)}) collective-permute-start(f32[3,4,768]{2,1,0:T(4,128)} %get-tuple-element.69.refs_10_), channel_id=1, source_target_pairs={{0,64},{16,80},{32,96},{48,112},{64,128},{80,144},{96,160},{112,17... | collective-permute-start | bytes 110600 | tf_op jit(solution)/shard_map/ppermute | solution.py:24
  72.3 37.8 %collective-permute-start.17 = (bf16[2,192,384]{2,1,0:T(8,128)(2,1)}, bf16[2,192,384]{2,1,0:T(8,128)(2,1)S(1)}, u32[]{:S(2)}, u32[]{:S(2)}) collective-permute-start(bf16[2,192,384]{2,1,0:T(8,128)(2,1)} %get-tuple-element.78), channel_id=1, source_target_pairs={{0,48},{16,0},{32,16},{48,32},{64,112},{80,64},{96,80},{112,96},{1... | collective-permute-start | bytes 884744 | tf_op jit(solution)/shard_map/ppermute | solution.py:29
  73.9 36.2 %collective-permute-start.18 = (bf16[2,192,384]{2,1,0:T(8,128)(2,1)}, bf16[2,192,384]{2,1,0:T(8,128)(2,1)S(1)}, u32[]{:S(2)}, u32[]{:S(2)}) collective-permute-start(bf16[2,192,384]{2,1,0:T(8,128)(2,1)} %get-tuple-element.79), channel_id=1, source_target_pairs={{0,32},{16,48},{32,0},{48,16},{64,96},{80,112},{96,64},{112,80},{1... | collective-permute-start | bytes 884744 | tf_op jit(solution)/shard_map/ppermute | solution.py:29
  75.8 34.3 %collective-permute-start.19 = (bf16[2,192,384]{2,1,0:T(8,128)(2,1)}, bf16[2,192,384]{2,1,0:T(8,128)(2,1)S(1)}, u32[]{:S(2)}, u32[]{:S(2)}) collective-permute-start(bf16[2,192,384]{2,1,0:T(8,128)(2,1)} %get-tuple-element.80), channel_id=1, source_target_pairs={{0,16},{16,32},{32,48},{48,0},{64,80},{80,96},{96,112},{112,64},{1... | collective-permute-start | bytes 884744 | tf_op jit(solution)/shard_map/ppermute | solution.py:29
  77.2 33.0 %copy-start = (bf16[2,192,384]{2,1,0:T(8,128)(2,1)S(1)}, bf16[2,192,384]{2,1,0:T(8,128)(2,1)}, u32[]{:S(2)}) copy-start(bf16[2,192,384]{2,1,0:T(8,128)(2,1)} %get-tuple-element.77.refs_0_) | copy-start | bytes 884740
  92.7 4.8 %collective-permute-start.3 = (f32[8,384]{1,0:T(8,128)S(1)}, f32[8,384]{1,0:T(8,128)S(1)}, u32[]{:S(2)}, u32[]{:S(2)}) collective-permute-start(f32[8,384]{1,0:T(8,128)S(1)} %get-tuple-element.15), channel_id=1, source_target_pairs={{0,16},{16,0},{32,48},{48,32},{64,80},{80,64},{96,112},{112,96},{1... | collective-permute-start | bytes 36872 | tf_op jit(solution)/shard_map/cond/branch_1_fun/ppermute | solution.py:34
  97.5 3.9 %collective-permute-start.4 = (f32[8,384]{1,0:T(8,128)S(1)}, f32[8,384]{1,0:T(8,128)S(1)}, u32[]{:S(2)}, u32[]{:S(2)}) collective-permute-start(f32[8,384]{1,0:T(8,128)S(1)} %add.32), channel_id=1, source_target_pairs={{0,32},{16,48},{32,0},{48,16},{64,96},{80,112},{96,64},{112,80},{1... | collective-permute-start | bytes 36872 | tf_op jit(solution)/shard_map/cond/branch_1_fun/ppermute | solution.py:34
  101.4 7.2 %collective-permute-start.5 = (f32[8,384]{1,0:T(8,128)S(1)}, f32[8,384]{1,0:T(8,128)S(1)}, u32[]{:S(2)}, u32[]{:S(2)}) collective-permute-start(f32[8,384]{1,0:T(8,128)S(1)} %add.33), channel_id=1, source_target_pairs={{0,1},{1,0},{2,3},{3,2},{4,5},{5,4},{6,7},{7,6},{8,9},{9,8},{10,11... | collective-permute-start | bytes 36872 | tf_op jit(solution)/shard_map/cond/branch_1_fun/ppermute | solution.py:386
  (13 other events, 48.5 us)

commit v6 on v5

--- a/solution.py
+++ b/solution.py
@@ -83,42 +83,37 @@
     return jnp.concatenate([video, audio], axis=0)
 
 
-def prepare_kernel(place_ref, aq_ref, ak_ref, av_ref, vq_ref, vk_ref, vv_ref, dv_ref, da_ref, *outs):
-    audio_q, audio_kv, video_kv, queries = outs
-    rows = vq_ref.shape[1]
-    audio_q[...] = aq_ref[0]
-    audio_kv[0] = ak_ref[0]
-    audio_kv[1] = av_ref[0]
-    video_kv[0] = vk_ref[0]
-    video_kv[1] = vv_ref[0]
-    queries[:rows] = vq_ref[0]
-    queries[rows : 2 * rows] = dv_ref[0]
-    queries[2 * rows :] = da_ref[0]
-
-
-def prepare(place, audio_q, audio_k, audio_v, video_q, video_k, video_v, d_video, d_audio):
+def prepare_kernel(aq_ref, ak_ref, av_ref, vq_ref, vk_ref, vv_ref, dv_ref, da_ref, audio, video_kv, queries, sems):
+    vid = lax.axis_index("vid")
+    rows, width = vq_ref.shape[1:]
+    audio_rows = da_ref.shape[1]
+    taken = pl.ds(pl.multiple_of(lax.rem(vid, 2) * audio_rows, audio_rows), audio_rows)
+    columns = pl.ds(pl.multiple_of(lax.div(vid, 2) * width, HEAD_DIM), width)
+    pairs = [(ref.at[0, taken, columns], audio.at[index]) for index, ref in enumerate((aq_ref, ak_ref, av_ref))]
+    pairs += [(vk_ref.at[0], video_kv.at[0]), (vv_ref.at[0], video_kv.at[1])]
+    pairs += [(vq_ref.at[0], queries.at[pl.ds(0, rows)]), (dv_ref.at[0], queries.at[pl.ds(rows, rows)])]
+    pairs += [(da_ref.at[0], queries.at[pl.ds(2 * rows, audio_rows)])]
+    copies = [pltpu.make_async_copy(source, target, sems.at[index]) for index, (source, target) in enumerate(pairs)]
+    for copy in copies:
+        copy.start()
+    for copy in copies:
+        copy.wait()
+
+
+def prepare(audio_q, audio_k, audio_v, video_q, video_k, video_v, d_video, d_audio):
     _, video_rows, width = video_q.shape
     audio_rows = d_audio.shape[1]
-    cut = pl.BlockSpec((1, audio_rows, width), lambda i, place: (0, place[0], place[1]))
-    whole = lambda *shape: pl.BlockSpec(shape, lambda i, place: (0,) * len(shape))
-    shapes = [
-        (audio_rows, width),
-        (2, audio_rows, width),
-        (2, video_rows, width),
-        (2 * video_rows + audio_rows, width),
-    ]
+    given = (audio_q, audio_k, audio_v, video_q, video_k, video_v, d_video, d_audio)
+    shapes = [(3, audio_rows, width), (2, video_rows, width), (2 * video_rows + audio_rows, width)]
     return pl.pallas_call(
         prepare_kernel,
-        grid_spec=pltpu.PrefetchScalarGridSpec(
-            num_scalar_prefetch=1,
-            grid=(1,),
-            in_specs=[cut] * 3 + [whole(*video_q.shape)] * 4 + [whole(*d_audio.shape)],
-            out_specs=[whole(*shape) for shape in shapes],
-        ),
-        out_shape=[jax.ShapeDtypeStruct(shape, BF16) for shape in shapes],
+        in_specs=[pl.BlockSpec(memory_space=pl.ANY)] * len(given),
+        out_specs=[pl.BlockSpec(memory_space=pl.ANY)] * len(shapes),
+        out_shape=[like(*shape) for shape in shapes],
+        scratch_shapes=[pltpu.SemaphoreType.DMA((len(given),))],
         compiler_params=pltpu.CompilerParams(vmem_limit_bytes=VMEM),
         name="prepare",
-    )(place, audio_q, audio_k, audio_v, video_q, video_k, video_v, d_video, d_audio)
+    )(*given)
 
 
 def forward_kernel(video_rows, *refs):
@@ -353,20 +348,19 @@
     sizes = lax.axis_size("vid"), lax.axis_size("aud")
     video_rows, audio_rows = video_q.shape[1], d_audio_out.shape[1]
     holds = audio_len[0] > 0
-    place = jnp.stack([vid % 2, vid // 2]).astype(jnp.int32)
-    send_q, send_kv, video_kv, queries = prepare(
-        place, audio_q, audio_k, audio_v, video_q, video_k, video_v, d_video_out, d_audio_out
+    send_audio, video_kv, queries = prepare(
+        audio_q, audio_k, audio_v, video_q, video_k, video_v, d_video_out, d_audio_out
     )
 
     def video_chunks(video_kv, queries):
         return tuple(gathered(video_kv, along_z)[1:]), all_along_x(queries)
 
-    aud_q, aud_kv = own_audio(send_q, *sizes), own_audio(send_kv, *sizes)
+    audio = own_audio(send_audio, *sizes)
     video_keys, queries = fenced(holds, video_chunks, video_kv, queries)
-    aud_q, aud_kv, queries = lax.optimization_barrier((aud_q, aud_kv, queries))
+    audio, queries = lax.optimization_barrier((audio, queries))
     video_keys = [video_kv, *video_keys]
-    audio_queries = gathered(aud_q, along_x)
-    audio_keys = gathered(aud_kv, along_z)
+    audio_queries = gathered(audio[0], along_x)
+    audio_keys = gathered(audio[1:], along_z)
     gates = jnp.stack([video_gate, audio_gate])
     column, row = vid // SIDE, vid % SIDE
     limits = [audio_len[0] - (column * SIDE + (row - p) % SIDE) * audio_rows for p in range(SIDE)]
@@ -383,10 +377,11 @@
         *results, gate = finish_queries(parts, video_rows, audio_rows)
         for distance in (1, 2):
             gate = gate + beside_z(gate, distance)
-        return (*results, gate + lax.ppermute(gate, "pair", [(0, 1), (1, 0)]))
+        return (*results, gate)
 
     video_out, audio_out, grad_video_q, grad_audio_q, gate = fenced(holds, query_results, query_parts)
     key_parts = returned(key_parts, along_z)
+    gate = gate + lax.ppermute(gate, "pair", [(0, 1), (1, 0)])
     grad_video_k, grad_video_v, grad_audio_k, grad_audio_v = finish_keys(key_parts, video_rows, audio_rows)
     return (
         video_out,

time: 111 us -> 112 us (level)
  Pallas kernels: 17.7 us -> 20.9 us
  other arithmetic: 2.59 us -> 0.6 us
    pallas_call x1, Pallas kernels: 2.44 us -> 5.66 us  [prepare(): pl.pallas_call(prepare_kernel, in_specs=[pl.BlockSpec(memory_space=pl.ANY...]
    ppermute x2, waiting for transfers between devices: 8.68 us -> 6.77 us  [beside_z(): return lax.ppermute(array, 'vid', pairs)]
    all_gather x1, blocking collectives: 17.9 us -> 16.1 us  [all_along_x(): return lax.all_gather(array, 'vid', axis=0, axis_index_groups=ALONG_X)]
    ppermute x2 -> x1, starting transfers between devices: 2.99 us -> 1.57 us  [own_audio(): return lax.ppermute(array, ('vid', 'aud'), pairs)]
    all_to_all x1, blocking collectives: 14.8 us -> 16.2 us  [query_results(): lax.all_to_all(parts, 'vid', 0, 0, axis_index_groups=ALONG_X, tiled=True)]
  transfers between devices with their start and end apart: 20 -> 19, of which waited for: 7 -> 7; matrix products, arithmetic and copies ran while one was open for 3% -> 2% of each run, Pallas kernels for 1% -> 1%
where the time goes in v6:
time: 112 us; the launch traced here: 111 us
  starting transfers between devices  38.1 us (34%)
  blocking collectives  32.3 us (29%)
  Pallas kernels  20.9 us (19%)
  waiting for transfers between devices  14.8 us (13%)
  local copies, waits for them, and re-layouts  3.28 us (3%)
  between operations  1.48 us (1%)
    ppermute x9, starting transfers between devices, along_z(): return lax.ppermute(array, 'vid', pairs)  20.6 us
    all_to_all x1, blocking collectives, query_results(): lax.all_to_all(parts, 'vid', 0, 0, axis_index_groups=ALONG_X, tiled=True)  16.2 us
    all_gather x1, blocking collectives, all_along_x(): return lax.all_gather(array, 'vid', axis=0, axis_index_groups=ALONG_X)  16.1 us
    ppermute x6, starting transfers between devices, along_x(): return lax.ppermute(array, 'vid', pairs)  9.01 us
    pallas_call x1, Pallas kernels, attention_backward(): pl.pallas_call(functools.partial(backward_kernel, video_rows), grid=(head...  7.05 us
    ppermute x2, waiting for transfers between devices, beside_z(): return lax.ppermute(array, 'vid', pairs)  6.77 us
    pallas_call x1, Pallas kernels, attention_forward(): pl.pallas_call(functools.partial(forward_kernel, video_rows), grid=(heads...  6.62 us
    ppermute x1, starting transfers between devices, shards(): gate = gate + lax.ppermute(gate, 'pair', [(0, 1), (1, 0)])  6.52 us
  transfers between devices with their start and end apart: 19, of which 7 were waited for; matrix products, arithmetic and copies ran while one was open for 2% of the time, Pallas kernels for 1%

profile of v6, /device:TPU:1, one launch (start us, length us, event | category | flops | bytes accessed | tf_op | source)
XLA Modules:
  0.0 111.4 jit_solution(6064318280852261608)
XLA Ops:
  0.6 5.7 %prepare.1 = (bf16[3,64,384]{2,1,0:T(8,128)(2,1)}, bf16[2,128,384]{2,1,0:T(8,128)(2,1)S(1)}, bf16[320,384]{1,0:T(8,128)(2,1)S(1)}) custom-call(bf16[1,128,3072]{2,1,0:T(8,128)(2,1)} %aq_ref.1, bf16[1,128,3072]{2,1,0:T(8,128)(2,1)} %ak_ref.1, bf16[1,128,3072]{2,1,0:T(8,128)(2,1)} %av_ref.1, bf16[1,128,384]{2,1,0:T(8,128)(2,1)} %vq_ref.1, ...), custom_call_target="tpu_custom_call" | custom-call | tf_op jit(solution)/shard_map/prepare/pallas_call | solution.py:108
  6.3 1.6 %collective-permute-start.5 = (bf16[3,64,384]{2,1,0:T(8,128)(2,1)}, bf16[3,64,384]{2,1,0:T(8,128)(2,1)S(1)}, u32[]{:S(2)}, u32[]{:S(2)}) collective-permute-start(bf16[3,64,384]{2,1,0:T(8,128)(2,1)} %get-tuple-element.50), channel_id=1, source_target_pairs={{0,0},{2,32},{4,64},{6,96},{8,128},{10,160},{12,192},{14,224},{16,... | collective-permute-start | bytes 442376 | tf_op jit(solution)/shard_map/ppermute | solution.py:334
  8.6 26.0 %conditional.2 = (bf16[2,128,384]{2,1,0:T(8,128)(2,1)}, bf16[2,128,384]{2,1,0:T(8,128)(2,1)}, bf16[2,128,384]{2,1,0:T(8,128)(2,1)}, bf16[4,320,384]{2,1,0:T(8,128)(2,1)S(1)}) conditional(s32[]{:T(128)} %convert_element_type.4, () %tuple.26, (bf16[2,128,384]{2,1,0:T(8,128)(2,1)S(1)}, bf16[320,384]{1,0:T(8,128)(2,1)S(1)}) %tuple.27), branch_computations={%region_0.0_spmd, %region_1.0_spmd} | conditional | bytes 3588248 | solution.py:339
  8.6 8.9 %collective-permute-start.2 = (bf16[2,128,384]{2,1,0:T(8,128)(2,1)S(1)}, bf16[2,128,384]{2,1,0:T(8,128)(2,1)}, u32[]{:S(2)}, u32[]{:S(2)}) collective-permute-start(bf16[2,128,384]{2,1,0:T(8,128)(2,1)S(1)} %get-tuple-element.5), channel_id=1, source_target_pairs={{0,48},{16,0},{32,16},{48,32},{64,112},{80,64},{96,80},{112,96},{1... | collective-permute-start | bytes 589832 | tf_op jit(solution)/shard_map/cond/branch_1_fun/ppermute | solution.py:29
  17.5 1.0 collective-permute-start
  18.5 16.1 %all-gather = bf16[1280,384]{1,0:T(8,128)(2,1)S(1)} all-gather(bf16[320,384]{1,0:T(8,128)(2,1)S(1)} %get-tuple-element.6), channel_id=2, replica_groups={{0,64,128,192},{16,80,144,208},{32,96,160,224},{48,112,176,240},{1,65,1..., dimensions={0}, use_global_device_ids=true | all-gather | bytes 1228800 | tf_op jit(solution)/shard_map/cond/branch_1_fun/all_gather | solution.py:38
  34.6 4.4 %collective-permute-start.8 = (bf16[64,384]{1,0:T(8,128)(2,1)S(1)}, bf16[64,384]{1,0:T(8,128)(2,1)S(1)}, u32[]{:S(2)}, u32[]{:S(2)}) collective-permute-start(bf16[64,384]{1,0:T(8,128)(2,1)S(1)} %slice_bitcast_fusion.refs_1_), channel_id=1, source_target_pairs={{0,192},{16,208},{32,224},{48,240},{64,0},{80,16},{96,32},{112,48}... | collective-permute-start | bytes 147464 | tf_op jit(solution)/shard_map/ppermute | solution.py:24
  40.9 3.2 %collective-permute-start.10 = (bf16[2,64,384]{2,1,0:T(8,128)(2,1)S(1)}, bf16[2,64,384]{2,1,0:T(8,128)(2,1)S(1)}, u32[]{:S(2)}, u32[]{:S(2)}) collective-permute-start(bf16[2,64,384]{2,1,0:T(8,128)(2,1)S(1)} %slice.13.refs_9_.refs_6_), channel_id=1, source_target_pairs={{0,32},{16,48},{32,0},{48,16},{64,96},{80,112},{96,64},{112,80},{1... | collective-permute-start | bytes 294920 | tf_op jit(solution)/shard_map/ppermute | solution.py:29
  44.1 1.5 %collective-permute-start.9 = (bf16[2,64,384]{2,1,0:T(8,128)(2,1)S(1)}, bf16[2,64,384]{2,1,0:T(8,128)(2,1)S(1)}, u32[]{:S(2)}, u32[]{:S(2)}) collective-permute-start(bf16[2,64,384]{2,1,0:T(8,128)(2,1)S(1)} %slice.13.refs_9_.refs_6_), channel_id=1, source_target_pairs={{0,16},{16,32},{32,48},{48,0},{64,80},{80,96},{96,112},{112,64},{1... | collective-permute-start | bytes 294920 | tf_op jit(solution)/shard_map/ppermute | solution.py:29
  46.8 1.9 %collective-permute-done.10.refs_11_.refs_8_ = bf16[2,64,384]{2,1,0:T(8,128)(2,1)S(1)} collective-permute-done((bf16[2,64,384]{2,1,0:T(8,128)(2,1)S(1)}, bf16[2,64,384]{2,1,0:T(8,128)(2,1)S(1)}, u32[]{:S(2)}, u32[]{:S(2)}) %collective-permute-start.10) | collective-permute-done | bytes 98336 | tf_op jit(solution)/shard_map/ppermute | solution.py:29
  48.7 1.9 %collective-permute-done.9.refs_10_.refs_7_ = bf16[2,64,384]{2,1,0:T(8,128)(2,1)S(1)} collective-permute-done((bf16[2,64,384]{2,1,0:T(8,128)(2,1)S(1)}, bf16[2,64,384]{2,1,0:T(8,128)(2,1)S(1)}, u32[]{:S(2)}, u32[]{:S(2)}) %collective-permute-start.9) | collective-permute-done | bytes 98336 | tf_op jit(solution)/shard_map/ppermute | solution.py:29
  51.2 6.6 %forward.1 = (bf16[3,512,768]{2,1,0:T(8,128)(2,1)}, bf16[3,256,768]{2,1,0:T(8,128)(2,1)}, f32[3,2,128,768]{3,2,1,0:T(8,128)}, f32[3,4,768]{2,1,0:T(4,128)}, bf16[4,64,384]{2,1,0:T(8,128)(2,1)}) custom-call(bf16[4,320,384]{2,1,0:T(8,128)(2,1)S(1)} %get-tuple-element.54.refs_0_, bf16[64,384]{1,0:T(8,128)(2,1)} %copy-done.5, bf16[64,384]{1,0:T(8,128)(2,1)} %copy-done.14, ...), custom_call_target="tpu_custom_call" | custom-call | flops 905969664 | bytes 7077888 | tf_op jit(solution)/shard_map/forward/pallas_call | solution.py:247
  57.8 2.2 %collective-permute-start.14 = (f32[3,4,768]{2,1,0:T(4,128)}, f32[3,4,768]{2,1,0:T(4,128)S(1)}, u32[]{:S(2)}, u32[]{:S(2)}) collective-permute-start(f32[3,4,768]{2,1,0:T(4,128)} %get-tuple-element.60.refs_10_), channel_id=1, source_target_pairs={{0,192},{16,208},{32,224},{48,240},{64,0},{80,16},{96,32},{112,48}... | collective-permute-start | bytes 110600 | tf_op jit(solution)/shard_map/ppermute | solution.py:24
  60.0 1.0 collective-permute-start.13
  61.9 2.7 %collective-permute-done.13.refs_12_ = f32[3,4,768]{2,1,0:T(4,128)S(1)} collective-permute-done((f32[3,4,768]{2,1,0:T(4,128)}, f32[3,4,768]{2,1,0:T(4,128)S(1)}, u32[]{:S(2)}, u32[]{:S(2)}) %collective-permute-start.13) | collective-permute-done | bytes 36896 | tf_op jit(solution)/shard_map/ppermute | solution.py:24
  65.9 7.1 %backward.1 = (bf16[2,192,384]{2,1,0:T(8,128)(2,1)}, bf16[2,192,384]{2,1,0:T(8,128)(2,1)}, bf16[2,192,384]{2,1,0:T(8,128)(2,1)}, bf16[2,192,384]{2,1,0:T(8,128)(2,1)}, bf16[4,400,384]{2,1,0:T(8,128)(2,1)S(1)}) custom-call(bf16[4,320,384]{2,1,0:T(8,128)(2,1)S(1)} %get-tuple-element.54.refs_0_, bf16[4,64,384]{2,1,0:T(8,128)(2,1)} %get-tuple-element.59.refs_1_, ...), custom_call_target="tpu_custom_call" | custom-call | flops 1811939328 | bytes 7077888 | tf_op jit(solution)/shard_map/backward/pallas_call | solution.py:265
  72.9 3.0 %collective-permute-start.15 = (bf16[2,192,384]{2,1,0:T(8,128)(2,1)}, bf16[2,192,384]{2,1,0:T(8,128)(2,1)S(1)}, u32[]{:S(2)}, u32[]{:S(2)}) collective-permute-start(bf16[2,192,384]{2,1,0:T(8,128)(2,1)} %get-tuple-element.69), channel_id=1, source_target_pairs={{0,48},{16,0},{32,16},{48,32},{64,112},{80,64},{96,80},{112,96},{1... | collective-permute-start | bytes 884744 | tf_op jit(solution)/shard_map/ppermute | solution.py:29
  75.9 1.3 %collective-permute-start.16 = (bf16[2,192,384]{2,1,0:T(8,128)(2,1)}, bf16[2,192,384]{2,1,0:T(8,128)(2,1)S(1)}, u32[]{:S(2)}, u32[]{:S(2)}) collective-permute-start(bf16[2,192,384]{2,1,0:T(8,128)(2,1)} %get-tuple-element.70), channel_id=1, source_target_pairs={{0,32},{16,48},{32,0},{48,16},{64,96},{80,112},{96,64},{112,80},{1... | collective-permute-start | bytes 884744 | tf_op jit(solution)/shard_map/ppermute | solution.py:29
  77.2 1.4 %collective-permute-start.17 = (bf16[2,192,384]{2,1,0:T(8,128)(2,1)}, bf16[2,192,384]{2,1,0:T(8,128)(2,1)S(1)}, u32[]{:S(2)}, u32[]{:S(2)}) collective-permute-start(bf16[2,192,384]{2,1,0:T(8,128)(2,1)} %get-tuple-element.71), channel_id=1, source_target_pairs={{0,16},{16,32},{32,48},{48,0},{64,80},{80,96},{96,112},{112,64},{1... | collective-permute-start | bytes 884744 | tf_op jit(solution)/shard_map/ppermute | solution.py:29
  78.5 24.1 %conditional.3 = (bf16[1,128,384]{2,1,0:T(8,128)(2,1)}, bf16[1,64,384]{2,1,0:T(8,128)(2,1)}, bf16[1,128,384]{2,1,0:T(8,128)(2,1)}, bf16[1,64,384]{2,1,0:T(8,128)(2,1)}, f32[8,384]{1,0:T(8,128)S(1)}) conditional(s32[]{:T(128)} %convert_element_type.4, () %tuple.25, bf16[4,400,384]{2,1,0:T(8,128)(2,1)S(1)} %get-tuple-element.64), branch_computations={%region_2.3_spmd, %region_3.4_spmd} | conditional | flops 6144 | bytes 2629752 | solution.py:339
  78.5 16.2 %all_to_all.4.parts_ref = bf16[4,400,384]{2,1,0:T(8,128)(2,1)S(1)} all-to-all(bf16[4,400,384]{2,1,0:T(8,128)(2,1)S(1)} %param.3), channel_id=1, replica_groups={{0,64,128,192},{16,80,144,208},{32,96,160,224},{48,112,176,240},{1,65,1..., dimensions={0} | all-to-all | bytes 2457600 | tf_op jit(solution)/shard_map/cond/branch_1_fun/all_to_all | solution.py:376
  95.5 3.2 %collective-permute-done.3 = f32[8,384]{1,0:T(8,128)S(1)} collective-permute-done((f32[8,384]{1,0:T(8,128)S(1)}, f32[8,384]{1,0:T(8,128)S(1)}, u32[]{:S(2)}, u32[]{:S(2)}) %collective-permute-start.3) | collective-permute-done | bytes 12320 | tf_op jit(solution)/shard_map/cond/branch_1_fun/ppermute | solution.py:34
  99.1 3.5 %collective-permute-done.4 = f32[8,384]{1,0:T(8,128)S(1)} collective-permute-done((f32[8,384]{1,0:T(8,128)S(1)}, f32[8,384]{1,0:T(8,128)S(1)}, u32[]{:S(2)}, u32[]{:S(2)}) %collective-permute-start.4) | collective-permute-done | bytes 12320 | tf_op jit(solution)/shard_map/cond/branch_1_fun/ppermute | solution.py:34
  102.7 6.5 %collective-permute-start.18 = (f32[8,384]{1,0:T(8,128)S(1)}, f32[8,384]{1,0:T(8,128)S(1)}, u32[]{:S(2)}, u32[]{:S(2)}) collective-permute-start(f32[8,384]{1,0:T(8,128)S(1)} %get-tuple-element.77), channel_id=1, source_target_pairs={{0,1},{1,0},{2,3},{3,2},{4,5},{5,4},{6,7},{7,6},{8,9},{9,8},{10,11... | collective-permute-start | bytes 36872 | tf_op jit(solution)/shard_map/ppermute | solution.py:384
  (64 shorter events, 9.3 us)
Async XLA Ops:
  6.3 28.3 %collective-permute-start.5 = (bf16[3,64,384]{2,1,0:T(8,128)(2,1)}, bf16[3,64,384]{2,1,0:T(8,128)(2,1)S(1)}, u32[]{:S(2)}, u32[]{:S(2)}) collective-permute-start(bf16[3,64,384]{2,1,0:T(8,128)(2,1)} %get-tuple-element.50), channel_id=1, source_target_pairs={{0,0},{2,32},{4,64},{6,96},{8,128},{10,160},{12,192},{14,224},{16,... | collective-permute-start | bytes 442376 | tf_op jit(solution)/shard_map/ppermute | solution.py:334
  8.5 30.5 %copy-start.10 = (f32[384]{0:T(512)S(1)}, f32[384]{0:T(512)}, u32[]{:S(2)}) copy-start(f32[384]{0:T(512)} %param.21) | copy-start | bytes 4612
  8.6 30.5 %copy-start.11 = (f32[384]{0:T(512)S(1)}, f32[384]{0:T(512)}, u32[]{:S(2)}) copy-start(f32[384]{0:T(512)} %param.22) | copy-start | bytes 4612
  8.6 26.0 %collective-permute-start.2 = (bf16[2,128,384]{2,1,0:T(8,128)(2,1)S(1)}, bf16[2,128,384]{2,1,0:T(8,128)(2,1)}, u32[]{:S(2)}, u32[]{:S(2)}) collective-permute-start(bf16[2,128,384]{2,1,0:T(8,128)(2,1)S(1)} %get-tuple-element.5), channel_id=1, source_target_pairs={{0,48},{16,0},{32,16},{48,32},{64,112},{80,64},{96,80},{112,96},{1... | collective-permute-start | bytes 589832 | tf_op jit(solution)/shard_map/cond/branch_1_fun/ppermute | solution.py:29
  17.5 17.1 %collective-permute-start.1 = (bf16[2,128,384]{2,1,0:T(8,128)(2,1)S(1)}, bf16[2,128,384]{2,1,0:T(8,128)(2,1)}, u32[]{:S(2)}, u32[]{:S(2)}) collective-permute-start(bf16[2,128,384]{2,1,0:T(8,128)(2,1)S(1)} %get-tuple-element.5), channel_id=1, source_target_pairs={{0,32},{16,48},{32,0},{48,16},{64,96},{80,112},{96,64},{112,80},{1... | collective-permute-start | bytes 589832 | tf_op jit(solution)/shard_map/cond/branch_1_fun/ppermute | solution.py:29
  17.5 17.1 %collective-permute-start = (bf16[2,128,384]{2,1,0:T(8,128)(2,1)S(1)}, bf16[2,128,384]{2,1,0:T(8,128)(2,1)}, u32[]{:S(2)}, u32[]{:S(2)}) collective-permute-start(bf16[2,128,384]{2,1,0:T(8,128)(2,1)S(1)} %get-tuple-element.5), channel_id=1, source_target_pairs={{0,16},{16,32},{32,48},{48,0},{64,80},{80,96},{96,112},{112,64},{1... | collective-permute-start | bytes 589832 | tf_op jit(solution)/shard_map/cond/branch_1_fun/ppermute | solution.py:29
  34.6 16.0 %copy-start.5 = (bf16[64,384]{1,0:T(8,128)(2,1)}, bf16[64,384]{1,0:T(8,128)(2,1)S(1)}, u32[]{:S(2)}) copy-start(bf16[64,384]{1,0:T(8,128)(2,1)S(1)} %slice_bitcast_fusion.refs_1_) | copy-start | bytes 147460
  34.6 9.5 %collective-permute-start.8 = (bf16[64,384]{1,0:T(8,128)(2,1)S(1)}, bf16[64,384]{1,0:T(8,128)(2,1)S(1)}, u32[]{:S(2)}, u32[]{:S(2)}) collective-permute-start(bf16[64,384]{1,0:T(8,128)(2,1)S(1)} %slice_bitcast_fusion.refs_1_), channel_id=1, source_target_pairs={{0,192},{16,208},{32,224},{48,240},{64,0},{80,16},{96,32},{112,48}... | collective-permute-start | bytes 147464 | tf_op jit(solution)/shard_map/ppermute | solution.py:24
  39.1 11.5 %copy-start.1 = (bf16[2,64,384]{2,1,0:T(8,128)(2,1)}, bf16[2,64,384]{2,1,0:T(8,128)(2,1)S(1)}, u32[]{:S(2)}) copy-start(bf16[2,64,384]{2,1,0:T(8,128)(2,1)S(1)} %slice.13.refs_9_.refs_6_) | copy-start | bytes 294916
  39.1 7.7 %collective-permute-start.7 = (bf16[64,384]{1,0:T(8,128)(2,1)S(1)}, bf16[64,384]{1,0:T(8,128)(2,1)S(1)}, u32[]{:S(2)}, u32[]{:S(2)}) collective-permute-start(bf16[64,384]{1,0:T(8,128)(2,1)S(1)} %slice_bitcast_fusion.refs_1_), channel_id=1, source_target_pairs={{0,128},{16,144},{32,160},{48,176},{64,192},{80,208},{96,224},{112... | collective-permute-start | bytes 147464 | tf_op jit(solution)/shard_map/ppermute | solution.py:24
  39.7 7.1 %collective-permute-start.6 = (bf16[64,384]{1,0:T(8,128)(2,1)S(1)}, bf16[64,384]{1,0:T(8,128)(2,1)S(1)}, u32[]{:S(2)}, u32[]{:S(2)}) collective-permute-start(bf16[64,384]{1,0:T(8,128)(2,1)S(1)} %slice_bitcast_fusion.refs_1_), channel_id=1, source_target_pairs={{0,64},{16,80},{32,96},{48,112},{64,128},{80,144},{96,160},{112,17... | collective-permute-start | bytes 147464 | tf_op jit(solution)/shard_map/ppermute | solution.py:24
  40.5 6.3 %collective-permute-start.11 = (bf16[2,64,384]{2,1,0:T(8,128)(2,1)S(1)}, bf16[2,64,384]{2,1,0:T(8,128)(2,1)S(1)}, u32[]{:S(2)}, u32[]{:S(2)}) collective-permute-start(bf16[2,64,384]{2,1,0:T(8,128)(2,1)S(1)} %slice.13.refs_9_.refs_6_), channel_id=1, source_target_pairs={{0,48},{16,0},{32,16},{48,32},{64,112},{80,64},{96,80},{112,96},{1... | collective-permute-start | bytes 294920 | tf_op jit(solution)/shard_map/ppermute | solution.py:29
  40.9 7.7 %collective-permute-start.10 = (bf16[2,64,384]{2,1,0:T(8,128)(2,1)S(1)}, bf16[2,64,384]{2,1,0:T(8,128)(2,1)S(1)}, u32[]{:S(2)}, u32[]{:S(2)}) collective-permute-start(bf16[2,64,384]{2,1,0:T(8,128)(2,1)S(1)} %slice.13.refs_9_.refs_6_), channel_id=1, source_target_pairs={{0,32},{16,48},{32,0},{48,16},{64,96},{80,112},{96,64},{112,80},{1... | collective-permute-start | bytes 294920 | tf_op jit(solution)/shard_map/ppermute | solution.py:29
  44.1 6.5 %collective-permute-start.9 = (bf16[2,64,384]{2,1,0:T(8,128)(2,1)S(1)}, bf16[2,64,384]{2,1,0:T(8,128)(2,1)S(1)}, u32[]{:S(2)}, u32[]{:S(2)}) collective-permute-start(bf16[2,64,384]{2,1,0:T(8,128)(2,1)S(1)} %slice.13.refs_9_.refs_6_), channel_id=1, source_target_pairs={{0,16},{16,32},{32,48},{48,0},{64,80},{80,96},{96,112},{112,64},{1... | collective-permute-start | bytes 294920 | tf_op jit(solution)/shard_map/ppermute | solution.py:29
  57.8 4.0 %collective-permute-start.14 = (f32[3,4,768]{2,1,0:T(4,128)}, f32[3,4,768]{2,1,0:T(4,128)S(1)}, u32[]{:S(2)}, u32[]{:S(2)}) collective-permute-start(f32[3,4,768]{2,1,0:T(4,128)} %get-tuple-element.60.refs_10_), channel_id=1, source_target_pairs={{0,192},{16,208},{32,224},{48,240},{64,0},{80,16},{96,32},{112,48}... | collective-permute-start | bytes 110600 | tf_op jit(solution)/shard_map/ppermute | solution.py:24
  60.0 4.5 %collective-permute-start.13 = (f32[3,4,768]{2,1,0:T(4,128)}, f32[3,4,768]{2,1,0:T(4,128)S(1)}, u32[]{:S(2)}, u32[]{:S(2)}) collective-permute-start(f32[3,4,768]{2,1,0:T(4,128)} %get-tuple-element.60.refs_10_), channel_id=1, source_target_pairs={{0,128},{16,144},{32,160},{48,176},{64,192},{80,208},{96,224},{112... | collective-permute-start | bytes 110600 | tf_op jit(solution)/shard_map/ppermute | solution.py:24
  61.0 4.2 %collective-permute-start.12 = (f32[3,4,768]{2,1,0:T(4,128)}, f32[3,4,768]{2,1,0:T(4,128)S(1)}, u32[]{:S(2)}, u32[]{:S(2)}) collective-permute-start(f32[3,4,768]{2,1,0:T(4,128)} %get-tuple-element.60.refs_10_), channel_id=1, source_target_pairs={{0,64},{16,80},{32,96},{48,112},{64,128},{80,144},{96,160},{112,17... | collective-permute-start | bytes 110600 | tf_op jit(solution)/shard_map/ppermute | solution.py:24
  72.9 37.7 %collective-permute-start.15 = (bf16[2,192,384]{2,1,0:T(8,128)(2,1)}, bf16[2,192,384]{2,1,0:T(8,128)(2,1)S(1)}, u32[]{:S(2)}, u32[]{:S(2)}) collective-permute-start(bf16[2,192,384]{2,1,0:T(8,128)(2,1)} %get-tuple-element.69), channel_id=1, source_target_pairs={{0,48},{16,0},{32,16},{48,32},{64,112},{80,64},{96,80},{112,96},{1... | collective-permute-start | bytes 884744 | tf_op jit(solution)/shard_map/ppermute | solution.py:29
  75.9 34.8 %collective-permute-start.16 = (bf16[2,192,384]{2,1,0:T(8,128)(2,1)}, bf16[2,192,384]{2,1,0:T(8,128)(2,1)S(1)}, u32[]{:S(2)}, u32[]{:S(2)}) collective-permute-start(bf16[2,192,384]{2,1,0:T(8,128)(2,1)} %get-tuple-element.70), channel_id=1, source_target_pairs={{0,32},{16,48},{32,0},{48,16},{64,96},{80,112},{96,64},{112,80},{1... | collective-permute-start | bytes 884744 | tf_op jit(solution)/shard_map/ppermute | solution.py:29
  77.2 33.5 %collective-permute-start.17 = (bf16[2,192,384]{2,1,0:T(8,128)(2,1)}, bf16[2,192,384]{2,1,0:T(8,128)(2,1)S(1)}, u32[]{:S(2)}, u32[]{:S(2)}) collective-permute-start(bf16[2,192,384]{2,1,0:T(8,128)(2,1)} %get-tuple-element.71), channel_id=1, source_target_pairs={{0,16},{16,32},{32,48},{48,0},{64,80},{80,96},{96,112},{112,64},{1... | collective-permute-start | bytes 884744 | tf_op jit(solution)/shard_map/ppermute | solution.py:29
  78.5 32.1 %copy-start = (bf16[2,192,384]{2,1,0:T(8,128)(2,1)S(1)}, bf16[2,192,384]{2,1,0:T(8,128)(2,1)}, u32[]{:S(2)}) copy-start(bf16[2,192,384]{2,1,0:T(8,128)(2,1)} %get-tuple-element.68.refs_0_) | copy-start | bytes 884740
  95.5 3.2 %collective-permute-start.3 = (f32[8,384]{1,0:T(8,128)S(1)}, f32[8,384]{1,0:T(8,128)S(1)}, u32[]{:S(2)}, u32[]{:S(2)}) collective-permute-start(f32[8,384]{1,0:T(8,128)S(1)} %get-tuple-element.11), channel_id=1, source_target_pairs={{0,16},{16,0},{32,48},{48,32},{64,80},{80,64},{96,112},{112,96},{1... | collective-permute-start | bytes 36872 | tf_op jit(solution)/shard_map/cond/branch_1_fun/ppermute | solution.py:34
  98.7 3.9 %collective-permute-start.4 = (f32[8,384]{1,0:T(8,128)S(1)}, f32[8,384]{1,0:T(8,128)S(1)}, u32[]{:S(2)}, u32[]{:S(2)}) collective-permute-start(f32[8,384]{1,0:T(8,128)S(1)} %add.29), channel_id=1, source_target_pairs={{0,32},{16,48},{32,0},{48,16},{64,96},{80,112},{96,64},{112,80},{1... | collective-permute-start | bytes 36872 | tf_op jit(solution)/shard_map/cond/branch_1_fun/ppermute | solution.py:34
  102.7 7.4 %collective-permute-start.18 = (f32[8,384]{1,0:T(8,128)S(1)}, f32[8,384]{1,0:T(8,128)S(1)}, u32[]{:S(2)}, u32[]{:S(2)}) collective-permute-start(f32[8,384]{1,0:T(8,128)S(1)} %get-tuple-element.77), channel_id=1, source_target_pairs={{0,1},{1,0},{2,3},{3,2},{4,5},{5,4},{6,7},{7,6},{8,9},{9,8},{10,11... | collective-permute-start | bytes 36872 | tf_op jit(solution)/shard_map/ppermute | solution.py:384
  (10 other events, 35.2 us)

commit v7 on v6

--- a/solution.py
+++ b/solution.py
@@ -108,7 +108,7 @@
     return pl.pallas_call(
         prepare_kernel,
         in_specs=[pl.BlockSpec(memory_space=pl.ANY)] * len(given),
-        out_specs=[pl.BlockSpec(memory_space=pl.ANY)] * len(shapes),
+        out_specs=[pl.BlockSpec(memory_space=pltpu.VMEM)] * len(shapes),
         out_shape=[like(*shape) for shape in shapes],
         scratch_shapes=[pltpu.SemaphoreType.DMA((len(given),))],
         compiler_params=pltpu.CompilerParams(vmem_limit_bytes=VMEM),
@@ -117,7 +117,7 @@
 
 
 def forward_kernel(video_rows, *refs):
-    gathered_ref, audio_q, k_refs, numbers_ref, gates_ref = refs[0], refs[1:5], (refs[5:9], refs[9:13]), refs[13], refs[14]
+    gathered_ref, k_refs, audio_q, numbers_ref, gates_ref = refs[0], (refs[1:5], refs[5:9]), refs[9:13], refs[13], refs[14]
     e_refs, o_ref, stats_ref, ordered_ref = refs[15:17], refs[17], refs[18], refs[19]
     for place in range(SIDE):
         ordered_ref[lax.rem(numbers_ref[SIDE] + SIDE - place, SIDE)] = audio_q[place][...]
@@ -167,10 +167,14 @@
     return nn(joined(k_refs, 0).T, grad_scores), factor
 
 
+def column_of(row):
+    return jnp.broadcast_to(row, (HEAD_DIM, HEAD_DIM)).T[:, 0:1]
+
+
 def backward_kernel(video_rows, *refs):
     gathered_ref, audio_q, k_video, k_audio, stats_refs = refs[0], refs[1], refs[2:6], refs[6:10], refs[10:14]
-    gates_ref, columns_ref, e_video, e_audio, o_ref = refs[14:19]
-    k_outs, q_out = refs[19:23], refs[23]
+    gates_ref, e_video, e_audio, o_ref = refs[14:18]
+    k_outs, q_out = refs[18:22], refs[22]
     audio_rows = audio_q.shape[1]
     rows = video_rows + audio_rows
     video = SIDE * video_rows
@@ -185,8 +189,8 @@
     cross_video, cross_audio = on_audio[:, :video], on_video[:, video:]
     merged = jnp.concatenate(
         [
-            on_video[:, :video] + columns_ref[:, 0:1] * cross_video,
-            on_audio[:, video:] + columns_ref[:, 1:2] * cross_audio,
+            on_video[:, :video] + column_of(gates_ref[0:1, :]) * cross_video,
+            on_audio[:, video:] + column_of(gates_ref[1:2, :]) * cross_audio,
         ],
         axis=1,
     )
@@ -243,7 +247,7 @@
         like(heads, 4, total, kind=F32),
     ]
     ordered = like(SIDE, audio_rows, width)
-    chunks = [queries, *audio_q, *video_keys, *audio_keys]
+    chunks = [queries, *video_keys, *audio_keys, *audio_q]
     return pl.pallas_call(
         functools.partial(forward_kernel, video_rows),
         grid=(heads,),
@@ -267,14 +271,14 @@
         grid=(heads,),
         in_specs=[chunk_spec(array) for array in chunks]
         + [head_spec(array) for array in stats]
-        + [chunk_spec(gates), pl.BlockSpec((HEAD_DIM, 2), lambda h: (h, 0))]
+        + [chunk_spec(gates)]
         + [head_spec(array) for array in by_head],
         out_specs=[chunk_spec(array) for array in outs],
         out_shape=outs,
         cost_estimate=cost(SIDE * rows, SIDE * rows, heads, 4),
         compiler_params=pltpu.CompilerParams(vmem_limit_bytes=VMEM),
         name="backward",
-    )(*chunks, *stats, gates, gates.T, *by_head)
+    )(*chunks, *stats, gates, *by_head)
     return key_parts, query_parts
 
 
@@ -352,15 +356,14 @@
         audio_q, audio_k, audio_v, video_q, video_k, video_v, d_video_out, d_audio_out
     )
 
-    def video_chunks(video_kv, queries):
-        return tuple(gathered(video_kv, along_z)[1:]), all_along_x(queries)
-
-    audio = own_audio(send_audio, *sizes)
-    video_keys, queries = fenced(holds, video_chunks, video_kv, queries)
-    audio, queries = lax.optimization_barrier((audio, queries))
+    def first_chunks(send_audio, video_kv, queries):
+        return own_audio(send_audio, *sizes), tuple(gathered(video_kv, along_z)[1:]), all_along_x(queries)
+
+    audio, video_keys, queries = fenced(holds, first_chunks, send_audio, video_kv, queries)
     video_keys = [video_kv, *video_keys]
+    audio = lax.optimization_barrier(audio)
+    audio_keys = gathered(audio[1:], along_z)
     audio_queries = gathered(audio[0], along_x)
-    audio_keys = gathered(audio[1:], along_z)
     gates = jnp.stack([video_gate, audio_gate])
     column, row = vid // SIDE, vid % SIDE
     limits = [audio_len[0] - (column * SIDE + (row - p) % SIDE) * audio_rows for p in range(SIDE)]

time: 112 us -> 108 us (0.964)
  starting transfers between devices: 38.1 us -> 30 us
  Pallas kernels: 20.9 us -> 16.3 us
  blocking collectives: 32.3 us -> 36.1 us
  waiting for transfers between devices: 14.8 us -> 18.4 us
    ppermute x9, starting transfers between devices: 20.6 us -> 15.5 us  [along_z(): return lax.ppermute(array, 'vid', pairs)]
    all_gather x1, blocking collectives: 16.1 us -> 20.8 us  [all_along_x(): return lax.all_gather(array, 'vid', axis=0, axis_index_groups=ALONG_X)]
    pallas_call x1, Pallas kernels: 5.66 us -> 1.21 us  [prepare(): pl.pallas_call(prepare_kernel, in_specs=[pl.BlockSpec(memory_space=pl.ANY...]
    ppermute x9, waiting for transfers between devices: 3.81 us -> 6.61 us  [along_z(): return lax.ppermute(array, 'vid', pairs)]
    ppermute x6, starting transfers between devices: 9.01 us -> 6.24 us  [along_x(): return lax.ppermute(array, 'vid', pairs)]
  transfers between devices with their start and end apart: 19 -> 19, of which waited for: 7 -> 6; matrix products, arithmetic and copies ran while one was open for 2% -> 3% of each run, Pallas kernels for 1% -> 1%
where the time goes in v7:
time: 108 us; the launch traced here: 107 us
  blocking collectives  36.1 us (33%)
  starting transfers between devices  30 us (28%)
  waiting for transfers between devices  18.4 us (17%)
  Pallas kernels  16.3 us (15%)
  local copies, waits for them, and re-layouts  4.26 us (4%)
  between operations  1.48 us (1%)
    all_gather x1, blocking collectives, all_along_x(): return lax.all_gather(array, 'vid', axis=0, axis_index_groups=ALONG_X)  20.8 us
    ppermute x9, starting transfers between devices, along_z(): return lax.ppermute(array, 'vid', pairs)  15.5 us
    all_to_all x1, blocking collectives, query_results(): lax.all_to_all(parts, 'vid', 0, 0, axis_index_groups=ALONG_X, tiled=True)  15.4 us
    ppermute x2, waiting for transfers between devices, beside_z(): return lax.ppermute(array, 'vid', pairs)  7.48 us
    pallas_call x1, Pallas kernels, attention_backward(): pl.pallas_call(functools.partial(backward_kernel, video_rows), grid=(head...  6.92 us
    ppermute x9, waiting for transfers between devices, along_z(): return lax.ppermute(array, 'vid', pairs)  6.61 us
    pallas_call x1, Pallas kernels, attention_forward(): pl.pallas_call(functools.partial(forward_kernel, video_rows), grid=(heads...  6.61 us
    ppermute x1, starting transfers between devices, shards(): gate = gate + lax.ppermute(gate, 'pair', [(0, 1), (1, 0)])  6.6 us
  transfers between devices with their start and end apart: 19, of which 6 were waited for; matrix products, arithmetic and copies ran while one was open for 3% of the time, Pallas kernels for 1%

profile of v7, /device:TPU:1, one launch (start us, length us, event | category | flops | bytes accessed | tf_op | source)
XLA Modules:
  0.0 107.2 jit_solution(6094979500710874755)
XLA Ops:
  1.3 1.2 %prepare.1 = (bf16[3,64,384]{2,1,0:T(8,128)(2,1)S(1)}, bf16[2,128,384]{2,1,0:T(8,128)(2,1)S(1)}, bf16[320,384]{1,0:T(8,128)(2,1)S(1)}) custom-call(bf16[1,128,3072]{2,1,0:T(8,128)(2,1)} %aq_ref.1, bf16[1,128,3072]{2,1,0:T(8,128)(2,1)} %ak_ref.1, bf16[1,128,3072]{2,1,0:T(8,128)(2,1)} %av_ref.1, bf16[1,128,384]{2,1,0:T(8,128)(2,1)} %vq_ref.1, ...), custom_call_target="tpu_custom_call" | custom-call | tf_op jit(solution)/shard_map/prepare/pallas_call | solution.py:108
  2.5 27.7 %conditional.2 = (bf16[3,64,384]{2,1,0:T(8,128)(2,1)}, bf16[2,128,384]{2,1,0:T(8,128)(2,1)}, bf16[2,128,384]{2,1,0:T(8,128)(2,1)}, bf16[2,128,384]{2,1,0:T(8,128)(2,1)}, bf16[4,320,384]{2,1,0:T(8,128)(2,1)S(1)}) conditional(s32[]{:T(128)} %convert_element_type.4, () %tuple.24, (bf16[3,64,384]{2,1,0:T(8,128)(2,1)S(1)}, ...), branch_computations={%region_0.0_spmd, %region_1.0_spmd} | conditional | bytes 4178120 | solution.py:343
  2.6 5.3 %collective-permute-start.3 = (bf16[2,128,384]{2,1,0:T(8,128)(2,1)S(1)}, bf16[2,128,384]{2,1,0:T(8,128)(2,1)}, u32[]{:S(2)}, u32[]{:S(2)}) collective-permute-start(bf16[2,128,384]{2,1,0:T(8,128)(2,1)S(1)} %get-tuple-element.8), channel_id=1, source_target_pairs={{0,48},{16,0},{32,16},{48,32},{64,112},{80,64},{96,80},{112,96},{1... | collective-permute-start | bytes 589832 | tf_op jit(solution)/shard_map/cond/branch_1_fun/ppermute | solution.py:29
  8.2 1.3 %collective-permute-start = (bf16[3,64,384]{2,1,0:T(8,128)(2,1)S(1)}, bf16[3,64,384]{2,1,0:T(8,128)(2,1)}, u32[]{:S(2)}, u32[]{:S(2)}) collective-permute-start(bf16[3,64,384]{2,1,0:T(8,128)(2,1)S(1)} %get-tuple-element.7), channel_id=1, source_target_pairs={{0,0},{2,32},{4,64},{6,96},{8,128},{10,160},{12,192},{14,224},{16,... | collective-permute-start | bytes 442376 | tf_op jit(solution)/shard_map/cond/branch_1_fun/ppermute | solution.py:338
  9.5 20.8 %all-gather = bf16[1280,384]{1,0:T(8,128)(2,1)S(1)} all-gather(bf16[320,384]{1,0:T(8,128)(2,1)S(1)} %get-tuple-element.9), channel_id=2, replica_groups={{0,64,128,192},{16,80,144,208},{32,96,160,224},{48,112,176,240},{1,65,1..., dimensions={0}, use_global_device_ids=true | all-gather | bytes 1228800 | tf_op jit(solution)/shard_map/cond/branch_1_fun/all_gather | solution.py:38
  30.3 0.8 slice_bitcast_fusion.refs_9_
  31.1 1.5 %collective-permute-start.11 = (bf16[64,384]{1,0:T(8,128)(2,1)S(1)}, bf16[64,384]{1,0:T(8,128)(2,1)S(1)}, u32[]{:S(2)}, u32[]{:S(2)}) collective-permute-start(bf16[64,384]{1,0:T(8,128)(2,1)S(1)} %slice_bitcast_fusion.refs_9_), channel_id=1, source_target_pairs={{0,192},{16,208},{32,224},{48,240},{64,0},{80,16},{96,32},{112,48}... | collective-permute-start | bytes 147464 | tf_op jit(solution)/shard_map/ppermute | solution.py:24
  33.4 0.9 slice.16.refs_5_.refs_6_
  34.3 5.8 %collective-permute-start.8 = (bf16[2,64,384]{2,1,0:T(8,128)(2,1)S(1)}, bf16[2,64,384]{2,1,0:T(8,128)(2,1)S(1)}, u32[]{:S(2)}, u32[]{:S(2)}) collective-permute-start(bf16[2,64,384]{2,1,0:T(8,128)(2,1)S(1)} %slice.16.refs_5_.refs_6_), channel_id=1, source_target_pairs={{0,48},{16,0},{32,16},{48,32},{64,112},{80,64},{96,80},{112,96},{1... | collective-permute-start | bytes 294920 | tf_op jit(solution)/shard_map/ppermute | solution.py:29
  40.3 1.4 %collective-permute-start.6 = (bf16[2,64,384]{2,1,0:T(8,128)(2,1)S(1)}, bf16[2,64,384]{2,1,0:T(8,128)(2,1)S(1)}, u32[]{:S(2)}, u32[]{:S(2)}) collective-permute-start(bf16[2,64,384]{2,1,0:T(8,128)(2,1)S(1)} %slice.16.refs_5_.refs_6_), channel_id=1, source_target_pairs={{0,16},{16,32},{32,48},{48,0},{64,80},{80,96},{96,112},{112,64},{1... | collective-permute-start | bytes 294920 | tf_op jit(solution)/shard_map/ppermute | solution.py:29
  43.1 6.6 %collective-permute-done.7.refs_7_.refs_8_ = bf16[2,64,384]{2,1,0:T(8,128)(2,1)S(1)} collective-permute-done((bf16[2,64,384]{2,1,0:T(8,128)(2,1)S(1)}, bf16[2,64,384]{2,1,0:T(8,128)(2,1)S(1)}, u32[]{:S(2)}, u32[]{:S(2)}) %collective-permute-start.7) | collective-permute-done | bytes 98336 | tf_op jit(solution)/shard_map/ppermute | solution.py:29
  50.3 6.6 %forward.1 = (bf16[3,512,768]{2,1,0:T(8,128)(2,1)}, bf16[3,256,768]{2,1,0:T(8,128)(2,1)}, f32[3,2,128,768]{3,2,1,0:T(8,128)}, f32[3,4,768]{2,1,0:T(4,128)}, bf16[4,64,384]{2,1,0:T(8,128)(2,1)}) custom-call(bf16[4,320,384]{2,1,0:T(8,128)(2,1)S(1)} %get-tuple-element.50.refs_0_, bf16[2,128,384]{2,1,0:T(8,128)(2,1)S(1)} %get-tuple-element.51.refs_1_.refs_2_, ...), custom_call_target="tpu_custom_call" | custom-call | flops 905969664 | bytes 7077888 | tf_op jit(solution)/shard_map/forward/pallas_call | solution.py:251
  56.9 2.1 %collective-permute-start.14 = (f32[3,4,768]{2,1,0:T(4,128)}, f32[3,4,768]{2,1,0:T(4,128)S(1)}, u32[]{:S(2)}, u32[]{:S(2)}) collective-permute-start(f32[3,4,768]{2,1,0:T(4,128)} %get-tuple-element.57.refs_10_), channel_id=1, source_target_pairs={{0,192},{16,208},{32,224},{48,240},{64,0},{80,16},{96,32},{112,48}... | collective-permute-start | bytes 110600 | tf_op jit(solution)/shard_map/ppermute | solution.py:24
  59.0 1.1 %collective-permute-start.13 = (f32[3,4,768]{2,1,0:T(4,128)}, f32[3,4,768]{2,1,0:T(4,128)S(1)}, u32[]{:S(2)}, u32[]{:S(2)}) collective-permute-start(f32[3,4,768]{2,1,0:T(4,128)} %get-tuple-element.57.refs_10_), channel_id=1, source_target_pairs={{0,128},{16,144},{32,160},{48,176},{64,192},{80,208},{96,224},{112... | collective-permute-start | bytes 110600 | tf_op jit(solution)/shard_map/ppermute | solution.py:24
  60.9 2.7 %collective-permute-done.13.refs_12_ = f32[3,4,768]{2,1,0:T(4,128)S(1)} collective-permute-done((f32[3,4,768]{2,1,0:T(4,128)}, f32[3,4,768]{2,1,0:T(4,128)S(1)}, u32[]{:S(2)}, u32[]{:S(2)}) %collective-permute-start.13) | collective-permute-done | bytes 36896 | tf_op jit(solution)/shard_map/ppermute | solution.py:24
  65.0 6.9 %backward.1 = (bf16[2,192,384]{2,1,0:T(8,128)(2,1)}, bf16[2,192,384]{2,1,0:T(8,128)(2,1)}, bf16[2,192,384]{2,1,0:T(8,128)(2,1)}, bf16[2,192,384]{2,1,0:T(8,128)(2,1)}, bf16[4,400,384]{2,1,0:T(8,128)(2,1)S(1)}) custom-call(bf16[4,320,384]{2,1,0:T(8,128)(2,1)S(1)} %get-tuple-element.50.refs_0_, bf16[4,64,384]{2,1,0:T(8,128)(2,1)} %get-tuple-element.56.refs_1_, ...), custom_call_target="tpu_custom_call" | custom-call | flops 1811939328 | bytes 7077888 | tf_op jit(solution)/shard_map/backward/pallas_call | solution.py:269
  72.0 1.0 collective-permute-start.16
  73.0 1.4 %collective-permute-start.17 = (bf16[2,192,384]{2,1,0:T(8,128)(2,1)}, bf16[2,192,384]{2,1,0:T(8,128)(2,1)S(1)}, u32[]{:S(2)}, u32[]{:S(2)}) collective-permute-start(bf16[2,192,384]{2,1,0:T(8,128)(2,1)} %get-tuple-element.68), channel_id=1, source_target_pairs={{0,16},{16,32},{32,48},{48,0},{64,80},{80,96},{96,112},{112,64},{1... | collective-permute-start | bytes 884744 | tf_op jit(solution)/shard_map/ppermute | solution.py:29
  74.3 24.1 %conditional.3 = (bf16[1,128,384]{2,1,0:T(8,128)(2,1)}, bf16[1,64,384]{2,1,0:T(8,128)(2,1)}, bf16[1,128,384]{2,1,0:T(8,128)(2,1)}, bf16[1,64,384]{2,1,0:T(8,128)(2,1)}, f32[8,384]{1,0:T(8,128)S(1)}) conditional(s32[]{:T(128)} %convert_element_type.4, () %tuple.23, bf16[4,400,384]{2,1,0:T(8,128)(2,1)S(1)} %get-tuple-element.61), branch_computations={%region_2.3_spmd, %region_3.4_spmd} | conditional | flops 6144 | bytes 2629752 | solution.py:343
  74.3 15.4 %all_to_all.4.parts_ref = bf16[4,400,384]{2,1,0:T(8,128)(2,1)S(1)} all-to-all(bf16[4,400,384]{2,1,0:T(8,128)(2,1)S(1)} %param.3), channel_id=1, replica_groups={{0,64,128,192},{16,80,144,208},{32,96,160,224},{48,112,176,240},{1,65,1..., dimensions={0} | all-to-all | bytes 2457600 | tf_op jit(solution)/shard_map/cond/branch_1_fun/all_to_all | solution.py:379
  90.5 4.0 %collective-permute-done.4 = f32[8,384]{1,0:T(8,128)S(1)} collective-permute-done((f32[8,384]{1,0:T(8,128)S(1)}, f32[8,384]{1,0:T(8,128)S(1)}, u32[]{:S(2)}, u32[]{:S(2)}) %collective-permute-start.4) | collective-permute-done | bytes 12320 | tf_op jit(solution)/shard_map/cond/branch_1_fun/ppermute | solution.py:34
  94.9 3.5 %collective-permute-done.5 = f32[8,384]{1,0:T(8,128)S(1)} collective-permute-done((f32[8,384]{1,0:T(8,128)S(1)}, f32[8,384]{1,0:T(8,128)S(1)}, u32[]{:S(2)}, u32[]{:S(2)}) %collective-permute-start.5) | collective-permute-done | bytes 12320 | tf_op jit(solution)/shard_map/cond/branch_1_fun/ppermute | solution.py:34
  98.4 6.6 %collective-permute-start.18 = (f32[8,384]{1,0:T(8,128)S(1)}, f32[8,384]{1,0:T(8,128)S(1)}, u32[]{:S(2)}, u32[]{:S(2)}) collective-permute-start(f32[8,384]{1,0:T(8,128)S(1)} %get-tuple-element.74), channel_id=1, source_target_pairs={{0,1},{1,0},{2,3},{3,2},{4,5},{5,4},{6,7},{7,6},{8,9},{9,8},{10,11... | collective-permute-start | bytes 36872 | tf_op jit(solution)/shard_map/ppermute | solution.py:387
  105.0 0.8 collective-permute-done.18
  (61 shorter events, 8.2 us)
Async XLA Ops:
  2.5 37.8 %copy-start.9 = (f32[384]{0:T(512)S(1)}, f32[384]{0:T(512)}, u32[]{:S(2)}) copy-start(f32[384]{0:T(512)} %param.21) | copy-start | bytes 4612
  2.5 37.8 %copy-start.10 = (f32[384]{0:T(512)S(1)}, f32[384]{0:T(512)}, u32[]{:S(2)}) copy-start(f32[384]{0:T(512)} %param.22) | copy-start | bytes 4612
  2.6 27.7 %collective-permute-start.3 = (bf16[2,128,384]{2,1,0:T(8,128)(2,1)S(1)}, bf16[2,128,384]{2,1,0:T(8,128)(2,1)}, u32[]{:S(2)}, u32[]{:S(2)}) collective-permute-start(bf16[2,128,384]{2,1,0:T(8,128)(2,1)S(1)} %get-tuple-element.8), channel_id=1, source_target_pairs={{0,48},{16,0},{32,16},{48,32},{64,112},{80,64},{96,80},{112,96},{1... | collective-permute-start | bytes 589832 | tf_op jit(solution)/shard_map/cond/branch_1_fun/ppermute | solution.py:29
  7.8 22.5 %collective-permute-start.2 = (bf16[2,128,384]{2,1,0:T(8,128)(2,1)S(1)}, bf16[2,128,384]{2,1,0:T(8,128)(2,1)}, u32[]{:S(2)}, u32[]{:S(2)}) collective-permute-start(bf16[2,128,384]{2,1,0:T(8,128)(2,1)S(1)} %get-tuple-element.8), channel_id=1, source_target_pairs={{0,32},{16,48},{32,0},{48,16},{64,96},{80,112},{96,64},{112,80},{1... | collective-permute-start | bytes 589832 | tf_op jit(solution)/shard_map/cond/branch_1_fun/ppermute | solution.py:29
  7.8 22.5 %collective-permute-start.1 = (bf16[2,128,384]{2,1,0:T(8,128)(2,1)S(1)}, bf16[2,128,384]{2,1,0:T(8,128)(2,1)}, u32[]{:S(2)}, u32[]{:S(2)}) collective-permute-start(bf16[2,128,384]{2,1,0:T(8,128)(2,1)S(1)} %get-tuple-element.8), channel_id=1, source_target_pairs={{0,16},{16,32},{32,48},{48,0},{64,80},{80,96},{96,112},{112,64},{1... | collective-permute-start | bytes 589832 | tf_op jit(solution)/shard_map/cond/branch_1_fun/ppermute | solution.py:29
  8.2 22.1 %collective-permute-start = (bf16[3,64,384]{2,1,0:T(8,128)(2,1)S(1)}, bf16[3,64,384]{2,1,0:T(8,128)(2,1)}, u32[]{:S(2)}, u32[]{:S(2)}) collective-permute-start(bf16[3,64,384]{2,1,0:T(8,128)(2,1)S(1)} %get-tuple-element.7), channel_id=1, source_target_pairs={{0,0},{2,32},{4,64},{6,96},{8,128},{10,160},{12,192},{14,224},{16,... | collective-permute-start | bytes 442376 | tf_op jit(solution)/shard_map/cond/branch_1_fun/ppermute | solution.py:338
  31.1 18.6 %copy-start.5 = (bf16[64,384]{1,0:T(8,128)(2,1)}, bf16[64,384]{1,0:T(8,128)(2,1)S(1)}, u32[]{:S(2)}) copy-start(bf16[64,384]{1,0:T(8,128)(2,1)S(1)} %slice_bitcast_fusion.refs_9_) | copy-start | bytes 147460
  31.1 9.2 %collective-permute-start.11 = (bf16[64,384]{1,0:T(8,128)(2,1)S(1)}, bf16[64,384]{1,0:T(8,128)(2,1)S(1)}, u32[]{:S(2)}, u32[]{:S(2)}) collective-permute-start(bf16[64,384]{1,0:T(8,128)(2,1)S(1)} %slice_bitcast_fusion.refs_9_), channel_id=1, source_target_pairs={{0,192},{16,208},{32,224},{48,240},{64,0},{80,16},{96,32},{112,48}... | collective-permute-start | bytes 147464 | tf_op jit(solution)/shard_map/ppermute | solution.py:24
  32.6 10.5 %collective-permute-start.10 = (bf16[64,384]{1,0:T(8,128)(2,1)S(1)}, bf16[64,384]{1,0:T(8,128)(2,1)S(1)}, u32[]{:S(2)}, u32[]{:S(2)}) collective-permute-start(bf16[64,384]{1,0:T(8,128)(2,1)S(1)} %slice_bitcast_fusion.refs_9_), channel_id=1, source_target_pairs={{0,128},{16,144},{32,160},{48,176},{64,192},{80,208},{96,224},{112... | collective-permute-start | bytes 147464 | tf_op jit(solution)/shard_map/ppermute | solution.py:24
  33.1 9.9 %collective-permute-start.9 = (bf16[64,384]{1,0:T(8,128)(2,1)S(1)}, bf16[64,384]{1,0:T(8,128)(2,1)S(1)}, u32[]{:S(2)}, u32[]{:S(2)}) collective-permute-start(bf16[64,384]{1,0:T(8,128)(2,1)S(1)} %slice_bitcast_fusion.refs_9_), channel_id=1, source_target_pairs={{0,64},{16,80},{32,96},{48,112},{64,128},{80,144},{96,160},{112,17... | collective-permute-start | bytes 147464 | tf_op jit(solution)/shard_map/ppermute | solution.py:24
  34.3 15.4 %copy-start.1 = (bf16[2,64,384]{2,1,0:T(8,128)(2,1)}, bf16[2,64,384]{2,1,0:T(8,128)(2,1)S(1)}, u32[]{:S(2)}) copy-start(bf16[2,64,384]{2,1,0:T(8,128)(2,1)S(1)} %slice.16.refs_5_.refs_6_) | copy-start | bytes 294916
  34.3 8.7 %collective-permute-start.8 = (bf16[2,64,384]{2,1,0:T(8,128)(2,1)S(1)}, bf16[2,64,384]{2,1,0:T(8,128)(2,1)S(1)}, u32[]{:S(2)}, u32[]{:S(2)}) collective-permute-start(bf16[2,64,384]{2,1,0:T(8,128)(2,1)S(1)} %slice.16.refs_5_.refs_6_), channel_id=1, source_target_pairs={{0,48},{16,0},{32,16},{48,32},{64,112},{80,64},{96,80},{112,96},{1... | collective-permute-start | bytes 294920 | tf_op jit(solution)/shard_map/ppermute | solution.py:29
  40.1 9.6 %collective-permute-start.7 = (bf16[2,64,384]{2,1,0:T(8,128)(2,1)S(1)}, bf16[2,64,384]{2,1,0:T(8,128)(2,1)S(1)}, u32[]{:S(2)}, u32[]{:S(2)}) collective-permute-start(bf16[2,64,384]{2,1,0:T(8,128)(2,1)S(1)} %slice.16.refs_5_.refs_6_), channel_id=1, source_target_pairs={{0,32},{16,48},{32,0},{48,16},{64,96},{80,112},{96,64},{112,80},{1... | collective-permute-start | bytes 294920 | tf_op jit(solution)/shard_map/ppermute | solution.py:29
  40.3 9.4 %collective-permute-start.6 = (bf16[2,64,384]{2,1,0:T(8,128)(2,1)S(1)}, bf16[2,64,384]{2,1,0:T(8,128)(2,1)S(1)}, u32[]{:S(2)}, u32[]{:S(2)}) collective-permute-start(bf16[2,64,384]{2,1,0:T(8,128)(2,1)S(1)} %slice.16.refs_5_.refs_6_), channel_id=1, source_target_pairs={{0,16},{16,32},{32,48},{48,0},{64,80},{80,96},{96,112},{112,64},{1... | collective-permute-start | bytes 294920 | tf_op jit(solution)/shard_map/ppermute | solution.py:29
  56.9 3.9 %collective-permute-start.14 = (f32[3,4,768]{2,1,0:T(4,128)}, f32[3,4,768]{2,1,0:T(4,128)S(1)}, u32[]{:S(2)}, u32[]{:S(2)}) collective-permute-start(f32[3,4,768]{2,1,0:T(4,128)} %get-tuple-element.57.refs_10_), channel_id=1, source_target_pairs={{0,192},{16,208},{32,224},{48,240},{64,0},{80,16},{96,32},{112,48}... | collective-permute-start | bytes 110600 | tf_op jit(solution)/shard_map/ppermute | solution.py:24
  59.0 4.5 %collective-permute-start.13 = (f32[3,4,768]{2,1,0:T(4,128)}, f32[3,4,768]{2,1,0:T(4,128)S(1)}, u32[]{:S(2)}, u32[]{:S(2)}) collective-permute-start(f32[3,4,768]{2,1,0:T(4,128)} %get-tuple-element.57.refs_10_), channel_id=1, source_target_pairs={{0,128},{16,144},{32,160},{48,176},{64,192},{80,208},{96,224},{112... | collective-permute-start | bytes 110600 | tf_op jit(solution)/shard_map/ppermute | solution.py:24
  60.1 4.2 %collective-permute-start.12 = (f32[3,4,768]{2,1,0:T(4,128)}, f32[3,4,768]{2,1,0:T(4,128)S(1)}, u32[]{:S(2)}, u32[]{:S(2)}) collective-permute-start(f32[3,4,768]{2,1,0:T(4,128)} %get-tuple-element.57.refs_10_), channel_id=1, source_target_pairs={{0,64},{16,80},{32,96},{48,112},{64,128},{80,144},{96,160},{112,17... | collective-permute-start | bytes 110600 | tf_op jit(solution)/shard_map/ppermute | solution.py:24
  71.9 34.6 %collective-permute-start.15 = (bf16[2,192,384]{2,1,0:T(8,128)(2,1)}, bf16[2,192,384]{2,1,0:T(8,128)(2,1)S(1)}, u32[]{:S(2)}, u32[]{:S(2)}) collective-permute-start(bf16[2,192,384]{2,1,0:T(8,128)(2,1)} %get-tuple-element.66), channel_id=1, source_target_pairs={{0,48},{16,0},{32,16},{48,32},{64,112},{80,64},{96,80},{112,96},{1... | collective-permute-start | bytes 884744 | tf_op jit(solution)/shard_map/ppermute | solution.py:29
  72.0 34.5 %collective-permute-start.16 = (bf16[2,192,384]{2,1,0:T(8,128)(2,1)}, bf16[2,192,384]{2,1,0:T(8,128)(2,1)S(1)}, u32[]{:S(2)}, u32[]{:S(2)}) collective-permute-start(bf16[2,192,384]{2,1,0:T(8,128)(2,1)} %get-tuple-element.67), channel_id=1, source_target_pairs={{0,32},{16,48},{32,0},{48,16},{64,96},{80,112},{96,64},{112,80},{1... | collective-permute-start | bytes 884744 | tf_op jit(solution)/shard_map/ppermute | solution.py:29
  73.0 33.5 %collective-permute-start.17 = (bf16[2,192,384]{2,1,0:T(8,128)(2,1)}, bf16[2,192,384]{2,1,0:T(8,128)(2,1)S(1)}, u32[]{:S(2)}, u32[]{:S(2)}) collective-permute-start(bf16[2,192,384]{2,1,0:T(8,128)(2,1)} %get-tuple-element.68), channel_id=1, source_target_pairs={{0,16},{16,32},{32,48},{48,0},{64,80},{80,96},{96,112},{112,64},{1... | collective-permute-start | bytes 884744 | tf_op jit(solution)/shard_map/ppermute | solution.py:29
  74.3 32.1 %copy-start = (bf16[2,192,384]{2,1,0:T(8,128)(2,1)S(1)}, bf16[2,192,384]{2,1,0:T(8,128)(2,1)}, u32[]{:S(2)}) copy-start(bf16[2,192,384]{2,1,0:T(8,128)(2,1)} %get-tuple-element.65.refs_0_) | copy-start | bytes 884740
  90.5 4.0 %collective-permute-start.4 = (f32[8,384]{1,0:T(8,128)S(1)}, f32[8,384]{1,0:T(8,128)S(1)}, u32[]{:S(2)}, u32[]{:S(2)}) collective-permute-start(f32[8,384]{1,0:T(8,128)S(1)} %get-tuple-element.14), channel_id=1, source_target_pairs={{0,16},{16,0},{32,48},{48,32},{64,80},{80,64},{96,112},{112,96},{1... | collective-permute-start | bytes 36872 | tf_op jit(solution)/shard_map/cond/branch_1_fun/ppermute | solution.py:34
  94.5 3.9 %collective-permute-start.5 = (f32[8,384]{1,0:T(8,128)S(1)}, f32[8,384]{1,0:T(8,128)S(1)}, u32[]{:S(2)}, u32[]{:S(2)}) collective-permute-start(f32[8,384]{1,0:T(8,128)S(1)} %add.29), channel_id=1, source_target_pairs={{0,32},{16,48},{32,0},{48,16},{64,96},{80,112},{96,64},{112,80},{1... | collective-permute-start | bytes 36872 | tf_op jit(solution)/shard_map/cond/branch_1_fun/ppermute | solution.py:34
  98.4 7.4 %collective-permute-start.18 = (f32[8,384]{1,0:T(8,128)S(1)}, f32[8,384]{1,0:T(8,128)S(1)}, u32[]{:S(2)}, u32[]{:S(2)}) collective-permute-start(f32[8,384]{1,0:T(8,128)S(1)} %get-tuple-element.74), channel_id=1, source_target_pairs={{0,1},{1,0},{2,3},{3,2},{4,5},{5,4},{6,7},{7,6},{8,9},{9,8},{10,11... | collective-permute-start | bytes 36872 | tf_op jit(solution)/shard_map/ppermute | solution.py:387
  (9 other events, 35.6 us)

commit v8 on v7

--- a/solution.py
+++ b/solution.py
@@ -34,8 +34,8 @@
     return lax.ppermute(array, "vid", pairs)
 
 
-def all_along_x(array):
-    return lax.all_gather(array, "vid", axis=0, axis_index_groups=ALONG_X)
+def across_x(array):
+    return lax.all_to_all(array, "vid", 0, 0, axis_index_groups=ALONG_X, tiled=True)
 
 
 def gathered(array, along):
@@ -54,10 +54,6 @@
     return lax.dot_general(a, b, (((1,), (0,)), ((), ())), preferred_element_type=F32)
 
 
-def joined(refs, index):
-    return jnp.concatenate([ref[index] for ref in refs], axis=0)
-
-
 def gated(rows, gate_row):
     return (gate_row * rows.astype(F32)).astype(BF16)
 
@@ -66,12 +62,23 @@
     return block.reshape(-1, block.shape[-1])
 
 
-def queries_of(gathered_ref, audio_ref, video_rows):
-    return jnp.concatenate([flat(gathered_ref[:, :video_rows]), flat(audio_ref[...])], axis=0)
+def queries_of(gathered_ref, video_rows):
+    audio_rows = gathered_ref.shape[1] // 2 - video_rows
+    return jnp.concatenate([flat(gathered_ref[:, :video_rows]), flat(gathered_ref[:, -audio_rows:])], axis=0)
 
 
 def upstreams_of(gathered_ref, video_rows):
-    return flat(gathered_ref[:, video_rows : 2 * video_rows]), flat(gathered_ref[:, 2 * video_rows :])
+    audio_rows = gathered_ref.shape[1] // 2 - video_rows
+    return flat(gathered_ref[:, video_rows : 2 * video_rows]), flat(gathered_ref[:, 2 * video_rows : -audio_rows])
+
+
+def keys_of(refs, part, index, video_rows):
+    own, video_1, audio_1, both_2, video_3, audio_3 = refs
+    if part == VIDEO:
+        pieces = [own[index, :video_rows], video_1[index], both_2[index, :video_rows], video_3[index]]
+    else:
+        pieces = [own[index, video_rows:], audio_1[index], both_2[index, video_rows:], audio_3[index]]
+    return jnp.concatenate(pieces, axis=0)
 
 
 def upstream(gathered_ref, gates_ref, video_rows, part):
@@ -83,16 +90,21 @@
     return jnp.concatenate([video, audio], axis=0)
 
 
-def prepare_kernel(aq_ref, ak_ref, av_ref, vq_ref, vk_ref, vv_ref, dv_ref, da_ref, audio, video_kv, queries, sems):
+def prepare_kernel(
+    aq_ref, ak_ref, av_ref, vq_ref, vk_ref, vv_ref, dv_ref, da_ref, audio, video_kv, keys, queries, sems
+):
     vid = lax.axis_index("vid")
     rows, width = vq_ref.shape[1:]
     audio_rows = da_ref.shape[1]
     taken = pl.ds(pl.multiple_of(lax.rem(vid, 2) * audio_rows, audio_rows), audio_rows)
     columns = pl.ds(pl.multiple_of(lax.div(vid, 2) * width, HEAD_DIM), width)
     pairs = [(ref.at[0, taken, columns], audio.at[index]) for index, ref in enumerate((aq_ref, ak_ref, av_ref))]
-    pairs += [(vk_ref.at[0], video_kv.at[0]), (vv_ref.at[0], video_kv.at[1])]
-    pairs += [(vq_ref.at[0], queries.at[pl.ds(0, rows)]), (dv_ref.at[0], queries.at[pl.ds(rows, rows)])]
-    pairs += [(da_ref.at[0], queries.at[pl.ds(2 * rows, audio_rows)])]
+    for index, ref in enumerate((vk_ref, vv_ref)):
+        pairs += [(ref.at[0], video_kv.at[index]), (ref.at[0], keys.at[index, pl.ds(0, rows)])]
+    for place in range(SIDE):
+        pairs += [(vq_ref.at[0], queries.at[place, pl.ds(0, rows)])]
+        pairs += [(dv_ref.at[0], queries.at[place, pl.ds(rows, rows)])]
+        pairs += [(da_ref.at[0], queries.at[place, pl.ds(2 * rows, audio_rows)])]
     copies = [pltpu.make_async_copy(source, target, sems.at[index]) for index, (source, target) in enumerate(pairs)]
     for copy in copies:
         copy.start()
@@ -103,30 +115,29 @@
 def prepare(audio_q, audio_k, audio_v, video_q, video_k, video_v, d_video, d_audio):
     _, video_rows, width = video_q.shape
     audio_rows = d_audio.shape[1]
+    rows = video_rows + audio_rows
     given = (audio_q, audio_k, audio_v, video_q, video_k, video_v, d_video, d_audio)
-    shapes = [(3, audio_rows, width), (2, video_rows, width), (2 * video_rows + audio_rows, width)]
+    shapes = [(3, audio_rows, width), (2, video_rows, width), (2, rows, width), (SIDE, 2 * rows, width)]
     return pl.pallas_call(
         prepare_kernel,
         in_specs=[pl.BlockSpec(memory_space=pl.ANY)] * len(given),
         out_specs=[pl.BlockSpec(memory_space=pltpu.VMEM)] * len(shapes),
         out_shape=[like(*shape) for shape in shapes],
-        scratch_shapes=[pltpu.SemaphoreType.DMA((len(given),))],
+        scratch_shapes=[pltpu.SemaphoreType.DMA((7 + 3 * SIDE,))],
         compiler_params=pltpu.CompilerParams(vmem_limit_bytes=VMEM),
         name="prepare",
     )(*given)
 
 
 def forward_kernel(video_rows, *refs):
-    gathered_ref, k_refs, audio_q, numbers_ref, gates_ref = refs[0], (refs[1:5], refs[5:9]), refs[9:13], refs[13], refs[14]
-    e_refs, o_ref, stats_ref, ordered_ref = refs[15:17], refs[17], refs[18], refs[19]
-    for place in range(SIDE):
-        ordered_ref[lax.rem(numbers_ref[SIDE] + SIDE - place, SIDE)] = audio_q[place][...]
-    queries = queries_of(gathered_ref, ordered_ref, video_rows)
+    gathered_ref, k_refs, numbers_ref, gates_ref = refs[0], refs[1:7], refs[7], refs[8]
+    e_refs, o_ref, stats_ref = refs[9:11], refs[11], refs[12]
+    queries = queries_of(gathered_ref, video_rows)
     stats = []
     for part in (VIDEO, AUDIO):
-        raw = nt(joined(k_refs[part], 0), queries)
+        raw = nt(keys_of(k_refs, part, 0, video_rows), queries)
         if part == AUDIO:
-            rows = k_refs[part][0].shape[1]
+            rows = raw.shape[0] // SIDE
             position = lax.broadcasted_iota(jnp.int32, (rows, raw.shape[1]), 0)
             pieces = [raw[place * rows : (place + 1) * rows] for place in range(SIDE)]
             pieces = [jnp.where(position < numbers_ref[place], pieces[place], -1e30) for place in range(SIDE)]
@@ -136,7 +147,7 @@
         total = jnp.sum(expon, axis=0, keepdims=True)
         expon = (expon * (1.0 / total)).astype(BF16)
         e_refs[part][0] = expon
-        output = nn(joined(k_refs[part], 1).T, expon)
+        output = nn(keys_of(k_refs, part, 1, video_rows).T, expon)
         o_ref[0, part] = output
         up = upstream(gathered_ref, gates_ref, video_rows, part)
         stats.append(peak * SCALE + jnp.log(total))
@@ -153,18 +164,18 @@
     return weights[0] * scale, delta
 
 
-def backward_keys(part, queries, up, stats_refs, k_refs, e_ref, k_outs, first):
+def backward_keys(part, queries, up, stats_refs, k_refs, e_ref, k_outs, video_rows):
     factor, delta = merged_stats(stats_refs, part)
     probs = e_ref[0].astype(F32) * factor
     grad_values = nn(probs.astype(BF16), up).astype(BF16)
-    grad_probs = nt(joined(k_refs, 1), up)
+    grad_probs = nt(keys_of(k_refs, part, 1, video_rows), up)
     grad_scores = (probs * (grad_probs - delta)).astype(BF16)
     grad_keys = (nn(grad_scores, queries) * SCALE).astype(BF16)
-    rows = k_refs[0].shape[1]
+    rows, first = probs.shape[0] // SIDE, part * video_rows
     for place in range(SIDE):
         k_outs[place][0, first : first + rows] = grad_keys[place * rows : (place + 1) * rows]
         k_outs[place][1, first : first + rows] = grad_values[place * rows : (place + 1) * rows]
-    return nn(joined(k_refs, 0).T, grad_scores), factor
+    return nn(keys_of(k_refs, part, 0, video_rows).T, grad_scores), factor
 
 
 def column_of(row):
@@ -172,18 +183,18 @@
 
 
 def backward_kernel(video_rows, *refs):
-    gathered_ref, audio_q, k_video, k_audio, stats_refs = refs[0], refs[1], refs[2:6], refs[6:10], refs[10:14]
-    gates_ref, e_video, e_audio, o_ref = refs[14:18]
-    k_outs, q_out = refs[18:22], refs[22]
-    audio_rows = audio_q.shape[1]
-    rows = video_rows + audio_rows
+    gathered_ref, k_refs, stats_refs = refs[0], refs[1:7], refs[7:11]
+    gates_ref, e_video, e_audio, o_ref = refs[11:15]
+    k_outs, q_out = refs[15:19], refs[19]
+    rows = gathered_ref.shape[1] // 2
+    audio_rows = rows - video_rows
     video = SIDE * video_rows
-    queries = queries_of(gathered_ref, audio_q, video_rows)
+    queries = queries_of(gathered_ref, video_rows)
     up = upstream(gathered_ref, gates_ref, video_rows, VIDEO)
-    term_video, factor = backward_keys(VIDEO, queries, up, stats_refs, k_video, e_video, k_outs, 0)
+    term_video, factor = backward_keys(VIDEO, queries, up, stats_refs, k_refs, e_video, k_outs, video_rows)
     on_video = o_ref[0, VIDEO] * factor
     up = upstream(gathered_ref, gates_ref, video_rows, AUDIO)
-    term_audio, factor = backward_keys(AUDIO, queries, up, stats_refs, k_audio, e_audio, k_outs, video_rows)
+    term_audio, factor = backward_keys(AUDIO, queries, up, stats_refs, k_refs, e_audio, k_outs, video_rows)
     on_audio = o_ref[0, AUDIO] * factor
     grad_queries = term_video + term_audio
     cross_video, cross_audio = on_audio[:, :video], on_video[:, video:]
@@ -235,37 +246,35 @@
     )
 
 
-def attention_forward(queries, audio_q, video_keys, audio_keys, numbers, gates, video_rows):
+def attention_forward(queries, keys, numbers, gates, video_rows):
     heads = gates.shape[1] // HEAD_DIM
-    audio_rows, width = audio_q[0].shape
-    video, audio = SIDE * video_rows, SIDE * audio_rows
-    total = video + audio
+    total = SIDE * (queries.shape[1] // 2)
+    video = SIDE * video_rows
     outs = [
         like(heads, video, total),
-        like(heads, audio, total),
+        like(heads, total - video, total),
         like(heads, 2, HEAD_DIM, total, kind=F32),
         like(heads, 4, total, kind=F32),
     ]
-    ordered = like(SIDE, audio_rows, width)
-    chunks = [queries, *video_keys, *audio_keys, *audio_q]
+    chunks = [queries, *keys]
     return pl.pallas_call(
         functools.partial(forward_kernel, video_rows),
         grid=(heads,),
         in_specs=[chunk_spec(array) for array in chunks] + [pl.BlockSpec(memory_space=pltpu.SMEM), chunk_spec(gates)],
-        out_specs=[head_spec(array) for array in outs] + [chunk_spec(ordered)],
-        out_shape=[*outs, ordered],
+        out_specs=[head_spec(array) for array in outs],
+        out_shape=outs,
         cost_estimate=cost(total, total, heads, 2),
         compiler_params=pltpu.CompilerParams(vmem_limit_bytes=VMEM),
         name="forward",
     )(*chunks, numbers, gates)
 
 
-def attention_backward(queries, audio_q, video_keys, audio_keys, stats, gates, by_head, video_rows):
+def attention_backward(queries, keys, stats, gates, by_head, video_rows):
     width = gates.shape[1]
     heads = width // HEAD_DIM
-    rows = video_rows + audio_q.shape[1]
+    rows = queries.shape[1] // 2
     outs = [like(2, rows, width)] * SIDE + [like(SIDE, 2 * rows + GATE_ROWS, width)]
-    chunks = [queries, audio_q, *video_keys, *audio_keys]
+    chunks = [queries, *keys]
     *key_parts, query_parts = pl.pallas_call(
         functools.partial(backward_kernel, video_rows),
         grid=(heads,),
@@ -352,31 +361,32 @@
     sizes = lax.axis_size("vid"), lax.axis_size("aud")
     video_rows, audio_rows = video_q.shape[1], d_audio_out.shape[1]
     holds = audio_len[0] > 0
-    send_audio, video_kv, queries = prepare(
+    send_audio, video_kv, keys, queries = prepare(
         audio_q, audio_k, audio_v, video_q, video_k, video_v, d_video_out, d_audio_out
     )
 
-    def first_chunks(send_audio, video_kv, queries):
-        return own_audio(send_audio, *sizes), tuple(gathered(video_kv, along_z)[1:]), all_along_x(queries)
-
-    audio, video_keys, queries = fenced(holds, first_chunks, send_audio, video_kv, queries)
-    video_keys = [video_kv, *video_keys]
+    def first_chunks(send_audio, video_kv):
+        return own_audio(send_audio, *sizes), along_z(video_kv, 1), along_z(video_kv, SIDE - 1)
+
+    audio, video_1, video_3 = fenced(holds, first_chunks, send_audio, video_kv)
     audio = lax.optimization_barrier(audio)
-    audio_keys = gathered(audio[1:], along_z)
-    audio_queries = gathered(audio[0], along_x)
+    audio_kv = audio[1:]
+    keys = lax.dynamic_update_slice(keys, audio_kv, (0, video_rows, 0))
+    audio_q = jnp.broadcast_to(audio[0:1], (SIDE, *audio.shape[1:]))
+    queries = lax.dynamic_update_slice(queries, audio_q, (0, 2 * video_rows + audio_rows, 0))
+    audio_1, audio_3, both_2 = along_z(audio_kv, 1), along_z(audio_kv, SIDE - 1), along_z(keys, 2)
+    queries = across_x(queries)
+    keys = keys, video_1, audio_1, both_2, video_3, audio_3
     gates = jnp.stack([video_gate, audio_gate])
     column, row = vid // SIDE, vid % SIDE
-    limits = [audio_len[0] - (column * SIDE + (row - p) % SIDE) * audio_rows for p in range(SIDE)]
-    numbers = jnp.stack([*limits, column])
-    *by_head, stats, audio_queries = attention_forward(
-        queries, audio_queries, video_keys, audio_keys, numbers, gates, video_rows
-    )
+    limits = jnp.stack([audio_len[0] - (column * SIDE + (row - p) % SIDE) * audio_rows for p in range(SIDE)])
+    *by_head, stats = attention_forward(queries, keys, limits, gates, video_rows)
     key_parts, query_parts = attention_backward(
-        queries, audio_queries, video_keys, audio_keys, gathered(stats, along_x), gates, by_head, video_rows
+        queries, keys, gathered(stats, along_x), gates, by_head, video_rows
     )
 
     def query_results(parts):
-        parts = lax.all_to_all(parts, "vid", 0, 0, axis_index_groups=ALONG_X, tiled=True)
+        parts = across_x(parts)
         *results, gate = finish_queries(parts, video_rows, audio_rows)
         for distance in (1, 2):
             gate = gate + beside_z(gate, distance)

time: 108 us -> 110 us (1.019)
  blocking collectives: 36.1 us -> 14.8 us
  starting transfers between devices: 30 us -> 42.2 us
  waiting for transfers between devices: 18.4 us -> 27.4 us
  Pallas kernels: 16.3 us -> 17.9 us
    all_gather x1 -> x0, blocking collectives: 20.8 us -> none  [all_along_x(): return lax.all_gather(array, 'vid', axis=0, axis_index_groups=ALONG_X)]
    ppermute x9 -> x8, waiting for transfers between devices: 6.61 us -> 17.4 us  [along_z(): return lax.ppermute(array, 'vid', pairs)]
    ppermute x9 -> x8, starting transfers between devices: 15.5 us -> 22.3 us  [along_z(): return lax.ppermute(array, 'vid', pairs)]
    all_to_all x0 -> x1, starting transfers between devices: none -> 4.16 us  [across_x(): lax.all_to_all(array, 'vid', 0, 0, axis_index_groups=ALONG_X, tiled=True)]
    ppermute x2, starting transfers between devices: 0.43 us -> 3.16 us  [beside_z(): return lax.ppermute(array, 'vid', pairs)]
    ppermute x6 -> x3, starting transfers between devices: 6.24 us -> 3.59 us  [along_x(): return lax.ppermute(array, 'vid', pairs)]
    ppermute x2, waiting for transfers between devices: 7.48 us -> 5.38 us  [beside_z(): return lax.ppermute(array, 'vid', pairs)]
    pallas_call x1, Pallas kernels: 1.21 us -> 2.77 us  [prepare(): pl.pallas_call(prepare_kernel, in_specs=[pl.BlockSpec(memory_space=pl.ANY...]
  transfers between devices with their start and end apart: 19 -> 16, of which waited for: 6 -> 9; matrix products, arithmetic and copies ran while one was open for 3% -> 2% of each run, Pallas kernels for 1% -> 1%
where the time goes in v8:
time: 110 us
  starting transfers between devices  42.2 us (38%)
  waiting for transfers between devices  27.4 us (25%)
  Pallas kernels  17.9 us (16%)
  blocking collectives  14.8 us (13%)
  local copies, waits for them, and re-layouts  4.81 us (4%)
  between operations  1.41 us (1%)
  other arithmetic  1.18 us (1%)
    ppermute x8, starting transfers between devices, along_z(): return lax.ppermute(array, 'vid', pairs)  22.3 us
    ppermute x8, waiting for transfers between devices, along_z(): return lax.ppermute(array, 'vid', pairs)  17.4 us
    all_to_all x1, blocking collectives, across_x(): lax.all_to_all(array, 'vid', 0, 0, axis_index_groups=ALONG_X, tiled=True)  14.8 us
    ppermute x1, starting transfers between devices, shards(): gate = gate + lax.ppermute(gate, 'pair', [(0, 1), (1, 0)])  7.75 us
    pallas_call x1, Pallas kernels, attention_backward(): pl.pallas_call(functools.partial(backward_kernel, video_rows), grid=(head...  7.04 us
    pallas_call x1, Pallas kernels, attention_forward(): pl.pallas_call(functools.partial(forward_kernel, video_rows), grid=(heads...  6.52 us
    ppermute x2, waiting for transfers between devices, beside_z(): return lax.ppermute(array, 'vid', pairs)  5.38 us
    all_to_all x1, starting transfers between devices, across_x(): lax.all_to_all(array, 'vid', 0, 0, axis_index_groups=ALONG_X, tiled=True)  4.16 us
  transfers between devices with their start and end apart: 16, of which 9 were waited for; matrix products, arithmetic and copies ran while one was open for 2% of the time, Pallas kernels for 1%

profile of v8, /device:TPU:1, one launch (start us, length us, event | category | flops | bytes accessed | tf_op | source)
XLA Modules:
  0.0 109.7 jit_solution(10741523443235225291)
XLA Ops:
  1.3 2.8 %prepare.1 = (bf16[3,64,384]{2,1,0:T(8,128)(2,1)S(1)}, bf16[2,128,384]{2,1,0:T(8,128)(2,1)S(1)}, bf16[2,192,384]{2,1,0:T(8,128)(2,1)}, bf16[4,384,384]{2,1,0:T(8,128)(2,1)}) custom-call(bf16[1,128,3072]{2,1,0:T(8,128)(2,1)} %aq_ref.1, bf16[1,128,3072]{2,1,0:T(8,128)(2,1)} %ak_ref.1, bf16[1,128,3072]{2,1,0:T(8,128)(2,1)} %av_ref.1, ...), custom_call_target="tpu_custom_call" | custom-call | tf_op jit(solution)/shard_map/prepare/pallas_call | solution.py:121
  4.1 17.3 %conditional.2 = (bf16[3,64,384]{2,1,0:T(8,128)(2,1)}, bf16[2,128,384]{2,1,0:T(8,128)(2,1)}, bf16[2,128,384]{2,1,0:T(8,128)(2,1)}) conditional(s32[]{:T(128)} %convert_element_type.4, () %tuple.25, (bf16[3,64,384]{2,1,0:T(8,128)(2,1)S(1)}, bf16[2,128,384]{2,1,0:T(8,128)(2,1)S(1)}) %tuple.26), branch_computations={%region_0.0_spmd, %region_1.0_spmd} | conditional | bytes 2162832 | solution.py:352
  4.1 5.2 %collective-permute-start.2 = (bf16[2,128,384]{2,1,0:T(8,128)(2,1)S(1)}, bf16[2,128,384]{2,1,0:T(8,128)(2,1)}, u32[]{:S(2)}, u32[]{:S(2)}) collective-permute-start(bf16[2,128,384]{2,1,0:T(8,128)(2,1)S(1)} %get-tuple-element.6), channel_id=1, source_target_pairs={{0,48},{16,0},{32,16},{48,32},{64,112},{80,64},{96,80},{112,96},{1... | collective-permute-start | bytes 589832 | tf_op jit(solution)/shard_map/cond/branch_1_fun/ppermute | solution.py:29
  9.3 1.3 %collective-permute-start = (bf16[3,64,384]{2,1,0:T(8,128)(2,1)S(1)}, bf16[3,64,384]{2,1,0:T(8,128)(2,1)}, u32[]{:S(2)}, u32[]{:S(2)}) collective-permute-start(bf16[3,64,384]{2,1,0:T(8,128)(2,1)S(1)} %get-tuple-element.5), channel_id=1, source_target_pairs={{0,0},{2,32},{4,64},{6,96},{8,128},{10,160},{12,192},{14,224},{16,... | collective-permute-start | bytes 442376 | tf_op jit(solution)/shard_map/cond/branch_1_fun/ppermute | solution.py:347
  10.6 2.3 %collective-permute-done.2 = bf16[2,128,384]{2,1,0:T(8,128)(2,1)} collective-permute-done((bf16[2,128,384]{2,1,0:T(8,128)(2,1)S(1)}, bf16[2,128,384]{2,1,0:T(8,128)(2,1)}, u32[]{:S(2)}, u32[]{:S(2)}) %collective-permute-start.2) | collective-permute-done | bytes 196640 | tf_op jit(solution)/shard_map/cond/branch_1_fun/ppermute | solution.py:29
  13.0 8.4 %collective-permute-done.1 = bf16[2,128,384]{2,1,0:T(8,128)(2,1)} collective-permute-done((bf16[2,128,384]{2,1,0:T(8,128)(2,1)S(1)}, bf16[2,128,384]{2,1,0:T(8,128)(2,1)}, u32[]{:S(2)}, u32[]{:S(2)}) %collective-permute-start.1) | collective-permute-done | bytes 196640 | tf_op jit(solution)/shard_map/cond/branch_1_fun/ppermute | solution.py:29
  22.9 4.2 %all-to-all-start.1 = ((bf16[4,384,384]{2,1,0:T(8,128)(2,1)}), bf16[4,384,384]{2,1,0:T(8,128)(2,1)S(1)}, u32[]{:S(2)}, u32[]{:S(2)}) async-start(bf16[4,384,384]{2,1,0:T(8,128)(2,1)} %broadcast_dynamic-update-slice_fusion), calls=%async_computation.1 | async-start | bytes 2359296 | tf_op jit(solution)/shard_map/all_to_all | solution.py:38
  27.0 0.9 fusion
  28.0 3.5 %collective-permute-start.6 = (bf16[2,192,384]{2,1,0:T(8,128)(2,1)S(1)}, bf16[2,192,384]{2,1,0:T(8,128)(2,1)S(1)}, u32[]{:S(2)}, u32[]{:S(2)}) collective-permute-start(bf16[2,192,384]{2,1,0:T(8,128)(2,1)S(1)} %get-tuple-element.75.refs_1_), channel_id=1, source_target_pairs={{0,32},{16,48},{32,0},{48,16},{64,96},{80,112},{96,64},{112,80},{1... | collective-permute-start | bytes 884744 | tf_op jit(solution)/shard_map/ppermute | solution.py:29
  31.5 7.9 %collective-permute-start.5 = (bf16[2,64,384]{2,1,0:T(8,128)(2,1)S(1)}, bf16[2,64,384]{2,1,0:T(8,128)(2,1)S(1)}, u32[]{:S(2)}, u32[]{:S(2)}) collective-permute-start(bf16[2,64,384]{2,1,0:T(8,128)(2,1)S(1)} %get-tuple-element.74), channel_id=1, source_target_pairs={{0,16},{16,32},{32,48},{48,0},{64,80},{80,96},{96,112},{112,64},{1... | collective-permute-start | bytes 294920 | tf_op jit(solution)/shard_map/ppermute | solution.py:29
  40.6 6.7 %collective-permute-done.5.refs_3_ = bf16[2,64,384]{2,1,0:T(8,128)(2,1)S(1)} collective-permute-done((bf16[2,64,384]{2,1,0:T(8,128)(2,1)S(1)}, bf16[2,64,384]{2,1,0:T(8,128)(2,1)S(1)}, u32[]{:S(2)}, u32[]{:S(2)}) %collective-permute-start.5) | collective-permute-done | bytes 98336 | tf_op jit(solution)/shard_map/ppermute | solution.py:29
  48.5 6.5 %forward.1 = (bf16[3,512,768]{2,1,0:T(8,128)(2,1)}, bf16[3,256,768]{2,1,0:T(8,128)(2,1)}, f32[3,2,128,768]{3,2,1,0:T(8,128)}, f32[3,4,768]{2,1,0:T(4,128)}) custom-call(bf16[4,384,384]{2,1,0:T(8,128)(2,1)} %copy-done.1, bf16[2,192,384]{2,1,0:T(8,128)(2,1)} %copy-done.4, bf16[2,128,384]{2,1,0:T(8,128)(2,1)} %get-tuple-element.52.refs_2_, ...), custom_call_target="tpu_custom_call" | custom-call | flops 905969664 | bytes 7077888 | tf_op jit(solution)/shard_map/forward/pallas_call | solution.py:260
  55.1 2.4 %collective-permute-start.10 = (f32[3,4,768]{2,1,0:T(4,128)}, f32[3,4,768]{2,1,0:T(4,128)S(1)}, u32[]{:S(2)}, u32[]{:S(2)}) collective-permute-start(f32[3,4,768]{2,1,0:T(4,128)} %get-tuple-element.54.refs_7_), channel_id=1, source_target_pairs={{0,192},{16,208},{32,224},{48,240},{64,0},{80,16},{96,32},{112,48}... | collective-permute-start | bytes 110600 | tf_op jit(solution)/shard_map/ppermute | solution.py:24
  58.9 3.2 %collective-permute-done.9.refs_9_ = f32[3,4,768]{2,1,0:T(4,128)S(1)} collective-permute-done((f32[3,4,768]{2,1,0:T(4,128)}, f32[3,4,768]{2,1,0:T(4,128)S(1)}, u32[]{:S(2)}, u32[]{:S(2)}) %collective-permute-start.9) | collective-permute-done | bytes 36896 | tf_op jit(solution)/shard_map/ppermute | solution.py:24
  63.0 7.0 %backward.1 = (bf16[2,192,384]{2,1,0:T(8,128)(2,1)}, bf16[2,192,384]{2,1,0:T(8,128)(2,1)}, bf16[2,192,384]{2,1,0:T(8,128)(2,1)}, bf16[2,192,384]{2,1,0:T(8,128)(2,1)}, bf16[4,400,384]{2,1,0:T(8,128)(2,1)S(1)}) custom-call(bf16[4,384,384]{2,1,0:T(8,128)(2,1)} %copy-done.1, bf16[2,192,384]{2,1,0:T(8,128)(2,1)} %copy-done.4, ...), custom_call_target="tpu_custom_call" | custom-call | flops 1811939328 | bytes 7077888 | tf_op jit(solution)/shard_map/backward/pallas_call | solution.py:278
  70.1 5.2 %collective-permute-start.11 = (bf16[2,192,384]{2,1,0:T(8,128)(2,1)}, bf16[2,192,384]{2,1,0:T(8,128)(2,1)S(1)}, u32[]{:S(2)}, u32[]{:S(2)}) collective-permute-start(bf16[2,192,384]{2,1,0:T(8,128)(2,1)} %get-tuple-element.63), channel_id=1, source_target_pairs={{0,48},{16,0},{32,16},{48,32},{64,112},{80,64},{96,80},{112,96},{1... | collective-permute-start | bytes 884744 | tf_op jit(solution)/shard_map/ppermute | solution.py:29
  75.6 24.1 %conditional.3 = (bf16[1,128,384]{2,1,0:T(8,128)(2,1)}, bf16[1,64,384]{2,1,0:T(8,128)(2,1)}, bf16[1,128,384]{2,1,0:T(8,128)(2,1)}, bf16[1,64,384]{2,1,0:T(8,128)(2,1)}, f32[8,384]{1,0:T(8,128)S(1)}) conditional(s32[]{:T(128)} %convert_element_type.4, () %tuple.24, bf16[4,400,384]{2,1,0:T(8,128)(2,1)S(1)} %get-tuple-element.58), branch_computations={%region_2.3_spmd, %region_3.4_spmd} | conditional | flops 6144 | bytes 2629752 | solution.py:352
  75.6 14.8 %all_to_all.9.parts_ref = bf16[4,400,384]{2,1,0:T(8,128)(2,1)S(1)} all-to-all(bf16[4,400,384]{2,1,0:T(8,128)(2,1)S(1)} %param.3), channel_id=1, replica_groups={{0,64,128,192},{16,80,144,208},{32,96,160,224},{48,112,176,240},{1,65,1..., dimensions={0} | all-to-all | bytes 2457600 | tf_op jit(solution)/shard_map/cond/branch_1_fun/all_to_all | solution.py:38
  91.2 2.3 %collective-permute-start.3 = (f32[8,384]{1,0:T(8,128)S(1)}, f32[8,384]{1,0:T(8,128)S(1)}, u32[]{:S(2)}, u32[]{:S(2)}) collective-permute-start(f32[8,384]{1,0:T(8,128)S(1)} %get-tuple-element.11), channel_id=1, source_target_pairs={{0,16},{16,0},{32,48},{48,32},{64,80},{80,64},{96,112},{112,96},{1... | collective-permute-start | bytes 36872 | tf_op jit(solution)/shard_map/cond/branch_1_fun/ppermute | solution.py:34
  93.5 2.2 %collective-permute-done.3 = f32[8,384]{1,0:T(8,128)S(1)} collective-permute-done((f32[8,384]{1,0:T(8,128)S(1)}, f32[8,384]{1,0:T(8,128)S(1)}, u32[]{:S(2)}, u32[]{:S(2)}) %collective-permute-start.3) | collective-permute-done | bytes 12320 | tf_op jit(solution)/shard_map/cond/branch_1_fun/ppermute | solution.py:34
  95.8 0.9 collective-permute-start.4
  96.6 3.1 %collective-permute-done.4 = f32[8,384]{1,0:T(8,128)S(1)} collective-permute-done((f32[8,384]{1,0:T(8,128)S(1)}, f32[8,384]{1,0:T(8,128)S(1)}, u32[]{:S(2)}, u32[]{:S(2)}) %collective-permute-start.4) | collective-permute-done | bytes 12320 | tf_op jit(solution)/shard_map/cond/branch_1_fun/ppermute | solution.py:34
  99.8 7.7 %collective-permute-start.14 = (f32[8,384]{1,0:T(8,128)S(1)}, f32[8,384]{1,0:T(8,128)S(1)}, u32[]{:S(2)}, u32[]{:S(2)}) collective-permute-start(f32[8,384]{1,0:T(8,128)S(1)} %get-tuple-element.71), channel_id=1, source_target_pairs={{0,1},{1,0},{2,3},{3,2},{4,5},{5,4},{6,7},{7,6},{8,9},{9,8},{10,11... | collective-permute-start | bytes 36872 | tf_op jit(solution)/shard_map/ppermute | solution.py:397
  107.5 0.8 collective-permute-done.14
  (51 shorter events, 8.8 us)
Async XLA Ops:
  4.1 8.9 %collective-permute-start.2 = (bf16[2,128,384]{2,1,0:T(8,128)(2,1)S(1)}, bf16[2,128,384]{2,1,0:T(8,128)(2,1)}, u32[]{:S(2)}, u32[]{:S(2)}) collective-permute-start(bf16[2,128,384]{2,1,0:T(8,128)(2,1)S(1)} %get-tuple-element.6), channel_id=1, source_target_pairs={{0,48},{16,0},{32,16},{48,32},{64,112},{80,64},{96,80},{112,96},{1... | collective-permute-start | bytes 589832 | tf_op jit(solution)/shard_map/cond/branch_1_fun/ppermute | solution.py:29
  9.3 12.0 %collective-permute-start.1 = (bf16[2,128,384]{2,1,0:T(8,128)(2,1)S(1)}, bf16[2,128,384]{2,1,0:T(8,128)(2,1)}, u32[]{:S(2)}, u32[]{:S(2)}) collective-permute-start(bf16[2,128,384]{2,1,0:T(8,128)(2,1)S(1)} %get-tuple-element.6), channel_id=1, source_target_pairs={{0,16},{16,32},{32,48},{48,0},{64,80},{80,96},{96,112},{112,64},{1... | collective-permute-start | bytes 589832 | tf_op jit(solution)/shard_map/cond/branch_1_fun/ppermute | solution.py:29
  9.3 1.3 %collective-permute-start = (bf16[3,64,384]{2,1,0:T(8,128)(2,1)S(1)}, bf16[3,64,384]{2,1,0:T(8,128)(2,1)}, u32[]{:S(2)}, u32[]{:S(2)}) collective-permute-start(bf16[3,64,384]{2,1,0:T(8,128)(2,1)S(1)} %get-tuple-element.5), channel_id=1, source_target_pairs={{0,0},{2,32},{4,64},{6,96},{8,128},{10,160},{12,192},{14,224},{16,... | collective-permute-start | bytes 442376 | tf_op jit(solution)/shard_map/cond/branch_1_fun/ppermute | solution.py:347
  22.9 4.2 %copy-start.3 = (bf16[2,192,384]{2,1,0:T(8,128)(2,1)S(1)}, bf16[2,192,384]{2,1,0:T(8,128)(2,1)}, u32[]{:S(2)}) copy-start(bf16[2,192,384]{2,1,0:T(8,128)(2,1)} %get-tuple-element.51) | copy-start | bytes 884740
  22.9 16.5 %copy-start.10 = (f32[384]{0:T(512)S(1)}, f32[384]{0:T(512)}, u32[]{:S(2)}) copy-start(f32[384]{0:T(512)} %param.21) | copy-start | bytes 4612
  22.9 16.6 %copy-start.11 = (f32[384]{0:T(512)S(1)}, f32[384]{0:T(512)}, u32[]{:S(2)}) copy-start(f32[384]{0:T(512)} %param.22) | copy-start | bytes 4612
  22.9 24.5 %all-to-all-start.1 = ((bf16[4,384,384]{2,1,0:T(8,128)(2,1)}), bf16[4,384,384]{2,1,0:T(8,128)(2,1)S(1)}, u32[]{:S(2)}, u32[]{:S(2)}) async-start(bf16[4,384,384]{2,1,0:T(8,128)(2,1)} %broadcast_dynamic-update-slice_fusion), calls=%async_computation.1 | async-start | bytes 2359296 | tf_op jit(solution)/shard_map/all_to_all | solution.py:38
  28.0 19.4 %copy-start.4 = (bf16[2,192,384]{2,1,0:T(8,128)(2,1)}, bf16[2,192,384]{2,1,0:T(8,128)(2,1)S(1)}, u32[]{:S(2)}) copy-start(bf16[2,192,384]{2,1,0:T(8,128)(2,1)S(1)} %get-tuple-element.75.refs_1_) | copy-start | bytes 884740
  28.0 19.4 %collective-permute-start.6 = (bf16[2,192,384]{2,1,0:T(8,128)(2,1)S(1)}, bf16[2,192,384]{2,1,0:T(8,128)(2,1)S(1)}, u32[]{:S(2)}, u32[]{:S(2)}) collective-permute-start(bf16[2,192,384]{2,1,0:T(8,128)(2,1)S(1)} %get-tuple-element.75.refs_1_), channel_id=1, source_target_pairs={{0,32},{16,48},{32,0},{48,16},{64,96},{80,112},{96,64},{112,80},{1... | collective-permute-start | bytes 884744 | tf_op jit(solution)/shard_map/ppermute | solution.py:29
  31.5 15.8 %collective-permute-start.5 = (bf16[2,64,384]{2,1,0:T(8,128)(2,1)S(1)}, bf16[2,64,384]{2,1,0:T(8,128)(2,1)S(1)}, u32[]{:S(2)}, u32[]{:S(2)}) collective-permute-start(bf16[2,64,384]{2,1,0:T(8,128)(2,1)S(1)} %get-tuple-element.74), channel_id=1, source_target_pairs={{0,16},{16,32},{32,48},{48,0},{64,80},{80,96},{96,112},{112,64},{1... | collective-permute-start | bytes 294920 | tf_op jit(solution)/shard_map/ppermute | solution.py:29
  39.4 7.9 %collective-permute-start.7 = (bf16[2,64,384]{2,1,0:T(8,128)(2,1)S(1)}, bf16[2,64,384]{2,1,0:T(8,128)(2,1)S(1)}, u32[]{:S(2)}, u32[]{:S(2)}) collective-permute-start(bf16[2,64,384]{2,1,0:T(8,128)(2,1)S(1)} %get-tuple-element.74), channel_id=1, source_target_pairs={{0,48},{16,0},{32,16},{48,32},{64,112},{80,64},{96,80},{112,96},{1... | collective-permute-start | bytes 294920 | tf_op jit(solution)/shard_map/ppermute | solution.py:29
  47.3 0.8 copy-start.2
  47.4 1.2 %copy-start.1 = (bf16[4,384,384]{2,1,0:T(8,128)(2,1)}, bf16[4,384,384]{2,1,0:T(8,128)(2,1)S(1)}, u32[]{:S(2)}) copy-start(bf16[4,384,384]{2,1,0:T(8,128)(2,1)S(1)} %all-to-all-done.1.refs_0_) | copy-start | bytes 3538948
  55.1 3.8 %collective-permute-start.10 = (f32[3,4,768]{2,1,0:T(4,128)}, f32[3,4,768]{2,1,0:T(4,128)S(1)}, u32[]{:S(2)}, u32[]{:S(2)}) collective-permute-start(f32[3,4,768]{2,1,0:T(4,128)} %get-tuple-element.54.refs_7_), channel_id=1, source_target_pairs={{0,192},{16,208},{32,224},{48,240},{64,0},{80,16},{96,32},{112,48}... | collective-permute-start | bytes 110600 | tf_op jit(solution)/shard_map/ppermute | solution.py:24
  57.5 4.5 %collective-permute-start.9 = (f32[3,4,768]{2,1,0:T(4,128)}, f32[3,4,768]{2,1,0:T(4,128)S(1)}, u32[]{:S(2)}, u32[]{:S(2)}) collective-permute-start(f32[3,4,768]{2,1,0:T(4,128)} %get-tuple-element.54.refs_7_), channel_id=1, source_target_pairs={{0,128},{16,144},{32,160},{48,176},{64,192},{80,208},{96,224},{112... | collective-permute-start | bytes 110600 | tf_op jit(solution)/shard_map/ppermute | solution.py:24
  58.1 4.3 %collective-permute-start.8 = (f32[3,4,768]{2,1,0:T(4,128)}, f32[3,4,768]{2,1,0:T(4,128)S(1)}, u32[]{:S(2)}, u32[]{:S(2)}) collective-permute-start(f32[3,4,768]{2,1,0:T(4,128)} %get-tuple-element.54.refs_7_), channel_id=1, source_target_pairs={{0,64},{16,80},{32,96},{48,112},{64,128},{80,144},{96,160},{112,17... | collective-permute-start | bytes 110600 | tf_op jit(solution)/shard_map/ppermute | solution.py:24
  58.9 3.5 %copy-start.7 = (f32[3,4,768]{2,1,0:T(4,128)}, f32[3,4,768]{2,1,0:T(4,128)S(1)}, u32[]{:S(2)}) copy-start(f32[3,4,768]{2,1,0:T(4,128)S(1)} %collective-permute-done.10.refs_10_) | copy-start | bytes 110596
  70.1 38.9 %collective-permute-start.11 = (bf16[2,192,384]{2,1,0:T(8,128)(2,1)}, bf16[2,192,384]{2,1,0:T(8,128)(2,1)S(1)}, u32[]{:S(2)}, u32[]{:S(2)}) collective-permute-start(bf16[2,192,384]{2,1,0:T(8,128)(2,1)} %get-tuple-element.63), channel_id=1, source_target_pairs={{0,48},{16,0},{32,16},{48,32},{64,112},{80,64},{96,80},{112,96},{1... | collective-permute-start | bytes 884744 | tf_op jit(solution)/shard_map/ppermute | solution.py:29
  75.3 33.7 %collective-permute-start.12 = (bf16[2,192,384]{2,1,0:T(8,128)(2,1)}, bf16[2,192,384]{2,1,0:T(8,128)(2,1)S(1)}, u32[]{:S(2)}, u32[]{:S(2)}) collective-permute-start(bf16[2,192,384]{2,1,0:T(8,128)(2,1)} %get-tuple-element.64), channel_id=1, source_target_pairs={{0,32},{16,48},{32,0},{48,16},{64,96},{80,112},{96,64},{112,80},{1... | collective-permute-start | bytes 884744 | tf_op jit(solution)/shard_map/ppermute | solution.py:29
  75.4 33.6 %collective-permute-start.13 = (bf16[2,192,384]{2,1,0:T(8,128)(2,1)}, bf16[2,192,384]{2,1,0:T(8,128)(2,1)S(1)}, u32[]{:S(2)}, u32[]{:S(2)}) collective-permute-start(bf16[2,192,384]{2,1,0:T(8,128)(2,1)} %get-tuple-element.65), channel_id=1, source_target_pairs={{0,16},{16,32},{32,48},{48,0},{64,80},{80,96},{96,112},{112,64},{1... | collective-permute-start | bytes 884744 | tf_op jit(solution)/shard_map/ppermute | solution.py:29
  75.6 33.3 %copy-start = (bf16[2,192,384]{2,1,0:T(8,128)(2,1)S(1)}, bf16[2,192,384]{2,1,0:T(8,128)(2,1)}, u32[]{:S(2)}) copy-start(bf16[2,192,384]{2,1,0:T(8,128)(2,1)} %get-tuple-element.62.refs_0_) | copy-start | bytes 884740
  91.2 4.5 %collective-permute-start.3 = (f32[8,384]{1,0:T(8,128)S(1)}, f32[8,384]{1,0:T(8,128)S(1)}, u32[]{:S(2)}, u32[]{:S(2)}) collective-permute-start(f32[8,384]{1,0:T(8,128)S(1)} %get-tuple-element.11), channel_id=1, source_target_pairs={{0,16},{16,0},{32,48},{48,32},{64,80},{80,64},{96,112},{112,96},{1... | collective-permute-start | bytes 36872 | tf_op jit(solution)/shard_map/cond/branch_1_fun/ppermute | solution.py:34
  95.8 4.0 %collective-permute-start.4 = (f32[8,384]{1,0:T(8,128)S(1)}, f32[8,384]{1,0:T(8,128)S(1)}, u32[]{:S(2)}, u32[]{:S(2)}) collective-permute-start(f32[8,384]{1,0:T(8,128)S(1)} %add.29), channel_id=1, source_target_pairs={{0,32},{16,48},{32,0},{48,16},{64,96},{80,112},{96,64},{112,80},{1... | collective-permute-start | bytes 36872 | tf_op jit(solution)/shard_map/cond/branch_1_fun/ppermute | solution.py:34
  99.8 8.6 %collective-permute-start.14 = (f32[8,384]{1,0:T(8,128)S(1)}, f32[8,384]{1,0:T(8,128)S(1)}, u32[]{:S(2)}, u32[]{:S(2)}) collective-permute-start(f32[8,384]{1,0:T(8,128)S(1)} %get-tuple-element.71), channel_id=1, source_target_pairs={{0,1},{1,0},{2,3},{3,2},{4,5},{5,4},{6,7},{7,6},{8,9},{9,8},{10,11... | collective-permute-start | bytes 36872 | tf_op jit(solution)/shard_map/ppermute | solution.py:397
  (4 other events, 2.5 us)

commit v9 on v8

--- a/solution.py
+++ b/solution.py
@@ -72,13 +72,8 @@
     return flat(gathered_ref[:, video_rows : 2 * video_rows]), flat(gathered_ref[:, 2 * video_rows : -audio_rows])
 
 
-def keys_of(refs, part, index, video_rows):
-    own, video_1, audio_1, both_2, video_3, audio_3 = refs
-    if part == VIDEO:
-        pieces = [own[index, :video_rows], video_1[index], both_2[index, :video_rows], video_3[index]]
-    else:
-        pieces = [own[index, video_rows:], audio_1[index], both_2[index, video_rows:], audio_3[index]]
-    return jnp.concatenate(pieces, axis=0)
+def keys_of(refs, part, index):
+    return jnp.concatenate([ref[index] for ref in refs[SIDE * part : SIDE * (part + 1)]], axis=0)
 
 
 def upstream(gathered_ref, gates_ref, video_rows, part):
@@ -90,21 +85,16 @@
     return jnp.concatenate([video, audio], axis=0)
 
 
-def prepare_kernel(
-    aq_ref, ak_ref, av_ref, vq_ref, vk_ref, vv_ref, dv_ref, da_ref, audio, video_kv, keys, queries, sems
-):
-    vid = lax.axis_index("vid")
-    rows, width = vq_ref.shape[1:]
-    audio_rows = da_ref.shape[1]
-    taken = pl.ds(pl.multiple_of(lax.rem(vid, 2) * audio_rows, audio_rows), audio_rows)
-    columns = pl.ds(pl.multiple_of(lax.div(vid, 2) * width, HEAD_DIM), width)
-    pairs = [(ref.at[0, taken, columns], audio.at[index]) for index, ref in enumerate((aq_ref, ak_ref, av_ref))]
-    for index, ref in enumerate((vk_ref, vv_ref)):
-        pairs += [(ref.at[0], video_kv.at[index]), (ref.at[0], keys.at[index, pl.ds(0, rows)])]
-    for place in range(SIDE):
-        pairs += [(vq_ref.at[0], queries.at[place, pl.ds(0, rows)])]
-        pairs += [(dv_ref.at[0], queries.at[place, pl.ds(rows, rows)])]
-        pairs += [(da_ref.at[0], queries.at[place, pl.ds(2 * rows, audio_rows)])]
+def audio_target(vid, aud):
+    x, z, y, half = vid >> 2, vid & 3, aud >> 1, aud & 1
+    offset = (x - y) & 3
+    to_y = (y - offset + 2 * (1 - (offset & 1))) & 3
+    to_z = 2 * half + ((z + 1) & 1)
+    to_half = (((z + 1) >> 1) + 1 + half) & 1
+    return SIDE * y + to_z, 2 * to_y + to_half
+
+
+def copy_all(pairs, sems):
     copies = [pltpu.make_async_copy(source, target, sems.at[index]) for index, (source, target) in enumerate(pairs)]
     for copy in copies:
         copy.start()
@@ -112,30 +102,45 @@
         copy.wait()
 
 
-def prepare(audio_q, audio_k, audio_v, video_q, video_k, video_v, d_video, d_audio):
-    _, video_rows, width = video_q.shape
-    audio_rows = d_audio.shape[1]
-    rows = video_rows + audio_rows
-    given = (audio_q, audio_k, audio_v, video_q, video_k, video_v, d_video, d_audio)
-    shapes = [(3, audio_rows, width), (2, video_rows, width), (2, rows, width), (SIDE, 2 * rows, width)]
+def laid_out(kernel, name, given, shapes, count):
     return pl.pallas_call(
-        prepare_kernel,
+        kernel,
         in_specs=[pl.BlockSpec(memory_space=pl.ANY)] * len(given),
         out_specs=[pl.BlockSpec(memory_space=pltpu.VMEM)] * len(shapes),
         out_shape=[like(*shape) for shape in shapes],
-        scratch_shapes=[pltpu.SemaphoreType.DMA((7 + 3 * SIDE,))],
+        scratch_shapes=[pltpu.SemaphoreType.DMA((count,))],
         compiler_params=pltpu.CompilerParams(vmem_limit_bytes=VMEM),
-        name="prepare",
+        name=name,
     )(*given)
 
 
+def prepare_keys_kernel(aq_ref, ak_ref, av_ref, vk_ref, vv_ref, audio, video_kv, sems):
+    to_vid, to_aud = audio_target(lax.axis_index("vid"), lax.axis_index("aud"))
+    rows, width = audio.shape[1:]
+    taken = pl.ds(pl.multiple_of((to_vid & 1) * rows, rows), rows)
+    columns = pl.ds(pl.multiple_of(to_aud * width, HEAD_DIM), width)
+    pairs = [(ref.at[0, taken, columns], audio.at[index]) for index, ref in enumerate((aq_ref, ak_ref, av_ref))]
+    pairs += [(ref.at[0], video_kv.at[index]) for index, ref in enumerate((vk_ref, vv_ref))]
+    copy_all(pairs, sems)
+
+
+def prepare_queries_kernel(vq_ref, dv_ref, da_ref, queries, sems):
+    rows, audio_rows = vq_ref.shape[1], da_ref.shape[1]
+    pairs = []
+    for place in range(SIDE):
+        pairs += [(vq_ref.at[0], queries.at[place, pl.ds(0, rows)])]
+        pairs += [(dv_ref.at[0], queries.at[place, pl.ds(rows, rows)])]
+        pairs += [(da_ref.at[0], queries.at[place, pl.ds(2 * rows, audio_rows)])]
+    copy_all(pairs, sems)
+
+
 def forward_kernel(video_rows, *refs):
-    gathered_ref, k_refs, numbers_ref, gates_ref = refs[0], refs[1:7], refs[7], refs[8]
-    e_refs, o_ref, stats_ref = refs[9:11], refs[11], refs[12]
+    gathered_ref, k_refs, numbers_ref, gates_ref = refs[0], refs[1:9], refs[9], refs[10]
+    e_refs, o_ref, stats_ref = refs[11:13], refs[13], refs[14]
     queries = queries_of(gathered_ref, video_rows)
     stats = []
     for part in (VIDEO, AUDIO):
-        raw = nt(keys_of(k_refs, part, 0, video_rows), queries)
+        raw = nt(keys_of(k_refs, part, 0), queries)
         if part == AUDIO:
             rows = raw.shape[0] // SIDE
             position = lax.broadcasted_iota(jnp.int32, (rows, raw.shape[1]), 0)
@@ -147,7 +152,7 @@
         total = jnp.sum(expon, axis=0, keepdims=True)
         expon = (expon * (1.0 / total)).astype(BF16)
         e_refs[part][0] = expon
-        output = nn(keys_of(k_refs, part, 1, video_rows).T, expon)
+        output = nn(keys_of(k_refs, part, 1).T, expon)
         o_ref[0, part] = output
         up = upstream(gathered_ref, gates_ref, video_rows, part)
         stats.append(peak * SCALE + jnp.log(total))
@@ -168,14 +173,14 @@
     factor, delta = merged_stats(stats_refs, part)
     probs = e_ref[0].astype(F32) * factor
     grad_values = nn(probs.astype(BF16), up).astype(BF16)
-    grad_probs = nt(keys_of(k_refs, part, 1, video_rows), up)
+    grad_probs = nt(keys_of(k_refs, part, 1), up)
     grad_scores = (probs * (grad_probs - delta)).astype(BF16)
     grad_keys = (nn(grad_scores, queries) * SCALE).astype(BF16)
     rows, first = probs.shape[0] // SIDE, part * video_rows
     for place in range(SIDE):
         k_outs[place][0, first : first + rows] = grad_keys[place * rows : (place + 1) * rows]
         k_outs[place][1, first : first + rows] = grad_values[place * rows : (place + 1) * rows]
-    return nn(keys_of(k_refs, part, 0, video_rows).T, grad_scores), factor
+    return nn(keys_of(k_refs, part, 0).T, grad_scores), factor
 
 
 def column_of(row):
@@ -183,9 +188,9 @@
 
 
 def backward_kernel(video_rows, *refs):
-    gathered_ref, k_refs, stats_refs = refs[0], refs[1:7], refs[7:11]
-    gates_ref, e_video, e_audio, o_ref = refs[11:15]
-    k_outs, q_out = refs[15:19], refs[19]
+    gathered_ref, k_refs, stats_refs = refs[0], refs[1:9], refs[9:13]
+    gates_ref, e_video, e_audio, o_ref = refs[13:17]
+    k_outs, q_out = refs[17:21], refs[21]
     rows = gathered_ref.shape[1] // 2
     audio_rows = rows - video_rows
     video = SIDE * video_rows
@@ -340,10 +345,13 @@
     )(*parts)
 
 
-def own_audio(array, vid_size, aud_size):
-    pairs = [
-        (v * aud_size + a, (2 * a + v % 2) * aud_size + v // 2) for v in range(vid_size) for a in range(aud_size)
-    ]
+def own_audio(array):
+    vid_size, aud_size = lax.axis_size("vid"), lax.axis_size("aud")
+    pairs = []
+    for vid in range(vid_size):
+        for aud in range(aud_size):
+            to_vid, to_aud = audio_target(vid, aud)
+            pairs.append((vid * aud_size + aud, to_vid * aud_size + to_aud))
     return lax.ppermute(array, ("vid", "aud"), pairs)
 
 
@@ -358,25 +366,31 @@
     video_q, video_k, video_v, audio_q, audio_k, audio_v, video_gate, audio_gate, audio_len, d_video_out, d_audio_out
 ):
     vid = lax.axis_index("vid")
-    sizes = lax.axis_size("vid"), lax.axis_size("aud")
     video_rows, audio_rows = video_q.shape[1], d_audio_out.shape[1]
     holds = audio_len[0] > 0
-    send_audio, video_kv, keys, queries = prepare(
-        audio_q, audio_k, audio_v, video_q, video_k, video_v, d_video_out, d_audio_out
-    )
-
-    def first_chunks(send_audio, video_kv):
-        return own_audio(send_audio, *sizes), along_z(video_kv, 1), along_z(video_kv, SIDE - 1)
-
-    audio, video_1, video_3 = fenced(holds, first_chunks, send_audio, video_kv)
+    width = video_q.shape[2]
+    send_audio, video_kv = laid_out(
+        prepare_keys_kernel,
+        "prepare_keys",
+        (audio_q, audio_k, audio_v, video_k, video_v),
+        [(3, audio_rows, width), (2, video_rows, width)],
+        5,
+    )
+
+    def first_chunks(send_audio, video_kv, *given):
+        shape = (SIDE, 2 * (video_rows + audio_rows), width)
+        (queries,) = laid_out(prepare_queries_kernel, "prepare_queries", given, [shape], 3 * SIDE)
+        return own_audio(send_audio), tuple(gathered(video_kv, along_z)[1:]), queries
+
+    audio, video_keys, queries = fenced(
+        holds, first_chunks, send_audio, video_kv, video_q, d_video_out, d_audio_out
+    )
     audio = lax.optimization_barrier(audio)
-    audio_kv = audio[1:]
-    keys = lax.dynamic_update_slice(keys, audio_kv, (0, video_rows, 0))
     audio_q = jnp.broadcast_to(audio[0:1], (SIDE, *audio.shape[1:]))
     queries = lax.dynamic_update_slice(queries, audio_q, (0, 2 * video_rows + audio_rows, 0))
-    audio_1, audio_3, both_2 = along_z(audio_kv, 1), along_z(audio_kv, SIDE - 1), along_z(keys, 2)
+    audio_keys = gathered(audio[1:], along_z)
     queries = across_x(queries)
-    keys = keys, video_1, audio_1, both_2, video_3, audio_3
+    keys = (video_kv, *video_keys, *audio_keys)
     gates = jnp.stack([video_gate, audio_gate])
     column, row = vid // SIDE, vid % SIDE
     limits = jnp.stack([audio_len[0] - (column * SIDE + (row - p) % SIDE) * audio_rows for p in range(SIDE)])

time: 110 us -> 109 us (level)
  waiting for transfers between devices: 27.4 us -> 24.6 us
  starting transfers between devices: 42.2 us -> 43.4 us
    ppermute x1, starting transfers between devices: 1.31 us -> 7.92 us  [own_audio(): return lax.ppermute(array, ('vid', 'aud'), pairs)]
    ppermute x8 -> x9, waiting for transfers between devices: 17.4 us -> 10.9 us  [along_z(): return lax.ppermute(array, 'vid', pairs)]
    ppermute x2, waiting for transfers between devices: 5.38 us -> 8.91 us  [beside_z(): return lax.ppermute(array, 'vid', pairs)]
    ppermute x8 -> x9, starting transfers between devices: 22.3 us -> 19.1 us  [along_z(): return lax.ppermute(array, 'vid', pairs)]
    ppermute x2, starting transfers between devices: 3.16 us -> 0.29 us  [beside_z(): return lax.ppermute(array, 'vid', pairs)]
    pallas_call x1 -> x2, Pallas kernels: 2.77 us -> 3.53 us  [laid_out(): pl.pallas_call(kernel, in_specs=[pl.BlockSpec(memory_space=pl.ANY)] * len...]
  transfers between devices with their start and end apart: 16 -> 17, of which waited for: 9 -> 8; matrix products, arithmetic and copies ran while one was open for 2% -> 3% of each run, Pallas kernels for 1% -> 3%
where the time goes in v9:
time: 109 us; the launch traced here: 108 us
  starting transfers between devices  43.4 us (40%)
  waiting for transfers between devices  24.6 us (23%)
  Pallas kernels  18.5 us (17%)
  blocking collectives  14.1 us (13%)
  local copies, waits for them, and re-layouts  4.72 us (4%)
  between operations  1.45 us (1%)
  other arithmetic  1.2 us (1%)
    ppermute x9, starting transfers between devices, along_z(): return lax.ppermute(array, 'vid', pairs)  19.1 us
    all_to_all x1, blocking collectives, across_x(): lax.all_to_all(array, 'vid', 0, 0, axis_index_groups=ALONG_X, tiled=True)  14.1 us
    ppermute x9, waiting for transfers between devices, along_z(): return lax.ppermute(array, 'vid', pairs)  10.9 us
    ppermute x2, waiting for transfers between devices, beside_z(): return lax.ppermute(array, 'vid', pairs)  8.91 us
    ppermute x1, starting transfers between devices, shards(): gate = gate + lax.ppermute(gate, 'pair', [(0, 1), (1, 0)])  8.06 us
    ppermute x1, starting transfers between devices, own_audio(): return lax.ppermute(array, ('vid', 'aud'), pairs)  7.92 us
    pallas_call x1, Pallas kernels, attention_backward(): pl.pallas_call(functools.partial(backward_kernel, video_rows), grid=(head...  6.98 us
    pallas_call x1, Pallas kernels, attention_forward(): pl.pallas_call(functools.partial(forward_kernel, video_rows), grid=(heads...  6.46 us
  transfers between devices with their start and end apart: 17, of which 8 were waited for; matrix products, arithmetic and copies ran while one was open for 3% of the time, Pallas kernels for 3%

profile of v9, /device:TPU:1, one launch (start us, length us, event | category | flops | bytes accessed | tf_op | source)
XLA Modules:
  0.0 108.0 jit_solution(17781078799466822170)
XLA Ops:
  1.3 1.1 %prepare_keys.1 = (bf16[3,64,384]{2,1,0:T(8,128)(2,1)S(1)}, bf16[2,128,384]{2,1,0:T(8,128)(2,1)S(1)}) custom-call(bf16[1,128,3072]{2,1,0:T(8,128)(2,1)} %aq_ref.1, bf16[1,128,3072]{2,1,0:T(8,128)(2,1)} %ak_ref.1, bf16[1,128,3072]{2,1,0:T(8,128)(2,1)} %av_ref.1, bf16[1,128,384]{2,1,0:T(8,128)(2,1)} %vk_ref.1, bf16[1,128,384]{2,1,0:T(8,128)(2,1)} %vv_ref.1), custom_call_target="tpu_custom_call" | custom-call | tf_op jit(solution)/shard_map/prepare_keys/pallas_call | solution.py:106
  2.5 21.4 %conditional.2 = (bf16[3,64,384]{2,1,0:T(8,128)(2,1)}, bf16[2,128,384]{2,1,0:T(8,128)(2,1)}, bf16[2,128,384]{2,1,0:T(8,128)(2,1)}, bf16[2,128,384]{2,1,0:T(8,128)(2,1)}, bf16[4,384,384]{2,1,0:T(8,128)(2,1)}) conditional(s32[]{:T(128)} %convert_element_type.4, () %tuple.25, (bf16[3,64,384]{2,1,0:T(8,128)(2,1)S(1)}, bf16[2,128,384]{2,1,0:T(8,128)(2,1)S(1)}, ...), branch_computations={%region_0.0_spmd, %region_1.0_spmd} | conditional | bytes 2949320 | solution.py:360
  2.5 5.3 %collective-permute-start.3 = (bf16[2,128,384]{2,1,0:T(8,128)(2,1)S(1)}, bf16[2,128,384]{2,1,0:T(8,128)(2,1)}, u32[]{:S(2)}, u32[]{:S(2)}) collective-permute-start(bf16[2,128,384]{2,1,0:T(8,128)(2,1)S(1)} %get-tuple-element.12), channel_id=1, source_target_pairs={{0,48},{16,0},{32,16},{48,32},{64,112},{80,64},{96,80},{112,96},{1... | collective-permute-start | bytes 589832 | tf_op jit(solution)/shard_map/cond/branch_1_fun/ppermute | solution.py:29
  8.2 7.9 %collective-permute-start = (bf16[3,64,384]{2,1,0:T(8,128)(2,1)S(1)}, bf16[3,64,384]{2,1,0:T(8,128)(2,1)}, u32[]{:S(2)}, u32[]{:S(2)}) collective-permute-start(bf16[3,64,384]{2,1,0:T(8,128)(2,1)S(1)} %get-tuple-element.11), channel_id=1, source_target_pairs={{0,26},{2,56},{4,90},{6,120},{8,154},{10,184},{12,218},{14,248},{1... | collective-permute-start | bytes 442376 | tf_op jit(solution)/shard_map/cond/branch_1_fun/ppermute | solution.py:355
  16.1 2.4 %prepare_queries.1 = bf16[4,384,384]{2,1,0:T(8,128)(2,1)} custom-call(bf16[1,128,384]{2,1,0:T(8,128)(2,1)S(1)} %get-tuple-element.84.vq_ref, bf16[1,128,384]{2,1,0:T(8,128)(2,1)S(1)} %get-tuple-element.85.dv_ref, bf16[1,64,384]{2,1,0:T(8,128)(2,1)S(1)} %get-tuple-element.86.da_ref), custom_call_target="tpu_custom_call" | custom-call | tf_op jit(solution)/shard_map/cond/branch_1_fun/prepare_queries/pallas_call | solution.py:106
  18.5 5.4 %collective-permute-done.2 = bf16[2,128,384]{2,1,0:T(8,128)(2,1)} collective-permute-done((bf16[2,128,384]{2,1,0:T(8,128)(2,1)S(1)}, bf16[2,128,384]{2,1,0:T(8,128)(2,1)}, u32[]{:S(2)}, u32[]{:S(2)}) %collective-permute-start.2) | collective-permute-done | bytes 196640 | tf_op jit(solution)/shard_map/cond/branch_1_fun/ppermute | solution.py:29
  23.9 0.8 slice_bitcast_fusion
  25.4 5.1 %all-to-all-start.1 = ((bf16[4,384,384]{2,1,0:T(8,128)(2,1)}), bf16[4,384,384]{2,1,0:T(8,128)(2,1)S(1)}, u32[]{:S(2)}, u32[]{:S(2)}) async-start(bf16[4,384,384]{2,1,0:T(8,128)(2,1)} %broadcast_dynamic-update-slice_fusion), calls=%async_computation.1 | async-start | bytes 2359296 | tf_op jit(solution)/shard_map/all_to_all | solution.py:38
  30.6 0.9 slice.17.refs_5_
  31.5 1.7 %collective-permute-start.8 = (bf16[2,64,384]{2,1,0:T(8,128)(2,1)S(1)}, bf16[2,64,384]{2,1,0:T(8,128)(2,1)S(1)}, u32[]{:S(2)}, u32[]{:S(2)}) collective-permute-start(bf16[2,64,384]{2,1,0:T(8,128)(2,1)S(1)} %slice.17.refs_5_), channel_id=1, source_target_pairs={{0,48},{16,0},{32,16},{48,32},{64,112},{80,64},{96,80},{112,96},{1... | collective-permute-start | bytes 294920 | tf_op jit(solution)/shard_map/ppermute | solution.py:29
  33.2 5.7 %collective-permute-start.7 = (bf16[2,64,384]{2,1,0:T(8,128)(2,1)S(1)}, bf16[2,64,384]{2,1,0:T(8,128)(2,1)S(1)}, u32[]{:S(2)}, u32[]{:S(2)}) collective-permute-start(bf16[2,64,384]{2,1,0:T(8,128)(2,1)S(1)} %slice.17.refs_5_), channel_id=1, source_target_pairs={{0,32},{16,48},{32,0},{48,16},{64,96},{80,112},{96,64},{112,80},{1... | collective-permute-start | bytes 294920 | tf_op jit(solution)/shard_map/ppermute | solution.py:29
  40.1 5.4 %collective-permute-done.7.refs_7_ = bf16[2,64,384]{2,1,0:T(8,128)(2,1)S(1)} collective-permute-done((bf16[2,64,384]{2,1,0:T(8,128)(2,1)S(1)}, bf16[2,64,384]{2,1,0:T(8,128)(2,1)S(1)}, u32[]{:S(2)}, u32[]{:S(2)}) %collective-permute-start.7) | collective-permute-done | bytes 98336 | tf_op jit(solution)/shard_map/ppermute | solution.py:29
  46.6 6.5 %forward.1 = (bf16[3,512,768]{2,1,0:T(8,128)(2,1)}, bf16[3,256,768]{2,1,0:T(8,128)(2,1)}, f32[3,2,128,768]{3,2,1,0:T(8,128)}, f32[3,4,768]{2,1,0:T(4,128)}) custom-call(bf16[4,384,384]{2,1,0:T(8,128)(2,1)} %copy-done.1, bf16[2,128,384]{2,1,0:T(8,128)(2,1)S(1)} %get-tuple-element.57.refs_1_, bf16[2,128,384]{2,1,0:T(8,128)(2,1)} %get-tuple-element.60.refs_2_, ...), custom_call_target="tpu_custom_call" | custom-call | flops 905969664 | bytes 7077888 | tf_op jit(solution)/shard_map/forward/pallas_call | solution.py:265
  53.1 1.9 %collective-permute-start.11 = (f32[3,4,768]{2,1,0:T(4,128)}, f32[3,4,768]{2,1,0:T(4,128)S(1)}, u32[]{:S(2)}, u32[]{:S(2)}) collective-permute-start(f32[3,4,768]{2,1,0:T(4,128)} %get-tuple-element.63.refs_9_), channel_id=1, source_target_pairs={{0,192},{16,208},{32,224},{48,240},{64,0},{80,16},{96,32},{112,48}... | collective-permute-start | bytes 110600 | tf_op jit(solution)/shard_map/ppermute | solution.py:24
  56.4 3.2 %collective-permute-done.10.refs_11_ = f32[3,4,768]{2,1,0:T(4,128)S(1)} collective-permute-done((f32[3,4,768]{2,1,0:T(4,128)}, f32[3,4,768]{2,1,0:T(4,128)S(1)}, u32[]{:S(2)}, u32[]{:S(2)}) %collective-permute-start.10) | collective-permute-done | bytes 36896 | tf_op jit(solution)/shard_map/ppermute | solution.py:24
  60.5 7.0 %backward.1 = (bf16[2,192,384]{2,1,0:T(8,128)(2,1)}, bf16[2,192,384]{2,1,0:T(8,128)(2,1)}, bf16[2,192,384]{2,1,0:T(8,128)(2,1)}, bf16[2,192,384]{2,1,0:T(8,128)(2,1)}, bf16[4,400,384]{2,1,0:T(8,128)(2,1)S(1)}) custom-call(bf16[4,384,384]{2,1,0:T(8,128)(2,1)} %copy-done.1, bf16[2,128,384]{2,1,0:T(8,128)(2,1)S(1)} %get-tuple-element.57.refs_1_, ...), custom_call_target="tpu_custom_call" | custom-call | flops 1811939328 | bytes 7077888 | tf_op jit(solution)/shard_map/backward/pallas_call | solution.py:283
  67.8 5.9 %collective-permute-start.13 = (bf16[2,192,384]{2,1,0:T(8,128)(2,1)}, bf16[2,192,384]{2,1,0:T(8,128)(2,1)S(1)}, u32[]{:S(2)}, u32[]{:S(2)}) collective-permute-start(bf16[2,192,384]{2,1,0:T(8,128)(2,1)} %get-tuple-element.73), channel_id=1, source_target_pairs={{0,32},{16,48},{32,0},{48,16},{64,96},{80,112},{96,64},{112,80},{1... | collective-permute-start | bytes 884744 | tf_op jit(solution)/shard_map/ppermute | solution.py:29
  73.6 24.1 %conditional.3 = (bf16[1,128,384]{2,1,0:T(8,128)(2,1)}, bf16[1,64,384]{2,1,0:T(8,128)(2,1)}, bf16[1,128,384]{2,1,0:T(8,128)(2,1)}, bf16[1,64,384]{2,1,0:T(8,128)(2,1)}, f32[8,384]{1,0:T(8,128)S(1)}) conditional(s32[]{:T(128)} %convert_element_type.4, () %tuple.24, bf16[4,400,384]{2,1,0:T(8,128)(2,1)S(1)} %get-tuple-element.67), branch_computations={%region_2.3_spmd, %region_3.4_spmd} | conditional | flops 6144 | bytes 2629752 | solution.py:360
  73.6 14.1 %all_to_all.9.parts_ref = bf16[4,400,384]{2,1,0:T(8,128)(2,1)S(1)} all-to-all(bf16[4,400,384]{2,1,0:T(8,128)(2,1)S(1)} %param.3), channel_id=1, replica_groups={{0,64,128,192},{16,80,144,208},{32,96,160,224},{48,112,176,240},{1,65,1..., dimensions={0} | all-to-all | bytes 2457600 | tf_op jit(solution)/shard_map/cond/branch_1_fun/all_to_all | solution.py:38
  87.7 0.8 finish_queries.1
  88.8 5.0 %collective-permute-done.4 = f32[8,384]{1,0:T(8,128)S(1)} collective-permute-done((f32[8,384]{1,0:T(8,128)S(1)}, f32[8,384]{1,0:T(8,128)S(1)}, u32[]{:S(2)}, u32[]{:S(2)}) %collective-permute-start.4) | collective-permute-done | bytes 12320 | tf_op jit(solution)/shard_map/cond/branch_1_fun/ppermute | solution.py:34
  93.8 3.9 %collective-permute-done.5 = f32[8,384]{1,0:T(8,128)S(1)} collective-permute-done((f32[8,384]{1,0:T(8,128)S(1)}, f32[8,384]{1,0:T(8,128)S(1)}, u32[]{:S(2)}, u32[]{:S(2)}) %collective-permute-start.5) | collective-permute-done | bytes 12320 | tf_op jit(solution)/shard_map/cond/branch_1_fun/ppermute | solution.py:34
  97.7 8.1 %collective-permute-start.15 = (f32[8,384]{1,0:T(8,128)S(1)}, f32[8,384]{1,0:T(8,128)S(1)}, u32[]{:S(2)}, u32[]{:S(2)}) collective-permute-start(f32[8,384]{1,0:T(8,128)S(1)} %get-tuple-element.80), channel_id=1, source_target_pairs={{0,1},{1,0},{2,3},{3,2},{4,5},{5,4},{6,7},{7,6},{8,9},{9,8},{10,11... | collective-permute-start | bytes 36872 | tf_op jit(solution)/shard_map/ppermute | solution.py:411
  105.8 0.8 collective-permute-done.15
  (58 shorter events, 7.7 us)
Async XLA Ops:
  1.3 1.2 %copy-start.6 = (bf16[1,128,384]{2,1,0:T(8,128)(2,1)S(1)}, bf16[1,128,384]{2,1,0:T(8,128)(2,1)}, u32[]{:S(2)}) copy-start(bf16[1,128,384]{2,1,0:T(8,128)(2,1)} %param.15) | copy-start | bytes 294916
  2.5 16.0 %collective-permute-start.3 = (bf16[2,128,384]{2,1,0:T(8,128)(2,1)S(1)}, bf16[2,128,384]{2,1,0:T(8,128)(2,1)}, u32[]{:S(2)}, u32[]{:S(2)}) collective-permute-start(bf16[2,128,384]{2,1,0:T(8,128)(2,1)S(1)} %get-tuple-element.12), channel_id=1, source_target_pairs={{0,48},{16,0},{32,16},{48,32},{64,112},{80,64},{96,80},{112,96},{1... | collective-permute-start | bytes 589832 | tf_op jit(solution)/shard_map/cond/branch_1_fun/ppermute | solution.py:29
  7.8 16.1 %collective-permute-start.2 = (bf16[2,128,384]{2,1,0:T(8,128)(2,1)S(1)}, bf16[2,128,384]{2,1,0:T(8,128)(2,1)}, u32[]{:S(2)}, u32[]{:S(2)}) collective-permute-start(bf16[2,128,384]{2,1,0:T(8,128)(2,1)S(1)} %get-tuple-element.12), channel_id=1, source_target_pairs={{0,32},{16,48},{32,0},{48,16},{64,96},{80,112},{96,64},{112,80},{1... | collective-permute-start | bytes 589832 | tf_op jit(solution)/shard_map/cond/branch_1_fun/ppermute | solution.py:29
  7.8 16.1 %collective-permute-start.1 = (bf16[2,128,384]{2,1,0:T(8,128)(2,1)S(1)}, bf16[2,128,384]{2,1,0:T(8,128)(2,1)}, u32[]{:S(2)}, u32[]{:S(2)}) collective-permute-start(bf16[2,128,384]{2,1,0:T(8,128)(2,1)S(1)} %get-tuple-element.12), channel_id=1, source_target_pairs={{0,16},{16,32},{32,48},{48,0},{64,80},{80,96},{96,112},{112,64},{1... | collective-permute-start | bytes 589832 | tf_op jit(solution)/shard_map/cond/branch_1_fun/ppermute | solution.py:29
  8.2 10.3 %collective-permute-start = (bf16[3,64,384]{2,1,0:T(8,128)(2,1)S(1)}, bf16[3,64,384]{2,1,0:T(8,128)(2,1)}, u32[]{:S(2)}, u32[]{:S(2)}) collective-permute-start(bf16[3,64,384]{2,1,0:T(8,128)(2,1)S(1)} %get-tuple-element.11), channel_id=1, source_target_pairs={{0,26},{2,56},{4,90},{6,120},{8,154},{10,184},{12,218},{14,248},{1... | collective-permute-start | bytes 442376 | tf_op jit(solution)/shard_map/cond/branch_1_fun/ppermute | solution.py:355
  25.4 13.4 %copy-start.12 = (f32[384]{0:T(512)S(1)}, f32[384]{0:T(512)}, u32[]{:S(2)}) copy-start(f32[384]{0:T(512)} %param.21) | copy-start | bytes 4612
  25.4 13.4 %copy-start.13 = (f32[384]{0:T(512)S(1)}, f32[384]{0:T(512)}, u32[]{:S(2)}) copy-start(f32[384]{0:T(512)} %param.22) | copy-start | bytes 4612
  25.4 20.1 %all-to-all-start.1 = ((bf16[4,384,384]{2,1,0:T(8,128)(2,1)}), bf16[4,384,384]{2,1,0:T(8,128)(2,1)S(1)}, u32[]{:S(2)}, u32[]{:S(2)}) async-start(bf16[4,384,384]{2,1,0:T(8,128)(2,1)} %broadcast_dynamic-update-slice_fusion), calls=%async_computation.1 | async-start | bytes 2359296 | tf_op jit(solution)/shard_map/all_to_all | solution.py:38
  31.5 14.1 %copy-start.2 = (bf16[2,64,384]{2,1,0:T(8,128)(2,1)}, bf16[2,64,384]{2,1,0:T(8,128)(2,1)S(1)}, u32[]{:S(2)}) copy-start(bf16[2,64,384]{2,1,0:T(8,128)(2,1)S(1)} %slice.17.refs_5_) | copy-start | bytes 294916
  31.5 8.6 %collective-permute-start.8 = (bf16[2,64,384]{2,1,0:T(8,128)(2,1)S(1)}, bf16[2,64,384]{2,1,0:T(8,128)(2,1)S(1)}, u32[]{:S(2)}, u32[]{:S(2)}) collective-permute-start(bf16[2,64,384]{2,1,0:T(8,128)(2,1)S(1)} %slice.17.refs_5_), channel_id=1, source_target_pairs={{0,48},{16,0},{32,16},{48,32},{64,112},{80,64},{96,80},{112,96},{1... | collective-permute-start | bytes 294920 | tf_op jit(solution)/shard_map/ppermute | solution.py:29
  33.2 12.3 %collective-permute-start.7 = (bf16[2,64,384]{2,1,0:T(8,128)(2,1)S(1)}, bf16[2,64,384]{2,1,0:T(8,128)(2,1)S(1)}, u32[]{:S(2)}, u32[]{:S(2)}) collective-permute-start(bf16[2,64,384]{2,1,0:T(8,128)(2,1)S(1)} %slice.17.refs_5_), channel_id=1, source_target_pairs={{0,32},{16,48},{32,0},{48,16},{64,96},{80,112},{96,64},{112,80},{1... | collective-permute-start | bytes 294920 | tf_op jit(solution)/shard_map/ppermute | solution.py:29
  38.9 6.7 %collective-permute-start.6 = (bf16[2,64,384]{2,1,0:T(8,128)(2,1)S(1)}, bf16[2,64,384]{2,1,0:T(8,128)(2,1)S(1)}, u32[]{:S(2)}, u32[]{:S(2)}) collective-permute-start(bf16[2,64,384]{2,1,0:T(8,128)(2,1)S(1)} %slice.17.refs_5_), channel_id=1, source_target_pairs={{0,16},{16,32},{32,48},{48,0},{64,80},{80,96},{96,112},{112,64},{1... | collective-permute-start | bytes 294920 | tf_op jit(solution)/shard_map/ppermute | solution.py:29
  40.1 5.5 %copy-start.3 = (bf16[2,64,384]{2,1,0:T(8,128)(2,1)}, bf16[2,64,384]{2,1,0:T(8,128)(2,1)S(1)}, u32[]{:S(2)}) copy-start(bf16[2,64,384]{2,1,0:T(8,128)(2,1)S(1)} %collective-permute-done.8.refs_8_) | copy-start | bytes 294916
  53.1 3.3 %collective-permute-start.11 = (f32[3,4,768]{2,1,0:T(4,128)}, f32[3,4,768]{2,1,0:T(4,128)S(1)}, u32[]{:S(2)}, u32[]{:S(2)}) collective-permute-start(f32[3,4,768]{2,1,0:T(4,128)} %get-tuple-element.63.refs_9_), channel_id=1, source_target_pairs={{0,192},{16,208},{32,224},{48,240},{64,0},{80,16},{96,32},{112,48}... | collective-permute-start | bytes 110600 | tf_op jit(solution)/shard_map/ppermute | solution.py:24
  55.0 4.6 %collective-permute-start.10 = (f32[3,4,768]{2,1,0:T(4,128)}, f32[3,4,768]{2,1,0:T(4,128)S(1)}, u32[]{:S(2)}, u32[]{:S(2)}) collective-permute-start(f32[3,4,768]{2,1,0:T(4,128)} %get-tuple-element.63.refs_9_), channel_id=1, source_target_pairs={{0,128},{16,144},{32,160},{48,176},{64,192},{80,208},{96,224},{112... | collective-permute-start | bytes 110600 | tf_op jit(solution)/shard_map/ppermute | solution.py:24
  55.3 4.6 %collective-permute-start.9 = (f32[3,4,768]{2,1,0:T(4,128)}, f32[3,4,768]{2,1,0:T(4,128)S(1)}, u32[]{:S(2)}, u32[]{:S(2)}) collective-permute-start(f32[3,4,768]{2,1,0:T(4,128)} %get-tuple-element.63.refs_9_), channel_id=1, source_target_pairs={{0,64},{16,80},{32,96},{48,112},{64,128},{80,144},{96,160},{112,17... | collective-permute-start | bytes 110600 | tf_op jit(solution)/shard_map/ppermute | solution.py:24
  56.4 3.5 %copy-start.9 = (f32[3,4,768]{2,1,0:T(4,128)}, f32[3,4,768]{2,1,0:T(4,128)S(1)}, u32[]{:S(2)}) copy-start(f32[3,4,768]{2,1,0:T(4,128)S(1)} %collective-permute-done.11.refs_12_) | copy-start | bytes 110596
  67.5 39.7 %collective-permute-start.12 = (bf16[2,192,384]{2,1,0:T(8,128)(2,1)}, bf16[2,192,384]{2,1,0:T(8,128)(2,1)S(1)}, u32[]{:S(2)}, u32[]{:S(2)}) collective-permute-start(bf16[2,192,384]{2,1,0:T(8,128)(2,1)} %get-tuple-element.72), channel_id=1, source_target_pairs={{0,48},{16,0},{32,16},{48,32},{64,112},{80,64},{96,80},{112,96},{1... | collective-permute-start | bytes 884744 | tf_op jit(solution)/shard_map/ppermute | solution.py:29
  67.8 39.4 %collective-permute-start.13 = (bf16[2,192,384]{2,1,0:T(8,128)(2,1)}, bf16[2,192,384]{2,1,0:T(8,128)(2,1)S(1)}, u32[]{:S(2)}, u32[]{:S(2)}) collective-permute-start(bf16[2,192,384]{2,1,0:T(8,128)(2,1)} %get-tuple-element.73), channel_id=1, source_target_pairs={{0,32},{16,48},{32,0},{48,16},{64,96},{80,112},{96,64},{112,80},{1... | collective-permute-start | bytes 884744 | tf_op jit(solution)/shard_map/ppermute | solution.py:29
  73.6 33.6 %collective-permute-start.14 = (bf16[2,192,384]{2,1,0:T(8,128)(2,1)}, bf16[2,192,384]{2,1,0:T(8,128)(2,1)S(1)}, u32[]{:S(2)}, u32[]{:S(2)}) collective-permute-start(bf16[2,192,384]{2,1,0:T(8,128)(2,1)} %get-tuple-element.74), channel_id=1, source_target_pairs={{0,16},{16,32},{32,48},{48,0},{64,80},{80,96},{96,112},{112,64},{1... | collective-permute-start | bytes 884744 | tf_op jit(solution)/shard_map/ppermute | solution.py:29
  73.6 33.6 %copy-start = (bf16[2,192,384]{2,1,0:T(8,128)(2,1)S(1)}, bf16[2,192,384]{2,1,0:T(8,128)(2,1)}, u32[]{:S(2)}) copy-start(bf16[2,192,384]{2,1,0:T(8,128)(2,1)} %get-tuple-element.71.refs_0_) | copy-start | bytes 884740
  88.5 5.3 %collective-permute-start.4 = (f32[8,384]{1,0:T(8,128)S(1)}, f32[8,384]{1,0:T(8,128)S(1)}, u32[]{:S(2)}, u32[]{:S(2)}) collective-permute-start(f32[8,384]{1,0:T(8,128)S(1)} %get-tuple-element.20), channel_id=1, source_target_pairs={{0,16},{16,0},{32,48},{48,32},{64,80},{80,64},{96,112},{112,96},{1... | collective-permute-start | bytes 36872 | tf_op jit(solution)/shard_map/cond/branch_1_fun/ppermute | solution.py:34
  93.8 3.9 %collective-permute-start.5 = (f32[8,384]{1,0:T(8,128)S(1)}, f32[8,384]{1,0:T(8,128)S(1)}, u32[]{:S(2)}, u32[]{:S(2)}) collective-permute-start(f32[8,384]{1,0:T(8,128)S(1)} %add.29), channel_id=1, source_target_pairs={{0,32},{16,48},{32,0},{48,16},{64,96},{80,112},{96,64},{112,80},{1... | collective-permute-start | bytes 36872 | tf_op jit(solution)/shard_map/cond/branch_1_fun/ppermute | solution.py:34
  97.7 8.9 %collective-permute-start.15 = (f32[8,384]{1,0:T(8,128)S(1)}, f32[8,384]{1,0:T(8,128)S(1)}, u32[]{:S(2)}, u32[]{:S(2)}) collective-permute-start(f32[8,384]{1,0:T(8,128)S(1)} %get-tuple-element.80), channel_id=1, source_target_pairs={{0,1},{1,0},{2,3},{3,2},{4,5},{5,4},{6,7},{7,6},{8,9},{9,8},{10,11... | collective-permute-start | bytes 36872 | tf_op jit(solution)/shard_map/ppermute | solution.py:411
  (7 other events, 6.0 us)

commit v10 on v7

--- a/solution.py
+++ b/solution.py
@@ -83,12 +83,19 @@
     return jnp.concatenate([video, audio], axis=0)
 
 
+def audio_target(vid, aud):
+    x, z, y, half = vid >> 2, vid & 3, aud >> 1, aud & 1
+    offset = (x - y) & 3
+    to_y = (y - offset + 2 * (1 - (offset & 1))) & 3
+    return SIDE * y + 2 * half + (z & 1), 2 * to_y + (z >> 1)
+
+
 def prepare_kernel(aq_ref, ak_ref, av_ref, vq_ref, vk_ref, vv_ref, dv_ref, da_ref, audio, video_kv, queries, sems):
-    vid = lax.axis_index("vid")
+    to_vid, to_aud = audio_target(lax.axis_index("vid"), lax.axis_index("aud"))
     rows, width = vq_ref.shape[1:]
     audio_rows = da_ref.shape[1]
-    taken = pl.ds(pl.multiple_of(lax.rem(vid, 2) * audio_rows, audio_rows), audio_rows)
-    columns = pl.ds(pl.multiple_of(lax.div(vid, 2) * width, HEAD_DIM), width)
+    taken = pl.ds(pl.multiple_of((to_vid & 1) * audio_rows, audio_rows), audio_rows)
+    columns = pl.ds(pl.multiple_of(to_aud * width, HEAD_DIM), width)
     pairs = [(ref.at[0, taken, columns], audio.at[index]) for index, ref in enumerate((aq_ref, ak_ref, av_ref))]
     pairs += [(vk_ref.at[0], video_kv.at[0]), (vv_ref.at[0], video_kv.at[1])]
     pairs += [(vq_ref.at[0], queries.at[pl.ds(0, rows)]), (dv_ref.at[0], queries.at[pl.ds(rows, rows)])]
@@ -331,10 +338,13 @@
     )(*parts)
 
 
-def own_audio(array, vid_size, aud_size):
-    pairs = [
-        (v * aud_size + a, (2 * a + v % 2) * aud_size + v // 2) for v in range(vid_size) for a in range(aud_size)
-    ]
+def own_audio(array):
+    vid_size, aud_size = lax.axis_size("vid"), lax.axis_size("aud")
+    pairs = []
+    for vid in range(vid_size):
+        for aud in range(aud_size):
+            to_vid, to_aud = audio_target(vid, aud)
+            pairs.append((vid * aud_size + aud, to_vid * aud_size + to_aud))
     return lax.ppermute(array, ("vid", "aud"), pairs)
 
 
@@ -349,7 +359,6 @@
     video_q, video_k, video_v, audio_q, audio_k, audio_v, video_gate, audio_gate, audio_len, d_video_out, d_audio_out
 ):
     vid = lax.axis_index("vid")
-    sizes = lax.axis_size("vid"), lax.axis_size("aud")
     video_rows, audio_rows = video_q.shape[1], d_audio_out.shape[1]
     holds = audio_len[0] > 0
     send_audio, video_kv, queries = prepare(
@@ -357,7 +366,7 @@
     )
 
     def first_chunks(send_audio, video_kv, queries):
-        return own_audio(send_audio, *sizes), tuple(gathered(video_kv, along_z)[1:]), all_along_x(queries)
+        return own_audio(send_audio), tuple(gathered(video_kv, along_z)[1:]), all_along_x(queries)
 
     audio, video_keys, queries = fenced(holds, first_chunks, send_audio, video_kv, queries)
     video_keys = [video_kv, *video_keys]

time: 108 us -> 106 us (0.981)
  blocking collectives: 36.1 us -> 32.1 us
  starting transfers between devices: 30 us -> 33 us
    all_gather x1, blocking collectives: 20.8 us -> 16.5 us  [all_along_x(): return lax.all_gather(array, 'vid', axis=0, axis_index_groups=ALONG_X)]
    ppermute x9, starting transfers between devices: 15.5 us -> 17.7 us  [along_z(): return lax.ppermute(array, 'vid', pairs)]
    ppermute x1, starting transfers between devices: 1.3 us -> 2.91 us  [own_audio(): return lax.ppermute(array, ('vid', 'aud'), pairs)]
    ppermute x9, waiting for transfers between devices: 6.61 us -> 5.48 us  [along_z(): return lax.ppermute(array, 'vid', pairs)]
where the time goes in v10:
time: 106 us; the launch traced here: 105 us
  starting transfers between devices  33 us (31%)
  blocking collectives  32.1 us (30%)
  waiting for transfers between devices  17.6 us (17%)
  Pallas kernels  16.3 us (15%)
  local copies, waits for them, and re-layouts  4.26 us (4%)
  between operations  1.49 us (1%)
    ppermute x9, starting transfers between devices, along_z(): return lax.ppermute(array, 'vid', pairs)  17.7 us
    all_gather x1, blocking collectives, all_along_x(): return lax.all_gather(array, 'vid', axis=0, axis_index_groups=ALONG_X)  16.5 us
    all_to_all x1, blocking collectives, query_results(): lax.all_to_all(parts, 'vid', 0, 0, axis_index_groups=ALONG_X, tiled=True)  15.6 us
    ppermute x2, waiting for transfers between devices, beside_z(): return lax.ppermute(array, 'vid', pairs)  7.82 us
    pallas_call x1, Pallas kernels, attention_backward(): pl.pallas_call(functools.partial(backward_kernel, video_rows), grid=(head...  6.92 us
    pallas_call x1, Pallas kernels, attention_forward(): pl.pallas_call(functools.partial(forward_kernel, video_rows), grid=(heads...  6.61 us
    ppermute x1, starting transfers between devices, shards(): gate = gate + lax.ppermute(gate, 'pair', [(0, 1), (1, 0)])  6.46 us
    ppermute x6, starting transfers between devices, along_x(): return lax.ppermute(array, 'vid', pairs)  5.98 us
  transfers between devices with their start and end apart: 19, of which 6 were waited for; matrix products, arithmetic and copies ran while one was open for 3% of the time, Pallas kernels for 1%

profile of v10, /device:TPU:1, one launch (start us, length us, event | category | flops | bytes accessed | tf_op | source)
XLA Modules:
  0.0 105.4 jit_solution(16182546678359095316)
XLA Ops:
  1.3 1.2 %prepare.1 = (bf16[3,64,384]{2,1,0:T(8,128)(2,1)S(1)}, bf16[2,128,384]{2,1,0:T(8,128)(2,1)S(1)}, bf16[320,384]{1,0:T(8,128)(2,1)S(1)}) custom-call(bf16[1,128,3072]{2,1,0:T(8,128)(2,1)} %aq_ref.1, bf16[1,128,3072]{2,1,0:T(8,128)(2,1)} %ak_ref.1, bf16[1,128,3072]{2,1,0:T(8,128)(2,1)} %av_ref.1, bf16[1,128,384]{2,1,0:T(8,128)(2,1)} %vq_ref.1, ...), custom_call_target="tpu_custom_call" | custom-call | tf_op jit(solution)/shard_map/prepare/pallas_call | solution.py:115
  2.5 25.1 %conditional.2 = (bf16[3,64,384]{2,1,0:T(8,128)(2,1)}, bf16[2,128,384]{2,1,0:T(8,128)(2,1)}, bf16[2,128,384]{2,1,0:T(8,128)(2,1)}, bf16[2,128,384]{2,1,0:T(8,128)(2,1)}, bf16[4,320,384]{2,1,0:T(8,128)(2,1)S(1)}) conditional(s32[]{:T(128)} %convert_element_type.4, () %tuple.24, (bf16[3,64,384]{2,1,0:T(8,128)(2,1)S(1)}, ...), branch_computations={%region_0.0_spmd, %region_1.0_spmd} | conditional | bytes 4178120 | solution.py:353
  2.6 5.3 %collective-permute-start.3 = (bf16[2,128,384]{2,1,0:T(8,128)(2,1)S(1)}, bf16[2,128,384]{2,1,0:T(8,128)(2,1)}, u32[]{:S(2)}, u32[]{:S(2)}) collective-permute-start(bf16[2,128,384]{2,1,0:T(8,128)(2,1)S(1)} %get-tuple-element.8), channel_id=1, source_target_pairs={{0,48},{16,0},{32,16},{48,32},{64,112},{80,64},{96,80},{112,96},{1... | collective-permute-start | bytes 589832 | tf_op jit(solution)/shard_map/cond/branch_1_fun/ppermute | solution.py:29
  8.2 2.9 %collective-permute-start = (bf16[3,64,384]{2,1,0:T(8,128)(2,1)S(1)}, bf16[3,64,384]{2,1,0:T(8,128)(2,1)}, u32[]{:S(2)}, u32[]{:S(2)}) collective-permute-start(bf16[3,64,384]{2,1,0:T(8,128)(2,1)S(1)} %get-tuple-element.7), channel_id=1, source_target_pairs={{0,8},{2,40},{4,72},{6,104},{8,136},{10,168},{12,200},{14,232},{16... | collective-permute-start | bytes 442376 | tf_op jit(solution)/shard_map/cond/branch_1_fun/ppermute | solution.py:348
  11.1 16.5 %all-gather = bf16[1280,384]{1,0:T(8,128)(2,1)S(1)} all-gather(bf16[320,384]{1,0:T(8,128)(2,1)S(1)} %get-tuple-element.9), channel_id=2, replica_groups={{0,64,128,192},{16,80,144,208},{32,96,160,224},{48,112,176,240},{1,65,1..., dimensions={0}, use_global_device_ids=true | all-gather | bytes 1228800 | tf_op jit(solution)/shard_map/cond/branch_1_fun/all_gather | solution.py:38
  27.7 0.8 slice_bitcast_fusion.refs_9_
  28.5 0.9 collective-permute-start.11
  30.5 0.9 slice.16.refs_5_.refs_6_
  31.4 7.0 %collective-permute-start.8 = (bf16[2,64,384]{2,1,0:T(8,128)(2,1)S(1)}, bf16[2,64,384]{2,1,0:T(8,128)(2,1)S(1)}, u32[]{:S(2)}, u32[]{:S(2)}) collective-permute-start(bf16[2,64,384]{2,1,0:T(8,128)(2,1)S(1)} %slice.16.refs_5_.refs_6_), channel_id=1, source_target_pairs={{0,48},{16,0},{32,16},{48,32},{64,112},{80,64},{96,80},{112,96},{1... | collective-permute-start | bytes 294920 | tf_op jit(solution)/shard_map/ppermute | solution.py:29
  40.3 5.5 %collective-permute-done.7.refs_7_.refs_8_ = bf16[2,64,384]{2,1,0:T(8,128)(2,1)S(1)} collective-permute-done((bf16[2,64,384]{2,1,0:T(8,128)(2,1)S(1)}, bf16[2,64,384]{2,1,0:T(8,128)(2,1)S(1)}, u32[]{:S(2)}, u32[]{:S(2)}) %collective-permute-start.7) | collective-permute-done | bytes 98336 | tf_op jit(solution)/shard_map/ppermute | solution.py:29
  46.4 6.6 %forward.1 = (bf16[3,512,768]{2,1,0:T(8,128)(2,1)}, bf16[3,256,768]{2,1,0:T(8,128)(2,1)}, f32[3,2,128,768]{3,2,1,0:T(8,128)}, f32[3,4,768]{2,1,0:T(4,128)}, bf16[4,64,384]{2,1,0:T(8,128)(2,1)}) custom-call(bf16[4,320,384]{2,1,0:T(8,128)(2,1)S(1)} %get-tuple-element.50.refs_0_, bf16[2,128,384]{2,1,0:T(8,128)(2,1)S(1)} %get-tuple-element.51.refs_1_.refs_2_, ...), custom_call_target="tpu_custom_call" | custom-call | flops 905969664 | bytes 7077888 | tf_op jit(solution)/shard_map/forward/pallas_call | solution.py:258
  53.0 1.6 %collective-permute-start.14 = (f32[3,4,768]{2,1,0:T(4,128)}, f32[3,4,768]{2,1,0:T(4,128)S(1)}, u32[]{:S(2)}, u32[]{:S(2)}) collective-permute-start(f32[3,4,768]{2,1,0:T(4,128)} %get-tuple-element.57.refs_10_), channel_id=1, source_target_pairs={{0,192},{16,208},{32,224},{48,240},{64,0},{80,16},{96,32},{112,48}... | collective-permute-start | bytes 110600 | tf_op jit(solution)/shard_map/ppermute | solution.py:24
  54.6 1.6 %collective-permute-start.13 = (f32[3,4,768]{2,1,0:T(4,128)}, f32[3,4,768]{2,1,0:T(4,128)S(1)}, u32[]{:S(2)}, u32[]{:S(2)}) collective-permute-start(f32[3,4,768]{2,1,0:T(4,128)} %get-tuple-element.57.refs_10_), channel_id=1, source_target_pairs={{0,128},{16,144},{32,160},{48,176},{64,192},{80,208},{96,224},{112... | collective-permute-start | bytes 110600 | tf_op jit(solution)/shard_map/ppermute | solution.py:24
  56.9 2.2 %collective-permute-done.13.refs_12_ = f32[3,4,768]{2,1,0:T(4,128)S(1)} collective-permute-done((f32[3,4,768]{2,1,0:T(4,128)}, f32[3,4,768]{2,1,0:T(4,128)S(1)}, u32[]{:S(2)}, u32[]{:S(2)}) %collective-permute-start.13) | collective-permute-done | bytes 36896 | tf_op jit(solution)/shard_map/ppermute | solution.py:24
  59.1 1.3 %collective-permute-done.12.refs_11_ = f32[3,4,768]{2,1,0:T(4,128)S(1)} collective-permute-done((f32[3,4,768]{2,1,0:T(4,128)}, f32[3,4,768]{2,1,0:T(4,128)S(1)}, u32[]{:S(2)}, u32[]{:S(2)}) %collective-permute-start.12) | collective-permute-done | bytes 36896 | tf_op jit(solution)/shard_map/ppermute | solution.py:24
  61.0 6.9 %backward.1 = (bf16[2,192,384]{2,1,0:T(8,128)(2,1)}, bf16[2,192,384]{2,1,0:T(8,128)(2,1)}, bf16[2,192,384]{2,1,0:T(8,128)(2,1)}, bf16[2,192,384]{2,1,0:T(8,128)(2,1)}, bf16[4,400,384]{2,1,0:T(8,128)(2,1)S(1)}) custom-call(bf16[4,320,384]{2,1,0:T(8,128)(2,1)S(1)} %get-tuple-element.50.refs_0_, bf16[4,64,384]{2,1,0:T(8,128)(2,1)} %get-tuple-element.56.refs_1_, ...), custom_call_target="tpu_custom_call" | custom-call | flops 1811939328 | bytes 7077888 | tf_op jit(solution)/shard_map/backward/pallas_call | solution.py:276
  68.0 3.1 %collective-permute-start.16 = (bf16[2,192,384]{2,1,0:T(8,128)(2,1)}, bf16[2,192,384]{2,1,0:T(8,128)(2,1)S(1)}, u32[]{:S(2)}, u32[]{:S(2)}) collective-permute-start(bf16[2,192,384]{2,1,0:T(8,128)(2,1)} %get-tuple-element.67), channel_id=1, source_target_pairs={{0,32},{16,48},{32,0},{48,16},{64,96},{80,112},{96,64},{112,80},{1... | collective-permute-start | bytes 884744 | tf_op jit(solution)/shard_map/ppermute | solution.py:29
  71.2 1.4 %collective-permute-start.17 = (bf16[2,192,384]{2,1,0:T(8,128)(2,1)}, bf16[2,192,384]{2,1,0:T(8,128)(2,1)S(1)}, u32[]{:S(2)}, u32[]{:S(2)}) collective-permute-start(bf16[2,192,384]{2,1,0:T(8,128)(2,1)} %get-tuple-element.68), channel_id=1, source_target_pairs={{0,16},{16,32},{32,48},{48,0},{64,80},{80,96},{96,112},{112,64},{1... | collective-permute-start | bytes 884744 | tf_op jit(solution)/shard_map/ppermute | solution.py:29
  72.5 24.2 %conditional.3 = (bf16[1,128,384]{2,1,0:T(8,128)(2,1)}, bf16[1,64,384]{2,1,0:T(8,128)(2,1)}, bf16[1,128,384]{2,1,0:T(8,128)(2,1)}, bf16[1,64,384]{2,1,0:T(8,128)(2,1)}, f32[8,384]{1,0:T(8,128)S(1)}) conditional(s32[]{:T(128)} %convert_element_type.4, () %tuple.23, bf16[4,400,384]{2,1,0:T(8,128)(2,1)S(1)} %get-tuple-element.61), branch_computations={%region_2.3_spmd, %region_3.4_spmd} | conditional | flops 6144 | bytes 2629752 | solution.py:353
  72.5 15.6 %all_to_all.4.parts_ref = bf16[4,400,384]{2,1,0:T(8,128)(2,1)S(1)} all-to-all(bf16[4,400,384]{2,1,0:T(8,128)(2,1)S(1)} %param.3), channel_id=1, replica_groups={{0,64,128,192},{16,80,144,208},{32,96,160,224},{48,112,176,240},{1,65,1..., dimensions={0} | all-to-all | bytes 2457600 | tf_op jit(solution)/shard_map/cond/branch_1_fun/all_to_all | solution.py:388
  88.9 3.9 %collective-permute-done.4 = f32[8,384]{1,0:T(8,128)S(1)} collective-permute-done((f32[8,384]{1,0:T(8,128)S(1)}, f32[8,384]{1,0:T(8,128)S(1)}, u32[]{:S(2)}, u32[]{:S(2)}) %collective-permute-start.4) | collective-permute-done | bytes 12320 | tf_op jit(solution)/shard_map/cond/branch_1_fun/ppermute | solution.py:34
  92.8 3.9 %collective-permute-done.5 = f32[8,384]{1,0:T(8,128)S(1)} collective-permute-done((f32[8,384]{1,0:T(8,128)S(1)}, f32[8,384]{1,0:T(8,128)S(1)}, u32[]{:S(2)}, u32[]{:S(2)}) %collective-permute-start.5) | collective-permute-done | bytes 12320 | tf_op jit(solution)/shard_map/cond/branch_1_fun/ppermute | solution.py:34
  96.7 6.5 %collective-permute-start.18 = (f32[8,384]{1,0:T(8,128)S(1)}, f32[8,384]{1,0:T(8,128)S(1)}, u32[]{:S(2)}, u32[]{:S(2)}) collective-permute-start(f32[8,384]{1,0:T(8,128)S(1)} %get-tuple-element.74), channel_id=1, source_target_pairs={{0,1},{1,0},{2,3},{3,2},{4,5},{5,4},{6,7},{7,6},{8,9},{9,8},{10,11... | collective-permute-start | bytes 36872 | tf_op jit(solution)/shard_map/ppermute | solution.py:396
  103.2 0.8 collective-permute-done.18
  (61 shorter events, 7.6 us)
Async XLA Ops:
  2.5 35.9 %copy-start.9 = (f32[384]{0:T(512)S(1)}, f32[384]{0:T(512)}, u32[]{:S(2)}) copy-start(f32[384]{0:T(512)} %param.21) | copy-start | bytes 4612
  2.5 35.9 %copy-start.10 = (f32[384]{0:T(512)S(1)}, f32[384]{0:T(512)}, u32[]{:S(2)}) copy-start(f32[384]{0:T(512)} %param.22) | copy-start | bytes 4612
  2.6 25.1 %collective-permute-start.3 = (bf16[2,128,384]{2,1,0:T(8,128)(2,1)S(1)}, bf16[2,128,384]{2,1,0:T(8,128)(2,1)}, u32[]{:S(2)}, u32[]{:S(2)}) collective-permute-start(bf16[2,128,384]{2,1,0:T(8,128)(2,1)S(1)} %get-tuple-element.8), channel_id=1, source_target_pairs={{0,48},{16,0},{32,16},{48,32},{64,112},{80,64},{96,80},{112,96},{1... | collective-permute-start | bytes 589832 | tf_op jit(solution)/shard_map/cond/branch_1_fun/ppermute | solution.py:29
  7.8 19.8 %collective-permute-start.2 = (bf16[2,128,384]{2,1,0:T(8,128)(2,1)S(1)}, bf16[2,128,384]{2,1,0:T(8,128)(2,1)}, u32[]{:S(2)}, u32[]{:S(2)}) collective-permute-start(bf16[2,128,384]{2,1,0:T(8,128)(2,1)S(1)} %get-tuple-element.8), channel_id=1, source_target_pairs={{0,32},{16,48},{32,0},{48,16},{64,96},{80,112},{96,64},{112,80},{1... | collective-permute-start | bytes 589832 | tf_op jit(solution)/shard_map/cond/branch_1_fun/ppermute | solution.py:29
  7.8 19.9 %collective-permute-start.1 = (bf16[2,128,384]{2,1,0:T(8,128)(2,1)S(1)}, bf16[2,128,384]{2,1,0:T(8,128)(2,1)}, u32[]{:S(2)}, u32[]{:S(2)}) collective-permute-start(bf16[2,128,384]{2,1,0:T(8,128)(2,1)S(1)} %get-tuple-element.8), channel_id=1, source_target_pairs={{0,16},{16,32},{32,48},{48,0},{64,80},{80,96},{96,112},{112,64},{1... | collective-permute-start | bytes 589832 | tf_op jit(solution)/shard_map/cond/branch_1_fun/ppermute | solution.py:29
  8.2 19.5 %collective-permute-start = (bf16[3,64,384]{2,1,0:T(8,128)(2,1)S(1)}, bf16[3,64,384]{2,1,0:T(8,128)(2,1)}, u32[]{:S(2)}, u32[]{:S(2)}) collective-permute-start(bf16[3,64,384]{2,1,0:T(8,128)(2,1)S(1)} %get-tuple-element.7), channel_id=1, source_target_pairs={{0,8},{2,40},{4,72},{6,104},{8,136},{10,168},{12,200},{14,232},{16... | collective-permute-start | bytes 442376 | tf_op jit(solution)/shard_map/cond/branch_1_fun/ppermute | solution.py:348
  28.5 17.2 %copy-start.5 = (bf16[64,384]{1,0:T(8,128)(2,1)}, bf16[64,384]{1,0:T(8,128)(2,1)S(1)}, u32[]{:S(2)}) copy-start(bf16[64,384]{1,0:T(8,128)(2,1)S(1)} %slice_bitcast_fusion.refs_9_) | copy-start | bytes 147460
  28.5 10.0 %collective-permute-start.11 = (bf16[64,384]{1,0:T(8,128)(2,1)S(1)}, bf16[64,384]{1,0:T(8,128)(2,1)S(1)}, u32[]{:S(2)}, u32[]{:S(2)}) collective-permute-start(bf16[64,384]{1,0:T(8,128)(2,1)S(1)} %slice_bitcast_fusion.refs_9_), channel_id=1, source_target_pairs={{0,192},{16,208},{32,224},{48,240},{64,0},{80,16},{96,32},{112,48}... | collective-permute-start | bytes 147464 | tf_op jit(solution)/shard_map/ppermute | solution.py:24
  29.4 10.8 %collective-permute-start.10 = (bf16[64,384]{1,0:T(8,128)(2,1)S(1)}, bf16[64,384]{1,0:T(8,128)(2,1)S(1)}, u32[]{:S(2)}, u32[]{:S(2)}) collective-permute-start(bf16[64,384]{1,0:T(8,128)(2,1)S(1)} %slice_bitcast_fusion.refs_9_), channel_id=1, source_target_pairs={{0,128},{16,144},{32,160},{48,176},{64,192},{80,208},{96,224},{112... | collective-permute-start | bytes 147464 | tf_op jit(solution)/shard_map/ppermute | solution.py:24
  30.0 10.3 %collective-permute-start.9 = (bf16[64,384]{1,0:T(8,128)(2,1)S(1)}, bf16[64,384]{1,0:T(8,128)(2,1)S(1)}, u32[]{:S(2)}, u32[]{:S(2)}) collective-permute-start(bf16[64,384]{1,0:T(8,128)(2,1)S(1)} %slice_bitcast_fusion.refs_9_), channel_id=1, source_target_pairs={{0,64},{16,80},{32,96},{48,112},{64,128},{80,144},{96,160},{112,17... | collective-permute-start | bytes 147464 | tf_op jit(solution)/shard_map/ppermute | solution.py:24
  31.4 14.3 %copy-start.1 = (bf16[2,64,384]{2,1,0:T(8,128)(2,1)}, bf16[2,64,384]{2,1,0:T(8,128)(2,1)S(1)}, u32[]{:S(2)}) copy-start(bf16[2,64,384]{2,1,0:T(8,128)(2,1)S(1)} %slice.16.refs_5_.refs_6_) | copy-start | bytes 294916
  31.4 8.8 %collective-permute-start.8 = (bf16[2,64,384]{2,1,0:T(8,128)(2,1)S(1)}, bf16[2,64,384]{2,1,0:T(8,128)(2,1)S(1)}, u32[]{:S(2)}, u32[]{:S(2)}) collective-permute-start(bf16[2,64,384]{2,1,0:T(8,128)(2,1)S(1)} %slice.16.refs_5_.refs_6_), channel_id=1, source_target_pairs={{0,48},{16,0},{32,16},{48,32},{64,112},{80,64},{96,80},{112,96},{1... | collective-permute-start | bytes 294920 | tf_op jit(solution)/shard_map/ppermute | solution.py:29
  38.4 7.3 %collective-permute-start.7 = (bf16[2,64,384]{2,1,0:T(8,128)(2,1)S(1)}, bf16[2,64,384]{2,1,0:T(8,128)(2,1)S(1)}, u32[]{:S(2)}, u32[]{:S(2)}) collective-permute-start(bf16[2,64,384]{2,1,0:T(8,128)(2,1)S(1)} %slice.16.refs_5_.refs_6_), channel_id=1, source_target_pairs={{0,32},{16,48},{32,0},{48,16},{64,96},{80,112},{96,64},{112,80},{1... | collective-permute-start | bytes 294920 | tf_op jit(solution)/shard_map/ppermute | solution.py:29
  38.5 7.2 %collective-permute-start.6 = (bf16[2,64,384]{2,1,0:T(8,128)(2,1)S(1)}, bf16[2,64,384]{2,1,0:T(8,128)(2,1)S(1)}, u32[]{:S(2)}, u32[]{:S(2)}) collective-permute-start(bf16[2,64,384]{2,1,0:T(8,128)(2,1)S(1)} %slice.16.refs_5_.refs_6_), channel_id=1, source_target_pairs={{0,16},{16,32},{32,48},{48,0},{64,80},{80,96},{96,112},{112,64},{1... | collective-permute-start | bytes 294920 | tf_op jit(solution)/shard_map/ppermute | solution.py:29
  53.0 3.9 %collective-permute-start.14 = (f32[3,4,768]{2,1,0:T(4,128)}, f32[3,4,768]{2,1,0:T(4,128)S(1)}, u32[]{:S(2)}, u32[]{:S(2)}) collective-permute-start(f32[3,4,768]{2,1,0:T(4,128)} %get-tuple-element.57.refs_10_), channel_id=1, source_target_pairs={{0,192},{16,208},{32,224},{48,240},{64,0},{80,16},{96,32},{112,48}... | collective-permute-start | bytes 110600 | tf_op jit(solution)/shard_map/ppermute | solution.py:24
  54.6 4.5 %collective-permute-start.13 = (f32[3,4,768]{2,1,0:T(4,128)}, f32[3,4,768]{2,1,0:T(4,128)S(1)}, u32[]{:S(2)}, u32[]{:S(2)}) collective-permute-start(f32[3,4,768]{2,1,0:T(4,128)} %get-tuple-element.57.refs_10_), channel_id=1, source_target_pairs={{0,128},{16,144},{32,160},{48,176},{64,192},{80,208},{96,224},{112... | collective-permute-start | bytes 110600 | tf_op jit(solution)/shard_map/ppermute | solution.py:24
  56.2 4.2 %collective-permute-start.12 = (f32[3,4,768]{2,1,0:T(4,128)}, f32[3,4,768]{2,1,0:T(4,128)S(1)}, u32[]{:S(2)}, u32[]{:S(2)}) collective-permute-start(f32[3,4,768]{2,1,0:T(4,128)} %get-tuple-element.57.refs_10_), channel_id=1, source_target_pairs={{0,64},{16,80},{32,96},{48,112},{64,128},{80,144},{96,160},{112,17... | collective-permute-start | bytes 110600 | tf_op jit(solution)/shard_map/ppermute | solution.py:24
  67.9 36.7 %collective-permute-start.15 = (bf16[2,192,384]{2,1,0:T(8,128)(2,1)}, bf16[2,192,384]{2,1,0:T(8,128)(2,1)S(1)}, u32[]{:S(2)}, u32[]{:S(2)}) collective-permute-start(bf16[2,192,384]{2,1,0:T(8,128)(2,1)} %get-tuple-element.66), channel_id=1, source_target_pairs={{0,48},{16,0},{32,16},{48,32},{64,112},{80,64},{96,80},{112,96},{1... | collective-permute-start | bytes 884744 | tf_op jit(solution)/shard_map/ppermute | solution.py:29
  68.0 36.6 %collective-permute-start.16 = (bf16[2,192,384]{2,1,0:T(8,128)(2,1)}, bf16[2,192,384]{2,1,0:T(8,128)(2,1)S(1)}, u32[]{:S(2)}, u32[]{:S(2)}) collective-permute-start(bf16[2,192,384]{2,1,0:T(8,128)(2,1)} %get-tuple-element.67), channel_id=1, source_target_pairs={{0,32},{16,48},{32,0},{48,16},{64,96},{80,112},{96,64},{112,80},{1... | collective-permute-start | bytes 884744 | tf_op jit(solution)/shard_map/ppermute | solution.py:29
  71.2 33.5 %collective-permute-start.17 = (bf16[2,192,384]{2,1,0:T(8,128)(2,1)}, bf16[2,192,384]{2,1,0:T(8,128)(2,1)S(1)}, u32[]{:S(2)}, u32[]{:S(2)}) collective-permute-start(bf16[2,192,384]{2,1,0:T(8,128)(2,1)} %get-tuple-element.68), channel_id=1, source_target_pairs={{0,16},{16,32},{32,48},{48,0},{64,80},{80,96},{96,112},{112,64},{1... | collective-permute-start | bytes 884744 | tf_op jit(solution)/shard_map/ppermute | solution.py:29
  72.5 32.1 %copy-start = (bf16[2,192,384]{2,1,0:T(8,128)(2,1)S(1)}, bf16[2,192,384]{2,1,0:T(8,128)(2,1)}, u32[]{:S(2)}) copy-start(bf16[2,192,384]{2,1,0:T(8,128)(2,1)} %get-tuple-element.65.refs_0_) | copy-start | bytes 884740
  88.9 3.9 %collective-permute-start.4 = (f32[8,384]{1,0:T(8,128)S(1)}, f32[8,384]{1,0:T(8,128)S(1)}, u32[]{:S(2)}, u32[]{:S(2)}) collective-permute-start(f32[8,384]{1,0:T(8,128)S(1)} %get-tuple-element.14), channel_id=1, source_target_pairs={{0,16},{16,0},{32,48},{48,32},{64,80},{80,64},{96,112},{112,96},{1... | collective-permute-start | bytes 36872 | tf_op jit(solution)/shard_map/cond/branch_1_fun/ppermute | solution.py:34
  92.8 3.9 %collective-permute-start.5 = (f32[8,384]{1,0:T(8,128)S(1)}, f32[8,384]{1,0:T(8,128)S(1)}, u32[]{:S(2)}, u32[]{:S(2)}) collective-permute-start(f32[8,384]{1,0:T(8,128)S(1)} %add.29), channel_id=1, source_target_pairs={{0,32},{16,48},{32,0},{48,16},{64,96},{80,112},{96,64},{112,80},{1... | collective-permute-start | bytes 36872 | tf_op jit(solution)/shard_map/cond/branch_1_fun/ppermute | solution.py:34
  96.7 7.3 %collective-permute-start.18 = (f32[8,384]{1,0:T(8,128)S(1)}, f32[8,384]{1,0:T(8,128)S(1)}, u32[]{:S(2)}, u32[]{:S(2)}) collective-permute-start(f32[8,384]{1,0:T(8,128)S(1)} %get-tuple-element.74), channel_id=1, source_target_pairs={{0,1},{1,0},{2,3},{3,2},{4,5},{5,4},{6,7},{7,6},{8,9},{9,8},{10,11... | collective-permute-start | bytes 36872 | tf_op jit(solution)/shard_map/ppermute | solution.py:396
  (9 other events, 30.5 us)

commit v11 on v10

--- a/solution.py
+++ b/solution.py
@@ -15,6 +15,7 @@
 VIDEO, AUDIO = 0, 1
 GATE_ROWS = 16
 VMEM = 60 * 2**20
+LOG2_E = 1.4426950408889634
 
 ALONG_X = [[x * SIDE + z for x in range(SIDE)] for z in range(SIDE)]
 
@@ -123,46 +124,62 @@
     )(*given)
 
 
+def scores(keys, queries, part, numbers_ref):
+    raw = nt(keys, queries)
+    if part == AUDIO:
+        rows = raw.shape[0] // SIDE
+        position = lax.broadcasted_iota(jnp.int32, (rows, raw.shape[1]), 0)
+        pieces = [raw[place * rows : (place + 1) * rows] for place in range(SIDE)]
+        pieces = [jnp.where(position < numbers_ref[place], pieces[place], -1e30) for place in range(SIDE)]
+        raw = jnp.concatenate(pieces, axis=0)
+    return raw
+
+
+def attend(raw, values, up):
+    peak = jnp.max(raw, axis=0, keepdims=True)
+    expon = jnp.exp2((raw - peak) * (SCALE * LOG2_E))
+    total = jnp.sum(expon, axis=0, keepdims=True)
+    output = nn(values.T, expon.astype(BF16)) * (1.0 / total)
+    delta = jnp.sum(up.T.astype(F32) * output, axis=0, keepdims=True)
+    return output.astype(BF16), jnp.concatenate([peak * SCALE + jnp.log(total), delta], axis=0)
+
+
+def forward_video_kernel(video_rows, *refs):
+    gathered_ref, k_refs, o_ref, stats_ref = refs[0], refs[1:5], refs[5], refs[6]
+    raw = scores(joined(k_refs, 0), flat(gathered_ref[:, :video_rows]), VIDEO, None)
+    o_ref[0], stats_ref[0] = attend(raw, joined(k_refs, 1), upstreams_of(gathered_ref, video_rows)[0])
+
+
 def forward_kernel(video_rows, *refs):
     gathered_ref, k_refs, audio_q, numbers_ref, gates_ref = refs[0], (refs[1:5], refs[5:9]), refs[9:13], refs[13], refs[14]
-    e_refs, o_ref, stats_ref, ordered_ref = refs[15:17], refs[17], refs[18], refs[19]
+    o_video_ref, stats_video_ref, o_ref, stats_ref, ordered_ref = refs[15:20]
     for place in range(SIDE):
         ordered_ref[lax.rem(numbers_ref[SIDE] + SIDE - place, SIDE)] = audio_q[place][...]
-    queries = queries_of(gathered_ref, ordered_ref, video_rows)
-    stats = []
-    for part in (VIDEO, AUDIO):
-        raw = nt(joined(k_refs[part], 0), queries)
-        if part == AUDIO:
-            rows = k_refs[part][0].shape[1]
-            position = lax.broadcasted_iota(jnp.int32, (rows, raw.shape[1]), 0)
-            pieces = [raw[place * rows : (place + 1) * rows] for place in range(SIDE)]
-            pieces = [jnp.where(position < numbers_ref[place], pieces[place], -1e30) for place in range(SIDE)]
-            raw = jnp.concatenate(pieces, axis=0)
-        peak = jnp.max(raw, axis=0, keepdims=True)
-        expon = jnp.exp((raw - peak) * SCALE)
-        total = jnp.sum(expon, axis=0, keepdims=True)
-        expon = (expon * (1.0 / total)).astype(BF16)
-        e_refs[part][0] = expon
-        output = nn(joined(k_refs[part], 1).T, expon)
-        o_ref[0, part] = output
-        up = upstream(gathered_ref, gates_ref, video_rows, part)
-        stats.append(peak * SCALE + jnp.log(total))
-        stats.append(jnp.sum(up.astype(F32).T * output, axis=0, keepdims=True))
-    stats_ref[0] = jnp.concatenate(stats, axis=0)
+    up_audio = gated(upstreams_of(gathered_ref, video_rows)[1], gates_ref[1:2, :])
+    raw = scores(joined(k_refs[VIDEO], 0), flat(ordered_ref[...]), VIDEO, None)
+    output, stats = attend(raw, joined(k_refs[VIDEO], 1), up_audio)
+    o_ref[0, VIDEO] = jnp.concatenate([o_video_ref[0], output], axis=1)
+    stats_video = jnp.concatenate([stats_video_ref[0], stats], axis=1)
+    raw = scores(joined(k_refs[AUDIO], 0), queries_of(gathered_ref, ordered_ref, video_rows), AUDIO, numbers_ref)
+    up = upstream(gathered_ref, gates_ref, video_rows, AUDIO)
+    o_ref[0, AUDIO], stats = attend(raw, joined(k_refs[AUDIO], 1), up)
+    stats_ref[0] = jnp.concatenate([stats_video, stats], axis=0)
 
 
 def merged_stats(refs, part):
     logs = [ref[0, 2 * part : 2 * part + 1] for ref in refs]
     peak = functools.reduce(jnp.maximum, logs)
     weights = [jnp.exp(local - peak) for local in logs]
-    scale = 1.0 / sum(weights)
+    total = sum(weights)
+    scale = 1.0 / total
     delta = sum(weight * ref[0, 2 * part + 1 : 2 * part + 2] for weight, ref in zip(weights, refs)) * scale
-    return weights[0] * scale, delta
-
-
-def backward_keys(part, queries, up, stats_refs, k_refs, e_ref, k_outs, first):
-    factor, delta = merged_stats(stats_refs, part)
-    probs = e_ref[0].astype(F32) * factor
+    return peak + jnp.log(total), delta, weights[0] * scale
+
+
+def backward_keys(part, queries, up, stats_refs, k_refs, numbers_ref, k_outs, first):
+    log_total, delta, factor = merged_stats(stats_refs, part)
+    raw = scores(joined(k_refs, 0), queries, part, numbers_ref)
+    probs = jnp.exp2(raw * (SCALE * LOG2_E) - log_total * LOG2_E)
     grad_values = nn(probs.astype(BF16), up).astype(BF16)
     grad_probs = nt(joined(k_refs, 1), up)
     grad_scores = (probs * (grad_probs - delta)).astype(BF16)
@@ -180,18 +197,18 @@
 
 def backward_kernel(video_rows, *refs):
     gathered_ref, audio_q, k_video, k_audio, stats_refs = refs[0], refs[1], refs[2:6], refs[6:10], refs[10:14]
-    gates_ref, e_video, e_audio, o_ref = refs[14:18]
-    k_outs, q_out = refs[18:22], refs[22]
+    gates_ref, numbers_ref, o_ref = refs[14:17]
+    k_outs, q_out = refs[17:21], refs[21]
     audio_rows = audio_q.shape[1]
     rows = video_rows + audio_rows
     video = SIDE * video_rows
     queries = queries_of(gathered_ref, audio_q, video_rows)
     up = upstream(gathered_ref, gates_ref, video_rows, VIDEO)
-    term_video, factor = backward_keys(VIDEO, queries, up, stats_refs, k_video, e_video, k_outs, 0)
-    on_video = o_ref[0, VIDEO] * factor
+    term_video, factor = backward_keys(VIDEO, queries, up, stats_refs, k_video, numbers_ref, k_outs, 0)
+    on_video = o_ref[0, VIDEO].astype(F32) * factor
     up = upstream(gathered_ref, gates_ref, video_rows, AUDIO)
-    term_audio, factor = backward_keys(AUDIO, queries, up, stats_refs, k_audio, e_audio, k_outs, video_rows)
-    on_audio = o_ref[0, AUDIO] * factor
+    term_audio, factor = backward_keys(AUDIO, queries, up, stats_refs, k_audio, numbers_ref, k_outs, video_rows)
+    on_audio = o_ref[0, AUDIO].astype(F32) * factor
     grad_queries = term_video + term_audio
     cross_video, cross_audio = on_audio[:, :video], on_video[:, video:]
     merged = jnp.concatenate(
@@ -202,8 +219,8 @@
         axis=1,
     )
     up_video, up_audio = upstreams_of(gathered_ref, video_rows)
-    video_sum = jnp.sum(up_video.astype(F32).T * cross_video, axis=1, keepdims=True)
-    audio_sum = jnp.sum(up_audio.astype(F32).T * cross_audio, axis=1, keepdims=True)
+    video_sum = jnp.sum(up_video.T.astype(F32) * cross_video, axis=1, keepdims=True)
+    audio_sum = jnp.sum(up_audio.T.astype(F32) * cross_audio, axis=1, keepdims=True)
     sums = jnp.concatenate(
         [jnp.broadcast_to(video_sum, (HEAD_DIM, 4)), jnp.broadcast_to(audio_sum, (HEAD_DIM, HEAD_DIM - 4))], axis=1
     ).T[0:GATE_ROWS]
@@ -211,8 +228,8 @@
     low = (sums - high.astype(F32)).astype(BF16)
     even = lax.broadcasted_iota(jnp.int32, sums.shape, 0) % 2 == 0
     sums = jnp.where(even, high.astype(F32), low.astype(F32)).astype(BF16)
-    merged = merged.T.astype(BF16)
-    grad_queries = (grad_queries.T * SCALE).astype(BF16)
+    merged = merged.astype(BF16).T
+    grad_queries = (grad_queries * SCALE).astype(BF16).T
     for index, array in ((0, merged), (1, grad_queries)):
         first = index * rows
         q_out[:, first : first + video_rows] = array[:video].reshape(SIDE, video_rows, HEAD_DIM)
@@ -242,32 +259,45 @@
     )
 
 
-def attention_forward(queries, audio_q, video_keys, audio_keys, numbers, gates, video_rows):
+def attention_forward_video(queries, video_keys, video_rows):
+    heads = queries.shape[2] // HEAD_DIM
+    video = SIDE * video_rows
+    outs = [like(heads, HEAD_DIM, video), like(heads, 2, video, kind=F32)]
+    chunks = [queries, *video_keys]
+    return pl.pallas_call(
+        functools.partial(forward_video_kernel, video_rows),
+        grid=(heads,),
+        in_specs=[chunk_spec(array) for array in chunks],
+        out_specs=[head_spec(array) for array in outs],
+        out_shape=outs,
+        cost_estimate=cost(video, video, heads, 2),
+        compiler_params=pltpu.CompilerParams(vmem_limit_bytes=VMEM),
+        name="forward_video",
+    )(*chunks)
+
+
+def attention_forward(queries, audio_q, video_keys, audio_keys, numbers, gates, earlier, video_rows):
     heads = gates.shape[1] // HEAD_DIM
     audio_rows, width = audio_q[0].shape
-    video, audio = SIDE * video_rows, SIDE * audio_rows
-    total = video + audio
-    outs = [
-        like(heads, video, total),
-        like(heads, audio, total),
-        like(heads, 2, HEAD_DIM, total, kind=F32),
-        like(heads, 4, total, kind=F32),
-    ]
+    total = SIDE * (video_rows + audio_rows)
+    outs = [like(heads, 2, HEAD_DIM, total), like(heads, 4, total, kind=F32)]
     ordered = like(SIDE, audio_rows, width)
     chunks = [queries, *video_keys, *audio_keys, *audio_q]
     return pl.pallas_call(
         functools.partial(forward_kernel, video_rows),
         grid=(heads,),
-        in_specs=[chunk_spec(array) for array in chunks] + [pl.BlockSpec(memory_space=pltpu.SMEM), chunk_spec(gates)],
+        in_specs=[chunk_spec(array) for array in chunks]
+        + [pl.BlockSpec(memory_space=pltpu.SMEM), chunk_spec(gates)]
+        + [head_spec(array) for array in earlier],
         out_specs=[head_spec(array) for array in outs] + [chunk_spec(ordered)],
         out_shape=[*outs, ordered],
-        cost_estimate=cost(total, total, heads, 2),
+        cost_estimate=cost(total, total, heads, 1),
         compiler_params=pltpu.CompilerParams(vmem_limit_bytes=VMEM),
         name="forward",
-    )(*chunks, numbers, gates)
-
-
-def attention_backward(queries, audio_q, video_keys, audio_keys, stats, gates, by_head, video_rows):
+    )(*chunks, numbers, gates, *earlier)
+
+
+def attention_backward(queries, audio_q, video_keys, audio_keys, stats, gates, numbers, outputs, video_rows):
     width = gates.shape[1]
     heads = width // HEAD_DIM
     rows = video_rows + audio_q.shape[1]
@@ -278,14 +308,13 @@
         grid=(heads,),
         in_specs=[chunk_spec(array) for array in chunks]
         + [head_spec(array) for array in stats]
-        + [chunk_spec(gates)]
-        + [head_spec(array) for array in by_head],
+        + [chunk_spec(gates), pl.BlockSpec(memory_space=pltpu.SMEM), head_spec(outputs)],
         out_specs=[chunk_spec(array) for array in outs],
         out_shape=outs,
         cost_estimate=cost(SIDE * rows, SIDE * rows, heads, 4),
         compiler_params=pltpu.CompilerParams(vmem_limit_bytes=VMEM),
         name="backward",
-    )(*chunks, *stats, gates, *by_head)
+    )(*chunks, *stats, gates, numbers, outputs)
     return key_parts, query_parts
 
 
@@ -377,11 +406,12 @@
     column, row = vid // SIDE, vid % SIDE
     limits = [audio_len[0] - (column * SIDE + (row - p) % SIDE) * audio_rows for p in range(SIDE)]
     numbers = jnp.stack([*limits, column])
-    *by_head, stats, audio_queries = attention_forward(
-        queries, audio_queries, video_keys, audio_keys, numbers, gates, video_rows
+    earlier = attention_forward_video(queries, video_keys, video_rows)
+    outputs, stats, audio_queries = attention_forward(
+        queries, audio_queries, video_keys, audio_keys, numbers, gates, earlier, video_rows
     )
     key_parts, query_parts = attention_backward(
-        queries, audio_queries, video_keys, audio_keys, gathered(stats, along_x), gates, by_head, video_rows
+        queries, audio_queries, video_keys, audio_keys, gathered(stats, along_x), gates, numbers, outputs, video_rows
     )
 
     def query_results(parts):

time: 106 us -> 105 us (level)
  waiting for transfers between devices: 17.6 us -> 13.7 us
  Pallas kernels: 16.3 us -> 19.3 us
    pallas_call x0 -> x1, Pallas kernels: none -> 3.94 us  [attention_forward_video(): pl.pallas_call(functools.partial(forward_video_kernel, video_rows), grid=...]
    ppermute x9, waiting for transfers between devices: 5.48 us -> 1.58 us  [along_z(): return lax.ppermute(array, 'vid', pairs)]
    pallas_call x1, Pallas kernels: 6.61 us -> 5.27 us  [attention_forward(): pl.pallas_call(functools.partial(forward_kernel, video_rows), grid=(heads...]
  transfers between devices with their start and end apart: 19 -> 19, of which waited for: 6 -> 6; matrix products, arithmetic and copies ran while one was open for 3% -> 3% of each run, Pallas kernels for 1% -> 5%
where the time goes in v11:
time: 105 us; the launch traced here: 104 us
  starting transfers between devices  33 us (31%)
  blocking collectives  32.1 us (31%)
  Pallas kernels  19.3 us (18%)
  waiting for transfers between devices  13.7 us (13%)
  local copies, waits for them, and re-layouts  4.2 us (4%)
  between operations  1.49 us (1%)
    ppermute x9, starting transfers between devices, along_z(): return lax.ppermute(array, 'vid', pairs)  17.7 us
    all_gather x1, blocking collectives, all_along_x(): return lax.all_gather(array, 'vid', axis=0, axis_index_groups=ALONG_X)  16.5 us
    all_to_all x1, blocking collectives, query_results(): lax.all_to_all(parts, 'vid', 0, 0, axis_index_groups=ALONG_X, tiled=True)  15.6 us
    ppermute x2, waiting for transfers between devices, beside_z(): return lax.ppermute(array, 'vid', pairs)  7.82 us
    pallas_call x1, Pallas kernels, attention_backward(): pl.pallas_call(functools.partial(backward_kernel, video_rows), grid=(head...  7.29 us
    ppermute x1, starting transfers between devices, shards(): gate = gate + lax.ppermute(gate, 'pair', [(0, 1), (1, 0)])  6.46 us
    ppermute x6, starting transfers between devices, along_x(): return lax.ppermute(array, 'vid', pairs)  5.97 us
    pallas_call x1, Pallas kernels, attention_forward(): pl.pallas_call(functools.partial(forward_kernel, video_rows), grid=(heads...  5.27 us
  transfers between devices with their start and end apart: 19, of which 6 were waited for; matrix products, arithmetic and copies ran while one was open for 3% of the time, Pallas kernels for 5%

profile of v11, /device:TPU:1, one launch (start us, length us, event | category | flops | bytes accessed | tf_op | source)
XLA Modules:
  0.0 104.5 jit_solution(10969616828182505478)
XLA Ops:
  1.3 1.2 %prepare.1 = (bf16[3,64,384]{2,1,0:T(8,128)(2,1)S(1)}, bf16[2,128,384]{2,1,0:T(8,128)(2,1)S(1)}, bf16[320,384]{1,0:T(8,128)(2,1)S(1)}) custom-call(bf16[1,128,3072]{2,1,0:T(8,128)(2,1)} %aq_ref.1, bf16[1,128,3072]{2,1,0:T(8,128)(2,1)} %ak_ref.1, bf16[1,128,3072]{2,1,0:T(8,128)(2,1)} %av_ref.1, bf16[1,128,384]{2,1,0:T(8,128)(2,1)} %vq_ref.1, ...), custom_call_target="tpu_custom_call" | custom-call | tf_op jit(solution)/shard_map/prepare/pallas_call | solution.py:116
  2.5 25.1 %conditional.2 = (bf16[3,64,384]{2,1,0:T(8,128)(2,1)}, bf16[2,128,384]{2,1,0:T(8,128)(2,1)}, bf16[2,128,384]{2,1,0:T(8,128)(2,1)}, bf16[2,128,384]{2,1,0:T(8,128)(2,1)}, bf16[4,320,384]{2,1,0:T(8,128)(2,1)S(1)}) conditional(s32[]{:T(128)} %convert_element_type.4, () %tuple.24, (bf16[3,64,384]{2,1,0:T(8,128)(2,1)S(1)}, ...), branch_computations={%region_0.0_spmd, %region_1.0_spmd} | conditional | bytes 4178120 | solution.py:382
  2.6 5.3 %collective-permute-start.3 = (bf16[2,128,384]{2,1,0:T(8,128)(2,1)S(1)}, bf16[2,128,384]{2,1,0:T(8,128)(2,1)}, u32[]{:S(2)}, u32[]{:S(2)}) collective-permute-start(bf16[2,128,384]{2,1,0:T(8,128)(2,1)S(1)} %get-tuple-element.8), channel_id=1, source_target_pairs={{0,48},{16,0},{32,16},{48,32},{64,112},{80,64},{96,80},{112,96},{1... | collective-permute-start | bytes 589832 | tf_op jit(solution)/shard_map/cond/branch_1_fun/ppermute | solution.py:30
  8.2 2.9 %collective-permute-start = (bf16[3,64,384]{2,1,0:T(8,128)(2,1)S(1)}, bf16[3,64,384]{2,1,0:T(8,128)(2,1)}, u32[]{:S(2)}, u32[]{:S(2)}) collective-permute-start(bf16[3,64,384]{2,1,0:T(8,128)(2,1)S(1)} %get-tuple-element.7), channel_id=1, source_target_pairs={{0,8},{2,40},{4,72},{6,104},{8,136},{10,168},{12,200},{14,232},{16... | collective-permute-start | bytes 442376 | tf_op jit(solution)/shard_map/cond/branch_1_fun/ppermute | solution.py:377
  11.1 16.5 %all-gather = bf16[1280,384]{1,0:T(8,128)(2,1)S(1)} all-gather(bf16[320,384]{1,0:T(8,128)(2,1)S(1)} %get-tuple-element.9), channel_id=2, replica_groups={{0,64,128,192},{16,80,144,208},{32,96,160,224},{48,112,176,240},{1,65,1..., dimensions={0}, use_global_device_ids=true | all-gather | bytes 1228800 | tf_op jit(solution)/shard_map/cond/branch_1_fun/all_gather | solution.py:39
  28.5 0.9 collective-permute-start.11
  30.5 0.9 slice.16.refs_5_.refs_6_
  31.4 7.0 %collective-permute-start.8 = (bf16[2,64,384]{2,1,0:T(8,128)(2,1)S(1)}, bf16[2,64,384]{2,1,0:T(8,128)(2,1)S(1)}, u32[]{:S(2)}, u32[]{:S(2)}) collective-permute-start(bf16[2,64,384]{2,1,0:T(8,128)(2,1)S(1)} %slice.16.refs_5_.refs_6_), channel_id=1, source_target_pairs={{0,48},{16,0},{32,16},{48,32},{64,112},{80,64},{96,80},{112,96},{1... | collective-permute-start | bytes 294920 | tf_op jit(solution)/shard_map/ppermute | solution.py:30
  40.2 3.9 %forward_video.1 = (bf16[3,128,512]{2,1,0:T(8,128)(2,1)}, f32[3,2,512]{2,1,0:T(2,128)}) custom-call(bf16[4,320,384]{2,1,0:T(8,128)(2,1)S(1)} %get-tuple-element.50.refs_0_, bf16[2,128,384]{2,1,0:T(8,128)(2,1)S(1)} %get-tuple-element.51.refs_1_.refs_2_, bf16[2,128,384]{2,1,0:T(8,128)(2,1)} %get-tuple-element.52.refs_2_.refs_3_, ...), custom_call_target="tpu_custom_call" | custom-call | flops 402653184 | bytes 3145728 | tf_op jit(solution)/shard_map/forward_video/pallas_call | solution.py:267
  44.2 1.6 %collective-permute-done.7.refs_7_.refs_8_ = bf16[2,64,384]{2,1,0:T(8,128)(2,1)S(1)} collective-permute-done((bf16[2,64,384]{2,1,0:T(8,128)(2,1)S(1)}, bf16[2,64,384]{2,1,0:T(8,128)(2,1)S(1)}, u32[]{:S(2)}, u32[]{:S(2)}) %collective-permute-start.7) | collective-permute-done | bytes 98336 | tf_op jit(solution)/shard_map/ppermute | solution.py:30
  46.4 5.3 %forward.1 = (bf16[3,2,128,768]{3,2,1,0:T(8,128)(2,1)}, f32[3,4,768]{2,1,0:T(4,128)}, bf16[4,64,384]{2,1,0:T(8,128)(2,1)}) custom-call(bf16[4,320,384]{2,1,0:T(8,128)(2,1)S(1)} %get-tuple-element.50.refs_0_, bf16[2,128,384]{2,1,0:T(8,128)(2,1)S(1)} %get-tuple-element.51.refs_1_.refs_2_, bf16[2,128,384]{2,1,0:T(8,128)(2,1)} %get-tuple-element.52.refs_2_.refs_3_, ...), custom_call_target="tpu_custom_call" | custom-call | flops 452984832 | bytes 7077888 | tf_op jit(solution)/shard_map/forward/pallas_call | solution.py:286
  51.7 1.6 %collective-permute-start.14 = (f32[3,4,768]{2,1,0:T(4,128)}, f32[3,4,768]{2,1,0:T(4,128)S(1)}, u32[]{:S(2)}, u32[]{:S(2)}) collective-permute-start(f32[3,4,768]{2,1,0:T(4,128)} %get-tuple-element.59.refs_10_), channel_id=1, source_target_pairs={{0,192},{16,208},{32,224},{48,240},{64,0},{80,16},{96,32},{112,48}... | collective-permute-start | bytes 110600 | tf_op jit(solution)/shard_map/ppermute | solution.py:25
  53.2 1.6 %collective-permute-start.13 = (f32[3,4,768]{2,1,0:T(4,128)}, f32[3,4,768]{2,1,0:T(4,128)S(1)}, u32[]{:S(2)}, u32[]{:S(2)}) collective-permute-start(f32[3,4,768]{2,1,0:T(4,128)} %get-tuple-element.59.refs_10_), channel_id=1, source_target_pairs={{0,128},{16,144},{32,160},{48,176},{64,192},{80,208},{96,224},{112... | collective-permute-start | bytes 110600 | tf_op jit(solution)/shard_map/ppermute | solution.py:25
  55.6 2.2 %collective-permute-done.13.refs_12_ = f32[3,4,768]{2,1,0:T(4,128)S(1)} collective-permute-done((f32[3,4,768]{2,1,0:T(4,128)}, f32[3,4,768]{2,1,0:T(4,128)S(1)}, u32[]{:S(2)}, u32[]{:S(2)}) %collective-permute-start.13) | collective-permute-done | bytes 36896 | tf_op jit(solution)/shard_map/ppermute | solution.py:25
  57.8 1.3 %collective-permute-done.12.refs_11_ = f32[3,4,768]{2,1,0:T(4,128)S(1)} collective-permute-done((f32[3,4,768]{2,1,0:T(4,128)}, f32[3,4,768]{2,1,0:T(4,128)S(1)}, u32[]{:S(2)}, u32[]{:S(2)}) %collective-permute-start.12) | collective-permute-done | bytes 36896 | tf_op jit(solution)/shard_map/ppermute | solution.py:25
  59.7 7.3 %backward.1 = (bf16[2,192,384]{2,1,0:T(8,128)(2,1)}, bf16[2,192,384]{2,1,0:T(8,128)(2,1)}, bf16[2,192,384]{2,1,0:T(8,128)(2,1)}, bf16[2,192,384]{2,1,0:T(8,128)(2,1)}, bf16[4,400,384]{2,1,0:T(8,128)(2,1)S(1)}) custom-call(bf16[4,320,384]{2,1,0:T(8,128)(2,1)S(1)} %get-tuple-element.50.refs_0_, bf16[4,64,384]{2,1,0:T(8,128)(2,1)} %get-tuple-element.58.refs_1_, ...), custom_call_target="tpu_custom_call" | custom-call | flops 1811939328 | bytes 7077888 | tf_op jit(solution)/shard_map/backward/pallas_call | solution.py:306
  67.0 1.5 %collective-permute-start.15 = (bf16[2,192,384]{2,1,0:T(8,128)(2,1)}, bf16[2,192,384]{2,1,0:T(8,128)(2,1)S(1)}, u32[]{:S(2)}, u32[]{:S(2)}) collective-permute-start(bf16[2,192,384]{2,1,0:T(8,128)(2,1)} %get-tuple-element.66), channel_id=1, source_target_pairs={{0,48},{16,0},{32,16},{48,32},{64,112},{80,64},{96,80},{112,96},{1... | collective-permute-start | bytes 884744 | tf_op jit(solution)/shard_map/ppermute | solution.py:30
  68.5 1.7 %collective-permute-start.16 = (bf16[2,192,384]{2,1,0:T(8,128)(2,1)}, bf16[2,192,384]{2,1,0:T(8,128)(2,1)S(1)}, u32[]{:S(2)}, u32[]{:S(2)}) collective-permute-start(bf16[2,192,384]{2,1,0:T(8,128)(2,1)} %get-tuple-element.67), channel_id=1, source_target_pairs={{0,32},{16,48},{32,0},{48,16},{64,96},{80,112},{96,64},{112,80},{1... | collective-permute-start | bytes 884744 | tf_op jit(solution)/shard_map/ppermute | solution.py:30
  70.2 1.4 %collective-permute-start.17 = (bf16[2,192,384]{2,1,0:T(8,128)(2,1)}, bf16[2,192,384]{2,1,0:T(8,128)(2,1)S(1)}, u32[]{:S(2)}, u32[]{:S(2)}) collective-permute-start(bf16[2,192,384]{2,1,0:T(8,128)(2,1)} %get-tuple-element.68), channel_id=1, source_target_pairs={{0,16},{16,32},{32,48},{48,0},{64,80},{80,96},{96,112},{112,64},{1... | collective-permute-start | bytes 884744 | tf_op jit(solution)/shard_map/ppermute | solution.py:30
  71.6 24.2 %conditional.3 = (bf16[1,128,384]{2,1,0:T(8,128)(2,1)}, bf16[1,64,384]{2,1,0:T(8,128)(2,1)}, bf16[1,128,384]{2,1,0:T(8,128)(2,1)}, bf16[1,64,384]{2,1,0:T(8,128)(2,1)}, f32[8,384]{1,0:T(8,128)S(1)}) conditional(s32[]{:T(128)} %convert_element_type.4, () %tuple.23, bf16[4,400,384]{2,1,0:T(8,128)(2,1)S(1)} %get-tuple-element.61), branch_computations={%region_2.3_spmd, %region_3.4_spmd} | conditional | flops 6144 | bytes 2629752 | solution.py:382
  71.6 15.6 %all_to_all.4.parts_ref = bf16[4,400,384]{2,1,0:T(8,128)(2,1)S(1)} all-to-all(bf16[4,400,384]{2,1,0:T(8,128)(2,1)S(1)} %param.3), channel_id=1, replica_groups={{0,64,128,192},{16,80,144,208},{32,96,160,224},{48,112,176,240},{1,65,1..., dimensions={0} | all-to-all | bytes 2457600 | tf_op jit(solution)/shard_map/cond/branch_1_fun/all_to_all | solution.py:418
  87.9 3.9 %collective-permute-done.4 = f32[8,384]{1,0:T(8,128)S(1)} collective-permute-done((f32[8,384]{1,0:T(8,128)S(1)}, f32[8,384]{1,0:T(8,128)S(1)}, u32[]{:S(2)}, u32[]{:S(2)}) %collective-permute-start.4) | collective-permute-done | bytes 12320 | tf_op jit(solution)/shard_map/cond/branch_1_fun/ppermute | solution.py:35
  91.8 3.9 %collective-permute-done.5 = f32[8,384]{1,0:T(8,128)S(1)} collective-permute-done((f32[8,384]{1,0:T(8,128)S(1)}, f32[8,384]{1,0:T(8,128)S(1)}, u32[]{:S(2)}, u32[]{:S(2)}) %collective-permute-start.5) | collective-permute-done | bytes 12320 | tf_op jit(solution)/shard_map/cond/branch_1_fun/ppermute | solution.py:35
  95.8 6.5 %collective-permute-start.18 = (f32[8,384]{1,0:T(8,128)S(1)}, f32[8,384]{1,0:T(8,128)S(1)}, u32[]{:S(2)}, u32[]{:S(2)}) collective-permute-start(f32[8,384]{1,0:T(8,128)S(1)} %get-tuple-element.74), channel_id=1, source_target_pairs={{0,1},{1,0},{2,3},{3,2},{4,5},{5,4},{6,7},{7,6},{8,9},{9,8},{10,11... | collective-permute-start | bytes 36872 | tf_op jit(solution)/shard_map/ppermute | solution.py:426
  (62 shorter events, 9.1 us)
Async XLA Ops:
  2.5 35.9 %copy-start.3 = (f32[384]{0:T(512)S(1)}, f32[384]{0:T(512)}, u32[]{:S(2)}) copy-start(f32[384]{0:T(512)} %param.21) | copy-start | bytes 4612
  2.5 35.9 %copy-start.4 = (f32[384]{0:T(512)S(1)}, f32[384]{0:T(512)}, u32[]{:S(2)}) copy-start(f32[384]{0:T(512)} %param.22) | copy-start | bytes 4612
  2.6 25.1 %collective-permute-start.3 = (bf16[2,128,384]{2,1,0:T(8,128)(2,1)S(1)}, bf16[2,128,384]{2,1,0:T(8,128)(2,1)}, u32[]{:S(2)}, u32[]{:S(2)}) collective-permute-start(bf16[2,128,384]{2,1,0:T(8,128)(2,1)S(1)} %get-tuple-element.8), channel_id=1, source_target_pairs={{0,48},{16,0},{32,16},{48,32},{64,112},{80,64},{96,80},{112,96},{1... | collective-permute-start | bytes 589832 | tf_op jit(solution)/shard_map/cond/branch_1_fun/ppermute | solution.py:30
  7.8 19.8 %collective-permute-start.2 = (bf16[2,128,384]{2,1,0:T(8,128)(2,1)S(1)}, bf16[2,128,384]{2,1,0:T(8,128)(2,1)}, u32[]{:S(2)}, u32[]{:S(2)}) collective-permute-start(bf16[2,128,384]{2,1,0:T(8,128)(2,1)S(1)} %get-tuple-element.8), channel_id=1, source_target_pairs={{0,32},{16,48},{32,0},{48,16},{64,96},{80,112},{96,64},{112,80},{1... | collective-permute-start | bytes 589832 | tf_op jit(solution)/shard_map/cond/branch_1_fun/ppermute | solution.py:30
  7.8 19.9 %collective-permute-start.1 = (bf16[2,128,384]{2,1,0:T(8,128)(2,1)S(1)}, bf16[2,128,384]{2,1,0:T(8,128)(2,1)}, u32[]{:S(2)}, u32[]{:S(2)}) collective-permute-start(bf16[2,128,384]{2,1,0:T(8,128)(2,1)S(1)} %get-tuple-element.8), channel_id=1, source_target_pairs={{0,16},{16,32},{32,48},{48,0},{64,80},{80,96},{96,112},{112,64},{1... | collective-permute-start | bytes 589832 | tf_op jit(solution)/shard_map/cond/branch_1_fun/ppermute | solution.py:30
  8.2 19.5 %collective-permute-start = (bf16[3,64,384]{2,1,0:T(8,128)(2,1)S(1)}, bf16[3,64,384]{2,1,0:T(8,128)(2,1)}, u32[]{:S(2)}, u32[]{:S(2)}) collective-permute-start(bf16[3,64,384]{2,1,0:T(8,128)(2,1)S(1)} %get-tuple-element.7), channel_id=1, source_target_pairs={{0,8},{2,40},{4,72},{6,104},{8,136},{10,168},{12,200},{14,232},{16... | collective-permute-start | bytes 442376 | tf_op jit(solution)/shard_map/cond/branch_1_fun/ppermute | solution.py:377
  28.5 17.2 %copy-start.2 = (bf16[64,384]{1,0:T(8,128)(2,1)}, bf16[64,384]{1,0:T(8,128)(2,1)S(1)}, u32[]{:S(2)}) copy-start(bf16[64,384]{1,0:T(8,128)(2,1)S(1)} %slice_bitcast_fusion.refs_9_) | copy-start | bytes 147460
  28.5 10.0 %collective-permute-start.11 = (bf16[64,384]{1,0:T(8,128)(2,1)S(1)}, bf16[64,384]{1,0:T(8,128)(2,1)S(1)}, u32[]{:S(2)}, u32[]{:S(2)}) collective-permute-start(bf16[64,384]{1,0:T(8,128)(2,1)S(1)} %slice_bitcast_fusion.refs_9_), channel_id=1, source_target_pairs={{0,192},{16,208},{32,224},{48,240},{64,0},{80,16},{96,32},{112,48}... | collective-permute-start | bytes 147464 | tf_op jit(solution)/shard_map/ppermute | solution.py:25
  29.4 14.7 %collective-permute-start.10 = (bf16[64,384]{1,0:T(8,128)(2,1)S(1)}, bf16[64,384]{1,0:T(8,128)(2,1)S(1)}, u32[]{:S(2)}, u32[]{:S(2)}) collective-permute-start(bf16[64,384]{1,0:T(8,128)(2,1)S(1)} %slice_bitcast_fusion.refs_9_), channel_id=1, source_target_pairs={{0,128},{16,144},{32,160},{48,176},{64,192},{80,208},{96,224},{112... | collective-permute-start | bytes 147464 | tf_op jit(solution)/shard_map/ppermute | solution.py:25
  30.0 14.2 %collective-permute-start.9 = (bf16[64,384]{1,0:T(8,128)(2,1)S(1)}, bf16[64,384]{1,0:T(8,128)(2,1)S(1)}, u32[]{:S(2)}, u32[]{:S(2)}) collective-permute-start(bf16[64,384]{1,0:T(8,128)(2,1)S(1)} %slice_bitcast_fusion.refs_9_), channel_id=1, source_target_pairs={{0,64},{16,80},{32,96},{48,112},{64,128},{80,144},{96,160},{112,17... | collective-permute-start | bytes 147464 | tf_op jit(solution)/shard_map/ppermute | solution.py:25
  31.4 14.3 %copy-start.1 = (bf16[2,64,384]{2,1,0:T(8,128)(2,1)}, bf16[2,64,384]{2,1,0:T(8,128)(2,1)S(1)}, u32[]{:S(2)}) copy-start(bf16[2,64,384]{2,1,0:T(8,128)(2,1)S(1)} %slice.16.refs_5_.refs_6_) | copy-start | bytes 294916
  31.4 12.7 %collective-permute-start.8 = (bf16[2,64,384]{2,1,0:T(8,128)(2,1)S(1)}, bf16[2,64,384]{2,1,0:T(8,128)(2,1)S(1)}, u32[]{:S(2)}, u32[]{:S(2)}) collective-permute-start(bf16[2,64,384]{2,1,0:T(8,128)(2,1)S(1)} %slice.16.refs_5_.refs_6_), channel_id=1, source_target_pairs={{0,48},{16,0},{32,16},{48,32},{64,112},{80,64},{96,80},{112,96},{1... | collective-permute-start | bytes 294920 | tf_op jit(solution)/shard_map/ppermute | solution.py:30
  38.4 7.3 %collective-permute-start.7 = (bf16[2,64,384]{2,1,0:T(8,128)(2,1)S(1)}, bf16[2,64,384]{2,1,0:T(8,128)(2,1)S(1)}, u32[]{:S(2)}, u32[]{:S(2)}) collective-permute-start(bf16[2,64,384]{2,1,0:T(8,128)(2,1)S(1)} %slice.16.refs_5_.refs_6_), channel_id=1, source_target_pairs={{0,32},{16,48},{32,0},{48,16},{64,96},{80,112},{96,64},{112,80},{1... | collective-permute-start | bytes 294920 | tf_op jit(solution)/shard_map/ppermute | solution.py:30
  38.5 7.2 %collective-permute-start.6 = (bf16[2,64,384]{2,1,0:T(8,128)(2,1)S(1)}, bf16[2,64,384]{2,1,0:T(8,128)(2,1)S(1)}, u32[]{:S(2)}, u32[]{:S(2)}) collective-permute-start(bf16[2,64,384]{2,1,0:T(8,128)(2,1)S(1)} %slice.16.refs_5_.refs_6_), channel_id=1, source_target_pairs={{0,16},{16,32},{32,48},{48,0},{64,80},{80,96},{96,112},{112,64},{1... | collective-permute-start | bytes 294920 | tf_op jit(solution)/shard_map/ppermute | solution.py:30
  51.7 3.9 %collective-permute-start.14 = (f32[3,4,768]{2,1,0:T(4,128)}, f32[3,4,768]{2,1,0:T(4,128)S(1)}, u32[]{:S(2)}, u32[]{:S(2)}) collective-permute-start(f32[3,4,768]{2,1,0:T(4,128)} %get-tuple-element.59.refs_10_), channel_id=1, source_target_pairs={{0,192},{16,208},{32,224},{48,240},{64,0},{80,16},{96,32},{112,48}... | collective-permute-start | bytes 110600 | tf_op jit(solution)/shard_map/ppermute | solution.py:25
  53.2 4.5 %collective-permute-start.13 = (f32[3,4,768]{2,1,0:T(4,128)}, f32[3,4,768]{2,1,0:T(4,128)S(1)}, u32[]{:S(2)}, u32[]{:S(2)}) collective-permute-start(f32[3,4,768]{2,1,0:T(4,128)} %get-tuple-element.59.refs_10_), channel_id=1, source_target_pairs={{0,128},{16,144},{32,160},{48,176},{64,192},{80,208},{96,224},{112... | collective-permute-start | bytes 110600 | tf_op jit(solution)/shard_map/ppermute | solution.py:25
  54.8 4.2 %collective-permute-start.12 = (f32[3,4,768]{2,1,0:T(4,128)}, f32[3,4,768]{2,1,0:T(4,128)S(1)}, u32[]{:S(2)}, u32[]{:S(2)}) collective-permute-start(f32[3,4,768]{2,1,0:T(4,128)} %get-tuple-element.59.refs_10_), channel_id=1, source_target_pairs={{0,64},{16,80},{32,96},{48,112},{64,128},{80,144},{96,160},{112,17... | collective-permute-start | bytes 110600 | tf_op jit(solution)/shard_map/ppermute | solution.py:25
  67.0 36.7 %collective-permute-start.15 = (bf16[2,192,384]{2,1,0:T(8,128)(2,1)}, bf16[2,192,384]{2,1,0:T(8,128)(2,1)S(1)}, u32[]{:S(2)}, u32[]{:S(2)}) collective-permute-start(bf16[2,192,384]{2,1,0:T(8,128)(2,1)} %get-tuple-element.66), channel_id=1, source_target_pairs={{0,48},{16,0},{32,16},{48,32},{64,112},{80,64},{96,80},{112,96},{1... | collective-permute-start | bytes 884744 | tf_op jit(solution)/shard_map/ppermute | solution.py:30
  68.5 35.2 %collective-permute-start.16 = (bf16[2,192,384]{2,1,0:T(8,128)(2,1)}, bf16[2,192,384]{2,1,0:T(8,128)(2,1)S(1)}, u32[]{:S(2)}, u32[]{:S(2)}) collective-permute-start(bf16[2,192,384]{2,1,0:T(8,128)(2,1)} %get-tuple-element.67), channel_id=1, source_target_pairs={{0,32},{16,48},{32,0},{48,16},{64,96},{80,112},{96,64},{112,80},{1... | collective-permute-start | bytes 884744 | tf_op jit(solution)/shard_map/ppermute | solution.py:30
  70.2 33.5 %collective-permute-start.17 = (bf16[2,192,384]{2,1,0:T(8,128)(2,1)}, bf16[2,192,384]{2,1,0:T(8,128)(2,1)S(1)}, u32[]{:S(2)}, u32[]{:S(2)}) collective-permute-start(bf16[2,192,384]{2,1,0:T(8,128)(2,1)} %get-tuple-element.68), channel_id=1, source_target_pairs={{0,16},{16,32},{32,48},{48,0},{64,80},{80,96},{96,112},{112,64},{1... | collective-permute-start | bytes 884744 | tf_op jit(solution)/shard_map/ppermute | solution.py:30
  71.6 32.1 %copy-start = (bf16[2,192,384]{2,1,0:T(8,128)(2,1)S(1)}, bf16[2,192,384]{2,1,0:T(8,128)(2,1)}, u32[]{:S(2)}) copy-start(bf16[2,192,384]{2,1,0:T(8,128)(2,1)} %get-tuple-element.65.refs_0_) | copy-start | bytes 884740
  87.9 3.9 %collective-permute-start.4 = (f32[8,384]{1,0:T(8,128)S(1)}, f32[8,384]{1,0:T(8,128)S(1)}, u32[]{:S(2)}, u32[]{:S(2)}) collective-permute-start(f32[8,384]{1,0:T(8,128)S(1)} %get-tuple-element.14), channel_id=1, source_target_pairs={{0,16},{16,0},{32,48},{48,32},{64,80},{80,64},{96,112},{112,96},{1... | collective-permute-start | bytes 36872 | tf_op jit(solution)/shard_map/cond/branch_1_fun/ppermute | solution.py:35
  91.8 3.9 %collective-permute-start.5 = (f32[8,384]{1,0:T(8,128)S(1)}, f32[8,384]{1,0:T(8,128)S(1)}, u32[]{:S(2)}, u32[]{:S(2)}) collective-permute-start(f32[8,384]{1,0:T(8,128)S(1)} %add.29), channel_id=1, source_target_pairs={{0,32},{16,48},{32,0},{48,16},{64,96},{80,112},{96,64},{112,80},{1... | collective-permute-start | bytes 36872 | tf_op jit(solution)/shard_map/cond/branch_1_fun/ppermute | solution.py:35
  95.8 7.3 %collective-permute-start.18 = (f32[8,384]{1,0:T(8,128)S(1)}, f32[8,384]{1,0:T(8,128)S(1)}, u32[]{:S(2)}, u32[]{:S(2)}) collective-permute-start(f32[8,384]{1,0:T(8,128)S(1)} %get-tuple-element.74), channel_id=1, source_target_pairs={{0,1},{1,0},{2,3},{3,2},{4,5},{5,4},{6,7},{7,6},{8,9},{9,8},{10,11... | collective-permute-start | bytes 36872 | tf_op jit(solution)/shard_map/ppermute | solution.py:426
  (9 other events, 18.9 us)

commit v12 on v11

--- a/solution.py
+++ b/solution.py
@@ -20,17 +20,12 @@
 ALONG_X = [[x * SIDE + z for x in range(SIDE)] for z in range(SIDE)]
 
 
-def along_x(array, shift):
-    pairs = [(x * SIDE + z, (x + shift) % SIDE * SIDE + z) for x in range(SIDE) for z in range(SIDE)]
+def along_x(array, distance):
+    pairs = [(x * SIDE + z, (x ^ distance) * SIDE + z) for x in range(SIDE) for z in range(SIDE)]
     return lax.ppermute(array, "vid", pairs)
 
 
-def along_z(array, shift):
-    pairs = [(x * SIDE + z, x * SIDE + (z + shift) % SIDE) for x in range(SIDE) for z in range(SIDE)]
-    return lax.ppermute(array, "vid", pairs)
-
-
-def beside_z(array, distance):
+def along_z(array, distance):
     pairs = [(x * SIDE + z, x * SIDE + (z ^ distance)) for x in range(SIDE) for z in range(SIDE)]
     return lax.ppermute(array, "vid", pairs)
 
@@ -40,11 +35,11 @@
 
 
 def gathered(array, along):
-    return [array] + [along(array, shift) for shift in range(1, SIDE)]
+    return [array] + [along(array, distance) for distance in range(1, SIDE)]
 
 
 def returned(parts, along):
-    return [parts[0]] + [along(parts[place], SIDE - place) for place in range(1, SIDE)]
+    return [parts[0]] + [along(parts[place], place) for place in range(1, SIDE)]
 
 
 def nt(a, b):
@@ -82,6 +77,22 @@
     else:
         video = gated(video, gates_ref[0:1, :])
     return jnp.concatenate([video, audio], axis=0)
+
+
+def split_audio_kernel(audio_ref, queries_ref, keys_ref):
+    queries_ref[...] = audio_ref[0]
+    keys_ref[0] = audio_ref[1]
+    keys_ref[1] = audio_ref[2]
+
+
+def split_audio(audio):
+    _, rows, width = audio.shape
+    return pl.pallas_call(
+        split_audio_kernel,
+        out_shape=[like(rows, width), like(2, rows, width)],
+        compiler_params=pltpu.CompilerParams(vmem_limit_bytes=8 * 2**20),
+        name="split_audio",
+    )(audio)
 
 
 def audio_target(vid, aud):
@@ -154,7 +165,7 @@
     gathered_ref, k_refs, audio_q, numbers_ref, gates_ref = refs[0], (refs[1:5], refs[5:9]), refs[9:13], refs[13], refs[14]
     o_video_ref, stats_video_ref, o_ref, stats_ref, ordered_ref = refs[15:20]
     for place in range(SIDE):
-        ordered_ref[lax.rem(numbers_ref[SIDE] + SIDE - place, SIDE)] = audio_q[place][...]
+        ordered_ref[numbers_ref[SIDE] ^ place] = audio_q[place][...]
     up_audio = gated(upstreams_of(gathered_ref, video_rows)[1], gates_ref[1:2, :])
     raw = scores(joined(k_refs[VIDEO], 0), flat(ordered_ref[...]), VIDEO, None)
     output, stats = attend(raw, joined(k_refs[VIDEO], 1), up_audio)
@@ -399,12 +410,12 @@
 
     audio, video_keys, queries = fenced(holds, first_chunks, send_audio, video_kv, queries)
     video_keys = [video_kv, *video_keys]
-    audio = lax.optimization_barrier(audio)
-    audio_keys = gathered(audio[1:], along_z)
-    audio_queries = gathered(audio[0], along_x)
+    audio_queries, audio_keys = split_audio(audio)
+    audio_keys = gathered(audio_keys, along_z)
+    audio_queries = gathered(audio_queries, along_x)
     gates = jnp.stack([video_gate, audio_gate])
     column, row = vid // SIDE, vid % SIDE
-    limits = [audio_len[0] - (column * SIDE + (row - p) % SIDE) * audio_rows for p in range(SIDE)]
+    limits = [audio_len[0] - (column * SIDE + (row ^ p)) * audio_rows for p in range(SIDE)]
     numbers = jnp.stack([*limits, column])
     earlier = attention_forward_video(queries, video_keys, video_rows)
     outputs, stats, audio_queries = attention_forward(
@@ -418,13 +429,15 @@
         parts = lax.all_to_all(parts, "vid", 0, 0, axis_index_groups=ALONG_X, tiled=True)
         *results, gate = finish_queries(parts, video_rows, audio_rows)
         for distance in (1, 2):
-            gate = gate + beside_z(gate, distance)
+            gate = gate + along_z(gate, distance)
         return (*results, gate)
 
     video_out, audio_out, grad_video_q, grad_audio_q, gate = fenced(holds, query_results, query_parts)
     key_parts = returned(key_parts, along_z)
-    gate = gate + lax.ppermute(gate, "pair", [(0, 1), (1, 0)])
-    grad_video_k, grad_video_v, grad_audio_k, grad_audio_v = finish_keys(key_parts, video_rows, audio_rows)
+    other = lax.ppermute(gate, "pair", [(0, 1), (1, 0)])
+    key_grads = finish_keys(key_parts, video_rows, audio_rows)
+    other, (grad_video_k, grad_video_v, grad_audio_k, grad_audio_v) = lax.optimization_barrier((other, key_grads))
+    gate = gate + other
     return (
         video_out,
         audio_out,

time: 105 us -> 102 us (0.971)
  blocking collectives: 32.1 us -> 28.7 us
  starting transfers between devices: 33 us -> 35.6 us
  local copies, waits for them, and re-layouts: 4.2 us -> 2.57 us
  waiting for transfers between devices: 13.7 us -> 12.1 us
    ppermute x3 -> x1, waiting for transfers between devices: 8.65 us -> 0.04 us  [shards(): other = lax.ppermute(gate, 'pair', [(0, 1), (1, 0)])]
    ppermute x9 -> x11, waiting for transfers between devices: 1.58 us -> 10.1 us  [along_z(): return lax.ppermute(array, 'vid', pairs)]
    all_gather x1, blocking collectives: 16.5 us -> 14.8 us  [all_along_x(): return lax.all_gather(array, 'vid', axis=0, axis_index_groups=ALONG_X)]
    all_to_all x1, blocking collectives: 15.6 us -> 13.9 us  [query_results(): lax.all_to_all(parts, 'vid', 0, 0, axis_index_groups=ALONG_X, tiled=True)]
    ppermute x6, waiting for transfers between devices: 3.47 us -> 1.95 us  [along_x(): return lax.ppermute(array, 'vid', pairs)]
    ppermute x3 -> x1, starting transfers between devices: 6.47 us -> 7.48 us  [shards(): other = lax.ppermute(gate, 'pair', [(0, 1), (1, 0)])]
    ppermute x9 -> x11, starting transfers between devices: 17.7 us -> 18.6 us  [along_z(): return lax.ppermute(array, 'vid', pairs)]
  transfers between devices with their start and end apart: 19 -> 19, of which waited for: 6 -> 6; matrix products, arithmetic and copies ran while one was open for 3% -> 1% of each run, Pallas kernels for 5% -> 5%
where the time goes in v12:
time: 102 us; the launch traced here: 101 us
  starting transfers between devices  35.6 us (35%)
  blocking collectives  28.7 us (28%)
  Pallas kernels  20.2 us (20%)
  waiting for transfers between devices  12.1 us (12%)
  local copies, waits for them, and re-layouts  2.57 us (3%)
  between operations  1.5 us (1%)
    ppermute x11, starting transfers between devices, along_z(): return lax.ppermute(array, 'vid', pairs)  18.6 us
    all_gather x1, blocking collectives, all_along_x(): return lax.all_gather(array, 'vid', axis=0, axis_index_groups=ALONG_X)  14.8 us
    all_to_all x1, blocking collectives, query_results(): lax.all_to_all(parts, 'vid', 0, 0, axis_index_groups=ALONG_X, tiled=True)  13.9 us
    ppermute x11, waiting for transfers between devices, along_z(): return lax.ppermute(array, 'vid', pairs)  10.1 us
    ppermute x1, starting transfers between devices, shards(): other = lax.ppermute(gate, 'pair', [(0, 1), (1, 0)])  7.48 us
    pallas_call x1, Pallas kernels, attention_backward(): pl.pallas_call(functools.partial(backward_kernel, video_rows), grid=(head...  7.34 us
    ppermute x6, starting transfers between devices, along_x(): return lax.ppermute(array, 'vid', pairs)  6.68 us
    pallas_call x1, Pallas kernels, attention_forward(): pl.pallas_call(functools.partial(forward_kernel, video_rows), grid=(heads...  5.23 us
  transfers between devices with their start and end apart: 19, of which 6 were waited for; matrix products, arithmetic and copies ran while one was open for 1% of the time, Pallas kernels for 5%

profile of v12, /device:TPU:1, one launch (start us, length us, event | category | flops | bytes accessed | tf_op | source)
XLA Modules:
  0.0 101.3 jit_solution(17741600483638974115)
XLA Ops:
  1.3 1.2 %prepare.1 = (bf16[3,64,384]{2,1,0:T(8,128)(2,1)S(1)}, bf16[2,128,384]{2,1,0:T(8,128)(2,1)S(1)}, bf16[320,384]{1,0:T(8,128)(2,1)S(1)}) custom-call(bf16[1,128,3072]{2,1,0:T(8,128)(2,1)} %aq_ref.1, bf16[1,128,3072]{2,1,0:T(8,128)(2,1)} %ak_ref.1, bf16[1,128,3072]{2,1,0:T(8,128)(2,1)} %av_ref.1, bf16[1,128,384]{2,1,0:T(8,128)(2,1)} %vq_ref.1, ...), custom_call_target="tpu_custom_call" | custom-call | tf_op jit(solution)/shard_map/prepare/pallas_call | solution.py:127
  2.5 23.4 %conditional.2 = (bf16[3,64,384]{2,1,0:T(8,128)(2,1)}, bf16[2,128,384]{2,1,0:T(8,128)(2,1)}, bf16[2,128,384]{2,1,0:T(8,128)(2,1)}, bf16[2,128,384]{2,1,0:T(8,128)(2,1)}, bf16[4,320,384]{2,1,0:T(8,128)(2,1)S(1)}) conditional(s32[]{:T(128)} %convert_element_type.4, () %tuple.25, (bf16[3,64,384]{2,1,0:T(8,128)(2,1)S(1)}, ...), branch_computations={%region_0.0_spmd, %region_1.0_spmd} | conditional | bytes 4178120 | solution.py:393
  2.6 5.3 %collective-permute-start.3 = (bf16[2,128,384]{2,1,0:T(8,128)(2,1)S(1)}, bf16[2,128,384]{2,1,0:T(8,128)(2,1)}, u32[]{:S(2)}, u32[]{:S(2)}) collective-permute-start(bf16[2,128,384]{2,1,0:T(8,128)(2,1)S(1)} %get-tuple-element.8), channel_id=1, source_target_pairs={{0,48},{16,32},{32,16},{48,0},{64,112},{80,96},{96,80},{112,64},{1... | collective-permute-start | bytes 589832 | tf_op jit(solution)/shard_map/cond/branch_1_fun/ppermute | solution.py:30
  8.2 2.9 %collective-permute-start = (bf16[3,64,384]{2,1,0:T(8,128)(2,1)S(1)}, bf16[3,64,384]{2,1,0:T(8,128)(2,1)}, u32[]{:S(2)}, u32[]{:S(2)}) collective-permute-start(bf16[3,64,384]{2,1,0:T(8,128)(2,1)S(1)} %get-tuple-element.7), channel_id=1, source_target_pairs={{0,8},{2,40},{4,72},{6,104},{8,136},{10,168},{12,200},{14,232},{16... | collective-permute-start | bytes 442376 | tf_op jit(solution)/shard_map/cond/branch_1_fun/ppermute | solution.py:388
  11.1 14.8 %all-gather = bf16[1280,384]{1,0:T(8,128)(2,1)S(1)} all-gather(bf16[320,384]{1,0:T(8,128)(2,1)S(1)} %get-tuple-element.9), channel_id=2, replica_groups={{0,64,128,192},{16,80,144,208},{32,96,160,224},{48,112,176,240},{1,65,1..., dimensions={0}, use_global_device_ids=true | all-gather | bytes 1228800 | tf_op jit(solution)/shard_map/cond/branch_1_fun/all_gather | solution.py:34
  26.0 0.9 split_audio.1
  26.9 1.3 %collective-permute-start.11 = (bf16[64,384]{1,0:T(8,128)(2,1)S(1)}, bf16[64,384]{1,0:T(8,128)(2,1)S(1)}, u32[]{:S(2)}, u32[]{:S(2)}) collective-permute-start(bf16[64,384]{1,0:T(8,128)(2,1)S(1)} %get-tuple-element.64.refs_9_), channel_id=1, source_target_pairs={{0,192},{16,208},{32,224},{48,240},{64,128},{80,144},{96,160},{112... | collective-permute-start | bytes 147464 | tf_op jit(solution)/shard_map/ppermute | solution.py:25
  28.8 1.5 %collective-permute-start.9 = (bf16[64,384]{1,0:T(8,128)(2,1)S(1)}, bf16[64,384]{1,0:T(8,128)(2,1)S(1)}, u32[]{:S(2)}, u32[]{:S(2)}) collective-permute-start(bf16[64,384]{1,0:T(8,128)(2,1)S(1)} %get-tuple-element.64.refs_9_), channel_id=1, source_target_pairs={{0,64},{16,80},{32,96},{48,112},{64,0},{80,16},{96,32},{112,48},{1... | collective-permute-start | bytes 147464 | tf_op jit(solution)/shard_map/ppermute | solution.py:25
  30.3 8.9 %collective-permute-start.8 = (bf16[2,64,384]{2,1,0:T(8,128)(2,1)S(1)}, bf16[2,64,384]{2,1,0:T(8,128)(2,1)S(1)}, u32[]{:S(2)}, u32[]{:S(2)}) collective-permute-start(bf16[2,64,384]{2,1,0:T(8,128)(2,1)S(1)} %get-tuple-element.63.refs_5_.refs_6_), channel_id=1, source_target_pairs={{0,48},{16,32},{32,16},{48,0},{64,112},{80,96},{96,80},{112,64},{1... | collective-permute-start | bytes 294920 | tf_op jit(solution)/shard_map/ppermute | solution.py:30
  40.9 3.9 %forward_video.1 = (bf16[3,128,512]{2,1,0:T(8,128)(2,1)}, f32[3,2,512]{2,1,0:T(2,128)}) custom-call(bf16[4,320,384]{2,1,0:T(8,128)(2,1)S(1)} %get-tuple-element.57.refs_0_, bf16[2,128,384]{2,1,0:T(8,128)(2,1)S(1)} %get-tuple-element.58.refs_1_.refs_2_, bf16[2,128,384]{2,1,0:T(8,128)(2,1)} %get-tuple-element.59.refs_2_.refs_3_, ...), custom_call_target="tpu_custom_call" | custom-call | flops 402653184 | bytes 3145728 | tf_op jit(solution)/shard_map/forward_video/pallas_call | solution.py:278
  44.9 0.8 collective-permute-done.7.refs_7_.refs_8_
  46.3 5.2 %forward.1 = (bf16[3,2,128,768]{3,2,1,0:T(8,128)(2,1)}, f32[3,4,768]{2,1,0:T(4,128)}, bf16[4,64,384]{2,1,0:T(8,128)(2,1)}) custom-call(bf16[4,320,384]{2,1,0:T(8,128)(2,1)S(1)} %get-tuple-element.57.refs_0_, bf16[2,128,384]{2,1,0:T(8,128)(2,1)S(1)} %get-tuple-element.58.refs_1_.refs_2_, bf16[2,128,384]{2,1,0:T(8,128)(2,1)} %get-tuple-element.59.refs_2_.refs_3_, ...), custom_call_target="tpu_custom_call" | custom-call | flops 452984832 | bytes 7077888 | tf_op jit(solution)/shard_map/forward/pallas_call | solution.py:297
  52.7 2.2 %collective-permute-start.12 = (f32[3,4,768]{2,1,0:T(4,128)}, f32[3,4,768]{2,1,0:T(4,128)S(1)}, u32[]{:S(2)}, u32[]{:S(2)}) collective-permute-start(f32[3,4,768]{2,1,0:T(4,128)} %get-tuple-element.68.refs_10_), channel_id=1, source_target_pairs={{0,64},{16,80},{32,96},{48,112},{64,0},{80,16},{96,32},{112,48},{1... | collective-permute-start | bytes 110600 | tf_op jit(solution)/shard_map/ppermute | solution.py:25
  54.9 1.0 collective-permute-done.14.refs_13_
  57.5 7.3 %backward.1 = (bf16[2,192,384]{2,1,0:T(8,128)(2,1)}, bf16[2,192,384]{2,1,0:T(8,128)(2,1)}, bf16[2,192,384]{2,1,0:T(8,128)(2,1)}, bf16[2,192,384]{2,1,0:T(8,128)(2,1)}, bf16[4,400,384]{2,1,0:T(8,128)(2,1)S(1)}) custom-call(bf16[4,320,384]{2,1,0:T(8,128)(2,1)S(1)} %get-tuple-element.57.refs_0_, bf16[4,64,384]{2,1,0:T(8,128)(2,1)} %get-tuple-element.67.refs_1_, ...), custom_call_target="tpu_custom_call" | custom-call | flops 1811939328 | bytes 7077888 | tf_op jit(solution)/shard_map/backward/pallas_call | solution.py:317
  64.8 1.1 %collective-permute-start.16 = (bf16[2,192,384]{2,1,0:T(8,128)(2,1)}, bf16[2,192,384]{2,1,0:T(8,128)(2,1)S(1)}, u32[]{:S(2)}, u32[]{:S(2)}) collective-permute-start(bf16[2,192,384]{2,1,0:T(8,128)(2,1)} %get-tuple-element.76), channel_id=1, source_target_pairs={{0,16},{16,0},{32,48},{48,32},{64,80},{80,64},{96,112},{112,96},{1... | collective-permute-start | bytes 884744 | tf_op jit(solution)/shard_map/ppermute | solution.py:30
  65.9 2.4 %collective-permute-start.17 = (bf16[2,192,384]{2,1,0:T(8,128)(2,1)}, bf16[2,192,384]{2,1,0:T(8,128)(2,1)S(1)}, u32[]{:S(2)}, u32[]{:S(2)}) collective-permute-start(bf16[2,192,384]{2,1,0:T(8,128)(2,1)} %get-tuple-element.77), channel_id=1, source_target_pairs={{0,32},{16,48},{32,0},{48,16},{64,96},{80,112},{96,64},{112,80},{1... | collective-permute-start | bytes 884744 | tf_op jit(solution)/shard_map/ppermute | solution.py:30
  68.5 24.0 %conditional.3 = (bf16[1,128,384]{2,1,0:T(8,128)(2,1)}, bf16[1,64,384]{2,1,0:T(8,128)(2,1)}, bf16[1,128,384]{2,1,0:T(8,128)(2,1)}, bf16[1,64,384]{2,1,0:T(8,128)(2,1)}, f32[8,384]{1,0:T(8,128)S(1)}) conditional(s32[]{:T(128)} %convert_element_type.4, () %tuple.24, bf16[4,400,384]{2,1,0:T(8,128)(2,1)S(1)} %get-tuple-element.70), branch_computations={%region_2.3_spmd, %region_3.4_spmd} | conditional | flops 6144 | bytes 2629752 | solution.py:393
  68.5 13.9 %all_to_all.4.parts_ref = bf16[4,400,384]{2,1,0:T(8,128)(2,1)S(1)} all-to-all(bf16[4,400,384]{2,1,0:T(8,128)(2,1)S(1)} %param.3), channel_id=1, replica_groups={{0,64,128,192},{16,80,144,208},{32,96,160,224},{48,112,176,240},{1,65,1..., dimensions={0} | all-to-all | bytes 2457600 | tf_op jit(solution)/shard_map/cond/branch_1_fun/all_to_all | solution.py:429
  82.3 0.8 finish_queries.1
  83.1 5.6 %collective-permute-done.4 = f32[8,384]{1,0:T(8,128)S(1)} collective-permute-done((f32[8,384]{1,0:T(8,128)S(1)}, f32[8,384]{1,0:T(8,128)S(1)}, u32[]{:S(2)}, u32[]{:S(2)}) %collective-permute-start.4) | collective-permute-done | bytes 12320 | tf_op jit(solution)/shard_map/cond/branch_1_fun/ppermute | solution.py:30
  88.8 3.6 %collective-permute-done.5 = f32[8,384]{1,0:T(8,128)S(1)} collective-permute-done((f32[8,384]{1,0:T(8,128)S(1)}, f32[8,384]{1,0:T(8,128)S(1)}, u32[]{:S(2)}, u32[]{:S(2)}) %collective-permute-start.5) | collective-permute-done | bytes 12320 | tf_op jit(solution)/shard_map/cond/branch_1_fun/ppermute | solution.py:30
  92.4 7.5 %collective-permute-start.15 = (f32[8,384]{1,0:T(8,128)S(1)}, f32[8,384]{1,0:T(8,128)S(1)}, u32[]{:S(2)}, u32[]{:S(2)}) collective-permute-start(f32[8,384]{1,0:T(8,128)S(1)} %get-tuple-element.74), channel_id=1, source_target_pairs={{0,1},{1,0},{2,3},{3,2},{4,5},{5,4},{6,7},{7,6},{8,9},{9,8},{10,11... | collective-permute-start | bytes 36872 | tf_op jit(solution)/shard_map/ppermute | solution.py:437
  99.9 0.8 finish_keys.1
  (61 shorter events, 6.9 us)
Async XLA Ops:
  2.5 36.7 %copy-start.3 = (f32[384]{0:T(512)S(1)}, f32[384]{0:T(512)}, u32[]{:S(2)}) copy-start(f32[384]{0:T(512)} %param.21) | copy-start | bytes 4612
  2.5 36.7 %copy-start.4 = (f32[384]{0:T(512)S(1)}, f32[384]{0:T(512)}, u32[]{:S(2)}) copy-start(f32[384]{0:T(512)} %param.22) | copy-start | bytes 4612
  2.6 23.4 %collective-permute-start.3 = (bf16[2,128,384]{2,1,0:T(8,128)(2,1)S(1)}, bf16[2,128,384]{2,1,0:T(8,128)(2,1)}, u32[]{:S(2)}, u32[]{:S(2)}) collective-permute-start(bf16[2,128,384]{2,1,0:T(8,128)(2,1)S(1)} %get-tuple-element.8), channel_id=1, source_target_pairs={{0,48},{16,32},{32,16},{48,0},{64,112},{80,96},{96,80},{112,64},{1... | collective-permute-start | bytes 589832 | tf_op jit(solution)/shard_map/cond/branch_1_fun/ppermute | solution.py:30
  7.8 18.1 %collective-permute-start.2 = (bf16[2,128,384]{2,1,0:T(8,128)(2,1)S(1)}, bf16[2,128,384]{2,1,0:T(8,128)(2,1)}, u32[]{:S(2)}, u32[]{:S(2)}) collective-permute-start(bf16[2,128,384]{2,1,0:T(8,128)(2,1)S(1)} %get-tuple-element.8), channel_id=1, source_target_pairs={{0,32},{16,48},{32,0},{48,16},{64,96},{80,112},{96,64},{112,80},{1... | collective-permute-start | bytes 589832 | tf_op jit(solution)/shard_map/cond/branch_1_fun/ppermute | solution.py:30
  7.8 18.1 %collective-permute-start.1 = (bf16[2,128,384]{2,1,0:T(8,128)(2,1)S(1)}, bf16[2,128,384]{2,1,0:T(8,128)(2,1)}, u32[]{:S(2)}, u32[]{:S(2)}) collective-permute-start(bf16[2,128,384]{2,1,0:T(8,128)(2,1)S(1)} %get-tuple-element.8), channel_id=1, source_target_pairs={{0,16},{16,0},{32,48},{48,32},{64,80},{80,64},{96,112},{112,96},{1... | collective-permute-start | bytes 589832 | tf_op jit(solution)/shard_map/cond/branch_1_fun/ppermute | solution.py:30
  8.2 17.7 %collective-permute-start = (bf16[3,64,384]{2,1,0:T(8,128)(2,1)S(1)}, bf16[3,64,384]{2,1,0:T(8,128)(2,1)}, u32[]{:S(2)}, u32[]{:S(2)}) collective-permute-start(bf16[3,64,384]{2,1,0:T(8,128)(2,1)S(1)} %get-tuple-element.7), channel_id=1, source_target_pairs={{0,8},{2,40},{4,72},{6,104},{8,136},{10,168},{12,200},{14,232},{16... | collective-permute-start | bytes 442376 | tf_op jit(solution)/shard_map/cond/branch_1_fun/ppermute | solution.py:388
  26.9 18.8 %copy-start.1 = (bf16[2,64,384]{2,1,0:T(8,128)(2,1)}, bf16[2,64,384]{2,1,0:T(8,128)(2,1)S(1)}, u32[]{:S(2)}) copy-start(bf16[2,64,384]{2,1,0:T(8,128)(2,1)S(1)} %get-tuple-element.63.refs_5_.refs_6_) | copy-start | bytes 294916
  26.9 18.8 %copy-start.2 = (bf16[64,384]{1,0:T(8,128)(2,1)}, bf16[64,384]{1,0:T(8,128)(2,1)S(1)}, u32[]{:S(2)}) copy-start(bf16[64,384]{1,0:T(8,128)(2,1)S(1)} %get-tuple-element.64.refs_9_) | copy-start | bytes 147460
  26.9 12.3 %collective-permute-start.11 = (bf16[64,384]{1,0:T(8,128)(2,1)S(1)}, bf16[64,384]{1,0:T(8,128)(2,1)S(1)}, u32[]{:S(2)}, u32[]{:S(2)}) collective-permute-start(bf16[64,384]{1,0:T(8,128)(2,1)S(1)} %get-tuple-element.64.refs_9_), channel_id=1, source_target_pairs={{0,192},{16,208},{32,224},{48,240},{64,128},{80,144},{96,160},{112... | collective-permute-start | bytes 147464 | tf_op jit(solution)/shard_map/ppermute | solution.py:25
  28.2 16.6 %collective-permute-start.10 = (bf16[64,384]{1,0:T(8,128)(2,1)S(1)}, bf16[64,384]{1,0:T(8,128)(2,1)S(1)}, u32[]{:S(2)}, u32[]{:S(2)}) collective-permute-start(bf16[64,384]{1,0:T(8,128)(2,1)S(1)} %get-tuple-element.64.refs_9_), channel_id=1, source_target_pairs={{0,128},{16,144},{32,160},{48,176},{64,192},{80,208},{96,224},{112... | collective-permute-start | bytes 147464 | tf_op jit(solution)/shard_map/ppermute | solution.py:25
  28.8 16.0 %collective-permute-start.9 = (bf16[64,384]{1,0:T(8,128)(2,1)S(1)}, bf16[64,384]{1,0:T(8,128)(2,1)S(1)}, u32[]{:S(2)}, u32[]{:S(2)}) collective-permute-start(bf16[64,384]{1,0:T(8,128)(2,1)S(1)} %get-tuple-element.64.refs_9_), channel_id=1, source_target_pairs={{0,64},{16,80},{32,96},{48,112},{64,0},{80,16},{96,32},{112,48},{1... | collective-permute-start | bytes 147464 | tf_op jit(solution)/shard_map/ppermute | solution.py:25
  30.3 14.6 %collective-permute-start.8 = (bf16[2,64,384]{2,1,0:T(8,128)(2,1)S(1)}, bf16[2,64,384]{2,1,0:T(8,128)(2,1)S(1)}, u32[]{:S(2)}, u32[]{:S(2)}) collective-permute-start(bf16[2,64,384]{2,1,0:T(8,128)(2,1)S(1)} %get-tuple-element.63.refs_5_.refs_6_), channel_id=1, source_target_pairs={{0,48},{16,32},{32,16},{48,0},{64,112},{80,96},{96,80},{112,64},{1... | collective-permute-start | bytes 294920 | tf_op jit(solution)/shard_map/ppermute | solution.py:30
  39.2 6.5 %collective-permute-start.7 = (bf16[2,64,384]{2,1,0:T(8,128)(2,1)S(1)}, bf16[2,64,384]{2,1,0:T(8,128)(2,1)S(1)}, u32[]{:S(2)}, u32[]{:S(2)}) collective-permute-start(bf16[2,64,384]{2,1,0:T(8,128)(2,1)S(1)} %get-tuple-element.63.refs_5_.refs_6_), channel_id=1, source_target_pairs={{0,32},{16,48},{32,0},{48,16},{64,96},{80,112},{96,64},{112,80},{1... | collective-permute-start | bytes 294920 | tf_op jit(solution)/shard_map/ppermute | solution.py:30
  39.2 6.4 %collective-permute-start.6 = (bf16[2,64,384]{2,1,0:T(8,128)(2,1)S(1)}, bf16[2,64,384]{2,1,0:T(8,128)(2,1)S(1)}, u32[]{:S(2)}, u32[]{:S(2)}) collective-permute-start(bf16[2,64,384]{2,1,0:T(8,128)(2,1)S(1)} %get-tuple-element.63.refs_5_.refs_6_), channel_id=1, source_target_pairs={{0,16},{16,0},{32,48},{48,32},{64,80},{80,64},{96,112},{112,96},{1... | collective-permute-start | bytes 294920 | tf_op jit(solution)/shard_map/ppermute | solution.py:30
  51.6 4.3 %collective-permute-start.14 = (f32[3,4,768]{2,1,0:T(4,128)}, f32[3,4,768]{2,1,0:T(4,128)S(1)}, u32[]{:S(2)}, u32[]{:S(2)}) collective-permute-start(f32[3,4,768]{2,1,0:T(4,128)} %get-tuple-element.68.refs_10_), channel_id=1, source_target_pairs={{0,192},{16,208},{32,224},{48,240},{64,128},{80,144},{96,160},{112... | collective-permute-start | bytes 110600 | tf_op jit(solution)/shard_map/ppermute | solution.py:25
  52.1 4.5 %collective-permute-start.13 = (f32[3,4,768]{2,1,0:T(4,128)}, f32[3,4,768]{2,1,0:T(4,128)S(1)}, u32[]{:S(2)}, u32[]{:S(2)}) collective-permute-start(f32[3,4,768]{2,1,0:T(4,128)} %get-tuple-element.68.refs_10_), channel_id=1, source_target_pairs={{0,128},{16,144},{32,160},{48,176},{64,192},{80,208},{96,224},{112... | collective-permute-start | bytes 110600 | tf_op jit(solution)/shard_map/ppermute | solution.py:25
  52.7 4.2 %collective-permute-start.12 = (f32[3,4,768]{2,1,0:T(4,128)}, f32[3,4,768]{2,1,0:T(4,128)S(1)}, u32[]{:S(2)}, u32[]{:S(2)}) collective-permute-start(f32[3,4,768]{2,1,0:T(4,128)} %get-tuple-element.68.refs_10_), channel_id=1, source_target_pairs={{0,64},{16,80},{32,96},{48,112},{64,0},{80,16},{96,32},{112,48},{1... | collective-permute-start | bytes 110600 | tf_op jit(solution)/shard_map/ppermute | solution.py:25
  64.8 35.1 %collective-permute-start.16 = (bf16[2,192,384]{2,1,0:T(8,128)(2,1)}, bf16[2,192,384]{2,1,0:T(8,128)(2,1)S(1)}, u32[]{:S(2)}, u32[]{:S(2)}) collective-permute-start(bf16[2,192,384]{2,1,0:T(8,128)(2,1)} %get-tuple-element.76), channel_id=1, source_target_pairs={{0,16},{16,0},{32,48},{48,32},{64,80},{80,64},{96,112},{112,96},{1... | collective-permute-start | bytes 884744 | tf_op jit(solution)/shard_map/ppermute | solution.py:30
  65.9 34.0 %collective-permute-start.17 = (bf16[2,192,384]{2,1,0:T(8,128)(2,1)}, bf16[2,192,384]{2,1,0:T(8,128)(2,1)S(1)}, u32[]{:S(2)}, u32[]{:S(2)}) collective-permute-start(bf16[2,192,384]{2,1,0:T(8,128)(2,1)} %get-tuple-element.77), channel_id=1, source_target_pairs={{0,32},{16,48},{32,0},{48,16},{64,96},{80,112},{96,64},{112,80},{1... | collective-permute-start | bytes 884744 | tf_op jit(solution)/shard_map/ppermute | solution.py:30
  68.2 31.7 %collective-permute-start.18 = (bf16[2,192,384]{2,1,0:T(8,128)(2,1)}, bf16[2,192,384]{2,1,0:T(8,128)(2,1)S(1)}, u32[]{:S(2)}, u32[]{:S(2)}) collective-permute-start(bf16[2,192,384]{2,1,0:T(8,128)(2,1)} %get-tuple-element.78), channel_id=1, source_target_pairs={{0,48},{16,32},{32,16},{48,0},{64,112},{80,96},{96,80},{112,64},{1... | collective-permute-start | bytes 884744 | tf_op jit(solution)/shard_map/ppermute | solution.py:30
  68.5 31.4 %copy-start = (bf16[2,192,384]{2,1,0:T(8,128)(2,1)S(1)}, bf16[2,192,384]{2,1,0:T(8,128)(2,1)}, u32[]{:S(2)}) copy-start(bf16[2,192,384]{2,1,0:T(8,128)(2,1)} %get-tuple-element.75.refs_0_) | copy-start | bytes 884740
  83.1 5.6 %collective-permute-start.4 = (f32[8,384]{1,0:T(8,128)S(1)}, f32[8,384]{1,0:T(8,128)S(1)}, u32[]{:S(2)}, u32[]{:S(2)}) collective-permute-start(f32[8,384]{1,0:T(8,128)S(1)} %get-tuple-element.14), channel_id=1, source_target_pairs={{0,16},{16,0},{32,48},{48,32},{64,80},{80,64},{96,112},{112,96},{1... | collective-permute-start | bytes 36872 | tf_op jit(solution)/shard_map/cond/branch_1_fun/ppermute | solution.py:30
  88.8 3.6 %collective-permute-start.5 = (f32[8,384]{1,0:T(8,128)S(1)}, f32[8,384]{1,0:T(8,128)S(1)}, u32[]{:S(2)}, u32[]{:S(2)}) collective-permute-start(f32[8,384]{1,0:T(8,128)S(1)} %add.18), channel_id=1, source_target_pairs={{0,32},{16,48},{32,0},{48,16},{64,96},{80,112},{96,64},{112,80},{1... | collective-permute-start | bytes 36872 | tf_op jit(solution)/shard_map/cond/branch_1_fun/ppermute | solution.py:30
  92.4 8.3 %collective-permute-start.15 = (f32[8,384]{1,0:T(8,128)S(1)}, f32[8,384]{1,0:T(8,128)S(1)}, u32[]{:S(2)}, u32[]{:S(2)}) collective-permute-start(f32[8,384]{1,0:T(8,128)S(1)} %get-tuple-element.74), channel_id=1, source_target_pairs={{0,1},{1,0},{2,3},{3,2},{4,5},{5,4},{6,7},{7,6},{8,9},{9,8},{10,11... | collective-permute-start | bytes 36872 | tf_op jit(solution)/shard_map/ppermute | solution.py:437
  (9 other events, 12.6 us)

commit v13 on v12

--- a/solution.py
+++ b/solution.py
@@ -63,15 +63,15 @@
 
 
 def queries_of(gathered_ref, audio_ref, video_rows):
-    return jnp.concatenate([flat(gathered_ref[:, :video_rows]), flat(audio_ref[...])], axis=0)
-
-
-def upstreams_of(gathered_ref, video_rows):
-    return flat(gathered_ref[:, video_rows : 2 * video_rows]), flat(gathered_ref[:, 2 * video_rows :])
-
-
-def upstream(gathered_ref, gates_ref, video_rows, part):
-    video, audio = upstreams_of(gathered_ref, video_rows)
+    return jnp.concatenate([flat(gathered_ref[:, :video_rows]), flat(audio_ref[:, 0])], axis=0)
+
+
+def upstreams_of(gathered_ref, audio_ref, video_rows):
+    return flat(gathered_ref[:, video_rows:]), flat(audio_ref[:, 1])
+
+
+def upstream(gathered_ref, audio_ref, gates_ref, video_rows, part):
+    video, audio = upstreams_of(gathered_ref, audio_ref, video_rows)
     if part == VIDEO:
         audio = gated(audio, gates_ref[1:2, :])
     else:
@@ -79,20 +79,21 @@
     return jnp.concatenate([video, audio], axis=0)
 
 
-def split_audio_kernel(audio_ref, queries_ref, keys_ref):
-    queries_ref[...] = audio_ref[0]
+def split_audio_kernel(audio_ref, up_ref, queries_ref, keys_ref):
+    queries_ref[0] = audio_ref[0]
+    queries_ref[1] = up_ref[0]
     keys_ref[0] = audio_ref[1]
     keys_ref[1] = audio_ref[2]
 
 
-def split_audio(audio):
+def split_audio(audio, d_audio):
     _, rows, width = audio.shape
     return pl.pallas_call(
         split_audio_kernel,
-        out_shape=[like(rows, width), like(2, rows, width)],
+        out_shape=[like(2, rows, width)] * 2,
         compiler_params=pltpu.CompilerParams(vmem_limit_bytes=8 * 2**20),
         name="split_audio",
-    )(audio)
+    )(audio, d_audio)
 
 
 def audio_target(vid, aud):
@@ -102,46 +103,48 @@
     return SIDE * y + 2 * half + (z & 1), 2 * to_y + (z >> 1)
 
 
-def prepare_kernel(aq_ref, ak_ref, av_ref, vq_ref, vk_ref, vv_ref, dv_ref, da_ref, audio, video_kv, queries, sems):
+def prepare_kernel(aq_ref, ak_ref, av_ref, vq_ref, vk_ref, vv_ref, dv_ref, vg_ref, ag_ref, *outs):
+    audio, video_kv, queries, gates, sems = outs
     to_vid, to_aud = audio_target(lax.axis_index("vid"), lax.axis_index("aud"))
     rows, width = vq_ref.shape[1:]
-    audio_rows = da_ref.shape[1]
+    audio_rows = audio.shape[1]
     taken = pl.ds(pl.multiple_of((to_vid & 1) * audio_rows, audio_rows), audio_rows)
     columns = pl.ds(pl.multiple_of(to_aud * width, HEAD_DIM), width)
     pairs = [(ref.at[0, taken, columns], audio.at[index]) for index, ref in enumerate((aq_ref, ak_ref, av_ref))]
     pairs += [(vk_ref.at[0], video_kv.at[0]), (vv_ref.at[0], video_kv.at[1])]
     pairs += [(vq_ref.at[0], queries.at[pl.ds(0, rows)]), (dv_ref.at[0], queries.at[pl.ds(rows, rows)])]
-    pairs += [(da_ref.at[0], queries.at[pl.ds(2 * rows, audio_rows)])]
     copies = [pltpu.make_async_copy(source, target, sems.at[index]) for index, (source, target) in enumerate(pairs)]
     for copy in copies:
         copy.start()
+    gates[...] = jnp.concatenate([vg_ref[...].reshape(1, width), ag_ref[...].reshape(1, width)], axis=0)
     for copy in copies:
         copy.wait()
 
 
-def prepare(audio_q, audio_k, audio_v, video_q, video_k, video_v, d_video, d_audio):
-    _, video_rows, width = video_q.shape
-    audio_rows = d_audio.shape[1]
-    given = (audio_q, audio_k, audio_v, video_q, video_k, video_v, d_video, d_audio)
-    shapes = [(3, audio_rows, width), (2, video_rows, width), (2 * video_rows + audio_rows, width)]
+def prepare(audio_rows, *given):
+    _, video_rows, width = given[3].shape
+    outs = [like(3, audio_rows, width), like(2, video_rows, width), like(2 * video_rows, width)]
     return pl.pallas_call(
         prepare_kernel,
-        in_specs=[pl.BlockSpec(memory_space=pl.ANY)] * len(given),
-        out_specs=[pl.BlockSpec(memory_space=pltpu.VMEM)] * len(shapes),
-        out_shape=[like(*shape) for shape in shapes],
-        scratch_shapes=[pltpu.SemaphoreType.DMA((len(given),))],
+        in_specs=[pl.BlockSpec(memory_space=pl.ANY)] * 7 + [pl.BlockSpec(memory_space=pltpu.VMEM)] * 2,
+        out_specs=[pl.BlockSpec(memory_space=pltpu.VMEM)] * 4,
+        out_shape=[*outs, like(2, width, kind=F32)],
+        scratch_shapes=[pltpu.SemaphoreType.DMA((7,))],
         compiler_params=pltpu.CompilerParams(vmem_limit_bytes=VMEM),
         name="prepare",
     )(*given)
 
 
-def scores(keys, queries, part, numbers_ref):
+def scores(keys, queries, part, length_ref):
     raw = nt(keys, queries)
     if part == AUDIO:
         rows = raw.shape[0] // SIDE
         position = lax.broadcasted_iota(jnp.int32, (rows, raw.shape[1]), 0)
         pieces = [raw[place * rows : (place + 1) * rows] for place in range(SIDE)]
-        pieces = [jnp.where(position < numbers_ref[place], pieces[place], -1e30) for place in range(SIDE)]
+        vid = lax.axis_index("vid")
+        for place in range(SIDE):
+            chunk = (vid & ~(SIDE - 1)) + ((vid & (SIDE - 1)) ^ place)
+            pieces[place] = jnp.where(position < length_ref[0] - chunk * rows, pieces[place], -1e30)
         raw = jnp.concatenate(pieces, axis=0)
     return raw
 
@@ -158,21 +161,21 @@
 def forward_video_kernel(video_rows, *refs):
     gathered_ref, k_refs, o_ref, stats_ref = refs[0], refs[1:5], refs[5], refs[6]
     raw = scores(joined(k_refs, 0), flat(gathered_ref[:, :video_rows]), VIDEO, None)
-    o_ref[0], stats_ref[0] = attend(raw, joined(k_refs, 1), upstreams_of(gathered_ref, video_rows)[0])
+    o_ref[0], stats_ref[0] = attend(raw, joined(k_refs, 1), flat(gathered_ref[:, video_rows:]))
 
 
 def forward_kernel(video_rows, *refs):
-    gathered_ref, k_refs, audio_q, numbers_ref, gates_ref = refs[0], (refs[1:5], refs[5:9]), refs[9:13], refs[13], refs[14]
+    gathered_ref, k_refs, audio_q, length_ref, gates_ref = refs[0], (refs[1:5], refs[5:9]), refs[9:13], refs[13], refs[14]
     o_video_ref, stats_video_ref, o_ref, stats_ref, ordered_ref = refs[15:20]
     for place in range(SIDE):
-        ordered_ref[numbers_ref[SIDE] ^ place] = audio_q[place][...]
-    up_audio = gated(upstreams_of(gathered_ref, video_rows)[1], gates_ref[1:2, :])
-    raw = scores(joined(k_refs[VIDEO], 0), flat(ordered_ref[...]), VIDEO, None)
+        ordered_ref[(lax.axis_index("vid") >> 2) ^ place] = audio_q[place][...]
+    up_audio = gated(flat(ordered_ref[:, 1]), gates_ref[1:2, :])
+    raw = scores(joined(k_refs[VIDEO], 0), flat(ordered_ref[:, 0]), VIDEO, None)
     output, stats = attend(raw, joined(k_refs[VIDEO], 1), up_audio)
     o_ref[0, VIDEO] = jnp.concatenate([o_video_ref[0], output], axis=1)
     stats_video = jnp.concatenate([stats_video_ref[0], stats], axis=1)
-    raw = scores(joined(k_refs[AUDIO], 0), queries_of(gathered_ref, ordered_ref, video_rows), AUDIO, numbers_ref)
-    up = upstream(gathered_ref, gates_ref, video_rows, AUDIO)
+    raw = scores(joined(k_refs[AUDIO], 0), queries_of(gathered_ref, ordered_ref, video_rows), AUDIO, length_ref)
+    up = upstream(gathered_ref, ordered_ref, gates_ref, video_rows, AUDIO)
     o_ref[0, AUDIO], stats = attend(raw, joined(k_refs[AUDIO], 1), up)
     stats_ref[0] = jnp.concatenate([stats_video, stats], axis=0)
 
@@ -187,9 +190,9 @@
     return peak + jnp.log(total), delta, weights[0] * scale
 
 
-def backward_keys(part, queries, up, stats_refs, k_refs, numbers_ref, k_outs, first):
+def backward_keys(part, queries, up, stats_refs, k_refs, length_ref, k_outs, first):
     log_total, delta, factor = merged_stats(stats_refs, part)
-    raw = scores(joined(k_refs, 0), queries, part, numbers_ref)
+    raw = scores(joined(k_refs, 0), queries, part, length_ref)
     probs = jnp.exp2(raw * (SCALE * LOG2_E) - log_total * LOG2_E)
     grad_values = nn(probs.astype(BF16), up).astype(BF16)
     grad_probs = nt(joined(k_refs, 1), up)
@@ -208,17 +211,17 @@
 
 def backward_kernel(video_rows, *refs):
     gathered_ref, audio_q, k_video, k_audio, stats_refs = refs[0], refs[1], refs[2:6], refs[6:10], refs[10:14]
-    gates_ref, numbers_ref, o_ref = refs[14:17]
+    gates_ref, length_ref, o_ref = refs[14:17]
     k_outs, q_out = refs[17:21], refs[21]
-    audio_rows = audio_q.shape[1]
+    audio_rows = audio_q.shape[2]
     rows = video_rows + audio_rows
     video = SIDE * video_rows
     queries = queries_of(gathered_ref, audio_q, video_rows)
-    up = upstream(gathered_ref, gates_ref, video_rows, VIDEO)
-    term_video, factor = backward_keys(VIDEO, queries, up, stats_refs, k_video, numbers_ref, k_outs, 0)
+    up = upstream(gathered_ref, audio_q, gates_ref, video_rows, VIDEO)
+    term_video, factor = backward_keys(VIDEO, queries, up, stats_refs, k_video, length_ref, k_outs, 0)
     on_video = o_ref[0, VIDEO].astype(F32) * factor
-    up = upstream(gathered_ref, gates_ref, video_rows, AUDIO)
-    term_audio, factor = backward_keys(AUDIO, queries, up, stats_refs, k_audio, numbers_ref, k_outs, video_rows)
+    up = upstream(gathered_ref, audio_q, gates_ref, video_rows, AUDIO)
+    term_audio, factor = backward_keys(AUDIO, queries, up, stats_refs, k_audio, length_ref, k_outs, video_rows)
     on_audio = o_ref[0, AUDIO].astype(F32) * factor
     grad_queries = term_video + term_audio
     cross_video, cross_audio = on_audio[:, :video], on_video[:, video:]
@@ -229,7 +232,7 @@
         ],
         axis=1,
     )
-    up_video, up_audio = upstreams_of(gathered_ref, video_rows)
+    up_video, up_audio = upstreams_of(gathered_ref, audio_q, video_rows)
     video_sum = jnp.sum(up_video.T.astype(F32) * cross_video, axis=1, keepdims=True)
     audio_sum = jnp.sum(up_audio.T.astype(F32) * cross_audio, axis=1, keepdims=True)
     sums = jnp.concatenate(
@@ -287,12 +290,12 @@
     )(*chunks)
 
 
-def attention_forward(queries, audio_q, video_keys, audio_keys, numbers, gates, earlier, video_rows):
+def attention_forward(queries, audio_q, video_keys, audio_keys, audio_len, gates, earlier, video_rows):
     heads = gates.shape[1] // HEAD_DIM
-    audio_rows, width = audio_q[0].shape
+    _, audio_rows, width = audio_q[0].shape
     total = SIDE * (video_rows + audio_rows)
     outs = [like(heads, 2, HEAD_DIM, total), like(heads, 4, total, kind=F32)]
-    ordered = like(SIDE, audio_rows, width)
+    ordered = like(SIDE, 2, audio_rows, width)
     chunks = [queries, *video_keys, *audio_keys, *audio_q]
     return pl.pallas_call(
         functools.partial(forward_kernel, video_rows),
@@ -305,13 +308,13 @@
         cost_estimate=cost(total, total, heads, 1),
         compiler_params=pltpu.CompilerParams(vmem_limit_bytes=VMEM),
         name="forward",
-    )(*chunks, numbers, gates, *earlier)
-
-
-def attention_backward(queries, audio_q, video_keys, audio_keys, stats, gates, numbers, outputs, video_rows):
+    )(*chunks, audio_len, gates, *earlier)
+
+
+def attention_backward(queries, audio_q, video_keys, audio_keys, stats, gates, audio_len, outputs, video_rows):
     width = gates.shape[1]
     heads = width // HEAD_DIM
-    rows = video_rows + audio_q.shape[1]
+    rows = video_rows + audio_q.shape[2]
     outs = [like(2, rows, width)] * SIDE + [like(SIDE, 2 * rows + GATE_ROWS, width)]
     chunks = [queries, audio_q, *video_keys, *audio_keys]
     *key_parts, query_parts = pl.pallas_call(
@@ -325,7 +328,7 @@
         cost_estimate=cost(SIDE * rows, SIDE * rows, heads, 4),
         compiler_params=pltpu.CompilerParams(vmem_limit_bytes=VMEM),
         name="backward",
-    )(*chunks, *stats, gates, numbers, outputs)
+    )(*chunks, *stats, gates, audio_len, outputs)
     return key_parts, query_parts
 
 
@@ -401,8 +404,8 @@
     vid = lax.axis_index("vid")
     video_rows, audio_rows = video_q.shape[1], d_audio_out.shape[1]
     holds = audio_len[0] > 0
-    send_audio, video_kv, queries = prepare(
-        audio_q, audio_k, audio_v, video_q, video_k, video_v, d_video_out, d_audio_out
+    send_audio, video_kv, queries, gates = prepare(
+        audio_rows, audio_q, audio_k, audio_v, video_q, video_k, video_v, d_video_out, video_gate, audio_gate
     )
 
     def first_chunks(send_audio, video_kv, queries):
@@ -410,19 +413,15 @@
 
     audio, video_keys, queries = fenced(holds, first_chunks, send_audio, video_kv, queries)
     video_keys = [video_kv, *video_keys]
-    audio_queries, audio_keys = split_audio(audio)
+    audio_queries, audio_keys = split_audio(audio, d_audio_out)
     audio_keys = gathered(audio_keys, along_z)
     audio_queries = gathered(audio_queries, along_x)
-    gates = jnp.stack([video_gate, audio_gate])
-    column, row = vid // SIDE, vid % SIDE
-    limits = [audio_len[0] - (column * SIDE + (row ^ p)) * audio_rows for p in range(SIDE)]
-    numbers = jnp.stack([*limits, column])
     earlier = attention_forward_video(queries, video_keys, video_rows)
     outputs, stats, audio_queries = attention_forward(
-        queries, audio_queries, video_keys, audio_keys, numbers, gates, earlier, video_rows
+        queries, audio_queries, video_keys, audio_keys, audio_len, gates, earlier, video_rows
     )
     key_parts, query_parts = attention_backward(
-        queries, audio_queries, video_keys, audio_keys, gathered(stats, along_x), gates, numbers, outputs, video_rows
+        queries, audio_queries, video_keys, audio_keys, gathered(stats, along_x), gates, audio_len, outputs, video_rows
     )
 
     def query_results(parts):

time: 102 us -> 102 us (level)
  Pallas kernels: 20.2 us -> 21.5 us
    pallas_call x1, Pallas kernels: 1.22 us -> 2.48 us  [prepare(): pl.pallas_call(prepare_kernel, in_specs=[pl.BlockSpec(memory_space=pl.ANY...]
  transfers between devices with their start and end apart: 19 -> 19, of which waited for: 6 -> 6; matrix products, arithmetic and copies ran while one was open for 1% -> 0% of each run, Pallas kernels for 5% -> 5%
where the time goes in v13:
time: 102 us
  starting transfers between devices  35.9 us (35%)
  blocking collectives  28.1 us (28%)
  Pallas kernels  21.5 us (21%)
  waiting for transfers between devices  12.8 us (13%)
  local copies, waits for them, and re-layouts  1.87 us (2%)
  between operations  1.47 us (1%)
    ppermute x11, starting transfers between devices, along_z(): return lax.ppermute(array, 'vid', pairs)  18.4 us
    all_gather x1, blocking collectives, all_along_x(): return lax.all_gather(array, 'vid', axis=0, axis_index_groups=ALONG_X)  14.2 us
    all_to_all x1, blocking collectives, query_results(): lax.all_to_all(parts, 'vid', 0, 0, axis_index_groups=ALONG_X, tiled=True)  13.9 us
    ppermute x11, waiting for transfers between devices, along_z(): return lax.ppermute(array, 'vid', pairs)  10.8 us
    ppermute x1, starting transfers between devices, shards(): other = lax.ppermute(gate, 'pair', [(0, 1), (1, 0)])  7.94 us
    pallas_call x1, Pallas kernels, attention_backward(): pl.pallas_call(functools.partial(backward_kernel, video_rows), grid=(head...  7.29 us
    ppermute x6, starting transfers between devices, along_x(): return lax.ppermute(array, 'vid', pairs)  6.68 us
    pallas_call x1, Pallas kernels, attention_forward(): pl.pallas_call(functools.partial(forward_kernel, video_rows), grid=(heads...  5.3 us
  transfers between devices with their start and end apart: 19, of which 6 were waited for; matrix products, arithmetic and copies ran while one was open for 0% of the time, Pallas kernels for 5%

profile of v13, /device:TPU:1, one launch (start us, length us, event | category | flops | bytes accessed | tf_op | source)
XLA Modules:
  0.0 101.6 jit_solution(10746308493093120820)
XLA Ops:
  1.3 2.5 %prepare.1 = (bf16[3,64,384]{2,1,0:T(8,128)(2,1)S(1)}, bf16[2,128,384]{2,1,0:T(8,128)(2,1)S(1)}, bf16[256,384]{1,0:T(8,128)(2,1)S(1)}, f32[2,384]{1,0:T(2,128)}) custom-call(bf16[1,128,3072]{2,1,0:T(8,128)(2,1)} %aq_ref.1, bf16[1,128,3072]{2,1,0:T(8,128)(2,1)} %ak_ref.1, bf16[1,128,3072]{2,1,0:T(8,128)(2,1)} %av_ref.1, bf16[1,128,384]{2,1,0:T(8,128)(2,1)} %vq_ref.1, ...), custom_call_target="tpu_custom_call" | custom-call | tf_op jit(solution)/shard_map/prepare/pallas_call | solution.py:127
  3.8 22.8 %conditional.2 = (bf16[3,64,384]{2,1,0:T(8,128)(2,1)}, bf16[2,128,384]{2,1,0:T(8,128)(2,1)}, bf16[2,128,384]{2,1,0:T(8,128)(2,1)}, bf16[2,128,384]{2,1,0:T(8,128)(2,1)}, bf16[4,256,384]{2,1,0:T(8,128)(2,1)S(1)}) conditional(s32[]{:T(128)} %bitcast.1, () %tuple.26, (bf16[3,64,384]{2,1,0:T(8,128)(2,1)S(1)}, bf16[2,128,384]{2,1,0:T(8,128)(2,1)S(1)}, ...), branch_computations={%region_0.0_spmd, %region_1.0_spmd} | conditional | bytes 3932360 | solution.py:396
  3.8 5.3 %collective-permute-start.3 = (bf16[2,128,384]{2,1,0:T(8,128)(2,1)S(1)}, bf16[2,128,384]{2,1,0:T(8,128)(2,1)}, u32[]{:S(2)}, u32[]{:S(2)}) collective-permute-start(bf16[2,128,384]{2,1,0:T(8,128)(2,1)S(1)} %get-tuple-element.8), channel_id=1, source_target_pairs={{0,48},{16,32},{32,16},{48,0},{64,112},{80,96},{96,80},{112,64},{1... | collective-permute-start | bytes 589832 | tf_op jit(solution)/shard_map/cond/branch_1_fun/ppermute | solution.py:30
  9.5 2.9 %collective-permute-start = (bf16[3,64,384]{2,1,0:T(8,128)(2,1)S(1)}, bf16[3,64,384]{2,1,0:T(8,128)(2,1)}, u32[]{:S(2)}, u32[]{:S(2)}) collective-permute-start(bf16[3,64,384]{2,1,0:T(8,128)(2,1)S(1)} %get-tuple-element.7), channel_id=1, source_target_pairs={{0,8},{2,40},{4,72},{6,104},{8,136},{10,168},{12,200},{14,232},{16... | collective-permute-start | bytes 442376 | tf_op jit(solution)/shard_map/cond/branch_1_fun/ppermute | solution.py:391
  12.4 14.2 %all-gather = bf16[1024,384]{1,0:T(8,128)(2,1)S(1)} all-gather(bf16[256,384]{1,0:T(8,128)(2,1)S(1)} %get-tuple-element.9), channel_id=2, replica_groups={{0,64,128,192},{16,80,144,208},{32,96,160,224},{48,112,176,240},{1,65,1..., dimensions={0}, use_global_device_ids=true | all-gather | bytes 983040 | tf_op jit(solution)/shard_map/cond/branch_1_fun/all_gather | solution.py:34
  26.6 0.9 split_audio.1
  27.5 1.0 collective-permute-start.11
  29.3 1.6 %collective-permute-start.9 = (bf16[2,64,384]{2,1,0:T(8,128)(2,1)S(1)}, bf16[2,64,384]{2,1,0:T(8,128)(2,1)S(1)}, u32[]{:S(2)}, u32[]{:S(2)}) collective-permute-start(bf16[2,64,384]{2,1,0:T(8,128)(2,1)S(1)} %get-tuple-element.69.refs_9_), channel_id=1, source_target_pairs={{0,64},{16,80},{32,96},{48,112},{64,0},{80,16},{96,32},{112,48},{1... | collective-permute-start | bytes 294920 | tf_op jit(solution)/shard_map/ppermute | solution.py:25
  30.9 8.8 %collective-permute-start.8 = (bf16[2,64,384]{2,1,0:T(8,128)(2,1)S(1)}, bf16[2,64,384]{2,1,0:T(8,128)(2,1)S(1)}, u32[]{:S(2)}, u32[]{:S(2)}) collective-permute-start(bf16[2,64,384]{2,1,0:T(8,128)(2,1)S(1)} %get-tuple-element.68.refs_5_.refs_6_), channel_id=1, source_target_pairs={{0,48},{16,32},{32,16},{48,0},{64,112},{80,96},{96,80},{112,64},{1... | collective-permute-start | bytes 294920 | tf_op jit(solution)/shard_map/ppermute | solution.py:30
  40.0 3.9 %forward_video.1 = (bf16[3,128,512]{2,1,0:T(8,128)(2,1)}, f32[3,2,512]{2,1,0:T(2,128)}) custom-call(bf16[4,256,384]{2,1,0:T(8,128)(2,1)S(1)} %get-tuple-element.63.refs_0_, bf16[2,128,384]{2,1,0:T(8,128)(2,1)S(1)} %get-tuple-element.61.refs_1_.refs_2_, bf16[2,128,384]{2,1,0:T(8,128)(2,1)} %get-tuple-element.64.refs_2_.refs_3_, ...), custom_call_target="tpu_custom_call" | custom-call | flops 402653184 | bytes 3145728 | tf_op jit(solution)/shard_map/forward_video/pallas_call | solution.py:281
  43.9 2.2 %collective-permute-done.7.refs_7_.refs_8_ = bf16[2,64,384]{2,1,0:T(8,128)(2,1)S(1)} collective-permute-done((bf16[2,64,384]{2,1,0:T(8,128)(2,1)S(1)}, bf16[2,64,384]{2,1,0:T(8,128)(2,1)S(1)}, u32[]{:S(2)}, u32[]{:S(2)}) %collective-permute-start.7) | collective-permute-done | bytes 98336 | tf_op jit(solution)/shard_map/ppermute | solution.py:30
  46.8 5.3 %forward.1 = (bf16[3,2,128,768]{3,2,1,0:T(8,128)(2,1)}, f32[3,4,768]{2,1,0:T(4,128)}, bf16[4,2,64,384]{3,2,1,0:T(8,128)(2,1)}) custom-call(bf16[4,256,384]{2,1,0:T(8,128)(2,1)S(1)} %get-tuple-element.63.refs_0_, bf16[2,128,384]{2,1,0:T(8,128)(2,1)S(1)} %get-tuple-element.61.refs_1_.refs_2_, bf16[2,128,384]{2,1,0:T(8,128)(2,1)} %get-tuple-element.64.refs_2_.refs_3_, ...), custom_call_target="tpu_custom_call" | custom-call | flops 452984832 | bytes 7077888 | tf_op jit(solution)/shard_map/forward/pallas_call | solution.py:300
  52.2 2.0 %collective-permute-start.13 = (f32[3,4,768]{2,1,0:T(4,128)}, f32[3,4,768]{2,1,0:T(4,128)S(1)}, u32[]{:S(2)}, u32[]{:S(2)}) collective-permute-start(f32[3,4,768]{2,1,0:T(4,128)} %get-tuple-element.74.refs_10_), channel_id=1, source_target_pairs={{0,128},{16,144},{32,160},{48,176},{64,192},{80,208},{96,224},{112... | collective-permute-start | bytes 110600 | tf_op jit(solution)/shard_map/ppermute | solution.py:25
  54.2 1.2 %collective-permute-start.12 = (f32[3,4,768]{2,1,0:T(4,128)}, f32[3,4,768]{2,1,0:T(4,128)S(1)}, u32[]{:S(2)}, u32[]{:S(2)}) collective-permute-start(f32[3,4,768]{2,1,0:T(4,128)} %get-tuple-element.74.refs_10_), channel_id=1, source_target_pairs={{0,64},{16,80},{32,96},{48,112},{64,0},{80,16},{96,32},{112,48},{1... | collective-permute-start | bytes 110600 | tf_op jit(solution)/shard_map/ppermute | solution.py:25
  55.4 1.0 collective-permute-done.14.refs_13_
  58.0 7.3 %backward.1 = (bf16[2,192,384]{2,1,0:T(8,128)(2,1)}, bf16[2,192,384]{2,1,0:T(8,128)(2,1)}, bf16[2,192,384]{2,1,0:T(8,128)(2,1)}, bf16[2,192,384]{2,1,0:T(8,128)(2,1)}, bf16[4,400,384]{2,1,0:T(8,128)(2,1)S(1)}) custom-call(bf16[4,256,384]{2,1,0:T(8,128)(2,1)S(1)} %get-tuple-element.63.refs_0_, bf16[4,2,64,384]{3,2,1,0:T(8,128)(2,1)} %get-tuple-element.73.refs_1_, ...), custom_call_target="tpu_custom_call" | custom-call | flops 1811939328 | bytes 7077888 | tf_op jit(solution)/shard_map/backward/pallas_call | solution.py:320
  65.7 2.3 %collective-permute-start.17 = (bf16[2,192,384]{2,1,0:T(8,128)(2,1)}, bf16[2,192,384]{2,1,0:T(8,128)(2,1)S(1)}, u32[]{:S(2)}, u32[]{:S(2)}) collective-permute-start(bf16[2,192,384]{2,1,0:T(8,128)(2,1)} %get-tuple-element.83), channel_id=1, source_target_pairs={{0,32},{16,48},{32,0},{48,16},{64,96},{80,112},{96,64},{112,80},{1... | collective-permute-start | bytes 884744 | tf_op jit(solution)/shard_map/ppermute | solution.py:30
  68.0 0.9 collective-permute-start.18
  68.9 23.3 %conditional.3 = (bf16[1,128,384]{2,1,0:T(8,128)(2,1)}, bf16[1,64,384]{2,1,0:T(8,128)(2,1)}, bf16[1,128,384]{2,1,0:T(8,128)(2,1)}, bf16[1,64,384]{2,1,0:T(8,128)(2,1)}, f32[8,384]{1,0:T(8,128)S(1)}) conditional(s32[]{:T(128)} %bitcast.1, () %tuple.25, bf16[4,400,384]{2,1,0:T(8,128)(2,1)S(1)} %get-tuple-element.76), branch_computations={%region_2.0_spmd, %region_3.0_spmd} | conditional | flops 6144 | bytes 2629752 | solution.py:396
  68.9 13.9 %all_to_all.4.parts_ref = bf16[4,400,384]{2,1,0:T(8,128)(2,1)S(1)} all-to-all(bf16[4,400,384]{2,1,0:T(8,128)(2,1)S(1)} %param.3), channel_id=1, replica_groups={{0,64,128,192},{16,80,144,208},{32,96,160,224},{48,112,176,240},{1,65,1..., dimensions={0} | all-to-all | bytes 2457600 | tf_op jit(solution)/shard_map/cond/branch_1_fun/all_to_all | solution.py:428
  82.8 0.8 finish_queries.1
  83.6 5.0 %collective-permute-done.4 = f32[8,384]{1,0:T(8,128)S(1)} collective-permute-done((f32[8,384]{1,0:T(8,128)S(1)}, f32[8,384]{1,0:T(8,128)S(1)}, u32[]{:S(2)}, u32[]{:S(2)}) %collective-permute-start.4) | collective-permute-done | bytes 12320 | tf_op jit(solution)/shard_map/cond/branch_1_fun/ppermute | solution.py:30
  88.6 3.6 %collective-permute-done.5 = f32[8,384]{1,0:T(8,128)S(1)} collective-permute-done((f32[8,384]{1,0:T(8,128)S(1)}, f32[8,384]{1,0:T(8,128)S(1)}, u32[]{:S(2)}, u32[]{:S(2)}) %collective-permute-start.5) | collective-permute-done | bytes 12320 | tf_op jit(solution)/shard_map/cond/branch_1_fun/ppermute | solution.py:30
  92.2 7.9 %collective-permute-start.15 = (f32[8,384]{1,0:T(8,128)S(1)}, f32[8,384]{1,0:T(8,128)S(1)}, u32[]{:S(2)}, u32[]{:S(2)}) collective-permute-start(f32[8,384]{1,0:T(8,128)S(1)} %get-tuple-element.80), channel_id=1, source_target_pairs={{0,1},{1,0},{2,3},{3,2},{4,5},{5,4},{6,7},{7,6},{8,9},{9,8},{10,11... | collective-permute-start | bytes 36872 | tf_op jit(solution)/shard_map/ppermute | solution.py:436
  (55 shorter events, 5.8 us)
Async XLA Ops:
  3.8 22.8 %copy-start.1 = (bf16[1,64,384]{2,1,0:T(8,128)(2,1)S(1)}, bf16[1,64,384]{2,1,0:T(8,128)(2,1)}, u32[]{:S(2)}) copy-start(bf16[1,64,384]{2,1,0:T(8,128)(2,1)} %up_ref.1) | copy-start | bytes 147460
  3.8 22.7 %collective-permute-start.3 = (bf16[2,128,384]{2,1,0:T(8,128)(2,1)S(1)}, bf16[2,128,384]{2,1,0:T(8,128)(2,1)}, u32[]{:S(2)}, u32[]{:S(2)}) collective-permute-start(bf16[2,128,384]{2,1,0:T(8,128)(2,1)S(1)} %get-tuple-element.8), channel_id=1, source_target_pairs={{0,48},{16,32},{32,16},{48,0},{64,112},{80,96},{96,80},{112,64},{1... | collective-permute-start | bytes 589832 | tf_op jit(solution)/shard_map/cond/branch_1_fun/ppermute | solution.py:30
  9.1 17.5 %collective-permute-start.2 = (bf16[2,128,384]{2,1,0:T(8,128)(2,1)S(1)}, bf16[2,128,384]{2,1,0:T(8,128)(2,1)}, u32[]{:S(2)}, u32[]{:S(2)}) collective-permute-start(bf16[2,128,384]{2,1,0:T(8,128)(2,1)S(1)} %get-tuple-element.8), channel_id=1, source_target_pairs={{0,32},{16,48},{32,0},{48,16},{64,96},{80,112},{96,64},{112,80},{1... | collective-permute-start | bytes 589832 | tf_op jit(solution)/shard_map/cond/branch_1_fun/ppermute | solution.py:30
  9.1 17.5 %collective-permute-start.1 = (bf16[2,128,384]{2,1,0:T(8,128)(2,1)S(1)}, bf16[2,128,384]{2,1,0:T(8,128)(2,1)}, u32[]{:S(2)}, u32[]{:S(2)}) collective-permute-start(bf16[2,128,384]{2,1,0:T(8,128)(2,1)S(1)} %get-tuple-element.8), channel_id=1, source_target_pairs={{0,16},{16,0},{32,48},{48,32},{64,80},{80,64},{96,112},{112,96},{1... | collective-permute-start | bytes 589832 | tf_op jit(solution)/shard_map/cond/branch_1_fun/ppermute | solution.py:30
  9.5 17.1 %collective-permute-start = (bf16[3,64,384]{2,1,0:T(8,128)(2,1)S(1)}, bf16[3,64,384]{2,1,0:T(8,128)(2,1)}, u32[]{:S(2)}, u32[]{:S(2)}) collective-permute-start(bf16[3,64,384]{2,1,0:T(8,128)(2,1)S(1)} %get-tuple-element.7), channel_id=1, source_target_pairs={{0,8},{2,40},{4,72},{6,104},{8,136},{10,168},{12,200},{14,232},{16... | collective-permute-start | bytes 442376 | tf_op jit(solution)/shard_map/cond/branch_1_fun/ppermute | solution.py:391
  27.5 18.6 %copy-start.2 = (bf16[2,64,384]{2,1,0:T(8,128)(2,1)}, bf16[2,64,384]{2,1,0:T(8,128)(2,1)S(1)}, u32[]{:S(2)}) copy-start(bf16[2,64,384]{2,1,0:T(8,128)(2,1)S(1)} %get-tuple-element.68.refs_5_.refs_6_) | copy-start | bytes 294916
  27.5 18.6 %copy-start.3 = (bf16[2,64,384]{2,1,0:T(8,128)(2,1)}, bf16[2,64,384]{2,1,0:T(8,128)(2,1)S(1)}, u32[]{:S(2)}) copy-start(bf16[2,64,384]{2,1,0:T(8,128)(2,1)S(1)} %get-tuple-element.69.refs_9_) | copy-start | bytes 294916
  27.5 12.1 %collective-permute-start.11 = (bf16[2,64,384]{2,1,0:T(8,128)(2,1)S(1)}, bf16[2,64,384]{2,1,0:T(8,128)(2,1)S(1)}, u32[]{:S(2)}, u32[]{:S(2)}) collective-permute-start(bf16[2,64,384]{2,1,0:T(8,128)(2,1)S(1)} %get-tuple-element.69.refs_9_), channel_id=1, source_target_pairs={{0,192},{16,208},{32,224},{48,240},{64,128},{80,144},{96,160},{112... | collective-permute-start | bytes 294920 | tf_op jit(solution)/shard_map/ppermute | solution.py:25
  28.5 15.3 %collective-permute-start.10 = (bf16[2,64,384]{2,1,0:T(8,128)(2,1)S(1)}, bf16[2,64,384]{2,1,0:T(8,128)(2,1)S(1)}, u32[]{:S(2)}, u32[]{:S(2)}) collective-permute-start(bf16[2,64,384]{2,1,0:T(8,128)(2,1)S(1)} %get-tuple-element.69.refs_9_), channel_id=1, source_target_pairs={{0,128},{16,144},{32,160},{48,176},{64,192},{80,208},{96,224},{112... | collective-permute-start | bytes 294920 | tf_op jit(solution)/shard_map/ppermute | solution.py:25
  29.3 14.6 %collective-permute-start.9 = (bf16[2,64,384]{2,1,0:T(8,128)(2,1)S(1)}, bf16[2,64,384]{2,1,0:T(8,128)(2,1)S(1)}, u32[]{:S(2)}, u32[]{:S(2)}) collective-permute-start(bf16[2,64,384]{2,1,0:T(8,128)(2,1)S(1)} %get-tuple-element.69.refs_9_), channel_id=1, source_target_pairs={{0,64},{16,80},{32,96},{48,112},{64,0},{80,16},{96,32},{112,48},{1... | collective-permute-start | bytes 294920 | tf_op jit(solution)/shard_map/ppermute | solution.py:25
  30.9 13.0 %collective-permute-start.8 = (bf16[2,64,384]{2,1,0:T(8,128)(2,1)S(1)}, bf16[2,64,384]{2,1,0:T(8,128)(2,1)S(1)}, u32[]{:S(2)}, u32[]{:S(2)}) collective-permute-start(bf16[2,64,384]{2,1,0:T(8,128)(2,1)S(1)} %get-tuple-element.68.refs_5_.refs_6_), channel_id=1, source_target_pairs={{0,48},{16,32},{32,16},{48,0},{64,112},{80,96},{96,80},{112,64},{1... | collective-permute-start | bytes 294920 | tf_op jit(solution)/shard_map/ppermute | solution.py:30
  39.7 6.4 %collective-permute-start.7 = (bf16[2,64,384]{2,1,0:T(8,128)(2,1)S(1)}, bf16[2,64,384]{2,1,0:T(8,128)(2,1)S(1)}, u32[]{:S(2)}, u32[]{:S(2)}) collective-permute-start(bf16[2,64,384]{2,1,0:T(8,128)(2,1)S(1)} %get-tuple-element.68.refs_5_.refs_6_), channel_id=1, source_target_pairs={{0,32},{16,48},{32,0},{48,16},{64,96},{80,112},{96,64},{112,80},{1... | collective-permute-start | bytes 294920 | tf_op jit(solution)/shard_map/ppermute | solution.py:30
  39.7 6.5 %copy-start.7 = (bf16[2,64,384]{2,1,0:T(8,128)(2,1)}, bf16[2,64,384]{2,1,0:T(8,128)(2,1)S(1)}, u32[]{:S(2)}) copy-start(bf16[2,64,384]{2,1,0:T(8,128)(2,1)S(1)} %collective-permute-done.11.refs_12_) | copy-start | bytes 294916
  39.7 6.4 %collective-permute-start.6 = (bf16[2,64,384]{2,1,0:T(8,128)(2,1)S(1)}, bf16[2,64,384]{2,1,0:T(8,128)(2,1)S(1)}, u32[]{:S(2)}, u32[]{:S(2)}) collective-permute-start(bf16[2,64,384]{2,1,0:T(8,128)(2,1)S(1)} %get-tuple-element.68.refs_5_.refs_6_), channel_id=1, source_target_pairs={{0,16},{16,0},{32,48},{48,32},{64,80},{80,64},{96,112},{112,96},{1... | collective-permute-start | bytes 294920 | tf_op jit(solution)/shard_map/ppermute | solution.py:30
  52.1 4.3 %collective-permute-start.14 = (f32[3,4,768]{2,1,0:T(4,128)}, f32[3,4,768]{2,1,0:T(4,128)S(1)}, u32[]{:S(2)}, u32[]{:S(2)}) collective-permute-start(f32[3,4,768]{2,1,0:T(4,128)} %get-tuple-element.74.refs_10_), channel_id=1, source_target_pairs={{0,192},{16,208},{32,224},{48,240},{64,128},{80,144},{96,160},{112... | collective-permute-start | bytes 110600 | tf_op jit(solution)/shard_map/ppermute | solution.py:25
  52.2 4.6 %collective-permute-start.13 = (f32[3,4,768]{2,1,0:T(4,128)}, f32[3,4,768]{2,1,0:T(4,128)S(1)}, u32[]{:S(2)}, u32[]{:S(2)}) collective-permute-start(f32[3,4,768]{2,1,0:T(4,128)} %get-tuple-element.74.refs_10_), channel_id=1, source_target_pairs={{0,128},{16,144},{32,160},{48,176},{64,192},{80,208},{96,224},{112... | collective-permute-start | bytes 110600 | tf_op jit(solution)/shard_map/ppermute | solution.py:25
  54.2 3.1 %collective-permute-start.12 = (f32[3,4,768]{2,1,0:T(4,128)}, f32[3,4,768]{2,1,0:T(4,128)S(1)}, u32[]{:S(2)}, u32[]{:S(2)}) collective-permute-start(f32[3,4,768]{2,1,0:T(4,128)} %get-tuple-element.74.refs_10_), channel_id=1, source_target_pairs={{0,64},{16,80},{32,96},{48,112},{64,0},{80,16},{96,32},{112,48},{1... | collective-permute-start | bytes 110600 | tf_op jit(solution)/shard_map/ppermute | solution.py:25
  65.3 34.9 %collective-permute-start.16 = (bf16[2,192,384]{2,1,0:T(8,128)(2,1)}, bf16[2,192,384]{2,1,0:T(8,128)(2,1)S(1)}, u32[]{:S(2)}, u32[]{:S(2)}) collective-permute-start(bf16[2,192,384]{2,1,0:T(8,128)(2,1)} %get-tuple-element.82), channel_id=1, source_target_pairs={{0,16},{16,0},{32,48},{48,32},{64,80},{80,64},{96,112},{112,96},{1... | collective-permute-start | bytes 884744 | tf_op jit(solution)/shard_map/ppermute | solution.py:30
  65.7 34.4 %collective-permute-start.17 = (bf16[2,192,384]{2,1,0:T(8,128)(2,1)}, bf16[2,192,384]{2,1,0:T(8,128)(2,1)S(1)}, u32[]{:S(2)}, u32[]{:S(2)}) collective-permute-start(bf16[2,192,384]{2,1,0:T(8,128)(2,1)} %get-tuple-element.83), channel_id=1, source_target_pairs={{0,32},{16,48},{32,0},{48,16},{64,96},{80,112},{96,64},{112,80},{1... | collective-permute-start | bytes 884744 | tf_op jit(solution)/shard_map/ppermute | solution.py:30
  68.0 32.2 %collective-permute-start.18 = (bf16[2,192,384]{2,1,0:T(8,128)(2,1)}, bf16[2,192,384]{2,1,0:T(8,128)(2,1)S(1)}, u32[]{:S(2)}, u32[]{:S(2)}) collective-permute-start(bf16[2,192,384]{2,1,0:T(8,128)(2,1)} %get-tuple-element.84), channel_id=1, source_target_pairs={{0,48},{16,32},{32,16},{48,0},{64,112},{80,96},{96,80},{112,64},{1... | collective-permute-start | bytes 884744 | tf_op jit(solution)/shard_map/ppermute | solution.py:30
  68.9 31.3 %copy-start = (bf16[2,192,384]{2,1,0:T(8,128)(2,1)S(1)}, bf16[2,192,384]{2,1,0:T(8,128)(2,1)}, u32[]{:S(2)}) copy-start(bf16[2,192,384]{2,1,0:T(8,128)(2,1)} %get-tuple-element.81.refs_0_) | copy-start | bytes 884740
  83.6 5.0 %collective-permute-start.4 = (f32[8,384]{1,0:T(8,128)S(1)}, f32[8,384]{1,0:T(8,128)S(1)}, u32[]{:S(2)}, u32[]{:S(2)}) collective-permute-start(f32[8,384]{1,0:T(8,128)S(1)} %get-tuple-element.14), channel_id=1, source_target_pairs={{0,16},{16,0},{32,48},{48,32},{64,80},{80,64},{96,112},{112,96},{1... | collective-permute-start | bytes 36872 | tf_op jit(solution)/shard_map/cond/branch_1_fun/ppermute | solution.py:30
  88.6 3.6 %collective-permute-start.5 = (f32[8,384]{1,0:T(8,128)S(1)}, f32[8,384]{1,0:T(8,128)S(1)}, u32[]{:S(2)}, u32[]{:S(2)}) collective-permute-start(f32[8,384]{1,0:T(8,128)S(1)} %add.6), channel_id=1, source_target_pairs={{0,32},{16,48},{32,0},{48,16},{64,96},{80,112},{96,64},{112,80},{1... | collective-permute-start | bytes 36872 | tf_op jit(solution)/shard_map/cond/branch_1_fun/ppermute | solution.py:30
  92.2 8.8 %collective-permute-start.15 = (f32[8,384]{1,0:T(8,128)S(1)}, f32[8,384]{1,0:T(8,128)S(1)}, u32[]{:S(2)}, u32[]{:S(2)}) collective-permute-start(f32[8,384]{1,0:T(8,128)S(1)} %get-tuple-element.80), channel_id=1, source_target_pairs={{0,1},{1,0},{2,3},{3,2},{4,5},{5,4},{6,7},{7,6},{8,9},{9,8},{10,11... | collective-permute-start | bytes 36872 | tf_op jit(solution)/shard_map/ppermute | solution.py:436
  (8 other events, 10.3 us)

commit v14 on v13

--- a/solution.py
+++ b/solution.py
@@ -70,12 +70,17 @@
     return flat(gathered_ref[:, video_rows:]), flat(audio_ref[:, 1])
 
 
-def upstream(gathered_ref, audio_ref, gates_ref, video_rows, part):
+def head_row(ref):
+    first = pl.multiple_of(pl.program_id(0) * HEAD_DIM, HEAD_DIM)
+    return ref[pl.ds(first, HEAD_DIM)].reshape(1, HEAD_DIM)
+
+
+def upstream(gathered_ref, audio_ref, gate_rows, video_rows, part):
     video, audio = upstreams_of(gathered_ref, audio_ref, video_rows)
     if part == VIDEO:
-        audio = gated(audio, gates_ref[1:2, :])
+        audio = gated(audio, gate_rows[AUDIO])
     else:
-        video = gated(video, gates_ref[0:1, :])
+        video = gated(video, gate_rows[VIDEO])
     return jnp.concatenate([video, audio], axis=0)
 
 
@@ -103,8 +108,7 @@
     return SIDE * y + 2 * half + (z & 1), 2 * to_y + (z >> 1)
 
 
-def prepare_kernel(aq_ref, ak_ref, av_ref, vq_ref, vk_ref, vv_ref, dv_ref, vg_ref, ag_ref, *outs):
-    audio, video_kv, queries, gates, sems = outs
+def prepare_kernel(aq_ref, ak_ref, av_ref, vq_ref, vk_ref, vv_ref, dv_ref, audio, video_kv, queries, sems):
     to_vid, to_aud = audio_target(lax.axis_index("vid"), lax.axis_index("aud"))
     rows, width = vq_ref.shape[1:]
     audio_rows = audio.shape[1]
@@ -116,7 +120,6 @@
     copies = [pltpu.make_async_copy(source, target, sems.at[index]) for index, (source, target) in enumerate(pairs)]
     for copy in copies:
         copy.start()
-    gates[...] = jnp.concatenate([vg_ref[...].reshape(1, width), ag_ref[...].reshape(1, width)], axis=0)
     for copy in copies:
         copy.wait()
 
@@ -126,9 +129,9 @@
     outs = [like(3, audio_rows, width), like(2, video_rows, width), like(2 * video_rows, width)]
     return pl.pallas_call(
         prepare_kernel,
-        in_specs=[pl.BlockSpec(memory_space=pl.ANY)] * 7 + [pl.BlockSpec(memory_space=pltpu.VMEM)] * 2,
-        out_specs=[pl.BlockSpec(memory_space=pltpu.VMEM)] * 4,
-        out_shape=[*outs, like(2, width, kind=F32)],
+        in_specs=[pl.BlockSpec(memory_space=pl.ANY)] * 7,
+        out_specs=[pl.BlockSpec(memory_space=pltpu.VMEM)] * 3,
+        out_shape=outs,
         scratch_shapes=[pltpu.SemaphoreType.DMA((7,))],
         compiler_params=pltpu.CompilerParams(vmem_limit_bytes=VMEM),
         name="prepare",
@@ -165,17 +168,18 @@
 
 
 def forward_kernel(video_rows, *refs):
-    gathered_ref, k_refs, audio_q, length_ref, gates_ref = refs[0], (refs[1:5], refs[5:9]), refs[9:13], refs[13], refs[14]
-    o_video_ref, stats_video_ref, o_ref, stats_ref, ordered_ref = refs[15:20]
+    gathered_ref, k_refs, audio_q, length_ref = refs[0], (refs[1:5], refs[5:9]), refs[9:13], refs[13]
+    gate_rows = head_row(refs[14]), head_row(refs[15])
+    o_video_ref, stats_video_ref, o_ref, stats_ref, ordered_ref = refs[16:21]
     for place in range(SIDE):
         ordered_ref[(lax.axis_index("vid") >> 2) ^ place] = audio_q[place][...]
-    up_audio = gated(flat(ordered_ref[:, 1]), gates_ref[1:2, :])
+    up_audio = gated(flat(ordered_ref[:, 1]), gate_rows[AUDIO])
     raw = scores(joined(k_refs[VIDEO], 0), flat(ordered_ref[:, 0]), VIDEO, None)
     output, stats = attend(raw, joined(k_refs[VIDEO], 1), up_audio)
     o_ref[0, VIDEO] = jnp.concatenate([o_video_ref[0], output], axis=1)
     stats_video = jnp.concatenate([stats_video_ref[0], stats], axis=1)
     raw = scores(joined(k_refs[AUDIO], 0), queries_of(gathered_ref, ordered_ref, video_rows), AUDIO, length_ref)
-    up = upstream(gathered_ref, ordered_ref, gates_ref, video_rows, AUDIO)
+    up = upstream(gathered_ref, ordered_ref, gate_rows, video_rows, AUDIO)
     o_ref[0, AUDIO], stats = attend(raw, joined(k_refs[AUDIO], 1), up)
     stats_ref[0] = jnp.concatenate([stats_video, stats], axis=0)
 
@@ -211,24 +215,24 @@
 
 def backward_kernel(video_rows, *refs):
     gathered_ref, audio_q, k_video, k_audio, stats_refs = refs[0], refs[1], refs[2:6], refs[6:10], refs[10:14]
-    gates_ref, length_ref, o_ref = refs[14:17]
-    k_outs, q_out = refs[17:21], refs[21]
+    gate_rows, length_ref, o_ref = (head_row(refs[14]), head_row(refs[15])), refs[16], refs[17]
+    k_outs, q_out = refs[18:22], refs[22]
     audio_rows = audio_q.shape[2]
     rows = video_rows + audio_rows
     video = SIDE * video_rows
     queries = queries_of(gathered_ref, audio_q, video_rows)
-    up = upstream(gathered_ref, audio_q, gates_ref, video_rows, VIDEO)
+    up = upstream(gathered_ref, audio_q, gate_rows, video_rows, VIDEO)
     term_video, factor = backward_keys(VIDEO, queries, up, stats_refs, k_video, length_ref, k_outs, 0)
     on_video = o_ref[0, VIDEO].astype(F32) * factor
-    up = upstream(gathered_ref, audio_q, gates_ref, video_rows, AUDIO)
+    up = upstream(gathered_ref, audio_q, gate_rows, video_rows, AUDIO)
     term_audio, factor = backward_keys(AUDIO, queries, up, stats_refs, k_audio, length_ref, k_outs, video_rows)
     on_audio = o_ref[0, AUDIO].astype(F32) * factor
     grad_queries = term_video + term_audio
     cross_video, cross_audio = on_audio[:, :video], on_video[:, video:]
     merged = jnp.concatenate(
         [
-            on_video[:, :video] + column_of(gates_ref[0:1, :]) * cross_video,
-            on_audio[:, video:] + column_of(gates_ref[1:2, :]) * cross_audio,
+            on_video[:, :video] + column_of(gate_rows[VIDEO]) * cross_video,
+            on_audio[:, video:] + column_of(gate_rows[AUDIO]) * cross_audio,
         ],
         axis=1,
     )
@@ -291,8 +295,8 @@
 
 
 def attention_forward(queries, audio_q, video_keys, audio_keys, audio_len, gates, earlier, video_rows):
-    heads = gates.shape[1] // HEAD_DIM
     _, audio_rows, width = audio_q[0].shape
+    heads = width // HEAD_DIM
     total = SIDE * (video_rows + audio_rows)
     outs = [like(heads, 2, HEAD_DIM, total), like(heads, 4, total, kind=F32)]
     ordered = like(SIDE, 2, audio_rows, width)
@@ -301,18 +305,19 @@
         functools.partial(forward_kernel, video_rows),
         grid=(heads,),
         in_specs=[chunk_spec(array) for array in chunks]
-        + [pl.BlockSpec(memory_space=pltpu.SMEM), chunk_spec(gates)]
+        + [pl.BlockSpec(memory_space=pltpu.SMEM)]
+        + [pl.BlockSpec(gate.shape, lambda h: (0,)) for gate in gates]
         + [head_spec(array) for array in earlier],
         out_specs=[head_spec(array) for array in outs] + [chunk_spec(ordered)],
         out_shape=[*outs, ordered],
         cost_estimate=cost(total, total, heads, 1),
         compiler_params=pltpu.CompilerParams(vmem_limit_bytes=VMEM),
         name="forward",
-    )(*chunks, audio_len, gates, *earlier)
+    )(*chunks, audio_len, *gates, *earlier)
 
 
 def attention_backward(queries, audio_q, video_keys, audio_keys, stats, gates, audio_len, outputs, video_rows):
-    width = gates.shape[1]
+    width = queries.shape[2]
     heads = width // HEAD_DIM
     rows = video_rows + audio_q.shape[2]
     outs = [like(2, rows, width)] * SIDE + [like(SIDE, 2 * rows + GATE_ROWS, width)]
@@ -322,13 +327,14 @@
         grid=(heads,),
         in_specs=[chunk_spec(array) for array in chunks]
         + [head_spec(array) for array in stats]
-        + [chunk_spec(gates), pl.BlockSpec(memory_space=pltpu.SMEM), head_spec(outputs)],
+        + [pl.BlockSpec(gate.shape, lambda h: (0,)) for gate in gates]
+        + [pl.BlockSpec(memory_space=pltpu.SMEM), head_spec(outputs)],
         out_specs=[chunk_spec(array) for array in outs],
         out_shape=outs,
         cost_estimate=cost(SIDE * rows, SIDE * rows, heads, 4),
         compiler_params=pltpu.CompilerParams(vmem_limit_bytes=VMEM),
         name="backward",
-    )(*chunks, *stats, gates, audio_len, outputs)
+    )(*chunks, *stats, *gates, audio_len, outputs)
     return key_parts, query_parts
 
 
@@ -404,9 +410,10 @@
     vid = lax.axis_index("vid")
     video_rows, audio_rows = video_q.shape[1], d_audio_out.shape[1]
     holds = audio_len[0] > 0
-    send_audio, video_kv, queries, gates = prepare(
-        audio_rows, audio_q, audio_k, audio_v, video_q, video_k, video_v, d_video_out, video_gate, audio_gate
-    )
+    send_audio, video_kv, queries = prepare(
+        audio_rows, audio_q, audio_k, audio_v, video_q, video_k, video_v, d_video_out
+    )
+    gates = video_gate, audio_gate
 
     def first_chunks(send_audio, video_kv, queries):
         return own_audio(send_audio), tuple(gathered(video_kv, along_z)[1:]), all_along_x(queries)

time: 102 us -> 101 us (level)
  Pallas kernels: 21.5 us -> 20 us
    pallas_call x1, Pallas kernels: 2.48 us -> 1.2 us  [prepare(): pl.pallas_call(prepare_kernel, in_specs=[pl.BlockSpec(memory_space=pl.ANY...]
where the time goes in v14:
time: 101 us; the launch traced here: 100 us
  starting transfers between devices  35.9 us (36%)
  blocking collectives  28.1 us (28%)
  Pallas kernels  20 us (20%)
  waiting for transfers between devices  12.8 us (13%)
  local copies, waits for them, and re-layouts  1.87 us (2%)
  between operations  1.47 us (1%)
    ppermute x11, starting transfers between devices, along_z(): return lax.ppermute(array, 'vid', pairs)  18.4 us
    all_gather x1, blocking collectives, all_along_x(): return lax.all_gather(array, 'vid', axis=0, axis_index_groups=ALONG_X)  14.2 us
    all_to_all x1, blocking collectives, query_results(): lax.all_to_all(parts, 'vid', 0, 0, axis_index_groups=ALONG_X, tiled=True)  13.9 us
    ppermute x11, waiting for transfers between devices, along_z(): return lax.ppermute(array, 'vid', pairs)  10.8 us
    ppermute x1, starting transfers between devices, shards(): other = lax.ppermute(gate, 'pair', [(0, 1), (1, 0)])  7.94 us
    pallas_call x1, Pallas kernels, attention_backward(): pl.pallas_call(functools.partial(backward_kernel, video_rows), grid=(head...  7.29 us
    ppermute x6, starting transfers between devices, along_x(): return lax.ppermute(array, 'vid', pairs)  6.68 us
    pallas_call x1, Pallas kernels, attention_forward(): pl.pallas_call(functools.partial(forward_kernel, video_rows), grid=(heads...  5.09 us
  transfers between devices with their start and end apart: 19, of which 6 were waited for; matrix products, arithmetic and copies ran while one was open for 0% of the time, Pallas kernels for 5%

profile of v14, /device:TPU:1, one launch (start us, length us, event | category | flops | bytes accessed | tf_op | source)
XLA Modules:
  0.0 100.1 jit_solution(2653002613592557969)
XLA Ops:
  1.3 1.2 %prepare.1 = (bf16[3,64,384]{2,1,0:T(8,128)(2,1)S(1)}, bf16[2,128,384]{2,1,0:T(8,128)(2,1)S(1)}, bf16[256,384]{1,0:T(8,128)(2,1)S(1)}) custom-call(bf16[1,128,3072]{2,1,0:T(8,128)(2,1)} %aq_ref.1, bf16[1,128,3072]{2,1,0:T(8,128)(2,1)} %ak_ref.1, bf16[1,128,3072]{2,1,0:T(8,128)(2,1)} %av_ref.1, bf16[1,128,384]{2,1,0:T(8,128)(2,1)} %vq_ref.1, ...), custom_call_target="tpu_custom_call" | custom-call | tf_op jit(solution)/shard_map/prepare/pallas_call | solution.py:130
  2.5 22.8 %conditional.2 = (bf16[3,64,384]{2,1,0:T(8,128)(2,1)}, bf16[2,128,384]{2,1,0:T(8,128)(2,1)}, bf16[2,128,384]{2,1,0:T(8,128)(2,1)}, bf16[2,128,384]{2,1,0:T(8,128)(2,1)}, bf16[4,256,384]{2,1,0:T(8,128)(2,1)S(1)}) conditional(s32[]{:T(128)} %bitcast.1, () %tuple.25, (bf16[3,64,384]{2,1,0:T(8,128)(2,1)S(1)}, bf16[2,128,384]{2,1,0:T(8,128)(2,1)S(1)}, ...), branch_computations={%region_0.0_spmd, %region_1.0_spmd} | conditional | bytes 3932360 | solution.py:402
  2.5 5.3 %collective-permute-start.3 = (bf16[2,128,384]{2,1,0:T(8,128)(2,1)S(1)}, bf16[2,128,384]{2,1,0:T(8,128)(2,1)}, u32[]{:S(2)}, u32[]{:S(2)}) collective-permute-start(bf16[2,128,384]{2,1,0:T(8,128)(2,1)S(1)} %get-tuple-element.8), channel_id=1, source_target_pairs={{0,48},{16,32},{32,16},{48,0},{64,112},{80,96},{96,80},{112,64},{1... | collective-permute-start | bytes 589832 | tf_op jit(solution)/shard_map/cond/branch_1_fun/ppermute | solution.py:30
  8.2 2.9 %collective-permute-start = (bf16[3,64,384]{2,1,0:T(8,128)(2,1)S(1)}, bf16[3,64,384]{2,1,0:T(8,128)(2,1)}, u32[]{:S(2)}, u32[]{:S(2)}) collective-permute-start(bf16[3,64,384]{2,1,0:T(8,128)(2,1)S(1)} %get-tuple-element.7), channel_id=1, source_target_pairs={{0,8},{2,40},{4,72},{6,104},{8,136},{10,168},{12,200},{14,232},{16... | collective-permute-start | bytes 442376 | tf_op jit(solution)/shard_map/cond/branch_1_fun/ppermute | solution.py:397
  11.1 14.2 %all-gather = bf16[1024,384]{1,0:T(8,128)(2,1)S(1)} all-gather(bf16[256,384]{1,0:T(8,128)(2,1)S(1)} %get-tuple-element.9), channel_id=2, replica_groups={{0,64,128,192},{16,80,144,208},{32,96,160,224},{48,112,176,240},{1,65,1..., dimensions={0}, use_global_device_ids=true | all-gather | bytes 983040 | tf_op jit(solution)/shard_map/cond/branch_1_fun/all_gather | solution.py:34
  25.3 0.9 split_audio.1
  26.3 1.0 collective-permute-start.11
  28.0 1.6 %collective-permute-start.9 = (bf16[2,64,384]{2,1,0:T(8,128)(2,1)S(1)}, bf16[2,64,384]{2,1,0:T(8,128)(2,1)S(1)}, u32[]{:S(2)}, u32[]{:S(2)}) collective-permute-start(bf16[2,64,384]{2,1,0:T(8,128)(2,1)S(1)} %get-tuple-element.64.refs_9_), channel_id=1, source_target_pairs={{0,64},{16,80},{32,96},{48,112},{64,0},{80,16},{96,32},{112,48},{1... | collective-permute-start | bytes 294920 | tf_op jit(solution)/shard_map/ppermute | solution.py:25
  29.6 8.8 %collective-permute-start.8 = (bf16[2,64,384]{2,1,0:T(8,128)(2,1)S(1)}, bf16[2,64,384]{2,1,0:T(8,128)(2,1)S(1)}, u32[]{:S(2)}, u32[]{:S(2)}) collective-permute-start(bf16[2,64,384]{2,1,0:T(8,128)(2,1)S(1)} %get-tuple-element.63.refs_5_.refs_6_), channel_id=1, source_target_pairs={{0,48},{16,32},{32,16},{48,0},{64,112},{80,96},{96,80},{112,64},{1... | collective-permute-start | bytes 294920 | tf_op jit(solution)/shard_map/ppermute | solution.py:30
  38.7 3.9 %forward_video.1 = (bf16[3,128,512]{2,1,0:T(8,128)(2,1)}, f32[3,2,512]{2,1,0:T(2,128)}) custom-call(bf16[4,256,384]{2,1,0:T(8,128)(2,1)S(1)} %get-tuple-element.57.refs_0_, bf16[2,128,384]{2,1,0:T(8,128)(2,1)S(1)} %get-tuple-element.58.refs_1_.refs_2_, bf16[2,128,384]{2,1,0:T(8,128)(2,1)} %get-tuple-element.59.refs_2_.refs_3_, ...), custom_call_target="tpu_custom_call" | custom-call | flops 402653184 | bytes 3145728 | tf_op jit(solution)/shard_map/forward_video/pallas_call | solution.py:285
  42.6 2.2 %collective-permute-done.7.refs_7_.refs_8_ = bf16[2,64,384]{2,1,0:T(8,128)(2,1)S(1)} collective-permute-done((bf16[2,64,384]{2,1,0:T(8,128)(2,1)S(1)}, bf16[2,64,384]{2,1,0:T(8,128)(2,1)S(1)}, u32[]{:S(2)}, u32[]{:S(2)}) %collective-permute-start.7) | collective-permute-done | bytes 98336 | tf_op jit(solution)/shard_map/ppermute | solution.py:30
  45.5 5.1 %forward.1 = (bf16[3,2,128,768]{3,2,1,0:T(8,128)(2,1)}, f32[3,4,768]{2,1,0:T(4,128)}, bf16[4,2,64,384]{3,2,1,0:T(8,128)(2,1)}) custom-call(bf16[4,256,384]{2,1,0:T(8,128)(2,1)S(1)} %get-tuple-element.57.refs_0_, bf16[2,128,384]{2,1,0:T(8,128)(2,1)S(1)} %get-tuple-element.58.refs_1_.refs_2_, bf16[2,128,384]{2,1,0:T(8,128)(2,1)} %get-tuple-element.59.refs_2_.refs_3_, ...), custom_call_target="tpu_custom_call" | custom-call | flops 452984832 | bytes 7077888 | tf_op jit(solution)/shard_map/forward/pallas_call | solution.py:304
  50.7 2.0 %collective-permute-start.13 = (f32[3,4,768]{2,1,0:T(4,128)}, f32[3,4,768]{2,1,0:T(4,128)S(1)}, u32[]{:S(2)}, u32[]{:S(2)}) collective-permute-start(f32[3,4,768]{2,1,0:T(4,128)} %get-tuple-element.68.refs_10_), channel_id=1, source_target_pairs={{0,128},{16,144},{32,160},{48,176},{64,192},{80,208},{96,224},{112... | collective-permute-start | bytes 110600 | tf_op jit(solution)/shard_map/ppermute | solution.py:25
  52.7 1.2 %collective-permute-start.12 = (f32[3,4,768]{2,1,0:T(4,128)}, f32[3,4,768]{2,1,0:T(4,128)S(1)}, u32[]{:S(2)}, u32[]{:S(2)}) collective-permute-start(f32[3,4,768]{2,1,0:T(4,128)} %get-tuple-element.68.refs_10_), channel_id=1, source_target_pairs={{0,64},{16,80},{32,96},{48,112},{64,0},{80,16},{96,32},{112,48},{1... | collective-permute-start | bytes 110600 | tf_op jit(solution)/shard_map/ppermute | solution.py:25
  53.9 1.0 collective-permute-done.14.refs_13_
  56.5 7.3 %backward.1 = (bf16[2,192,384]{2,1,0:T(8,128)(2,1)}, bf16[2,192,384]{2,1,0:T(8,128)(2,1)}, bf16[2,192,384]{2,1,0:T(8,128)(2,1)}, bf16[2,192,384]{2,1,0:T(8,128)(2,1)}, bf16[4,400,384]{2,1,0:T(8,128)(2,1)S(1)}) custom-call(bf16[4,256,384]{2,1,0:T(8,128)(2,1)S(1)} %get-tuple-element.57.refs_0_, bf16[4,2,64,384]{3,2,1,0:T(8,128)(2,1)} %get-tuple-element.67.refs_1_, ...), custom_call_target="tpu_custom_call" | custom-call | flops 1811939328 | bytes 7077888 | tf_op jit(solution)/shard_map/backward/pallas_call | solution.py:325
  64.3 2.3 %collective-permute-start.17 = (bf16[2,192,384]{2,1,0:T(8,128)(2,1)}, bf16[2,192,384]{2,1,0:T(8,128)(2,1)S(1)}, u32[]{:S(2)}, u32[]{:S(2)}) collective-permute-start(bf16[2,192,384]{2,1,0:T(8,128)(2,1)} %get-tuple-element.77), channel_id=1, source_target_pairs={{0,32},{16,48},{32,0},{48,16},{64,96},{80,112},{96,64},{112,80},{1... | collective-permute-start | bytes 884744 | tf_op jit(solution)/shard_map/ppermute | solution.py:30
  66.5 0.9 collective-permute-start.18
  67.4 23.3 %conditional.3 = (bf16[1,128,384]{2,1,0:T(8,128)(2,1)}, bf16[1,64,384]{2,1,0:T(8,128)(2,1)}, bf16[1,128,384]{2,1,0:T(8,128)(2,1)}, bf16[1,64,384]{2,1,0:T(8,128)(2,1)}, f32[8,384]{1,0:T(8,128)S(1)}) conditional(s32[]{:T(128)} %bitcast.1, () %tuple.24, bf16[4,400,384]{2,1,0:T(8,128)(2,1)S(1)} %get-tuple-element.70), branch_computations={%region_2.0_spmd, %region_3.0_spmd} | conditional | flops 6144 | bytes 2629752 | solution.py:402
  67.4 13.9 %all_to_all.4.parts_ref = bf16[4,400,384]{2,1,0:T(8,128)(2,1)S(1)} all-to-all(bf16[4,400,384]{2,1,0:T(8,128)(2,1)S(1)} %param.3), channel_id=1, replica_groups={{0,64,128,192},{16,80,144,208},{32,96,160,224},{48,112,176,240},{1,65,1..., dimensions={0} | all-to-all | bytes 2457600 | tf_op jit(solution)/shard_map/cond/branch_1_fun/all_to_all | solution.py:435
  81.3 0.8 finish_queries.1
  82.1 5.0 %collective-permute-done.4 = f32[8,384]{1,0:T(8,128)S(1)} collective-permute-done((f32[8,384]{1,0:T(8,128)S(1)}, f32[8,384]{1,0:T(8,128)S(1)}, u32[]{:S(2)}, u32[]{:S(2)}) %collective-permute-start.4) | collective-permute-done | bytes 12320 | tf_op jit(solution)/shard_map/cond/branch_1_fun/ppermute | solution.py:30
  87.1 3.6 %collective-permute-done.5 = f32[8,384]{1,0:T(8,128)S(1)} collective-permute-done((f32[8,384]{1,0:T(8,128)S(1)}, f32[8,384]{1,0:T(8,128)S(1)}, u32[]{:S(2)}, u32[]{:S(2)}) %collective-permute-start.5) | collective-permute-done | bytes 12320 | tf_op jit(solution)/shard_map/cond/branch_1_fun/ppermute | solution.py:30
  90.7 7.9 %collective-permute-start.15 = (f32[8,384]{1,0:T(8,128)S(1)}, f32[8,384]{1,0:T(8,128)S(1)}, u32[]{:S(2)}, u32[]{:S(2)}) collective-permute-start(f32[8,384]{1,0:T(8,128)S(1)} %get-tuple-element.74), channel_id=1, source_target_pairs={{0,1},{1,0},{2,3},{3,2},{4,5},{5,4},{6,7},{7,6},{8,9},{9,8},{10,11... | collective-permute-start | bytes 36872 | tf_op jit(solution)/shard_map/ppermute | solution.py:443
  (55 shorter events, 5.8 us)
Async XLA Ops:
  2.5 22.8 %copy-start.1 = (bf16[1,64,384]{2,1,0:T(8,128)(2,1)S(1)}, bf16[1,64,384]{2,1,0:T(8,128)(2,1)}, u32[]{:S(2)}) copy-start(bf16[1,64,384]{2,1,0:T(8,128)(2,1)} %up_ref.1) | copy-start | bytes 147460
  2.5 22.7 %collective-permute-start.3 = (bf16[2,128,384]{2,1,0:T(8,128)(2,1)S(1)}, bf16[2,128,384]{2,1,0:T(8,128)(2,1)}, u32[]{:S(2)}, u32[]{:S(2)}) collective-permute-start(bf16[2,128,384]{2,1,0:T(8,128)(2,1)S(1)} %get-tuple-element.8), channel_id=1, source_target_pairs={{0,48},{16,32},{32,16},{48,0},{64,112},{80,96},{96,80},{112,64},{1... | collective-permute-start | bytes 589832 | tf_op jit(solution)/shard_map/cond/branch_1_fun/ppermute | solution.py:30
  7.8 17.5 %collective-permute-start.2 = (bf16[2,128,384]{2,1,0:T(8,128)(2,1)S(1)}, bf16[2,128,384]{2,1,0:T(8,128)(2,1)}, u32[]{:S(2)}, u32[]{:S(2)}) collective-permute-start(bf16[2,128,384]{2,1,0:T(8,128)(2,1)S(1)} %get-tuple-element.8), channel_id=1, source_target_pairs={{0,32},{16,48},{32,0},{48,16},{64,96},{80,112},{96,64},{112,80},{1... | collective-permute-start | bytes 589832 | tf_op jit(solution)/shard_map/cond/branch_1_fun/ppermute | solution.py:30
  7.8 17.5 %collective-permute-start.1 = (bf16[2,128,384]{2,1,0:T(8,128)(2,1)S(1)}, bf16[2,128,384]{2,1,0:T(8,128)(2,1)}, u32[]{:S(2)}, u32[]{:S(2)}) collective-permute-start(bf16[2,128,384]{2,1,0:T(8,128)(2,1)S(1)} %get-tuple-element.8), channel_id=1, source_target_pairs={{0,16},{16,0},{32,48},{48,32},{64,80},{80,64},{96,112},{112,96},{1... | collective-permute-start | bytes 589832 | tf_op jit(solution)/shard_map/cond/branch_1_fun/ppermute | solution.py:30
  8.2 17.1 %collective-permute-start = (bf16[3,64,384]{2,1,0:T(8,128)(2,1)S(1)}, bf16[3,64,384]{2,1,0:T(8,128)(2,1)}, u32[]{:S(2)}, u32[]{:S(2)}) collective-permute-start(bf16[3,64,384]{2,1,0:T(8,128)(2,1)S(1)} %get-tuple-element.7), channel_id=1, source_target_pairs={{0,8},{2,40},{4,72},{6,104},{8,136},{10,168},{12,200},{14,232},{16... | collective-permute-start | bytes 442376 | tf_op jit(solution)/shard_map/cond/branch_1_fun/ppermute | solution.py:397
  26.2 18.6 %copy-start.2 = (bf16[2,64,384]{2,1,0:T(8,128)(2,1)}, bf16[2,64,384]{2,1,0:T(8,128)(2,1)S(1)}, u32[]{:S(2)}) copy-start(bf16[2,64,384]{2,1,0:T(8,128)(2,1)S(1)} %get-tuple-element.63.refs_5_.refs_6_) | copy-start | bytes 294916
  26.2 18.6 %copy-start.3 = (bf16[2,64,384]{2,1,0:T(8,128)(2,1)}, bf16[2,64,384]{2,1,0:T(8,128)(2,1)S(1)}, u32[]{:S(2)}) copy-start(bf16[2,64,384]{2,1,0:T(8,128)(2,1)S(1)} %get-tuple-element.64.refs_9_) | copy-start | bytes 294916
  26.3 12.1 %collective-permute-start.11 = (bf16[2,64,384]{2,1,0:T(8,128)(2,1)S(1)}, bf16[2,64,384]{2,1,0:T(8,128)(2,1)S(1)}, u32[]{:S(2)}, u32[]{:S(2)}) collective-permute-start(bf16[2,64,384]{2,1,0:T(8,128)(2,1)S(1)} %get-tuple-element.64.refs_9_), channel_id=1, source_target_pairs={{0,192},{16,208},{32,224},{48,240},{64,128},{80,144},{96,160},{112... | collective-permute-start | bytes 294920 | tf_op jit(solution)/shard_map/ppermute | solution.py:25
  27.2 15.3 %collective-permute-start.10 = (bf16[2,64,384]{2,1,0:T(8,128)(2,1)S(1)}, bf16[2,64,384]{2,1,0:T(8,128)(2,1)S(1)}, u32[]{:S(2)}, u32[]{:S(2)}) collective-permute-start(bf16[2,64,384]{2,1,0:T(8,128)(2,1)S(1)} %get-tuple-element.64.refs_9_), channel_id=1, source_target_pairs={{0,128},{16,144},{32,160},{48,176},{64,192},{80,208},{96,224},{112... | collective-permute-start | bytes 294920 | tf_op jit(solution)/shard_map/ppermute | solution.py:25
  28.0 14.6 %collective-permute-start.9 = (bf16[2,64,384]{2,1,0:T(8,128)(2,1)S(1)}, bf16[2,64,384]{2,1,0:T(8,128)(2,1)S(1)}, u32[]{:S(2)}, u32[]{:S(2)}) collective-permute-start(bf16[2,64,384]{2,1,0:T(8,128)(2,1)S(1)} %get-tuple-element.64.refs_9_), channel_id=1, source_target_pairs={{0,64},{16,80},{32,96},{48,112},{64,0},{80,16},{96,32},{112,48},{1... | collective-permute-start | bytes 294920 | tf_op jit(solution)/shard_map/ppermute | solution.py:25
  29.6 13.0 %collective-permute-start.8 = (bf16[2,64,384]{2,1,0:T(8,128)(2,1)S(1)}, bf16[2,64,384]{2,1,0:T(8,128)(2,1)S(1)}, u32[]{:S(2)}, u32[]{:S(2)}) collective-permute-start(bf16[2,64,384]{2,1,0:T(8,128)(2,1)S(1)} %get-tuple-element.63.refs_5_.refs_6_), channel_id=1, source_target_pairs={{0,48},{16,32},{32,16},{48,0},{64,112},{80,96},{96,80},{112,64},{1... | collective-permute-start | bytes 294920 | tf_op jit(solution)/shard_map/ppermute | solution.py:30
  38.4 6.4 %collective-permute-start.7 = (bf16[2,64,384]{2,1,0:T(8,128)(2,1)S(1)}, bf16[2,64,384]{2,1,0:T(8,128)(2,1)S(1)}, u32[]{:S(2)}, u32[]{:S(2)}) collective-permute-start(bf16[2,64,384]{2,1,0:T(8,128)(2,1)S(1)} %get-tuple-element.63.refs_5_.refs_6_), channel_id=1, source_target_pairs={{0,32},{16,48},{32,0},{48,16},{64,96},{80,112},{96,64},{112,80},{1... | collective-permute-start | bytes 294920 | tf_op jit(solution)/shard_map/ppermute | solution.py:30
  38.4 6.5 %copy-start.7 = (bf16[2,64,384]{2,1,0:T(8,128)(2,1)}, bf16[2,64,384]{2,1,0:T(8,128)(2,1)S(1)}, u32[]{:S(2)}) copy-start(bf16[2,64,384]{2,1,0:T(8,128)(2,1)S(1)} %collective-permute-done.11.refs_12_) | copy-start | bytes 294916
  38.4 6.4 %collective-permute-start.6 = (bf16[2,64,384]{2,1,0:T(8,128)(2,1)S(1)}, bf16[2,64,384]{2,1,0:T(8,128)(2,1)S(1)}, u32[]{:S(2)}, u32[]{:S(2)}) collective-permute-start(bf16[2,64,384]{2,1,0:T(8,128)(2,1)S(1)} %get-tuple-element.63.refs_5_.refs_6_), channel_id=1, source_target_pairs={{0,16},{16,0},{32,48},{48,32},{64,80},{80,64},{96,112},{112,96},{1... | collective-permute-start | bytes 294920 | tf_op jit(solution)/shard_map/ppermute | solution.py:30
  50.6 4.3 %collective-permute-start.14 = (f32[3,4,768]{2,1,0:T(4,128)}, f32[3,4,768]{2,1,0:T(4,128)S(1)}, u32[]{:S(2)}, u32[]{:S(2)}) collective-permute-start(f32[3,4,768]{2,1,0:T(4,128)} %get-tuple-element.68.refs_10_), channel_id=1, source_target_pairs={{0,192},{16,208},{32,224},{48,240},{64,128},{80,144},{96,160},{112... | collective-permute-start | bytes 110600 | tf_op jit(solution)/shard_map/ppermute | solution.py:25
  50.7 4.6 %collective-permute-start.13 = (f32[3,4,768]{2,1,0:T(4,128)}, f32[3,4,768]{2,1,0:T(4,128)S(1)}, u32[]{:S(2)}, u32[]{:S(2)}) collective-permute-start(f32[3,4,768]{2,1,0:T(4,128)} %get-tuple-element.68.refs_10_), channel_id=1, source_target_pairs={{0,128},{16,144},{32,160},{48,176},{64,192},{80,208},{96,224},{112... | collective-permute-start | bytes 110600 | tf_op jit(solution)/shard_map/ppermute | solution.py:25
  52.7 3.1 %collective-permute-start.12 = (f32[3,4,768]{2,1,0:T(4,128)}, f32[3,4,768]{2,1,0:T(4,128)S(1)}, u32[]{:S(2)}, u32[]{:S(2)}) collective-permute-start(f32[3,4,768]{2,1,0:T(4,128)} %get-tuple-element.68.refs_10_), channel_id=1, source_target_pairs={{0,64},{16,80},{32,96},{48,112},{64,0},{80,16},{96,32},{112,48},{1... | collective-permute-start | bytes 110600 | tf_op jit(solution)/shard_map/ppermute | solution.py:25
  63.8 34.9 %collective-permute-start.16 = (bf16[2,192,384]{2,1,0:T(8,128)(2,1)}, bf16[2,192,384]{2,1,0:T(8,128)(2,1)S(1)}, u32[]{:S(2)}, u32[]{:S(2)}) collective-permute-start(bf16[2,192,384]{2,1,0:T(8,128)(2,1)} %get-tuple-element.76), channel_id=1, source_target_pairs={{0,16},{16,0},{32,48},{48,32},{64,80},{80,64},{96,112},{112,96},{1... | collective-permute-start | bytes 884744 | tf_op jit(solution)/shard_map/ppermute | solution.py:30
  64.3 34.4 %collective-permute-start.17 = (bf16[2,192,384]{2,1,0:T(8,128)(2,1)}, bf16[2,192,384]{2,1,0:T(8,128)(2,1)S(1)}, u32[]{:S(2)}, u32[]{:S(2)}) collective-permute-start(bf16[2,192,384]{2,1,0:T(8,128)(2,1)} %get-tuple-element.77), channel_id=1, source_target_pairs={{0,32},{16,48},{32,0},{48,16},{64,96},{80,112},{96,64},{112,80},{1... | collective-permute-start | bytes 884744 | tf_op jit(solution)/shard_map/ppermute | solution.py:30
  66.5 32.2 %collective-permute-start.18 = (bf16[2,192,384]{2,1,0:T(8,128)(2,1)}, bf16[2,192,384]{2,1,0:T(8,128)(2,1)S(1)}, u32[]{:S(2)}, u32[]{:S(2)}) collective-permute-start(bf16[2,192,384]{2,1,0:T(8,128)(2,1)} %get-tuple-element.78), channel_id=1, source_target_pairs={{0,48},{16,32},{32,16},{48,0},{64,112},{80,96},{96,80},{112,64},{1... | collective-permute-start | bytes 884744 | tf_op jit(solution)/shard_map/ppermute | solution.py:30
  67.4 31.3 %copy-start = (bf16[2,192,384]{2,1,0:T(8,128)(2,1)S(1)}, bf16[2,192,384]{2,1,0:T(8,128)(2,1)}, u32[]{:S(2)}) copy-start(bf16[2,192,384]{2,1,0:T(8,128)(2,1)} %get-tuple-element.75.refs_0_) | copy-start | bytes 884740
  82.1 5.0 %collective-permute-start.4 = (f32[8,384]{1,0:T(8,128)S(1)}, f32[8,384]{1,0:T(8,128)S(1)}, u32[]{:S(2)}, u32[]{:S(2)}) collective-permute-start(f32[8,384]{1,0:T(8,128)S(1)} %get-tuple-element.14), channel_id=1, source_target_pairs={{0,16},{16,0},{32,48},{48,32},{64,80},{80,64},{96,112},{112,96},{1... | collective-permute-start | bytes 36872 | tf_op jit(solution)/shard_map/cond/branch_1_fun/ppermute | solution.py:30
  87.1 3.6 %collective-permute-start.5 = (f32[8,384]{1,0:T(8,128)S(1)}, f32[8,384]{1,0:T(8,128)S(1)}, u32[]{:S(2)}, u32[]{:S(2)}) collective-permute-start(f32[8,384]{1,0:T(8,128)S(1)} %add.6), channel_id=1, source_target_pairs={{0,32},{16,48},{32,0},{48,16},{64,96},{80,112},{96,64},{112,80},{1... | collective-permute-start | bytes 36872 | tf_op jit(solution)/shard_map/cond/branch_1_fun/ppermute | solution.py:30
  90.7 8.8 %collective-permute-start.15 = (f32[8,384]{1,0:T(8,128)S(1)}, f32[8,384]{1,0:T(8,128)S(1)}, u32[]{:S(2)}, u32[]{:S(2)}) collective-permute-start(f32[8,384]{1,0:T(8,128)S(1)} %get-tuple-element.74), channel_id=1, source_target_pairs={{0,1},{1,0},{2,3},{3,2},{4,5},{5,4},{6,7},{7,6},{8,9},{9,8},{10,11... | collective-permute-start | bytes 36872 | tf_op jit(solution)/shard_map/ppermute | solution.py:443
  (8 other events, 10.3 us)

commit v15 on v14

--- a/solution.py
+++ b/solution.py
@@ -433,13 +433,12 @@
 
     def query_results(parts):
         parts = lax.all_to_all(parts, "vid", 0, 0, axis_index_groups=ALONG_X, tiled=True)
-        *results, gate = finish_queries(parts, video_rows, audio_rows)
-        for distance in (1, 2):
-            gate = gate + along_z(gate, distance)
-        return (*results, gate)
+        return tuple(finish_queries(parts, video_rows, audio_rows))
 
     video_out, audio_out, grad_video_q, grad_audio_q, gate = fenced(holds, query_results, query_parts)
     key_parts = returned(key_parts, along_z)
+    gate, key_parts[1] = lax.optimization_barrier((gate, key_parts[1]))
+    gate = sum(gathered(gate, along_z))
     other = lax.ppermute(gate, "pair", [(0, 1), (1, 0)])
     key_grads = finish_keys(key_parts, video_rows, audio_rows)
     other, (grad_video_k, grad_video_v, grad_audio_k, grad_audio_v) = lax.optimization_barrier((other, key_grads))

time: 101 us -> 99.6 us (0.986)
  waiting for transfers between devices: 12.8 us -> 9.36 us
  starting transfers between devices: 35.9 us -> 38.4 us
    ppermute x11 -> x12, starting transfers between devices: 18.4 us -> 21.9 us  [along_z(): return lax.ppermute(array, 'vid', pairs)]
    ppermute x11 -> x12, waiting for transfers between devices: 10.8 us -> 7.36 us  [along_z(): return lax.ppermute(array, 'vid', pairs)]
    ppermute x1, starting transfers between devices: 7.94 us -> 6.91 us  [shards(): other = lax.ppermute(gate, 'pair', [(0, 1), (1, 0)])]
  transfers between devices with their start and end apart: 19 -> 20, of which waited for: 6 -> 6; matrix products, arithmetic and copies ran while one was open for 0% -> 0% of each run, Pallas kernels for 5% -> 5%
where the time goes in v15:
time: 99.6 us; the launch traced here: 99.2 us
  starting transfers between devices  38.4 us (39%)
  blocking collectives  28.1 us (28%)
  Pallas kernels  20 us (20%)
  waiting for transfers between devices  9.36 us (9%)
  local copies, waits for them, and re-layouts  1.87 us (2%)
  between operations  1.46 us (1%)
    ppermute x12, starting transfers between devices, along_z(): return lax.ppermute(array, 'vid', pairs)  21.9 us
    all_gather x1, blocking collectives, all_along_x(): return lax.all_gather(array, 'vid', axis=0, axis_index_groups=ALONG_X)  14.2 us
    all_to_all x1, blocking collectives, query_results(): lax.all_to_all(parts, 'vid', 0, 0, axis_index_groups=ALONG_X, tiled=True)  13.9 us
    ppermute x12, waiting for transfers between devices, along_z(): return lax.ppermute(array, 'vid', pairs)  7.36 us
    pallas_call x1, Pallas kernels, attention_backward(): pl.pallas_call(functools.partial(backward_kernel, video_rows), grid=(head...  7.3 us
    ppermute x1, starting transfers between devices, shards(): other = lax.ppermute(gate, 'pair', [(0, 1), (1, 0)])  6.91 us
    ppermute x6, starting transfers between devices, along_x(): return lax.ppermute(array, 'vid', pairs)  6.68 us
    pallas_call x1, Pallas kernels, attention_forward(): pl.pallas_call(functools.partial(forward_kernel, video_rows), grid=(heads...  5.11 us
  transfers between devices with their start and end apart: 20, of which 6 were waited for; matrix products, arithmetic and copies ran while one was open for 0% of the time, Pallas kernels for 5%

profile of v15, /device:TPU:1, one launch (start us, length us, event | category | flops | bytes accessed | tf_op | source)
XLA Modules:
  0.0 99.2 jit_solution(2941267844940718789)
XLA Ops:
  1.3 1.2 %prepare.1 = (bf16[3,64,384]{2,1,0:T(8,128)(2,1)S(1)}, bf16[2,128,384]{2,1,0:T(8,128)(2,1)S(1)}, bf16[256,384]{1,0:T(8,128)(2,1)S(1)}) custom-call(bf16[1,128,3072]{2,1,0:T(8,128)(2,1)} %aq_ref.1, bf16[1,128,3072]{2,1,0:T(8,128)(2,1)} %ak_ref.1, bf16[1,128,3072]{2,1,0:T(8,128)(2,1)} %av_ref.1, bf16[1,128,384]{2,1,0:T(8,128)(2,1)} %vq_ref.1, ...), custom_call_target="tpu_custom_call" | custom-call | tf_op jit(solution)/shard_map/prepare/pallas_call | solution.py:130
  2.5 22.8 %conditional.2 = (bf16[3,64,384]{2,1,0:T(8,128)(2,1)}, bf16[2,128,384]{2,1,0:T(8,128)(2,1)}, bf16[2,128,384]{2,1,0:T(8,128)(2,1)}, bf16[2,128,384]{2,1,0:T(8,128)(2,1)}, bf16[4,256,384]{2,1,0:T(8,128)(2,1)S(1)}) conditional(s32[]{:T(128)} %bitcast.1, () %tuple.25, (bf16[3,64,384]{2,1,0:T(8,128)(2,1)S(1)}, bf16[2,128,384]{2,1,0:T(8,128)(2,1)S(1)}, ...), branch_computations={%region_0.0_spmd, %region_1.0_spmd} | conditional | bytes 3932360 | solution.py:402
  2.5 5.3 %collective-permute-start.3 = (bf16[2,128,384]{2,1,0:T(8,128)(2,1)S(1)}, bf16[2,128,384]{2,1,0:T(8,128)(2,1)}, u32[]{:S(2)}, u32[]{:S(2)}) collective-permute-start(bf16[2,128,384]{2,1,0:T(8,128)(2,1)S(1)} %get-tuple-element.8), channel_id=1, source_target_pairs={{0,48},{16,32},{32,16},{48,0},{64,112},{80,96},{96,80},{112,64},{1... | collective-permute-start | bytes 589832 | tf_op jit(solution)/shard_map/cond/branch_1_fun/ppermute | solution.py:30
  8.2 2.9 %collective-permute-start = (bf16[3,64,384]{2,1,0:T(8,128)(2,1)S(1)}, bf16[3,64,384]{2,1,0:T(8,128)(2,1)}, u32[]{:S(2)}, u32[]{:S(2)}) collective-permute-start(bf16[3,64,384]{2,1,0:T(8,128)(2,1)S(1)} %get-tuple-element.7), channel_id=1, source_target_pairs={{0,8},{2,40},{4,72},{6,104},{8,136},{10,168},{12,200},{14,232},{16... | collective-permute-start | bytes 442376 | tf_op jit(solution)/shard_map/cond/branch_1_fun/ppermute | solution.py:397
  11.1 14.2 %all-gather = bf16[1024,384]{1,0:T(8,128)(2,1)S(1)} all-gather(bf16[256,384]{1,0:T(8,128)(2,1)S(1)} %get-tuple-element.9), channel_id=2, replica_groups={{0,64,128,192},{16,80,144,208},{32,96,160,224},{48,112,176,240},{1,65,1..., dimensions={0}, use_global_device_ids=true | all-gather | bytes 983040 | tf_op jit(solution)/shard_map/cond/branch_1_fun/all_gather | solution.py:34
  25.3 0.9 split_audio.1
  26.3 1.0 collective-permute-start.9
  28.0 1.6 %collective-permute-start.7 = (bf16[2,64,384]{2,1,0:T(8,128)(2,1)S(1)}, bf16[2,64,384]{2,1,0:T(8,128)(2,1)S(1)}, u32[]{:S(2)}, u32[]{:S(2)}) collective-permute-start(bf16[2,64,384]{2,1,0:T(8,128)(2,1)S(1)} %get-tuple-element.61.refs_9_), channel_id=1, source_target_pairs={{0,64},{16,80},{32,96},{48,112},{64,0},{80,16},{96,32},{112,48},{1... | collective-permute-start | bytes 294920 | tf_op jit(solution)/shard_map/ppermute | solution.py:25
  29.6 8.8 %collective-permute-start.6 = (bf16[2,64,384]{2,1,0:T(8,128)(2,1)S(1)}, bf16[2,64,384]{2,1,0:T(8,128)(2,1)S(1)}, u32[]{:S(2)}, u32[]{:S(2)}) collective-permute-start(bf16[2,64,384]{2,1,0:T(8,128)(2,1)S(1)} %get-tuple-element.60.refs_5_.refs_6_), channel_id=1, source_target_pairs={{0,48},{16,32},{32,16},{48,0},{64,112},{80,96},{96,80},{112,64},{1... | collective-permute-start | bytes 294920 | tf_op jit(solution)/shard_map/ppermute | solution.py:30
  38.7 3.9 %forward_video.1 = (bf16[3,128,512]{2,1,0:T(8,128)(2,1)}, f32[3,2,512]{2,1,0:T(2,128)}) custom-call(bf16[4,256,384]{2,1,0:T(8,128)(2,1)S(1)} %get-tuple-element.54.refs_0_, bf16[2,128,384]{2,1,0:T(8,128)(2,1)S(1)} %get-tuple-element.55.refs_1_.refs_2_, bf16[2,128,384]{2,1,0:T(8,128)(2,1)} %get-tuple-element.56.refs_2_.refs_3_, ...), custom_call_target="tpu_custom_call" | custom-call | flops 402653184 | bytes 3145728 | tf_op jit(solution)/shard_map/forward_video/pallas_call | solution.py:285
  42.6 2.2 %collective-permute-done.5.refs_7_.refs_8_ = bf16[2,64,384]{2,1,0:T(8,128)(2,1)S(1)} collective-permute-done((bf16[2,64,384]{2,1,0:T(8,128)(2,1)S(1)}, bf16[2,64,384]{2,1,0:T(8,128)(2,1)S(1)}, u32[]{:S(2)}, u32[]{:S(2)}) %collective-permute-start.5) | collective-permute-done | bytes 98336 | tf_op jit(solution)/shard_map/ppermute | solution.py:30
  45.5 5.1 %forward.1 = (bf16[3,2,128,768]{3,2,1,0:T(8,128)(2,1)}, f32[3,4,768]{2,1,0:T(4,128)}, bf16[4,2,64,384]{3,2,1,0:T(8,128)(2,1)}) custom-call(bf16[4,256,384]{2,1,0:T(8,128)(2,1)S(1)} %get-tuple-element.54.refs_0_, bf16[2,128,384]{2,1,0:T(8,128)(2,1)S(1)} %get-tuple-element.55.refs_1_.refs_2_, bf16[2,128,384]{2,1,0:T(8,128)(2,1)} %get-tuple-element.56.refs_2_.refs_3_, ...), custom_call_target="tpu_custom_call" | custom-call | flops 452984832 | bytes 7077888 | tf_op jit(solution)/shard_map/forward/pallas_call | solution.py:304
  50.7 2.0 %collective-permute-start.11 = (f32[3,4,768]{2,1,0:T(4,128)}, f32[3,4,768]{2,1,0:T(4,128)S(1)}, u32[]{:S(2)}, u32[]{:S(2)}) collective-permute-start(f32[3,4,768]{2,1,0:T(4,128)} %get-tuple-element.65.refs_10_), channel_id=1, source_target_pairs={{0,128},{16,144},{32,160},{48,176},{64,192},{80,208},{96,224},{112... | collective-permute-start | bytes 110600 | tf_op jit(solution)/shard_map/ppermute | solution.py:25
  52.8 1.2 %collective-permute-start.10 = (f32[3,4,768]{2,1,0:T(4,128)}, f32[3,4,768]{2,1,0:T(4,128)S(1)}, u32[]{:S(2)}, u32[]{:S(2)}) collective-permute-start(f32[3,4,768]{2,1,0:T(4,128)} %get-tuple-element.65.refs_10_), channel_id=1, source_target_pairs={{0,64},{16,80},{32,96},{48,112},{64,0},{80,16},{96,32},{112,48},{1... | collective-permute-start | bytes 110600 | tf_op jit(solution)/shard_map/ppermute | solution.py:25
  54.0 1.0 collective-permute-done.12.refs_13_
  56.5 7.3 %backward.1 = (bf16[2,192,384]{2,1,0:T(8,128)(2,1)}, bf16[2,192,384]{2,1,0:T(8,128)(2,1)}, bf16[2,192,384]{2,1,0:T(8,128)(2,1)}, bf16[2,192,384]{2,1,0:T(8,128)(2,1)}, bf16[4,400,384]{2,1,0:T(8,128)(2,1)S(1)}) custom-call(bf16[4,256,384]{2,1,0:T(8,128)(2,1)S(1)} %get-tuple-element.54.refs_0_, bf16[4,2,64,384]{3,2,1,0:T(8,128)(2,1)} %get-tuple-element.64.refs_1_, ...), custom_call_target="tpu_custom_call" | custom-call | flops 1811939328 | bytes 7077888 | tf_op jit(solution)/shard_map/backward/pallas_call | solution.py:325
  64.3 2.3 %collective-permute-start.18 = (bf16[2,192,384]{2,1,0:T(8,128)(2,1)}, bf16[2,192,384]{2,1,0:T(8,128)(2,1)S(1)}, u32[]{:S(2)}, u32[]{:S(2)}) collective-permute-start(bf16[2,192,384]{2,1,0:T(8,128)(2,1)} %get-tuple-element.76), channel_id=1, source_target_pairs={{0,32},{16,48},{32,0},{48,16},{64,96},{80,112},{96,64},{112,80},{1... | collective-permute-start | bytes 884744 | tf_op jit(solution)/shard_map/ppermute | solution.py:30
  67.5 14.7 %conditional.3 = ((bf16[1,128,384]{2,1,0:T(8,128)(2,1)}, bf16[1,64,384]{2,1,0:T(8,128)(2,1)}, bf16[1,128,384]{2,1,0:T(8,128)(2,1)}, bf16[1,64,384]{2,1,0:T(8,128)(2,1)}, f32[8,384]{1,0:T(8,128)S(1)})) conditional(s32[]{:T(128)} %bitcast.1, () %tuple.24, bf16[4,400,384]{2,1,0:T(8,128)(2,1)S(1)} %get-tuple-element.67), branch_computations={%region_2.0_spmd, %region_3.0_spmd} | conditional | bytes 2457608 | solution.py:402
  67.5 13.9 %all_to_all.4.parts_ref = bf16[4,400,384]{2,1,0:T(8,128)(2,1)S(1)} all-to-all(bf16[4,400,384]{2,1,0:T(8,128)(2,1)S(1)} %param.3), channel_id=1, replica_groups={{0,64,128,192},{16,80,144,208},{32,96,160,224},{48,112,176,240},{1,65,1..., dimensions={0} | all-to-all | bytes 2457600 | tf_op jit(solution)/shard_map/cond/branch_1_fun/all_to_all | solution.py:435
  82.1 1.8 %collective-permute-start.16 = (f32[8,384]{1,0:T(8,128)S(1)}, f32[8,384]{1,0:T(8,128)S(1)}, u32[]{:S(2)}, u32[]{:S(2)}) collective-permute-start(f32[8,384]{1,0:T(8,128)S(1)} %get-tuple-element.73), channel_id=1, source_target_pairs={{0,48},{16,32},{32,16},{48,0},{64,112},{80,96},{96,80},{112,64},{1... | collective-permute-start | bytes 36872 | tf_op jit(solution)/shard_map/ppermute | solution.py:30
  84.0 1.7 %collective-permute-start.14 = (f32[8,384]{1,0:T(8,128)S(1)}, f32[8,384]{1,0:T(8,128)S(1)}, u32[]{:S(2)}, u32[]{:S(2)}) collective-permute-start(f32[8,384]{1,0:T(8,128)S(1)} %get-tuple-element.73), channel_id=1, source_target_pairs={{0,16},{16,0},{32,48},{48,32},{64,80},{80,64},{96,112},{112,96},{1... | collective-permute-start | bytes 36872 | tf_op jit(solution)/shard_map/ppermute | solution.py:30
  85.7 1.2 %collective-permute-done.16 = f32[8,384]{1,0:T(8,128)S(1)} collective-permute-done((f32[8,384]{1,0:T(8,128)S(1)}, f32[8,384]{1,0:T(8,128)S(1)}, u32[]{:S(2)}, u32[]{:S(2)}) %collective-permute-start.16) | collective-permute-done | bytes 12320 | tf_op jit(solution)/shard_map/ppermute | solution.py:30
  86.9 4.0 %collective-permute-done.15 = f32[8,384]{1,0:T(8,128)S(1)} collective-permute-done((f32[8,384]{1,0:T(8,128)S(1)}, f32[8,384]{1,0:T(8,128)S(1)}, u32[]{:S(2)}, u32[]{:S(2)}) %collective-permute-start.15) | collective-permute-done | bytes 12320 | tf_op jit(solution)/shard_map/ppermute | solution.py:30
  90.9 6.9 %collective-permute-start.17 = (f32[8,384]{1,0:T(8,128)S(1)}, f32[8,384]{1,0:T(8,128)S(1)}, u32[]{:S(2)}, u32[]{:S(2)}) collective-permute-start(f32[8,384]{1,0:T(8,128)S(1)} %add_add_fusion), channel_id=1, source_target_pairs={{0,1},{1,0},{2,3},{3,2},{4,5},{5,4},{6,7},{7,6},{8,9},{9,8},{10,11... | collective-permute-start | bytes 36872 | tf_op jit(solution)/shard_map/ppermute | solution.py:442
  (56 shorter events, 7.4 us)
Async XLA Ops:
  2.5 22.8 %copy-start.1 = (bf16[1,64,384]{2,1,0:T(8,128)(2,1)S(1)}, bf16[1,64,384]{2,1,0:T(8,128)(2,1)}, u32[]{:S(2)}) copy-start(bf16[1,64,384]{2,1,0:T(8,128)(2,1)} %up_ref.1) | copy-start | bytes 147460
  2.5 22.7 %collective-permute-start.3 = (bf16[2,128,384]{2,1,0:T(8,128)(2,1)S(1)}, bf16[2,128,384]{2,1,0:T(8,128)(2,1)}, u32[]{:S(2)}, u32[]{:S(2)}) collective-permute-start(bf16[2,128,384]{2,1,0:T(8,128)(2,1)S(1)} %get-tuple-element.8), channel_id=1, source_target_pairs={{0,48},{16,32},{32,16},{48,0},{64,112},{80,96},{96,80},{112,64},{1... | collective-permute-start | bytes 589832 | tf_op jit(solution)/shard_map/cond/branch_1_fun/ppermute | solution.py:30
  7.8 17.5 %collective-permute-start.2 = (bf16[2,128,384]{2,1,0:T(8,128)(2,1)S(1)}, bf16[2,128,384]{2,1,0:T(8,128)(2,1)}, u32[]{:S(2)}, u32[]{:S(2)}) collective-permute-start(bf16[2,128,384]{2,1,0:T(8,128)(2,1)S(1)} %get-tuple-element.8), channel_id=1, source_target_pairs={{0,32},{16,48},{32,0},{48,16},{64,96},{80,112},{96,64},{112,80},{1... | collective-permute-start | bytes 589832 | tf_op jit(solution)/shard_map/cond/branch_1_fun/ppermute | solution.py:30
  7.8 17.5 %collective-permute-start.1 = (bf16[2,128,384]{2,1,0:T(8,128)(2,1)S(1)}, bf16[2,128,384]{2,1,0:T(8,128)(2,1)}, u32[]{:S(2)}, u32[]{:S(2)}) collective-permute-start(bf16[2,128,384]{2,1,0:T(8,128)(2,1)S(1)} %get-tuple-element.8), channel_id=1, source_target_pairs={{0,16},{16,0},{32,48},{48,32},{64,80},{80,64},{96,112},{112,96},{1... | collective-permute-start | bytes 589832 | tf_op jit(solution)/shard_map/cond/branch_1_fun/ppermute | solution.py:30
  8.2 17.1 %collective-permute-start = (bf16[3,64,384]{2,1,0:T(8,128)(2,1)S(1)}, bf16[3,64,384]{2,1,0:T(8,128)(2,1)}, u32[]{:S(2)}, u32[]{:S(2)}) collective-permute-start(bf16[3,64,384]{2,1,0:T(8,128)(2,1)S(1)} %get-tuple-element.7), channel_id=1, source_target_pairs={{0,8},{2,40},{4,72},{6,104},{8,136},{10,168},{12,200},{14,232},{16... | collective-permute-start | bytes 442376 | tf_op jit(solution)/shard_map/cond/branch_1_fun/ppermute | solution.py:397
  26.2 18.6 %copy-start.2 = (bf16[2,64,384]{2,1,0:T(8,128)(2,1)}, bf16[2,64,384]{2,1,0:T(8,128)(2,1)S(1)}, u32[]{:S(2)}) copy-start(bf16[2,64,384]{2,1,0:T(8,128)(2,1)S(1)} %get-tuple-element.60.refs_5_.refs_6_) | copy-start | bytes 294916
  26.2 18.6 %copy-start.3 = (bf16[2,64,384]{2,1,0:T(8,128)(2,1)}, bf16[2,64,384]{2,1,0:T(8,128)(2,1)S(1)}, u32[]{:S(2)}) copy-start(bf16[2,64,384]{2,1,0:T(8,128)(2,1)S(1)} %get-tuple-element.61.refs_9_) | copy-start | bytes 294916
  26.3 12.1 %collective-permute-start.9 = (bf16[2,64,384]{2,1,0:T(8,128)(2,1)S(1)}, bf16[2,64,384]{2,1,0:T(8,128)(2,1)S(1)}, u32[]{:S(2)}, u32[]{:S(2)}) collective-permute-start(bf16[2,64,384]{2,1,0:T(8,128)(2,1)S(1)} %get-tuple-element.61.refs_9_), channel_id=1, source_target_pairs={{0,192},{16,208},{32,224},{48,240},{64,128},{80,144},{96,160},{112... | collective-permute-start | bytes 294920 | tf_op jit(solution)/shard_map/ppermute | solution.py:25
  27.2 15.3 %collective-permute-start.8 = (bf16[2,64,384]{2,1,0:T(8,128)(2,1)S(1)}, bf16[2,64,384]{2,1,0:T(8,128)(2,1)S(1)}, u32[]{:S(2)}, u32[]{:S(2)}) collective-permute-start(bf16[2,64,384]{2,1,0:T(8,128)(2,1)S(1)} %get-tuple-element.61.refs_9_), channel_id=1, source_target_pairs={{0,128},{16,144},{32,160},{48,176},{64,192},{80,208},{96,224},{112... | collective-permute-start | bytes 294920 | tf_op jit(solution)/shard_map/ppermute | solution.py:25
  28.0 14.6 %collective-permute-start.7 = (bf16[2,64,384]{2,1,0:T(8,128)(2,1)S(1)}, bf16[2,64,384]{2,1,0:T(8,128)(2,1)S(1)}, u32[]{:S(2)}, u32[]{:S(2)}) collective-permute-start(bf16[2,64,384]{2,1,0:T(8,128)(2,1)S(1)} %get-tuple-element.61.refs_9_), channel_id=1, source_target_pairs={{0,64},{16,80},{32,96},{48,112},{64,0},{80,16},{96,32},{112,48},{1... | collective-permute-start | bytes 294920 | tf_op jit(solution)/shard_map/ppermute | solution.py:25
  29.6 13.0 %collective-permute-start.6 = (bf16[2,64,384]{2,1,0:T(8,128)(2,1)S(1)}, bf16[2,64,384]{2,1,0:T(8,128)(2,1)S(1)}, u32[]{:S(2)}, u32[]{:S(2)}) collective-permute-start(bf16[2,64,384]{2,1,0:T(8,128)(2,1)S(1)} %get-tuple-element.60.refs_5_.refs_6_), channel_id=1, source_target_pairs={{0,48},{16,32},{32,16},{48,0},{64,112},{80,96},{96,80},{112,64},{1... | collective-permute-start | bytes 294920 | tf_op jit(solution)/shard_map/ppermute | solution.py:30
  38.4 6.4 %collective-permute-start.5 = (bf16[2,64,384]{2,1,0:T(8,128)(2,1)S(1)}, bf16[2,64,384]{2,1,0:T(8,128)(2,1)S(1)}, u32[]{:S(2)}, u32[]{:S(2)}) collective-permute-start(bf16[2,64,384]{2,1,0:T(8,128)(2,1)S(1)} %get-tuple-element.60.refs_5_.refs_6_), channel_id=1, source_target_pairs={{0,32},{16,48},{32,0},{48,16},{64,96},{80,112},{96,64},{112,80},{1... | collective-permute-start | bytes 294920 | tf_op jit(solution)/shard_map/ppermute | solution.py:30
  38.4 6.4 %collective-permute-start.4 = (bf16[2,64,384]{2,1,0:T(8,128)(2,1)S(1)}, bf16[2,64,384]{2,1,0:T(8,128)(2,1)S(1)}, u32[]{:S(2)}, u32[]{:S(2)}) collective-permute-start(bf16[2,64,384]{2,1,0:T(8,128)(2,1)S(1)} %get-tuple-element.60.refs_5_.refs_6_), channel_id=1, source_target_pairs={{0,16},{16,0},{32,48},{48,32},{64,80},{80,64},{96,112},{112,96},{1... | collective-permute-start | bytes 294920 | tf_op jit(solution)/shard_map/ppermute | solution.py:30
  50.6 4.3 %collective-permute-start.12 = (f32[3,4,768]{2,1,0:T(4,128)}, f32[3,4,768]{2,1,0:T(4,128)S(1)}, u32[]{:S(2)}, u32[]{:S(2)}) collective-permute-start(f32[3,4,768]{2,1,0:T(4,128)} %get-tuple-element.65.refs_10_), channel_id=1, source_target_pairs={{0,192},{16,208},{32,224},{48,240},{64,128},{80,144},{96,160},{112... | collective-permute-start | bytes 110600 | tf_op jit(solution)/shard_map/ppermute | solution.py:25
  50.7 4.6 %collective-permute-start.11 = (f32[3,4,768]{2,1,0:T(4,128)}, f32[3,4,768]{2,1,0:T(4,128)S(1)}, u32[]{:S(2)}, u32[]{:S(2)}) collective-permute-start(f32[3,4,768]{2,1,0:T(4,128)} %get-tuple-element.65.refs_10_), channel_id=1, source_target_pairs={{0,128},{16,144},{32,160},{48,176},{64,192},{80,208},{96,224},{112... | collective-permute-start | bytes 110600 | tf_op jit(solution)/shard_map/ppermute | solution.py:25
  52.8 3.1 %collective-permute-start.10 = (f32[3,4,768]{2,1,0:T(4,128)}, f32[3,4,768]{2,1,0:T(4,128)S(1)}, u32[]{:S(2)}, u32[]{:S(2)}) collective-permute-start(f32[3,4,768]{2,1,0:T(4,128)} %get-tuple-element.65.refs_10_), channel_id=1, source_target_pairs={{0,64},{16,80},{32,96},{48,112},{64,0},{80,16},{96,32},{112,48},{1... | collective-permute-start | bytes 110600 | tf_op jit(solution)/shard_map/ppermute | solution.py:25
  63.8 18.3 %collective-permute-start.13 = (bf16[2,192,384]{2,1,0:T(8,128)(2,1)}, bf16[2,192,384]{2,1,0:T(8,128)(2,1)S(1)}, u32[]{:S(2)}, u32[]{:S(2)}) collective-permute-start(bf16[2,192,384]{2,1,0:T(8,128)(2,1)} %get-tuple-element.72), channel_id=1, source_target_pairs={{0,16},{16,0},{32,48},{48,32},{64,80},{80,64},{96,112},{112,96},{1... | collective-permute-start | bytes 884744 | tf_op jit(solution)/shard_map/ppermute | solution.py:30
  64.3 33.5 %collective-permute-start.18 = (bf16[2,192,384]{2,1,0:T(8,128)(2,1)}, bf16[2,192,384]{2,1,0:T(8,128)(2,1)S(1)}, u32[]{:S(2)}, u32[]{:S(2)}) collective-permute-start(bf16[2,192,384]{2,1,0:T(8,128)(2,1)} %get-tuple-element.76), channel_id=1, source_target_pairs={{0,32},{16,48},{32,0},{48,16},{64,96},{80,112},{96,64},{112,80},{1... | collective-permute-start | bytes 884744 | tf_op jit(solution)/shard_map/ppermute | solution.py:30
  66.6 31.2 %collective-permute-start.19 = (bf16[2,192,384]{2,1,0:T(8,128)(2,1)}, bf16[2,192,384]{2,1,0:T(8,128)(2,1)S(1)}, u32[]{:S(2)}, u32[]{:S(2)}) collective-permute-start(bf16[2,192,384]{2,1,0:T(8,128)(2,1)} %get-tuple-element.77), channel_id=1, source_target_pairs={{0,48},{16,32},{32,16},{48,0},{64,112},{80,96},{96,80},{112,64},{1... | collective-permute-start | bytes 884744 | tf_op jit(solution)/shard_map/ppermute | solution.py:30
  67.5 30.3 %copy-start = (bf16[2,192,384]{2,1,0:T(8,128)(2,1)S(1)}, bf16[2,192,384]{2,1,0:T(8,128)(2,1)}, u32[]{:S(2)}) copy-start(bf16[2,192,384]{2,1,0:T(8,128)(2,1)} %get-tuple-element.74.refs_0_) | copy-start | bytes 884740
  82.1 4.7 %collective-permute-start.16 = (f32[8,384]{1,0:T(8,128)S(1)}, f32[8,384]{1,0:T(8,128)S(1)}, u32[]{:S(2)}, u32[]{:S(2)}) collective-permute-start(f32[8,384]{1,0:T(8,128)S(1)} %get-tuple-element.73), channel_id=1, source_target_pairs={{0,48},{16,32},{32,16},{48,0},{64,112},{80,96},{96,80},{112,64},{1... | collective-permute-start | bytes 36872 | tf_op jit(solution)/shard_map/ppermute | solution.py:30
  84.0 6.9 %collective-permute-start.15 = (f32[8,384]{1,0:T(8,128)S(1)}, f32[8,384]{1,0:T(8,128)S(1)}, u32[]{:S(2)}, u32[]{:S(2)}) collective-permute-start(f32[8,384]{1,0:T(8,128)S(1)} %get-tuple-element.73), channel_id=1, source_target_pairs={{0,32},{16,48},{32,0},{48,16},{64,96},{80,112},{96,64},{112,80},{1... | collective-permute-start | bytes 36872 | tf_op jit(solution)/shard_map/ppermute | solution.py:30
  84.0 6.9 %collective-permute-start.14 = (f32[8,384]{1,0:T(8,128)S(1)}, f32[8,384]{1,0:T(8,128)S(1)}, u32[]{:S(2)}, u32[]{:S(2)}) collective-permute-start(f32[8,384]{1,0:T(8,128)S(1)} %get-tuple-element.73), channel_id=1, source_target_pairs={{0,16},{16,0},{32,48},{48,32},{64,80},{80,64},{96,112},{112,96},{1... | collective-permute-start | bytes 36872 | tf_op jit(solution)/shard_map/ppermute | solution.py:30
  90.9 7.7 %collective-permute-start.17 = (f32[8,384]{1,0:T(8,128)S(1)}, f32[8,384]{1,0:T(8,128)S(1)}, u32[]{:S(2)}, u32[]{:S(2)}) collective-permute-start(f32[8,384]{1,0:T(8,128)S(1)} %add_add_fusion), channel_id=1, source_target_pairs={{0,1},{1,0},{2,3},{3,2},{4,5},{5,4},{6,7},{7,6},{8,9},{9,8},{10,11... | collective-permute-start | bytes 36872 | tf_op jit(solution)/shard_map/ppermute | solution.py:442
  (9 other events, 16.8 us)

commit v16 on v15

--- a/solution.py
+++ b/solution.py
@@ -62,12 +62,12 @@
     return block.reshape(-1, block.shape[-1])
 
 
-def queries_of(gathered_ref, audio_ref, video_rows):
-    return jnp.concatenate([flat(gathered_ref[:, :video_rows]), flat(audio_ref[:, 0])], axis=0)
-
-
-def upstreams_of(gathered_ref, audio_ref, video_rows):
-    return flat(gathered_ref[:, video_rows:]), flat(audio_ref[:, 1])
+def queries_of(gathered_ref, audio_ref, audio_rows):
+    return jnp.concatenate([flat(gathered_ref[...]), flat(audio_ref[:, :audio_rows])], axis=0)
+
+
+def upstreams_of(audio_ref, audio_rows):
+    return flat(audio_ref[:, 2 * audio_rows :]), flat(audio_ref[:, audio_rows : 2 * audio_rows])
 
 
 def head_row(ref):
@@ -75,8 +75,8 @@
     return ref[pl.ds(first, HEAD_DIM)].reshape(1, HEAD_DIM)
 
 
-def upstream(gathered_ref, audio_ref, gate_rows, video_rows, part):
-    video, audio = upstreams_of(gathered_ref, audio_ref, video_rows)
+def upstream(audio_ref, gate_rows, audio_rows, part):
+    video, audio = upstreams_of(audio_ref, audio_rows)
     if part == VIDEO:
         audio = gated(audio, gate_rows[AUDIO])
     else:
@@ -84,21 +84,23 @@
     return jnp.concatenate([video, audio], axis=0)
 
 
-def split_audio_kernel(audio_ref, up_ref, queries_ref, keys_ref):
-    queries_ref[0] = audio_ref[0]
-    queries_ref[1] = up_ref[0]
+def split_audio_kernel(audio_ref, up_audio_ref, up_video_ref, queries_ref, keys_ref):
+    rows = audio_ref.shape[1]
+    queries_ref[:rows] = audio_ref[0]
+    queries_ref[rows : 2 * rows] = up_audio_ref[0]
+    queries_ref[2 * rows :] = up_video_ref[0]
     keys_ref[0] = audio_ref[1]
     keys_ref[1] = audio_ref[2]
 
 
-def split_audio(audio, d_audio):
+def split_audio(audio, d_audio, d_video):
     _, rows, width = audio.shape
     return pl.pallas_call(
         split_audio_kernel,
-        out_shape=[like(2, rows, width)] * 2,
+        out_shape=[like(2 * rows + d_video.shape[1], width), like(2, rows, width)],
         compiler_params=pltpu.CompilerParams(vmem_limit_bytes=8 * 2**20),
         name="split_audio",
-    )(audio, d_audio)
+    )(audio, d_audio, d_video)
 
 
 def audio_target(vid, aud):
@@ -108,15 +110,14 @@
     return SIDE * y + 2 * half + (z & 1), 2 * to_y + (z >> 1)
 
 
-def prepare_kernel(aq_ref, ak_ref, av_ref, vq_ref, vk_ref, vv_ref, dv_ref, audio, video_kv, queries, sems):
+def prepare_kernel(aq_ref, ak_ref, av_ref, vq_ref, vk_ref, vv_ref, audio, video_kv, queries, sems):
     to_vid, to_aud = audio_target(lax.axis_index("vid"), lax.axis_index("aud"))
-    rows, width = vq_ref.shape[1:]
-    audio_rows = audio.shape[1]
+    audio_rows, width = audio.shape[1:]
     taken = pl.ds(pl.multiple_of((to_vid & 1) * audio_rows, audio_rows), audio_rows)
     columns = pl.ds(pl.multiple_of(to_aud * width, HEAD_DIM), width)
     pairs = [(ref.at[0, taken, columns], audio.at[index]) for index, ref in enumerate((aq_ref, ak_ref, av_ref))]
     pairs += [(vk_ref.at[0], video_kv.at[0]), (vv_ref.at[0], video_kv.at[1])]
-    pairs += [(vq_ref.at[0], queries.at[pl.ds(0, rows)]), (dv_ref.at[0], queries.at[pl.ds(rows, rows)])]
+    pairs += [(vq_ref.at[0], queries)]
     copies = [pltpu.make_async_copy(source, target, sems.at[index]) for index, (source, target) in enumerate(pairs)]
     for copy in copies:
         copy.start()
@@ -126,13 +127,13 @@
 
 def prepare(audio_rows, *given):
     _, video_rows, width = given[3].shape
-    outs = [like(3, audio_rows, width), like(2, video_rows, width), like(2 * video_rows, width)]
+    outs = [like(3, audio_rows, width), like(2, video_rows, width), like(video_rows, width)]
     return pl.pallas_call(
         prepare_kernel,
-        in_specs=[pl.BlockSpec(memory_space=pl.ANY)] * 7,
+        in_specs=[pl.BlockSpec(memory_space=pl.ANY)] * 6,
         out_specs=[pl.BlockSpec(memory_space=pltpu.VMEM)] * 3,
         out_shape=outs,
-        scratch_shapes=[pltpu.SemaphoreType.DMA((7,))],
+        scratch_shapes=[pltpu.SemaphoreType.DMA((6,))],
         compiler_params=pltpu.CompilerParams(vmem_limit_bytes=VMEM),
         name="prepare",
     )(*given)
@@ -152,19 +153,24 @@
     return raw
 
 
+def row_delta(up, output):
+    return jnp.sum(up.T.astype(F32) * output, axis=0, keepdims=True)
+
+
 def attend(raw, values, up):
     peak = jnp.max(raw, axis=0, keepdims=True)
     expon = jnp.exp2((raw - peak) * (SCALE * LOG2_E))
     total = jnp.sum(expon, axis=0, keepdims=True)
     output = nn(values.T, expon.astype(BF16)) * (1.0 / total)
-    delta = jnp.sum(up.T.astype(F32) * output, axis=0, keepdims=True)
-    return output.astype(BF16), jnp.concatenate([peak * SCALE + jnp.log(total), delta], axis=0)
-
-
-def forward_video_kernel(video_rows, *refs):
+    log_total = peak * SCALE + jnp.log(total)
+    delta = log_total if up is None else row_delta(up, output)
+    return output.astype(BF16), jnp.concatenate([log_total, delta], axis=0)
+
+
+def forward_video_kernel(*refs):
     gathered_ref, k_refs, o_ref, stats_ref = refs[0], refs[1:5], refs[5], refs[6]
-    raw = scores(joined(k_refs, 0), flat(gathered_ref[:, :video_rows]), VIDEO, None)
-    o_ref[0], stats_ref[0] = attend(raw, joined(k_refs, 1), flat(gathered_ref[:, video_rows:]))
+    raw = scores(joined(k_refs, 0), flat(gathered_ref[...]), VIDEO, None)
+    o_ref[0], stats_ref[0] = attend(raw, joined(k_refs, 1), None)
 
 
 def forward_kernel(video_rows, *refs):
@@ -173,13 +179,16 @@
     o_video_ref, stats_video_ref, o_ref, stats_ref, ordered_ref = refs[16:21]
     for place in range(SIDE):
         ordered_ref[(lax.axis_index("vid") >> 2) ^ place] = audio_q[place][...]
-    up_audio = gated(flat(ordered_ref[:, 1]), gate_rows[AUDIO])
-    raw = scores(joined(k_refs[VIDEO], 0), flat(ordered_ref[:, 0]), VIDEO, None)
-    output, stats = attend(raw, joined(k_refs[VIDEO], 1), up_audio)
+    audio_rows = (ordered_ref.shape[1] - video_rows) // 2
+    up_video, up_audio = upstreams_of(ordered_ref, audio_rows)
+    raw = scores(joined(k_refs[VIDEO], 0), flat(ordered_ref[:, :audio_rows]), VIDEO, None)
+    output, stats = attend(raw, joined(k_refs[VIDEO], 1), gated(up_audio, gate_rows[AUDIO]))
     o_ref[0, VIDEO] = jnp.concatenate([o_video_ref[0], output], axis=1)
-    stats_video = jnp.concatenate([stats_video_ref[0], stats], axis=1)
-    raw = scores(joined(k_refs[AUDIO], 0), queries_of(gathered_ref, ordered_ref, video_rows), AUDIO, length_ref)
-    up = upstream(gathered_ref, ordered_ref, gate_rows, video_rows, AUDIO)
+    delta = row_delta(up_video, o_video_ref[0].astype(F32))
+    stats_video = jnp.concatenate([stats_video_ref[0, 0:1], delta], axis=0)
+    stats_video = jnp.concatenate([stats_video, stats], axis=1)
+    raw = scores(joined(k_refs[AUDIO], 0), queries_of(gathered_ref, ordered_ref, audio_rows), AUDIO, length_ref)
+    up = upstream(ordered_ref, gate_rows, audio_rows, AUDIO)
     o_ref[0, AUDIO], stats = attend(raw, joined(k_refs[AUDIO], 1), up)
     stats_ref[0] = jnp.concatenate([stats_video, stats], axis=0)
 
@@ -217,14 +226,14 @@
     gathered_ref, audio_q, k_video, k_audio, stats_refs = refs[0], refs[1], refs[2:6], refs[6:10], refs[10:14]
     gate_rows, length_ref, o_ref = (head_row(refs[14]), head_row(refs[15])), refs[16], refs[17]
     k_outs, q_out = refs[18:22], refs[22]
-    audio_rows = audio_q.shape[2]
+    audio_rows = (audio_q.shape[1] - video_rows) // 2
     rows = video_rows + audio_rows
     video = SIDE * video_rows
-    queries = queries_of(gathered_ref, audio_q, video_rows)
-    up = upstream(gathered_ref, audio_q, gate_rows, video_rows, VIDEO)
+    queries = queries_of(gathered_ref, audio_q, audio_rows)
+    up = upstream(audio_q, gate_rows, audio_rows, VIDEO)
     term_video, factor = backward_keys(VIDEO, queries, up, stats_refs, k_video, length_ref, k_outs, 0)
     on_video = o_ref[0, VIDEO].astype(F32) * factor
-    up = upstream(gathered_ref, audio_q, gate_rows, video_rows, AUDIO)
+    up = upstream(audio_q, gate_rows, audio_rows, AUDIO)
     term_audio, factor = backward_keys(AUDIO, queries, up, stats_refs, k_audio, length_ref, k_outs, video_rows)
     on_audio = o_ref[0, AUDIO].astype(F32) * factor
     grad_queries = term_video + term_audio
@@ -236,7 +245,7 @@
         ],
         axis=1,
     )
-    up_video, up_audio = upstreams_of(gathered_ref, audio_q, video_rows)
+    up_video, up_audio = upstreams_of(audio_q, audio_rows)
     video_sum = jnp.sum(up_video.T.astype(F32) * cross_video, axis=1, keepdims=True)
     audio_sum = jnp.sum(up_audio.T.astype(F32) * cross_audio, axis=1, keepdims=True)
     sums = jnp.concatenate(
@@ -283,7 +292,7 @@
     outs = [like(heads, HEAD_DIM, video), like(heads, 2, video, kind=F32)]
     chunks = [queries, *video_keys]
     return pl.pallas_call(
-        functools.partial(forward_video_kernel, video_rows),
+        forward_video_kernel,
         grid=(heads,),
         in_specs=[chunk_spec(array) for array in chunks],
         out_specs=[head_spec(array) for array in outs],
@@ -295,11 +304,11 @@
 
 
 def attention_forward(queries, audio_q, video_keys, audio_keys, audio_len, gates, earlier, video_rows):
-    _, audio_rows, width = audio_q[0].shape
+    audio_rows, width = audio_keys[0].shape[1:]
     heads = width // HEAD_DIM
     total = SIDE * (video_rows + audio_rows)
     outs = [like(heads, 2, HEAD_DIM, total), like(heads, 4, total, kind=F32)]
-    ordered = like(SIDE, 2, audio_rows, width)
+    ordered = like(SIDE, *audio_q[0].shape)
     chunks = [queries, *video_keys, *audio_keys, *audio_q]
     return pl.pallas_call(
         functools.partial(forward_kernel, video_rows),
@@ -319,7 +328,7 @@
 def attention_backward(queries, audio_q, video_keys, audio_keys, stats, gates, audio_len, outputs, video_rows):
     width = queries.shape[2]
     heads = width // HEAD_DIM
-    rows = video_rows + audio_q.shape[2]
+    rows = video_rows + audio_keys[0].shape[1]
     outs = [like(2, rows, width)] * SIDE + [like(SIDE, 2 * rows + GATE_ROWS, width)]
     chunks = [queries, audio_q, *video_keys, *audio_keys]
     *key_parts, query_parts = pl.pallas_call(
@@ -411,7 +420,7 @@
     video_rows, audio_rows = video_q.shape[1], d_audio_out.shape[1]
     holds = audio_len[0] > 0
     send_audio, video_kv, queries = prepare(
-        audio_rows, audio_q, audio_k, audio_v, video_q, video_k, video_v, d_video_out
+        audio_rows, audio_q, audio_k, audio_v, video_q, video_k, video_v
     )
     gates = video_gate, audio_gate
 
@@ -420,7 +429,7 @@
 
     audio, video_keys, queries = fenced(holds, first_chunks, send_audio, video_kv, queries)
     video_keys = [video_kv, *video_keys]
-    audio_queries, audio_keys = split_audio(audio, d_audio_out)
+    audio_queries, audio_keys = split_audio(audio, d_audio_out, d_video_out)
     audio_keys = gathered(audio_keys, along_z)
     audio_queries = gathered(audio_queries, along_x)
     earlier = attention_forward_video(queries, video_keys, video_rows)

time: 99.6 us -> 101 us (1.014)
  waiting for transfers between devices: 9.36 us -> 11.9 us
  starting transfers between devices: 38.4 us -> 36.4 us
    ppermute x6, waiting for transfers between devices: 1.95 us -> 6.46 us  [along_x(): return lax.ppermute(array, 'vid', pairs)]
    ppermute x1, starting transfers between devices: 6.91 us -> 2.89 us  [shards(): other = lax.ppermute(gate, 'pair', [(0, 1), (1, 0)])]
    ppermute x12, waiting for transfers between devices: 7.36 us -> 5.44 us  [along_z(): return lax.ppermute(array, 'vid', pairs)]
    all_to_all x1, blocking collectives: 13.9 us -> 15.6 us  [query_results(): lax.all_to_all(parts, 'vid', 0, 0, axis_index_groups=ALONG_X, tiled=True)]
    all_gather x1, blocking collectives: 14.2 us -> 12.6 us  [all_along_x(): return lax.all_gather(array, 'vid', axis=0, axis_index_groups=ALONG_X)]
    ppermute x12, starting transfers between devices: 21.9 us -> 22.9 us  [along_z(): return lax.ppermute(array, 'vid', pairs)]
  transfers between devices with their start and end apart: 20 -> 20, of which waited for: 6 -> 6; matrix products, arithmetic and copies ran while one was open for 0% -> 0% of each run, Pallas kernels for 5% -> 6%
where the time goes in v16:
time: 101 us; the launch traced here: 100 us
  starting transfers between devices  36.4 us (36%)
  blocking collectives  28.1 us (28%)
  Pallas kernels  20.3 us (20%)
  waiting for transfers between devices  11.9 us (12%)
  local copies, waits for them, and re-layouts  2.02 us (2%)
  between operations  1.44 us (1%)
    ppermute x12, starting transfers between devices, along_z(): return lax.ppermute(array, 'vid', pairs)  22.9 us
    all_to_all x1, blocking collectives, query_results(): lax.all_to_all(parts, 'vid', 0, 0, axis_index_groups=ALONG_X, tiled=True)  15.6 us
    all_gather x1, blocking collectives, all_along_x(): return lax.all_gather(array, 'vid', axis=0, axis_index_groups=ALONG_X)  12.6 us
    ppermute x6, starting transfers between devices, along_x(): return lax.ppermute(array, 'vid', pairs)  7.63 us
    pallas_call x1, Pallas kernels, attention_backward(): pl.pallas_call(functools.partial(backward_kernel, video_rows), grid=(head...  7.23 us
    ppermute x6, waiting for transfers between devices, along_x(): return lax.ppermute(array, 'vid', pairs)  6.46 us
    pallas_call x1, Pallas kernels, attention_forward(): pl.pallas_call(functools.partial(forward_kernel, video_rows), grid=(heads...  5.47 us
    ppermute x12, waiting for transfers between devices, along_z(): return lax.ppermute(array, 'vid', pairs)  5.44 us
  transfers between devices with their start and end apart: 20, of which 6 were waited for; matrix products, arithmetic and copies ran while one was open for 0% of the time, Pallas kernels for 6%

profile of v16, /device:TPU:1, one launch (start us, length us, event | category | flops | bytes accessed | tf_op | source)
XLA Modules:
  0.0 100.2 jit_solution(1972843979936389301)
XLA Ops:
  1.3 1.1 %prepare.1 = (bf16[3,64,384]{2,1,0:T(8,128)(2,1)S(1)}, bf16[2,128,384]{2,1,0:T(8,128)(2,1)S(1)}, bf16[128,384]{1,0:T(8,128)(2,1)S(1)}) custom-call(bf16[1,128,3072]{2,1,0:T(8,128)(2,1)} %aq_ref.1, bf16[1,128,3072]{2,1,0:T(8,128)(2,1)} %ak_ref.1, bf16[1,128,3072]{2,1,0:T(8,128)(2,1)} %av_ref.1, bf16[1,128,384]{2,1,0:T(8,128)(2,1)} %vq_ref.1, ...), custom_call_target="tpu_custom_call" | custom-call | tf_op jit(solution)/shard_map/prepare/pallas_call | solution.py:131
  2.5 21.2 %conditional.2 = (bf16[3,64,384]{2,1,0:T(8,128)(2,1)}, bf16[2,128,384]{2,1,0:T(8,128)(2,1)}, bf16[2,128,384]{2,1,0:T(8,128)(2,1)}, bf16[2,128,384]{2,1,0:T(8,128)(2,1)}, bf16[4,128,384]{2,1,0:T(8,128)(2,1)S(1)}) conditional(s32[]{:T(128)} %bitcast.1, () %tuple.25, (bf16[3,64,384]{2,1,0:T(8,128)(2,1)S(1)}, bf16[2,128,384]{2,1,0:T(8,128)(2,1)S(1)}, ...), branch_computations={%region_0.0_spmd, %region_1.0_spmd} | conditional | bytes 3440840 | solution.py:411
  2.5 5.3 %collective-permute-start.3 = (bf16[2,128,384]{2,1,0:T(8,128)(2,1)S(1)}, bf16[2,128,384]{2,1,0:T(8,128)(2,1)}, u32[]{:S(2)}, u32[]{:S(2)}) collective-permute-start(bf16[2,128,384]{2,1,0:T(8,128)(2,1)S(1)} %get-tuple-element.8), channel_id=1, source_target_pairs={{0,48},{16,32},{32,16},{48,0},{64,112},{80,96},{96,80},{112,64},{1... | collective-permute-start | bytes 589832 | tf_op jit(solution)/shard_map/cond/branch_1_fun/ppermute | solution.py:30
  8.1 2.9 %collective-permute-start = (bf16[3,64,384]{2,1,0:T(8,128)(2,1)S(1)}, bf16[3,64,384]{2,1,0:T(8,128)(2,1)}, u32[]{:S(2)}, u32[]{:S(2)}) collective-permute-start(bf16[3,64,384]{2,1,0:T(8,128)(2,1)S(1)} %get-tuple-element.7), channel_id=1, source_target_pairs={{0,8},{2,40},{4,72},{6,104},{8,136},{10,168},{12,200},{14,232},{16... | collective-permute-start | bytes 442376 | tf_op jit(solution)/shard_map/cond/branch_1_fun/ppermute | solution.py:406
  11.1 12.6 %all-gather = bf16[512,384]{1,0:T(8,128)(2,1)S(1)} all-gather(bf16[128,384]{1,0:T(8,128)(2,1)S(1)} %get-tuple-element.9), channel_id=2, replica_groups={{0,64,128,192},{16,80,144,208},{32,96,160,224},{48,112,176,240},{1,65,1..., dimensions={0}, use_global_device_ids=true | all-gather | bytes 491520 | tf_op jit(solution)/shard_map/cond/branch_1_fun/all_gather | solution.py:34
  23.7 0.9 split_audio.1
  24.6 9.6 %collective-permute-start.6 = (bf16[2,64,384]{2,1,0:T(8,128)(2,1)S(1)}, bf16[2,64,384]{2,1,0:T(8,128)(2,1)S(1)}, u32[]{:S(2)}, u32[]{:S(2)}) collective-permute-start(bf16[2,64,384]{2,1,0:T(8,128)(2,1)S(1)} %get-tuple-element.60.refs_5_.refs_6_), channel_id=1, source_target_pairs={{0,48},{16,32},{32,16},{48,0},{64,112},{80,96},{96,80},{112,64},{1... | collective-permute-start | bytes 294920 | tf_op jit(solution)/shard_map/ppermute | solution.py:30
  34.3 2.7 %collective-permute-start.9 = (bf16[256,384]{1,0:T(8,128)(2,1)S(1)}, bf16[256,384]{1,0:T(8,128)(2,1)S(1)}, u32[]{:S(2)}, u32[]{:S(2)}) collective-permute-start(bf16[256,384]{1,0:T(8,128)(2,1)S(1)} %get-tuple-element.61.refs_9_), channel_id=1, source_target_pairs={{0,192},{16,208},{32,224},{48,240},{64,128},{80,144},{96,160},{112... | collective-permute-start | bytes 589832 | tf_op jit(solution)/shard_map/ppermute | solution.py:25
  38.1 4.0 %forward_video.1 = (bf16[3,128,512]{2,1,0:T(8,128)(2,1)}, f32[3,2,512]{2,1,0:T(2,128)}) custom-call(bf16[4,128,384]{2,1,0:T(8,128)(2,1)S(1)} %get-tuple-element.54.refs_0_, bf16[2,128,384]{2,1,0:T(8,128)(2,1)S(1)} %get-tuple-element.55.refs_1_.refs_2_, bf16[2,128,384]{2,1,0:T(8,128)(2,1)} %get-tuple-element.56.refs_2_.refs_3_, ...), custom_call_target="tpu_custom_call" | custom-call | flops 402653184 | bytes 3145728 | tf_op jit(solution)/shard_map/forward_video/pallas_call | solution.py:294
  42.7 2.6 %collective-permute-done.9.refs_12_ = bf16[256,384]{1,0:T(8,128)(2,1)S(1)} collective-permute-done((bf16[256,384]{1,0:T(8,128)(2,1)S(1)}, bf16[256,384]{1,0:T(8,128)(2,1)S(1)}, u32[]{:S(2)}, u32[]{:S(2)}) %collective-permute-start.9) | collective-permute-done | bytes 196640 | tf_op jit(solution)/shard_map/ppermute | solution.py:25
  46.2 5.5 %forward.1 = (bf16[3,2,128,768]{3,2,1,0:T(8,128)(2,1)}, f32[3,4,768]{2,1,0:T(4,128)}, bf16[4,256,384]{2,1,0:T(8,128)(2,1)}) custom-call(bf16[4,128,384]{2,1,0:T(8,128)(2,1)S(1)} %get-tuple-element.54.refs_0_, bf16[2,128,384]{2,1,0:T(8,128)(2,1)S(1)} %get-tuple-element.55.refs_1_.refs_2_, bf16[2,128,384]{2,1,0:T(8,128)(2,1)} %get-tuple-element.56.refs_2_.refs_3_, ...), custom_call_target="tpu_custom_call" | custom-call | flops 452984832 | bytes 7077888 | tf_op jit(solution)/shard_map/forward/pallas_call | solution.py:313
  51.6 3.6 %collective-permute-start.12 = (f32[3,4,768]{2,1,0:T(4,128)}, f32[3,4,768]{2,1,0:T(4,128)S(1)}, u32[]{:S(2)}, u32[]{:S(2)}) collective-permute-start(f32[3,4,768]{2,1,0:T(4,128)} %get-tuple-element.65.refs_10_), channel_id=1, source_target_pairs={{0,192},{16,208},{32,224},{48,240},{64,128},{80,144},{96,160},{112... | collective-permute-start | bytes 110600 | tf_op jit(solution)/shard_map/ppermute | solution.py:25
  56.0 0.9 collective-permute-done.12.refs_13_
  56.8 3.0 %collective-permute-done.11.refs_12_ = f32[3,4,768]{2,1,0:T(4,128)S(1)} collective-permute-done((f32[3,4,768]{2,1,0:T(4,128)}, f32[3,4,768]{2,1,0:T(4,128)S(1)}, u32[]{:S(2)}, u32[]{:S(2)}) %collective-permute-start.11) | collective-permute-done | bytes 36896 | tf_op jit(solution)/shard_map/ppermute | solution.py:25
  60.4 7.2 %backward.1 = (bf16[2,192,384]{2,1,0:T(8,128)(2,1)}, bf16[2,192,384]{2,1,0:T(8,128)(2,1)}, bf16[2,192,384]{2,1,0:T(8,128)(2,1)}, bf16[2,192,384]{2,1,0:T(8,128)(2,1)}, bf16[4,400,384]{2,1,0:T(8,128)(2,1)S(1)}) custom-call(bf16[4,128,384]{2,1,0:T(8,128)(2,1)S(1)} %get-tuple-element.54.refs_0_, bf16[4,256,384]{2,1,0:T(8,128)(2,1)} %get-tuple-element.64.refs_1_, ...), custom_call_target="tpu_custom_call" | custom-call | flops 1811939328 | bytes 7077888 | tf_op jit(solution)/shard_map/backward/pallas_call | solution.py:334
  68.1 3.2 %collective-permute-start.19 = (bf16[2,192,384]{2,1,0:T(8,128)(2,1)}, bf16[2,192,384]{2,1,0:T(8,128)(2,1)S(1)}, u32[]{:S(2)}, u32[]{:S(2)}) collective-permute-start(bf16[2,192,384]{2,1,0:T(8,128)(2,1)} %get-tuple-element.77), channel_id=1, source_target_pairs={{0,48},{16,32},{32,16},{48,0},{64,112},{80,96},{96,80},{112,64},{1... | collective-permute-start | bytes 884744 | tf_op jit(solution)/shard_map/ppermute | solution.py:30
  71.3 16.3 %conditional.3 = ((bf16[1,128,384]{2,1,0:T(8,128)(2,1)}, bf16[1,64,384]{2,1,0:T(8,128)(2,1)}, bf16[1,128,384]{2,1,0:T(8,128)(2,1)}, bf16[1,64,384]{2,1,0:T(8,128)(2,1)}, f32[8,384]{1,0:T(8,128)S(1)})) conditional(s32[]{:T(128)} %bitcast.1, () %tuple.24, bf16[4,400,384]{2,1,0:T(8,128)(2,1)S(1)} %get-tuple-element.67), branch_computations={%region_2.0_spmd, %region_3.0_spmd} | conditional | bytes 2457608 | solution.py:411
  71.3 15.6 %all_to_all.4.parts_ref = bf16[4,400,384]{2,1,0:T(8,128)(2,1)S(1)} all-to-all(bf16[4,400,384]{2,1,0:T(8,128)(2,1)S(1)} %param.3), channel_id=1, replica_groups={{0,64,128,192},{16,80,144,208},{32,96,160,224},{48,112,176,240},{1,65,1..., dimensions={0} | all-to-all | bytes 2457600 | tf_op jit(solution)/shard_map/cond/branch_1_fun/all_to_all | solution.py:444
  86.9 0.8 finish_queries.1
  88.3 2.9 %collective-permute-start.14 = (f32[8,384]{1,0:T(8,128)S(1)}, f32[8,384]{1,0:T(8,128)S(1)}, u32[]{:S(2)}, u32[]{:S(2)}) collective-permute-start(f32[8,384]{1,0:T(8,128)S(1)} %get-tuple-element.73), channel_id=1, source_target_pairs={{0,16},{16,0},{32,48},{48,32},{64,80},{80,64},{96,112},{112,96},{1... | collective-permute-start | bytes 36872 | tf_op jit(solution)/shard_map/ppermute | solution.py:30
  91.2 0.9 collective-permute-done.16
  92.1 3.8 %collective-permute-done.15 = f32[8,384]{1,0:T(8,128)S(1)} collective-permute-done((f32[8,384]{1,0:T(8,128)S(1)}, f32[8,384]{1,0:T(8,128)S(1)}, u32[]{:S(2)}, u32[]{:S(2)}) %collective-permute-start.15) | collective-permute-done | bytes 12320 | tf_op jit(solution)/shard_map/ppermute | solution.py:30
  95.9 2.9 %collective-permute-start.17 = (f32[8,384]{1,0:T(8,128)S(1)}, f32[8,384]{1,0:T(8,128)S(1)}, u32[]{:S(2)}, u32[]{:S(2)}) collective-permute-start(f32[8,384]{1,0:T(8,128)S(1)} %add_add_fusion), channel_id=1, source_target_pairs={{0,1},{1,0},{2,3},{3,2},{4,5},{5,4},{6,7},{7,6},{8,9},{9,8},{10,11... | collective-permute-start | bytes 36872 | tf_op jit(solution)/shard_map/ppermute | solution.py:451
  98.8 0.8 finish_keys.1
  (58 shorter events, 6.0 us)
Async XLA Ops:
  2.5 21.2 %copy-start.1 = (bf16[1,128,384]{2,1,0:T(8,128)(2,1)S(1)}, bf16[1,128,384]{2,1,0:T(8,128)(2,1)}, u32[]{:S(2)}) copy-start(bf16[1,128,384]{2,1,0:T(8,128)(2,1)} %up_video_ref.1) | copy-start | bytes 294916
  2.5 21.2 %copy-start.2 = (bf16[1,64,384]{2,1,0:T(8,128)(2,1)S(1)}, bf16[1,64,384]{2,1,0:T(8,128)(2,1)}, u32[]{:S(2)}) copy-start(bf16[1,64,384]{2,1,0:T(8,128)(2,1)} %up_audio_ref.1) | copy-start | bytes 147460
  2.5 21.1 %collective-permute-start.3 = (bf16[2,128,384]{2,1,0:T(8,128)(2,1)S(1)}, bf16[2,128,384]{2,1,0:T(8,128)(2,1)}, u32[]{:S(2)}, u32[]{:S(2)}) collective-permute-start(bf16[2,128,384]{2,1,0:T(8,128)(2,1)S(1)} %get-tuple-element.8), channel_id=1, source_target_pairs={{0,48},{16,32},{32,16},{48,0},{64,112},{80,96},{96,80},{112,64},{1... | collective-permute-start | bytes 589832 | tf_op jit(solution)/shard_map/cond/branch_1_fun/ppermute | solution.py:30
  7.8 15.9 %collective-permute-start.2 = (bf16[2,128,384]{2,1,0:T(8,128)(2,1)S(1)}, bf16[2,128,384]{2,1,0:T(8,128)(2,1)}, u32[]{:S(2)}, u32[]{:S(2)}) collective-permute-start(bf16[2,128,384]{2,1,0:T(8,128)(2,1)S(1)} %get-tuple-element.8), channel_id=1, source_target_pairs={{0,32},{16,48},{32,0},{48,16},{64,96},{80,112},{96,64},{112,80},{1... | collective-permute-start | bytes 589832 | tf_op jit(solution)/shard_map/cond/branch_1_fun/ppermute | solution.py:30
  7.8 15.9 %collective-permute-start.1 = (bf16[2,128,384]{2,1,0:T(8,128)(2,1)S(1)}, bf16[2,128,384]{2,1,0:T(8,128)(2,1)}, u32[]{:S(2)}, u32[]{:S(2)}) collective-permute-start(bf16[2,128,384]{2,1,0:T(8,128)(2,1)S(1)} %get-tuple-element.8), channel_id=1, source_target_pairs={{0,16},{16,0},{32,48},{48,32},{64,80},{80,64},{96,112},{112,96},{1... | collective-permute-start | bytes 589832 | tf_op jit(solution)/shard_map/cond/branch_1_fun/ppermute | solution.py:30
  8.1 15.5 %collective-permute-start = (bf16[3,64,384]{2,1,0:T(8,128)(2,1)S(1)}, bf16[3,64,384]{2,1,0:T(8,128)(2,1)}, u32[]{:S(2)}, u32[]{:S(2)}) collective-permute-start(bf16[3,64,384]{2,1,0:T(8,128)(2,1)S(1)} %get-tuple-element.7), channel_id=1, source_target_pairs={{0,8},{2,40},{4,72},{6,104},{8,136},{10,168},{12,200},{14,232},{16... | collective-permute-start | bytes 442376 | tf_op jit(solution)/shard_map/cond/branch_1_fun/ppermute | solution.py:406
  24.6 20.7 %copy-start.3 = (bf16[256,384]{1,0:T(8,128)(2,1)}, bf16[256,384]{1,0:T(8,128)(2,1)S(1)}, u32[]{:S(2)}) copy-start(bf16[256,384]{1,0:T(8,128)(2,1)S(1)} %get-tuple-element.61.refs_9_) | copy-start | bytes 589828
  24.6 13.0 %collective-permute-start.6 = (bf16[2,64,384]{2,1,0:T(8,128)(2,1)S(1)}, bf16[2,64,384]{2,1,0:T(8,128)(2,1)S(1)}, u32[]{:S(2)}, u32[]{:S(2)}) collective-permute-start(bf16[2,64,384]{2,1,0:T(8,128)(2,1)S(1)} %get-tuple-element.60.refs_5_.refs_6_), channel_id=1, source_target_pairs={{0,48},{16,32},{32,16},{48,0},{64,112},{80,96},{96,80},{112,64},{1... | collective-permute-start | bytes 294920 | tf_op jit(solution)/shard_map/ppermute | solution.py:30
  34.3 11.1 %collective-permute-start.9 = (bf16[256,384]{1,0:T(8,128)(2,1)S(1)}, bf16[256,384]{1,0:T(8,128)(2,1)S(1)}, u32[]{:S(2)}, u32[]{:S(2)}) collective-permute-start(bf16[256,384]{1,0:T(8,128)(2,1)S(1)} %get-tuple-element.61.refs_9_), channel_id=1, source_target_pairs={{0,192},{16,208},{32,224},{48,240},{64,128},{80,144},{96,160},{112... | collective-permute-start | bytes 589832 | tf_op jit(solution)/shard_map/ppermute | solution.py:25
  37.0 8.3 %collective-permute-start.8 = (bf16[256,384]{1,0:T(8,128)(2,1)S(1)}, bf16[256,384]{1,0:T(8,128)(2,1)S(1)}, u32[]{:S(2)}, u32[]{:S(2)}) collective-permute-start(bf16[256,384]{1,0:T(8,128)(2,1)S(1)} %get-tuple-element.61.refs_9_), channel_id=1, source_target_pairs={{0,128},{16,144},{32,160},{48,176},{64,192},{80,208},{96,224},{112... | collective-permute-start | bytes 589832 | tf_op jit(solution)/shard_map/ppermute | solution.py:25
  37.2 8.2 %collective-permute-start.7 = (bf16[256,384]{1,0:T(8,128)(2,1)S(1)}, bf16[256,384]{1,0:T(8,128)(2,1)S(1)}, u32[]{:S(2)}, u32[]{:S(2)}) collective-permute-start(bf16[256,384]{1,0:T(8,128)(2,1)S(1)} %get-tuple-element.61.refs_9_), channel_id=1, source_target_pairs={{0,64},{16,80},{32,96},{48,112},{64,0},{80,16},{96,32},{112,48},{1... | collective-permute-start | bytes 589832 | tf_op jit(solution)/shard_map/ppermute | solution.py:25
  37.6 5.1 %collective-permute-start.5 = (bf16[2,64,384]{2,1,0:T(8,128)(2,1)S(1)}, bf16[2,64,384]{2,1,0:T(8,128)(2,1)S(1)}, u32[]{:S(2)}, u32[]{:S(2)}) collective-permute-start(bf16[2,64,384]{2,1,0:T(8,128)(2,1)S(1)} %get-tuple-element.60.refs_5_.refs_6_), channel_id=1, source_target_pairs={{0,32},{16,48},{32,0},{48,16},{64,96},{80,112},{96,64},{112,80},{1... | collective-permute-start | bytes 294920 | tf_op jit(solution)/shard_map/ppermute | solution.py:30
  37.6 5.1 %collective-permute-start.4 = (bf16[2,64,384]{2,1,0:T(8,128)(2,1)S(1)}, bf16[2,64,384]{2,1,0:T(8,128)(2,1)S(1)}, u32[]{:S(2)}, u32[]{:S(2)}) collective-permute-start(bf16[2,64,384]{2,1,0:T(8,128)(2,1)S(1)} %get-tuple-element.60.refs_5_.refs_6_), channel_id=1, source_target_pairs={{0,16},{16,0},{32,48},{48,32},{64,80},{80,64},{96,112},{112,96},{1... | collective-permute-start | bytes 294920 | tf_op jit(solution)/shard_map/ppermute | solution.py:30
  51.6 5.2 %collective-permute-start.12 = (f32[3,4,768]{2,1,0:T(4,128)}, f32[3,4,768]{2,1,0:T(4,128)S(1)}, u32[]{:S(2)}, u32[]{:S(2)}) collective-permute-start(f32[3,4,768]{2,1,0:T(4,128)} %get-tuple-element.65.refs_10_), channel_id=1, source_target_pairs={{0,192},{16,208},{32,224},{48,240},{64,128},{80,144},{96,160},{112... | collective-permute-start | bytes 110600 | tf_op jit(solution)/shard_map/ppermute | solution.py:25
  55.3 4.5 %collective-permute-start.11 = (f32[3,4,768]{2,1,0:T(4,128)}, f32[3,4,768]{2,1,0:T(4,128)S(1)}, u32[]{:S(2)}, u32[]{:S(2)}) collective-permute-start(f32[3,4,768]{2,1,0:T(4,128)} %get-tuple-element.65.refs_10_), channel_id=1, source_target_pairs={{0,128},{16,144},{32,160},{48,176},{64,192},{80,208},{96,224},{112... | collective-permute-start | bytes 110600 | tf_op jit(solution)/shard_map/ppermute | solution.py:25
  55.3 4.5 %collective-permute-start.10 = (f32[3,4,768]{2,1,0:T(4,128)}, f32[3,4,768]{2,1,0:T(4,128)S(1)}, u32[]{:S(2)}, u32[]{:S(2)}) collective-permute-start(f32[3,4,768]{2,1,0:T(4,128)} %get-tuple-element.65.refs_10_), channel_id=1, source_target_pairs={{0,64},{16,80},{32,96},{48,112},{64,0},{80,16},{96,32},{112,48},{1... | collective-permute-start | bytes 110600 | tf_op jit(solution)/shard_map/ppermute | solution.py:25
  67.7 20.0 %collective-permute-start.13 = (bf16[2,192,384]{2,1,0:T(8,128)(2,1)}, bf16[2,192,384]{2,1,0:T(8,128)(2,1)S(1)}, u32[]{:S(2)}, u32[]{:S(2)}) collective-permute-start(bf16[2,192,384]{2,1,0:T(8,128)(2,1)} %get-tuple-element.72), channel_id=1, source_target_pairs={{0,16},{16,0},{32,48},{48,32},{64,80},{80,64},{96,112},{112,96},{1... | collective-permute-start | bytes 884744 | tf_op jit(solution)/shard_map/ppermute | solution.py:30
  67.8 31.0 %collective-permute-start.18 = (bf16[2,192,384]{2,1,0:T(8,128)(2,1)}, bf16[2,192,384]{2,1,0:T(8,128)(2,1)S(1)}, u32[]{:S(2)}, u32[]{:S(2)}) collective-permute-start(bf16[2,192,384]{2,1,0:T(8,128)(2,1)} %get-tuple-element.76), channel_id=1, source_target_pairs={{0,32},{16,48},{32,0},{48,16},{64,96},{80,112},{96,64},{112,80},{1... | collective-permute-start | bytes 884744 | tf_op jit(solution)/shard_map/ppermute | solution.py:30
  68.1 30.8 %collective-permute-start.19 = (bf16[2,192,384]{2,1,0:T(8,128)(2,1)}, bf16[2,192,384]{2,1,0:T(8,128)(2,1)S(1)}, u32[]{:S(2)}, u32[]{:S(2)}) collective-permute-start(bf16[2,192,384]{2,1,0:T(8,128)(2,1)} %get-tuple-element.77), channel_id=1, source_target_pairs={{0,48},{16,32},{32,16},{48,0},{64,112},{80,96},{96,80},{112,64},{1... | collective-permute-start | bytes 884744 | tf_op jit(solution)/shard_map/ppermute | solution.py:30
  71.3 27.5 %copy-start = (bf16[2,192,384]{2,1,0:T(8,128)(2,1)S(1)}, bf16[2,192,384]{2,1,0:T(8,128)(2,1)}, u32[]{:S(2)}) copy-start(bf16[2,192,384]{2,1,0:T(8,128)(2,1)} %get-tuple-element.74.refs_0_) | copy-start | bytes 884740
  87.6 4.4 %collective-permute-start.16 = (f32[8,384]{1,0:T(8,128)S(1)}, f32[8,384]{1,0:T(8,128)S(1)}, u32[]{:S(2)}, u32[]{:S(2)}) collective-permute-start(f32[8,384]{1,0:T(8,128)S(1)} %get-tuple-element.73), channel_id=1, source_target_pairs={{0,48},{16,32},{32,16},{48,0},{64,112},{80,96},{96,80},{112,64},{1... | collective-permute-start | bytes 36872 | tf_op jit(solution)/shard_map/ppermute | solution.py:30
  87.7 8.2 %collective-permute-start.15 = (f32[8,384]{1,0:T(8,128)S(1)}, f32[8,384]{1,0:T(8,128)S(1)}, u32[]{:S(2)}, u32[]{:S(2)}) collective-permute-start(f32[8,384]{1,0:T(8,128)S(1)} %get-tuple-element.73), channel_id=1, source_target_pairs={{0,32},{16,48},{32,0},{48,16},{64,96},{80,112},{96,64},{112,80},{1... | collective-permute-start | bytes 36872 | tf_op jit(solution)/shard_map/ppermute | solution.py:30
  88.3 7.6 %collective-permute-start.14 = (f32[8,384]{1,0:T(8,128)S(1)}, f32[8,384]{1,0:T(8,128)S(1)}, u32[]{:S(2)}, u32[]{:S(2)}) collective-permute-start(f32[8,384]{1,0:T(8,128)S(1)} %get-tuple-element.73), channel_id=1, source_target_pairs={{0,16},{16,0},{32,48},{48,32},{64,80},{80,64},{96,112},{112,96},{1... | collective-permute-start | bytes 36872 | tf_op jit(solution)/shard_map/ppermute | solution.py:30
  95.9 3.7 %collective-permute-start.17 = (f32[8,384]{1,0:T(8,128)S(1)}, f32[8,384]{1,0:T(8,128)S(1)}, u32[]{:S(2)}, u32[]{:S(2)}) collective-permute-start(f32[8,384]{1,0:T(8,128)S(1)} %add_add_fusion), channel_id=1, source_target_pairs={{0,1},{1,0},{2,3},{3,2},{4,5},{5,4},{6,7},{7,6},{8,9},{9,8},{10,11... | collective-permute-start | bytes 36872 | tf_op jit(solution)/shard_map/ppermute | solution.py:451
  (10 other events, 40.3 us)

commit v17 on v15

--- a/solution.py
+++ b/solution.py
@@ -342,7 +342,7 @@
     return sum(ref[index].astype(F32) for ref in refs)
 
 
-def finish_queries_kernel(parts_ref, video_out, audio_out, video_q, audio_q, gate_ref):
+def finish_queries_kernel(parts_ref, video_out, audio_out, video_q, audio_q):
     video_rows, audio_rows = video_out.shape[1], audio_out.shape[1]
     rows = video_rows + audio_rows
     parts = [parts_ref.at[place] for place in range(SIDE)]
@@ -350,11 +350,26 @@
         first = index * rows
         video[0] = total_of(parts, slice(first, first + video_rows)).astype(BF16)
         audio[0] = total_of(parts, slice(first + video_rows, first + rows)).astype(BF16)
-    gates = total_of(parts, slice(2 * rows, None))
-    width = gates.shape[1]
-    video_gate = jnp.broadcast_to(gates[0:1] + gates[1:2], (4, width))
-    audio_gate = jnp.broadcast_to(gates[4:5] + gates[5:6], (4, width))
+
+
+def gate_sums_kernel(parts_ref, gate_ref):
+    gates = jnp.sum(parts_ref[...].astype(F32), axis=0)
+    video_gate = jnp.broadcast_to(gates[0:1] + gates[1:2], (4, gates.shape[1]))
+    audio_gate = jnp.broadcast_to(gates[4:5] + gates[5:6], (4, gates.shape[1]))
     gate_ref[...] = jnp.concatenate([video_gate, audio_gate], axis=0)
+
+
+def gate_sums(parts):
+    count, rows, width = parts.shape
+    return pl.pallas_call(
+        gate_sums_kernel,
+        grid=(1,),
+        in_specs=[pl.BlockSpec((count, GATE_ROWS, width), lambda i: (0, rows // GATE_ROWS - 1, 0))],
+        out_specs=pl.BlockSpec((8, width), lambda i: (0, 0)),
+        out_shape=like(8, width, kind=F32),
+        compiler_params=pltpu.CompilerParams(vmem_limit_bytes=8 * 2**20),
+        name="gate_sums",
+    )(parts)
 
 
 def finish_queries(parts, video_rows, audio_rows):
@@ -362,7 +377,7 @@
     video, audio = like(1, video_rows, width), like(1, audio_rows, width)
     return pl.pallas_call(
         finish_queries_kernel,
-        out_shape=[video, audio, video, audio, like(8, width, kind=F32)],
+        out_shape=[video, audio, video, audio],
         compiler_params=pltpu.CompilerParams(vmem_limit_bytes=8 * 2**20),
         name="finish_queries",
     )(parts)
@@ -431,11 +446,12 @@
         queries, audio_queries, video_keys, audio_keys, gathered(stats, along_x), gates, audio_len, outputs, video_rows
     )
 
-    def query_results(parts):
-        parts = lax.all_to_all(parts, "vid", 0, 0, axis_index_groups=ALONG_X, tiled=True)
-        return tuple(finish_queries(parts, video_rows, audio_rows))
-
-    video_out, audio_out, grad_video_q, grad_audio_q, gate = fenced(holds, query_results, query_parts)
+    def exchanged(parts):
+        return lax.all_to_all(parts, "vid", 0, 0, axis_index_groups=ALONG_X, tiled=True)
+
+    query_parts = fenced(holds, exchanged, query_parts)
+    gate = gate_sums(query_parts)
+    video_out, audio_out, grad_video_q, grad_audio_q = finish_queries(query_parts, video_rows, audio_rows)
     key_parts = returned(key_parts, along_z)
     gate, key_parts[1] = lax.optimization_barrier((gate, key_parts[1]))
     gate = sum(gathered(gate, along_z))

time: 99.6 us -> 99.5 us (level)
  transfers between devices with their start and end apart: 20 -> 20, of which waited for: 6 -> 6; matrix products, arithmetic and copies ran while one was open for 0% -> 0% of each run, Pallas kernels for 5% -> 6%
where the time goes in v17:
time: 99.5 us; the launch traced here: 99.2 us
  starting transfers between devices  37.7 us (38%)
  blocking collectives  27.9 us (28%)
  Pallas kernels  20 us (20%)
  waiting for transfers between devices  10.1 us (10%)
  local copies, waits for them, and re-layouts  1.87 us (2%)
  between operations  1.47 us (1%)
    ppermute x12, starting transfers between devices, along_z(): return lax.ppermute(array, 'vid', pairs)  22 us
    all_gather x1, blocking collectives, all_along_x(): return lax.all_gather(array, 'vid', axis=0, axis_index_groups=ALONG_X)  14.2 us
    all_to_all x1, blocking collectives, exchanged(): lax.all_to_all(parts, 'vid', 0, 0, axis_index_groups=ALONG_X, tiled=True)  13.8 us
    ppermute x12, waiting for transfers between devices, along_z(): return lax.ppermute(array, 'vid', pairs)  8.16 us
    pallas_call x1, Pallas kernels, attention_backward(): pl.pallas_call(functools.partial(backward_kernel, video_rows), grid=(head...  7.3 us
    ppermute x6, starting transfers between devices, along_x(): return lax.ppermute(array, 'vid', pairs)  6.68 us
    ppermute x1, starting transfers between devices, shards(): other = lax.ppermute(gate, 'pair', [(0, 1), (1, 0)])  6.11 us
    pallas_call x1, Pallas kernels, attention_forward(): pl.pallas_call(functools.partial(forward_kernel, video_rows), grid=(heads...  5.11 us
  transfers between devices with their start and end apart: 20, of which 6 were waited for; matrix products, arithmetic and copies ran while one was open for 0% of the time, Pallas kernels for 6%

profile of v17, /device:TPU:1, one launch (start us, length us, event | category | flops | bytes accessed | tf_op | source)
XLA Modules:
  0.0 99.2 jit_solution(11205384240742829458)
XLA Ops:
  1.3 1.2 %prepare.1 = (bf16[3,64,384]{2,1,0:T(8,128)(2,1)S(1)}, bf16[2,128,384]{2,1,0:T(8,128)(2,1)S(1)}, bf16[256,384]{1,0:T(8,128)(2,1)S(1)}) custom-call(bf16[1,128,3072]{2,1,0:T(8,128)(2,1)} %aq_ref.1, bf16[1,128,3072]{2,1,0:T(8,128)(2,1)} %ak_ref.1, bf16[1,128,3072]{2,1,0:T(8,128)(2,1)} %av_ref.1, bf16[1,128,384]{2,1,0:T(8,128)(2,1)} %vq_ref.1, ...), custom_call_target="tpu_custom_call" | custom-call | tf_op jit(solution)/shard_map/prepare/pallas_call | solution.py:130
  2.5 22.8 %conditional.2 = (bf16[3,64,384]{2,1,0:T(8,128)(2,1)}, bf16[2,128,384]{2,1,0:T(8,128)(2,1)}, bf16[2,128,384]{2,1,0:T(8,128)(2,1)}, bf16[2,128,384]{2,1,0:T(8,128)(2,1)}, bf16[4,256,384]{2,1,0:T(8,128)(2,1)S(1)}) conditional(s32[]{:T(128)} %bitcast.1, () %tuple.24, (bf16[3,64,384]{2,1,0:T(8,128)(2,1)S(1)}, bf16[2,128,384]{2,1,0:T(8,128)(2,1)S(1)}, ...), branch_computations={%region_0.0_spmd, %region_1.0_spmd} | conditional | bytes 3932360 | solution.py:417
  2.5 5.3 %collective-permute-start.3 = (bf16[2,128,384]{2,1,0:T(8,128)(2,1)S(1)}, bf16[2,128,384]{2,1,0:T(8,128)(2,1)}, u32[]{:S(2)}, u32[]{:S(2)}) collective-permute-start(bf16[2,128,384]{2,1,0:T(8,128)(2,1)S(1)} %get-tuple-element.11), channel_id=1, source_target_pairs={{0,48},{16,32},{32,16},{48,0},{64,112},{80,96},{96,80},{112,64},{1... | collective-permute-start | bytes 589832 | tf_op jit(solution)/shard_map/cond/branch_1_fun/ppermute | solution.py:30
  8.2 2.9 %collective-permute-start = (bf16[3,64,384]{2,1,0:T(8,128)(2,1)S(1)}, bf16[3,64,384]{2,1,0:T(8,128)(2,1)}, u32[]{:S(2)}, u32[]{:S(2)}) collective-permute-start(bf16[3,64,384]{2,1,0:T(8,128)(2,1)S(1)} %get-tuple-element.10), channel_id=1, source_target_pairs={{0,8},{2,40},{4,72},{6,104},{8,136},{10,168},{12,200},{14,232},{16... | collective-permute-start | bytes 442376 | tf_op jit(solution)/shard_map/cond/branch_1_fun/ppermute | solution.py:412
  11.1 14.2 %all-gather = bf16[1024,384]{1,0:T(8,128)(2,1)S(1)} all-gather(bf16[256,384]{1,0:T(8,128)(2,1)S(1)} %get-tuple-element.12), channel_id=2, replica_groups={{0,64,128,192},{16,80,144,208},{32,96,160,224},{48,112,176,240},{1,65,1..., dimensions={0}, use_global_device_ids=true | all-gather | bytes 983040 | tf_op jit(solution)/shard_map/cond/branch_1_fun/all_gather | solution.py:34
  25.3 0.9 split_audio.1
  26.3 1.0 collective-permute-start.9
  28.0 1.6 %collective-permute-start.7 = (bf16[2,64,384]{2,1,0:T(8,128)(2,1)S(1)}, bf16[2,64,384]{2,1,0:T(8,128)(2,1)S(1)}, u32[]{:S(2)}, u32[]{:S(2)}) collective-permute-start(bf16[2,64,384]{2,1,0:T(8,128)(2,1)S(1)} %get-tuple-element.63.refs_9_), channel_id=1, source_target_pairs={{0,64},{16,80},{32,96},{48,112},{64,0},{80,16},{96,32},{112,48},{1... | collective-permute-start | bytes 294920 | tf_op jit(solution)/shard_map/ppermute | solution.py:25
  29.6 8.8 %collective-permute-start.6 = (bf16[2,64,384]{2,1,0:T(8,128)(2,1)S(1)}, bf16[2,64,384]{2,1,0:T(8,128)(2,1)S(1)}, u32[]{:S(2)}, u32[]{:S(2)}) collective-permute-start(bf16[2,64,384]{2,1,0:T(8,128)(2,1)S(1)} %get-tuple-element.62.refs_5_.refs_6_), channel_id=1, source_target_pairs={{0,48},{16,32},{32,16},{48,0},{64,112},{80,96},{96,80},{112,64},{1... | collective-permute-start | bytes 294920 | tf_op jit(solution)/shard_map/ppermute | solution.py:30
  38.7 3.9 %forward_video.1 = (bf16[3,128,512]{2,1,0:T(8,128)(2,1)}, f32[3,2,512]{2,1,0:T(2,128)}) custom-call(bf16[4,256,384]{2,1,0:T(8,128)(2,1)S(1)} %get-tuple-element.56.refs_0_, bf16[2,128,384]{2,1,0:T(8,128)(2,1)S(1)} %get-tuple-element.57.refs_1_.refs_2_, bf16[2,128,384]{2,1,0:T(8,128)(2,1)} %get-tuple-element.58.refs_2_.refs_3_, ...), custom_call_target="tpu_custom_call" | custom-call | flops 402653184 | bytes 3145728 | tf_op jit(solution)/shard_map/forward_video/pallas_call | solution.py:285
  42.6 2.2 %collective-permute-done.5.refs_7_.refs_8_ = bf16[2,64,384]{2,1,0:T(8,128)(2,1)S(1)} collective-permute-done((bf16[2,64,384]{2,1,0:T(8,128)(2,1)S(1)}, bf16[2,64,384]{2,1,0:T(8,128)(2,1)S(1)}, u32[]{:S(2)}, u32[]{:S(2)}) %collective-permute-start.5) | collective-permute-done | bytes 98336 | tf_op jit(solution)/shard_map/ppermute | solution.py:30
  45.5 5.1 %forward.1 = (bf16[3,2,128,768]{3,2,1,0:T(8,128)(2,1)}, f32[3,4,768]{2,1,0:T(4,128)}, bf16[4,2,64,384]{3,2,1,0:T(8,128)(2,1)}) custom-call(bf16[4,256,384]{2,1,0:T(8,128)(2,1)S(1)} %get-tuple-element.56.refs_0_, bf16[2,128,384]{2,1,0:T(8,128)(2,1)S(1)} %get-tuple-element.57.refs_1_.refs_2_, bf16[2,128,384]{2,1,0:T(8,128)(2,1)} %get-tuple-element.58.refs_2_.refs_3_, ...), custom_call_target="tpu_custom_call" | custom-call | flops 452984832 | bytes 7077888 | tf_op jit(solution)/shard_map/forward/pallas_call | solution.py:304
  50.7 2.0 %collective-permute-start.11 = (f32[3,4,768]{2,1,0:T(4,128)}, f32[3,4,768]{2,1,0:T(4,128)S(1)}, u32[]{:S(2)}, u32[]{:S(2)}) collective-permute-start(f32[3,4,768]{2,1,0:T(4,128)} %get-tuple-element.67.refs_10_), channel_id=1, source_target_pairs={{0,128},{16,144},{32,160},{48,176},{64,192},{80,208},{96,224},{112... | collective-permute-start | bytes 110600 | tf_op jit(solution)/shard_map/ppermute | solution.py:25
  52.8 1.2 %collective-permute-start.10 = (f32[3,4,768]{2,1,0:T(4,128)}, f32[3,4,768]{2,1,0:T(4,128)S(1)}, u32[]{:S(2)}, u32[]{:S(2)}) collective-permute-start(f32[3,4,768]{2,1,0:T(4,128)} %get-tuple-element.67.refs_10_), channel_id=1, source_target_pairs={{0,64},{16,80},{32,96},{48,112},{64,0},{80,16},{96,32},{112,48},{1... | collective-permute-start | bytes 110600 | tf_op jit(solution)/shard_map/ppermute | solution.py:25
  54.0 1.0 collective-permute-done.12.refs_13_
  56.5 7.3 %backward.1 = (bf16[2,192,384]{2,1,0:T(8,128)(2,1)}, bf16[2,192,384]{2,1,0:T(8,128)(2,1)}, bf16[2,192,384]{2,1,0:T(8,128)(2,1)}, bf16[2,192,384]{2,1,0:T(8,128)(2,1)}, bf16[4,400,384]{2,1,0:T(8,128)(2,1)S(1)}) custom-call(bf16[4,256,384]{2,1,0:T(8,128)(2,1)S(1)} %get-tuple-element.56.refs_0_, bf16[4,2,64,384]{3,2,1,0:T(8,128)(2,1)} %get-tuple-element.66.refs_1_, ...), custom_call_target="tpu_custom_call" | custom-call | flops 1811939328 | bytes 7077888 | tf_op jit(solution)/shard_map/backward/pallas_call | solution.py:325
  64.3 2.3 %collective-permute-start.18 = (bf16[2,192,384]{2,1,0:T(8,128)(2,1)}, bf16[2,192,384]{2,1,0:T(8,128)(2,1)S(1)}, u32[]{:S(2)}, u32[]{:S(2)}) collective-permute-start(bf16[2,192,384]{2,1,0:T(8,128)(2,1)} %get-tuple-element.77), channel_id=1, source_target_pairs={{0,32},{16,48},{32,0},{48,16},{64,96},{80,112},{96,64},{112,80},{1... | collective-permute-start | bytes 884744 | tf_op jit(solution)/shard_map/ppermute | solution.py:30
  67.5 13.8 %conditional.3 = (bf16[4,400,384]{2,1,0:T(8,128)(2,1)S(1)}) conditional(s32[]{:T(128)} %bitcast.1, () %tuple.23, bf16[4,400,384]{2,1,0:T(8,128)(2,1)S(1)} %get-tuple-element.69), branch_computations={%region_2.0_spmd, %region_3.0_spmd} | conditional | bytes 2457608 | solution.py:417
  67.5 13.8 %all_to_all.4 = bf16[4,400,384]{2,1,0:T(8,128)(2,1)S(1)} all-to-all(bf16[4,400,384]{2,1,0:T(8,128)(2,1)S(1)} %param.3), channel_id=1, replica_groups={{0,64,128,192},{16,80,144,208},{32,96,160,224},{48,112,176,240},{1,65,1..., dimensions={0} | all-to-all | bytes 2457600 | tf_op jit(solution)/shard_map/cond/branch_1_fun/all_to_all | solution.py:450
  81.3 1.9 %collective-permute-start.16 = (f32[8,384]{1,0:T(8,128)S(1)}, f32[8,384]{1,0:T(8,128)S(1)}, u32[]{:S(2)}, u32[]{:S(2)}) collective-permute-start(f32[8,384]{1,0:T(8,128)S(1)} %gate_sums.1), channel_id=1, source_target_pairs={{0,48},{16,32},{32,16},{48,0},{64,112},{80,96},{96,80},{112,64},{1... | collective-permute-start | bytes 36872 | tf_op jit(solution)/shard_map/ppermute | solution.py:30
  83.2 1.7 %collective-permute-start.14 = (f32[8,384]{1,0:T(8,128)S(1)}, f32[8,384]{1,0:T(8,128)S(1)}, u32[]{:S(2)}, u32[]{:S(2)}) collective-permute-start(f32[8,384]{1,0:T(8,128)S(1)} %gate_sums.1), channel_id=1, source_target_pairs={{0,16},{16,0},{32,48},{48,32},{64,80},{80,64},{96,112},{112,96},{1... | collective-permute-start | bytes 36872 | tf_op jit(solution)/shard_map/ppermute | solution.py:30
  84.9 1.3 %collective-permute-done.16 = f32[8,384]{1,0:T(8,128)S(1)} collective-permute-done((f32[8,384]{1,0:T(8,128)S(1)}, f32[8,384]{1,0:T(8,128)S(1)}, u32[]{:S(2)}, u32[]{:S(2)}) %collective-permute-start.16) | collective-permute-done | bytes 12320 | tf_op jit(solution)/shard_map/ppermute | solution.py:30
  86.2 4.7 %collective-permute-done.15 = f32[8,384]{1,0:T(8,128)S(1)} collective-permute-done((f32[8,384]{1,0:T(8,128)S(1)}, f32[8,384]{1,0:T(8,128)S(1)}, u32[]{:S(2)}, u32[]{:S(2)}) %collective-permute-start.15) | collective-permute-done | bytes 12320 | tf_op jit(solution)/shard_map/ppermute | solution.py:30
  90.9 6.1 %collective-permute-start.17 = (f32[8,384]{1,0:T(8,128)S(1)}, f32[8,384]{1,0:T(8,128)S(1)}, u32[]{:S(2)}, u32[]{:S(2)}) collective-permute-start(f32[8,384]{1,0:T(8,128)S(1)} %add_add_fusion), channel_id=1, source_target_pairs={{0,1},{1,0},{2,3},{3,2},{4,5},{5,4},{6,7},{7,6},{8,9},{9,8},{10,11... | collective-permute-start | bytes 36872 | tf_op jit(solution)/shard_map/ppermute | solution.py:458
  (57 shorter events, 7.4 us)
Async XLA Ops:
  2.5 22.8 %copy-start.1 = (bf16[1,64,384]{2,1,0:T(8,128)(2,1)S(1)}, bf16[1,64,384]{2,1,0:T(8,128)(2,1)}, u32[]{:S(2)}) copy-start(bf16[1,64,384]{2,1,0:T(8,128)(2,1)} %up_ref.1) | copy-start | bytes 147460
  2.5 22.7 %collective-permute-start.3 = (bf16[2,128,384]{2,1,0:T(8,128)(2,1)S(1)}, bf16[2,128,384]{2,1,0:T(8,128)(2,1)}, u32[]{:S(2)}, u32[]{:S(2)}) collective-permute-start(bf16[2,128,384]{2,1,0:T(8,128)(2,1)S(1)} %get-tuple-element.11), channel_id=1, source_target_pairs={{0,48},{16,32},{32,16},{48,0},{64,112},{80,96},{96,80},{112,64},{1... | collective-permute-start | bytes 589832 | tf_op jit(solution)/shard_map/cond/branch_1_fun/ppermute | solution.py:30
  7.8 17.5 %collective-permute-start.2 = (bf16[2,128,384]{2,1,0:T(8,128)(2,1)S(1)}, bf16[2,128,384]{2,1,0:T(8,128)(2,1)}, u32[]{:S(2)}, u32[]{:S(2)}) collective-permute-start(bf16[2,128,384]{2,1,0:T(8,128)(2,1)S(1)} %get-tuple-element.11), channel_id=1, source_target_pairs={{0,32},{16,48},{32,0},{48,16},{64,96},{80,112},{96,64},{112,80},{1... | collective-permute-start | bytes 589832 | tf_op jit(solution)/shard_map/cond/branch_1_fun/ppermute | solution.py:30
  7.8 17.5 %collective-permute-start.1 = (bf16[2,128,384]{2,1,0:T(8,128)(2,1)S(1)}, bf16[2,128,384]{2,1,0:T(8,128)(2,1)}, u32[]{:S(2)}, u32[]{:S(2)}) collective-permute-start(bf16[2,128,384]{2,1,0:T(8,128)(2,1)S(1)} %get-tuple-element.11), channel_id=1, source_target_pairs={{0,16},{16,0},{32,48},{48,32},{64,80},{80,64},{96,112},{112,96},{1... | collective-permute-start | bytes 589832 | tf_op jit(solution)/shard_map/cond/branch_1_fun/ppermute | solution.py:30
  8.2 17.1 %collective-permute-start = (bf16[3,64,384]{2,1,0:T(8,128)(2,1)S(1)}, bf16[3,64,384]{2,1,0:T(8,128)(2,1)}, u32[]{:S(2)}, u32[]{:S(2)}) collective-permute-start(bf16[3,64,384]{2,1,0:T(8,128)(2,1)S(1)} %get-tuple-element.10), channel_id=1, source_target_pairs={{0,8},{2,40},{4,72},{6,104},{8,136},{10,168},{12,200},{14,232},{16... | collective-permute-start | bytes 442376 | tf_op jit(solution)/shard_map/cond/branch_1_fun/ppermute | solution.py:412
  26.2 18.6 %copy-start.2 = (bf16[2,64,384]{2,1,0:T(8,128)(2,1)}, bf16[2,64,384]{2,1,0:T(8,128)(2,1)S(1)}, u32[]{:S(2)}) copy-start(bf16[2,64,384]{2,1,0:T(8,128)(2,1)S(1)} %get-tuple-element.62.refs_5_.refs_6_) | copy-start | bytes 294916
  26.2 18.6 %copy-start.3 = (bf16[2,64,384]{2,1,0:T(8,128)(2,1)}, bf16[2,64,384]{2,1,0:T(8,128)(2,1)S(1)}, u32[]{:S(2)}) copy-start(bf16[2,64,384]{2,1,0:T(8,128)(2,1)S(1)} %get-tuple-element.63.refs_9_) | copy-start | bytes 294916
  26.3 12.1 %collective-permute-start.9 = (bf16[2,64,384]{2,1,0:T(8,128)(2,1)S(1)}, bf16[2,64,384]{2,1,0:T(8,128)(2,1)S(1)}, u32[]{:S(2)}, u32[]{:S(2)}) collective-permute-start(bf16[2,64,384]{2,1,0:T(8,128)(2,1)S(1)} %get-tuple-element.63.refs_9_), channel_id=1, source_target_pairs={{0,192},{16,208},{32,224},{48,240},{64,128},{80,144},{96,160},{112... | collective-permute-start | bytes 294920 | tf_op jit(solution)/shard_map/ppermute | solution.py:25
  27.2 15.3 %collective-permute-start.8 = (bf16[2,64,384]{2,1,0:T(8,128)(2,1)S(1)}, bf16[2,64,384]{2,1,0:T(8,128)(2,1)S(1)}, u32[]{:S(2)}, u32[]{:S(2)}) collective-permute-start(bf16[2,64,384]{2,1,0:T(8,128)(2,1)S(1)} %get-tuple-element.63.refs_9_), channel_id=1, source_target_pairs={{0,128},{16,144},{32,160},{48,176},{64,192},{80,208},{96,224},{112... | collective-permute-start | bytes 294920 | tf_op jit(solution)/shard_map/ppermute | solution.py:25
  28.0 14.6 %collective-permute-start.7 = (bf16[2,64,384]{2,1,0:T(8,128)(2,1)S(1)}, bf16[2,64,384]{2,1,0:T(8,128)(2,1)S(1)}, u32[]{:S(2)}, u32[]{:S(2)}) collective-permute-start(bf16[2,64,384]{2,1,0:T(8,128)(2,1)S(1)} %get-tuple-element.63.refs_9_), channel_id=1, source_target_pairs={{0,64},{16,80},{32,96},{48,112},{64,0},{80,16},{96,32},{112,48},{1... | collective-permute-start | bytes 294920 | tf_op jit(solution)/shard_map/ppermute | solution.py:25
  29.6 13.0 %collective-permute-start.6 = (bf16[2,64,384]{2,1,0:T(8,128)(2,1)S(1)}, bf16[2,64,384]{2,1,0:T(8,128)(2,1)S(1)}, u32[]{:S(2)}, u32[]{:S(2)}) collective-permute-start(bf16[2,64,384]{2,1,0:T(8,128)(2,1)S(1)} %get-tuple-element.62.refs_5_.refs_6_), channel_id=1, source_target_pairs={{0,48},{16,32},{32,16},{48,0},{64,112},{80,96},{96,80},{112,64},{1... | collective-permute-start | bytes 294920 | tf_op jit(solution)/shard_map/ppermute | solution.py:30
  38.4 6.4 %collective-permute-start.5 = (bf16[2,64,384]{2,1,0:T(8,128)(2,1)S(1)}, bf16[2,64,384]{2,1,0:T(8,128)(2,1)S(1)}, u32[]{:S(2)}, u32[]{:S(2)}) collective-permute-start(bf16[2,64,384]{2,1,0:T(8,128)(2,1)S(1)} %get-tuple-element.62.refs_5_.refs_6_), channel_id=1, source_target_pairs={{0,32},{16,48},{32,0},{48,16},{64,96},{80,112},{96,64},{112,80},{1... | collective-permute-start | bytes 294920 | tf_op jit(solution)/shard_map/ppermute | solution.py:30
  38.4 6.4 %collective-permute-start.4 = (bf16[2,64,384]{2,1,0:T(8,128)(2,1)S(1)}, bf16[2,64,384]{2,1,0:T(8,128)(2,1)S(1)}, u32[]{:S(2)}, u32[]{:S(2)}) collective-permute-start(bf16[2,64,384]{2,1,0:T(8,128)(2,1)S(1)} %get-tuple-element.62.refs_5_.refs_6_), channel_id=1, source_target_pairs={{0,16},{16,0},{32,48},{48,32},{64,80},{80,64},{96,112},{112,96},{1... | collective-permute-start | bytes 294920 | tf_op jit(solution)/shard_map/ppermute | solution.py:30
  50.6 4.3 %collective-permute-start.12 = (f32[3,4,768]{2,1,0:T(4,128)}, f32[3,4,768]{2,1,0:T(4,128)S(1)}, u32[]{:S(2)}, u32[]{:S(2)}) collective-permute-start(f32[3,4,768]{2,1,0:T(4,128)} %get-tuple-element.67.refs_10_), channel_id=1, source_target_pairs={{0,192},{16,208},{32,224},{48,240},{64,128},{80,144},{96,160},{112... | collective-permute-start | bytes 110600 | tf_op jit(solution)/shard_map/ppermute | solution.py:25
  50.7 4.6 %collective-permute-start.11 = (f32[3,4,768]{2,1,0:T(4,128)}, f32[3,4,768]{2,1,0:T(4,128)S(1)}, u32[]{:S(2)}, u32[]{:S(2)}) collective-permute-start(f32[3,4,768]{2,1,0:T(4,128)} %get-tuple-element.67.refs_10_), channel_id=1, source_target_pairs={{0,128},{16,144},{32,160},{48,176},{64,192},{80,208},{96,224},{112... | collective-permute-start | bytes 110600 | tf_op jit(solution)/shard_map/ppermute | solution.py:25
  52.8 3.1 %collective-permute-start.10 = (f32[3,4,768]{2,1,0:T(4,128)}, f32[3,4,768]{2,1,0:T(4,128)S(1)}, u32[]{:S(2)}, u32[]{:S(2)}) collective-permute-start(f32[3,4,768]{2,1,0:T(4,128)} %get-tuple-element.67.refs_10_), channel_id=1, source_target_pairs={{0,64},{16,80},{32,96},{48,112},{64,0},{80,16},{96,32},{112,48},{1... | collective-permute-start | bytes 110600 | tf_op jit(solution)/shard_map/ppermute | solution.py:25
  63.8 17.4 %collective-permute-start.13 = (bf16[2,192,384]{2,1,0:T(8,128)(2,1)}, bf16[2,192,384]{2,1,0:T(8,128)(2,1)S(1)}, u32[]{:S(2)}, u32[]{:S(2)}) collective-permute-start(bf16[2,192,384]{2,1,0:T(8,128)(2,1)} %get-tuple-element.73), channel_id=1, source_target_pairs={{0,16},{16,0},{32,48},{48,32},{64,80},{80,64},{96,112},{112,96},{1... | collective-permute-start | bytes 884744 | tf_op jit(solution)/shard_map/ppermute | solution.py:30
  64.3 33.5 %collective-permute-start.18 = (bf16[2,192,384]{2,1,0:T(8,128)(2,1)}, bf16[2,192,384]{2,1,0:T(8,128)(2,1)S(1)}, u32[]{:S(2)}, u32[]{:S(2)}) collective-permute-start(bf16[2,192,384]{2,1,0:T(8,128)(2,1)} %get-tuple-element.77), channel_id=1, source_target_pairs={{0,32},{16,48},{32,0},{48,16},{64,96},{80,112},{96,64},{112,80},{1... | collective-permute-start | bytes 884744 | tf_op jit(solution)/shard_map/ppermute | solution.py:30
  66.6 31.2 %collective-permute-start.19 = (bf16[2,192,384]{2,1,0:T(8,128)(2,1)}, bf16[2,192,384]{2,1,0:T(8,128)(2,1)S(1)}, u32[]{:S(2)}, u32[]{:S(2)}) collective-permute-start(bf16[2,192,384]{2,1,0:T(8,128)(2,1)} %get-tuple-element.78), channel_id=1, source_target_pairs={{0,48},{16,32},{32,16},{48,0},{64,112},{80,96},{96,80},{112,64},{1... | collective-permute-start | bytes 884744 | tf_op jit(solution)/shard_map/ppermute | solution.py:30
  81.2 16.5 %copy-start = (bf16[2,192,384]{2,1,0:T(8,128)(2,1)S(1)}, bf16[2,192,384]{2,1,0:T(8,128)(2,1)}, u32[]{:S(2)}) copy-start(bf16[2,192,384]{2,1,0:T(8,128)(2,1)} %get-tuple-element.75.refs_0_) | copy-start | bytes 884740
  81.3 4.9 %collective-permute-start.16 = (f32[8,384]{1,0:T(8,128)S(1)}, f32[8,384]{1,0:T(8,128)S(1)}, u32[]{:S(2)}, u32[]{:S(2)}) collective-permute-start(f32[8,384]{1,0:T(8,128)S(1)} %gate_sums.1), channel_id=1, source_target_pairs={{0,48},{16,32},{32,16},{48,0},{64,112},{80,96},{96,80},{112,64},{1... | collective-permute-start | bytes 36872 | tf_op jit(solution)/shard_map/ppermute | solution.py:30
  83.2 7.7 %collective-permute-start.15 = (f32[8,384]{1,0:T(8,128)S(1)}, f32[8,384]{1,0:T(8,128)S(1)}, u32[]{:S(2)}, u32[]{:S(2)}) collective-permute-start(f32[8,384]{1,0:T(8,128)S(1)} %gate_sums.1), channel_id=1, source_target_pairs={{0,32},{16,48},{32,0},{48,16},{64,96},{80,112},{96,64},{112,80},{1... | collective-permute-start | bytes 36872 | tf_op jit(solution)/shard_map/ppermute | solution.py:30
  83.2 7.7 %collective-permute-start.14 = (f32[8,384]{1,0:T(8,128)S(1)}, f32[8,384]{1,0:T(8,128)S(1)}, u32[]{:S(2)}, u32[]{:S(2)}) collective-permute-start(f32[8,384]{1,0:T(8,128)S(1)} %gate_sums.1), channel_id=1, source_target_pairs={{0,16},{16,0},{32,48},{48,32},{64,80},{80,64},{96,112},{112,96},{1... | collective-permute-start | bytes 36872 | tf_op jit(solution)/shard_map/ppermute | solution.py:30
  90.9 7.7 %collective-permute-start.17 = (f32[8,384]{1,0:T(8,128)S(1)}, f32[8,384]{1,0:T(8,128)S(1)}, u32[]{:S(2)}, u32[]{:S(2)}) collective-permute-start(f32[8,384]{1,0:T(8,128)S(1)} %add_add_fusion), channel_id=1, source_target_pairs={{0,1},{1,0},{2,3},{3,2},{4,5},{5,4},{6,7},{7,6},{8,9},{9,8},{10,11... | collective-permute-start | bytes 36872 | tf_op jit(solution)/shard_map/ppermute | solution.py:458
  (9 other events, 16.8 us)
